TPU v7x, 32 devices: a whole 2x2x4 slice. The times are simulated.
32 devices in a mesh: parts: 2 (over y), expert: 16 (over z, x, core), replica: 1.
Axes of the slice: x: 2, y: 2, z: 4, core: 2. Of those that a mesh axis runs over, the one named last changes fastest.
Arguments:
- layer_inputs: bfloat16 [4096, 2048], P(('parts', 'expert', 'replica')), parts along dimension 0, may hold values from -12 to 12, as said below
- specialist_picks: int32 [4096, 8], P(('parts', 'expert', 'replica')), parts along dimension 0, may hold values from 0 to 15, all different within a row
- coefficient_lookup_entry: int32 [4096, 8], P(('parts', 'expert', 'replica')), parts along dimension 0, may hold values from 0 to 255
- dispatch_coefficients: bfloat16 [256], replicated, may hold values from 0.019897461 to 0.59765625
- retained_specialist_flags: int32 [16], replicated, may hold values from 0 to 1, as said below
- specialist_quotas: int32 [16], replicated, may hold values from 24 to 48, as said below
- gating_projection: bfloat16 [16, 2048, 768], P('expert', 'replica'), may hold values from -0.125 to 0.125
- raising_projection: bfloat16 [16, 2048, 768], P('expert', 'replica'), may hold values from -0.125 to 0.125
Outputs:
- gram: float32 [32, 768, 768], P(('parts', 'expert'), 'replica'), parts along dimension 0
- self_cross: float32 [32, 768, 768], P(('parts', 'expert'), 'replica'), parts along dimension 0
- merge_cross: float32 [32, 768, 768], P(('parts', 'expert'), 'replica'), parts along dimension 0
There are 2 independent parts, one for each index of `parts`. A program takes and returns all parts, laid end to end along the dimension named above; an argument that names none is the same for every part. Nothing has to cross between parts.
Inputs may be any that keep to these rules, and one draw needn't show every extreme that they name: `layer_inputs`: tokens of order one with row scales that differ. `retained_specialist_flags`: in every pair of experts 2 j and 2 j + 1 at least one is kept; expert 0 is kept and expert 1 is not. `specialist_quotas`: the largest capacity equals 48.
All inputs are finite; a program needn't handle non-finite values.
Results may differ from a plain program's by a relative error of at most 0.012.
Values may be sent and summed in bfloat16 or wider, within the bound.
No kernel may reach another device: no remote copies, remote signals or barrier semaphores. Data moves between devices by JAX's collectives and lax.ppermute only.
A program may use at most 128 MiB of HBM per device.

v0:
```python
import jax
import jax.numpy as jnp
from jax import lax
from jax.sharding import PartitionSpec as P


def swapped(x, axis, stride):
    return lax.ppermute(x, axis, [(i, i ^ 1 << stride) for i in range(lax.axis_size(axis))])


def hidden_rows(slot_rows, w_gate, w_up):
    gate_out = jnp.einsum("nsd,dh->nsh", slot_rows, w_gate, preferred_element_type=jnp.float32)
    upward = jnp.einsum("nsd,dh->nsh", slot_rows, w_up, preferred_element_type=jnp.float32)
    return (jax.nn.silu(gate_out) * upward).astype(jnp.bfloat16)


def weigh_rows(slot_weights, hidden):
    return (slot_weights[..., None].astype(jnp.float32) * hidden.astype(jnp.float32)).astype(
        jnp.bfloat16
    )


def dispatches_at_position(segment_ordinals, specialist_quotas, position_ordinal):
    specialist_sequence = specialist_quotas.shape[0]
    flat_ids = segment_ordinals.reshape(-1)
    route_total = flat_ids.shape[0]
    indicator_vectors = (
        flat_ids[:, None] == jnp.arange(specialist_sequence, dtype=jnp.int32)[None, :]
    ).astype(jnp.int32)
    before = jnp.cumsum(indicator_vectors, axis=0) - indicator_vectors
    route_rank = jnp.sum(before * indicator_vectors, axis=1)
    dispatch_bound = jnp.sum(indicator_vectors * specialist_quotas[None, :], axis=1)
    target = jnp.where(
        route_rank < dispatch_bound,
        flat_ids * position_ordinal + route_rank,
        specialist_sequence * position_ordinal,
    )
    empty_table = jnp.full((specialist_sequence * position_ordinal,), route_total, jnp.int32)
    return empty_table.at[target].set(jnp.arange(route_total, dtype=jnp.int32), mode="drop")


def shards(
    layer_inputs,
    specialist_picks,
    coefficient_lookup_entry,
    dispatch_coefficients,
    retained_specialist_flags,
    specialist_quotas,
    gating_projection,
    raising_projection,
):
    specialist_sequence = retained_specialist_flags.shape[0]
    replica_count = lax.axis_size("replica")
    tok_rows, top_count = specialist_picks.shape
    model_width = layer_inputs.shape[1]
    position_ordinal = max(4, 3 * tok_rows * top_count // (4 * specialist_sequence))
    own_index = lax.axis_index("expert")
    partner_index = jnp.bitwise_xor(own_index, 1)
    expert_lane = jnp.arange(specialist_sequence, dtype=jnp.int32)
    keep_own = jnp.sum(jnp.where(expert_lane == own_index, retained_specialist_flags, 0))
    keep_partner = jnp.sum(jnp.where(expert_lane == partner_index, retained_specialist_flags, 0))
    keep_flag = keep_own.astype(jnp.bfloat16)
    merge_flag = (keep_own * (1 - keep_partner)).astype(jnp.bfloat16)
    gathered_gate, gathered_up = (
        lax.all_gather(gating_projection, "replica", axis=1, tiled=True),
        lax.all_gather(raising_projection, "replica", axis=1, tiled=True),
    )
    w_gate = gathered_gate[0]
    w_up = gathered_up[0]
    dispatch_sequence = dispatches_at_position(
        specialist_picks, specialist_quotas, position_ordinal
    )
    route_total = tok_rows * top_count
    token_slot = jnp.where(
        dispatch_sequence < route_total, dispatch_sequence // top_count, tok_rows
    )
    padded_tokens = jnp.concatenate(
        [layer_inputs, jnp.zeros((1, model_width), layer_inputs.dtype)], axis=0
    )
    send_rows = padded_tokens[token_slot].reshape(
        specialist_sequence, position_ordinal, model_width
    )
    levels = dispatch_coefficients.shape[0]
    onehot_levels = (
        coefficient_lookup_entry.reshape(-1)[:, None]
        == jnp.arange(levels, dtype=jnp.int32)[None, :]
    ).astype(jnp.bfloat16)
    route_weights = jnp.dot(
        onehot_levels, dispatch_coefficients, preferred_element_type=jnp.float32
    )
    padded_weights = jnp.concatenate([route_weights, jnp.zeros((1,), jnp.float32)], axis=0)
    send_weights = (
        padded_weights[dispatch_sequence]
        .astype(jnp.bfloat16)
        .reshape(specialist_sequence, position_ordinal)
    )
    slot_rows = lax.all_to_all(send_rows, "expert", split_axis=0, concat_axis=0, tiled=True)
    slot_weights = lax.all_to_all(send_weights, "expert", split_axis=0, concat_axis=0, tiled=True)
    own_hidden = hidden_rows(slot_rows, w_gate, w_up)
    arrived, own_hidden, own_weighted = (
        slot_rows,
        own_hidden,
        weigh_rows(slot_weights, own_hidden),
    )
    partner_rows, incoming = swapped((arrived, own_weighted), "expert", 0)
    crossed = hidden_rows(partner_rows, w_gate, w_up)
    hidden_width = own_hidden.shape[-1]
    own_flat = (own_hidden * keep_flag).reshape(-1, hidden_width)
    weighted_flat = own_weighted.reshape(-1, hidden_width)
    crossed_flat = (crossed * merge_flag).reshape(-1, hidden_width)
    incoming_flat = incoming.reshape(-1, hidden_width)
    both_rows = jnp.concatenate([own_flat, crossed_flat], axis=0)
    gram_part = jnp.einsum("mi,mj->ij", both_rows, both_rows, preferred_element_type=jnp.float32)
    self_part = jnp.einsum("mi,mj->ij", own_flat, weighted_flat, preferred_element_type=jnp.float32)
    merge_part = jnp.einsum(
        "mi,mj->ij", crossed_flat, incoming_flat, preferred_element_type=jnp.float32
    )
    shared_rows = lax.psum_scatter(
        jnp.concatenate([gram_part, self_part, merge_part], axis=1),
        "replica",
        scatter_dimension=0,
        tiled=True,
    )
    slot_total = jnp.float32(replica_count * specialist_sequence * position_ordinal)
    shared_rows = shared_rows / slot_total
    gram = shared_rows[:, :hidden_width]
    self_cross = shared_rows[:, hidden_width : 2 * hidden_width]
    merge_cross = shared_rows[:, 2 * hidden_width :]
    return (gram[None], self_cross[None], merge_cross[None])


def solution(mesh):
    in_specs = (
        P(("parts", "expert", "replica"), None),
        P(("parts", "expert", "replica"), None),
        P(("parts", "expert", "replica"), None),
        P(),
        P(),
        P(),
        P("expert", "replica", None),
        P("expert", "replica", None),
    )
    out_specs = (
        P(("parts", "expert"), "replica", None),
        P(("parts", "expert"), "replica", None),
        P(("parts", "expert"), "replica", None),
    )
    return jax.shard_map(shards, mesh=mesh, in_specs=in_specs, out_specs=out_specs, check_vma=False)
```

profile of v0, /device:TPU:0, one launch (start us, length us, event | category | flops | bytes accessed | tf_op | source)
XLA Modules:
  0.0 155.9 jit_solution(16114124232197404021)
XLA Ops:
  0.6 0.8 broadcast_multiply_fusion.1
  1.5 0.9 copy.34
  2.8 4.5 %reduce-window.6 = s32[16,8,128]{2,1,0:T(8,128)S(1)} reduce-window(s32[16,8,128]{2,1,0:T(8,128)S(1)} %fusion.20, s32[]{:T(128)} %constant.19.clone.1), window={size=1x1x128 pad=0_0x0_0x127_0}, to_apply=%region_0.1 | reduce-window | flops 2080768 | bytes 131076 | tf_op jit(solution)/shard_map/reduce-window
  7.7 0.7 select_reduce_fusion
  8.5 4.3 %scatter_custom_fusion = s32[768]{0:T(1024)S(1)} fusion(s32[1024]{0:T(1024)S(1)} %bitcast.72, s32[1024]{0:T(1024)S(1)} %iota.20, s32[]{:T(128)} %constant.17.clone.1), kind=kCustom, calls=%fused_computation.54 | custom fusion | bytes 3076 | tf_op jit(solution)/shard_map/scatter | solution.py:39
  12.8 1.9 %concatenate.12 = bf16[129,2048]{1,0:T(8,128)(2,1)} pad(bf16[128,2048]{1,0:T(8,128)(2,1)} %param.8, bf16[]{:T(256)} %constant.16.clone.1), padding=0_1x0_0 | pad | bytes 1052674 | tf_op jit(solution)/shard_map/concatenate | solution.py:77
  14.7 8.3 %gather_fusion = bf16[768,2048]{1,0:T(8,128)(2,1)} fusion(bf16[129,2048]{1,0:T(8,128)(2,1)} %concatenate.12, s32[1024]{0:T(1024)S(1)} %get-tuple-element.27), kind=kCustom, calls=%fused_computation | custom fusion | bytes 6294528 | tf_op jit(solution)/shard_map/gather | solution.py:80
  23.0 77.4 %all_to_all.11 = bf16[16,48,2048]{2,1,0:T(8,128)(2,1)} all-to-all(bf16[16,48,2048]{2,1,0:T(8,128)(2,1)} %bitcast.64), channel_id=1, replica_groups=mesh['parts'=2,'expert'=16,'replica'=1] {'expert'}, dimensions={0} | all-to-all | bytes 6291456 | tf_op jit(solution)/shard_map/all_to_all | solution.py:97
  100.4 0.8 collective-permute-start
  101.7 5.0 %gather_fusion.1 = bf16[768]{0:T(1024)(128)(2,1)S(1)} fusion(bf16[1025]{0:T(1024)(128)(2,1)S(1)} %pad_maximum_fusion, s32[1024]{0:T(1024)S(1)} %get-tuple-element.26), kind=kCustom, calls=%fused_computation.1 | custom fusion | bytes 6144 | tf_op jit(solution)/shard_map/gather | solution.py:93
  106.7 0.7 convert_element_type.64
  107.4 4.9 %all-to-all-start.1 = ((bf16[16,1,48]{2,1,0:T(2,128)(2,1)}), bf16[16,1,48]{2,1,0:T(2,128)(2,1)S(1)}, u32[]{:S(2)}, u32[]{:S(2)}) async-start(bf16[16,1,48]{2,1,0:T(2,128)(2,1)} %convert_element_type.64), calls=%async_computation.1 | async-start | bytes 16384 | tf_op jit(solution)/shard_map/all_to_all | solution.py:98
  114.9 3.5 %all-to-all-done.1 = bf16[16,1,48]{2,1,0:T(2,128)(2,1)S(1)} async-done(((bf16[16,1,48]{2,1,0:T(2,128)(2,1)}), bf16[16,1,48]{2,1,0:T(2,128)(2,1)S(1)}, u32[]{:S(2)}, u32[]{:S(2)}) %all-to-all-start.1) | async-done | bytes 1568 | tf_op jit(solution)/shard_map/all_to_all | solution.py:98
  118.5 5.4 %fusion.2 = f32[16,48,768]{2,1,0:T(8,128)S(1)} fusion(bf16[16,48,2048]{2,1,0:T(8,128)(2,1)} %all_to_all.11, bf16[1,2048,768]{2,1,0:T(8,128)(2,1)} %param.15), kind=kOutput, calls=%fused_computation.6 | convolution fusion | flops 2415919104 | bytes 8650752 | tf_op jit(solution)/shard_map/nsd,dh->nsh/dot_general | solution.py:13
  123.9 4.8 %multiply_convert_fusion = (bf16[16,48,768]{2,1,0:T(8,128)(2,1)S(1)}, bf16[16,48,768]{2,1,0:T(8,128)(2,1)S(1)}) fusion(f32[16,48]{1,0:T(8,128)S(1)} %bitcast.70, f32[16,48,768]{2,1,0:T(8,128)S(1)} %fusion.2, bf16[16,48,2048]{2,1,0:T(8,128)(2,1)} %all_to_all.11, bf16[1,2048,768]{2,1,0:T(8,128)(2,1)S(1)} %copy-done), kind=kOutput, calls=%fused_computation.19 | convolution fusion | flops 2421227520 | bytes 11013120 | tf_op jit(solution)/shard_map/nsd,dh->nsh/dot_general | solution.py:12
  128.9 1.2 convolution_bitcast_fusion.1
  130.1 4.6 %fusion.4 = f32[16,48,768]{2,1,0:T(8,128)S(1)} fusion(bf16[16,48,2048]{2,1,0:T(8,128)(2,1)} %collective-permute-done, bf16[1,2048,768]{2,1,0:T(8,128)(2,1)S(1)} %copy-done), kind=kOutput, calls=%fused_computation.8 | convolution fusion | flops 2415919104 | bytes 8650752 | tf_op jit(solution)/shard_map/nsd,dh->nsh/dot_general | solution.py:12
  134.7 4.8 %fusion.14 = bf16[16,48,768]{2,1,0:T(8,128)(2,1)S(1)} fusion(f32[16,48,768]{2,1,0:T(8,128)S(1)} %fusion.4, bf16[]{:T(256)S(6)} %convert_element_type.56, bf16[16,48,2048]{2,1,0:T(8,128)(2,1)} %collective-permute-done, bf16[1,2048,768]{2,1,0:T(8,128)(2,1)S(1)} %copy-done.3), kind=kOutput, calls=%fused_computation.24 | convolution fusion | flops 2420047872 | bytes 9830402 | tf_op jit(solution)/shard_map/nsd,dh->nsh/dot_general | solution.py:13
  139.5 2.3 %fusion.8 = f32[768,768]{0,1:T(8,128)S(1)} fusion(bf16[768,768]{1,0:T(8,128)(2,1)S(1)} %bitcast.73, bf16[768,768]{1,0:T(8,128)(2,1)S(1)} %bitcast.65), kind=kOutput, calls=%fused_computation.15 | convolution fusion | flops 1816657920 | bytes 4718592 | tf_op jit(solution)/shard_map/mi,mj->ij/dot_general | solution.py:113
  141.8 1.2 convolution_bitcast_fusion
  143.7 3.1 %slice_bitcast_fusion = (f32[1,768,768]{1,2,0:T(8,128)}, f32[1,768,768]{1,2,0:T(8,128)}, f32[1,768,768]{1,2,0:T(8,128)}) fusion(f32[768,2304]{0,1:T(8,128)S(1)} %maximum_multiply_fusion), kind=kLoop, calls=%fused_computation.12 | loop fusion | bytes 14155776 | tf_op jit(solution)/shard_map/broadcast_in_dim | solution.py:129
  146.8 3.0 %copy.43 = f32[1,768,768]{2,1,0:T(8,128)} copy(f32[1,768,768]{1,2,0:T(8,128)} %get-tuple-element.19) | data formatting | bytes 4718592
  149.8 3.0 %copy.42 = f32[1,768,768]{2,1,0:T(8,128)} copy(f32[1,768,768]{1,2,0:T(8,128)} %get-tuple-element.20) | data formatting | bytes 4718592
  152.9 3.0 %copy.41 = f32[1,768,768]{2,1,0:T(8,128)} copy(f32[1,768,768]{1,2,0:T(8,128)} %get-tuple-element.21) | data formatting | bytes 4718592
  (37 shorter events, 2.9 us)
Async XLA Ops:
  0.6 123.3 %copy-start = (bf16[1,2048,768]{2,1,0:T(8,128)(2,1)S(1)}, bf16[1,2048,768]{2,1,0:T(8,128)(2,1)}, u32[]{:S(2)}) copy-start(bf16[1,2048,768]{2,1,0:T(8,128)(2,1)} %param.14) | copy-start | bytes 9437188
  23.0 78.2 %copy-start.4 = (bf16[256]{0:T(256)(128)(2,1)S(1)}, bf16[256]{0:T(256)(128)(2,1)}, u32[]{:S(2)}) copy-start(bf16[256]{0:T(256)(128)(2,1)} %param.11) | copy-start | bytes 1540
  23.0 78.2 %copy-start.1 = (s32[128,8]{0,1:T(8,128)S(1)}, s32[128,8]{0,1:T(8,128)}, u32[]{:S(2)}) copy-start(s32[128,8]{0,1:T(8,128)} %param.10) | copy-start | bytes 12292
  100.4 11.9 %copy-start.2 = (s32[16]{0:T(128)S(1)}, s32[16]{0:T(128)}, u32[]{:S(2)}) copy-start(s32[16]{0:T(128)} %param.12) | copy-start | bytes 196
  100.4 29.7 %collective-permute-start = (bf16[16,48,2048]{2,1,0:T(8,128)(2,1)}, bf16[16,48,2048]{2,1,0:T(8,128)(2,1)}, u32[]{:S(2)}, u32[]{:S(2)}) collective-permute-start(bf16[16,48,2048]{2,1,0:T(8,128)(2,1)} %all_to_all.11), channel_id=1, source_target_pairs={{0,1},{1,0},{2,3},{3,2},{4,5},{5,4},{6,7},{7,6},{8,9},{9,8},{10,11... | collective-permute-start | bytes 9437192 | tf_op jit(solution)/shard_map/ppermute | solution.py:8
  107.4 11.1 %all-to-all-start.1 = ((bf16[16,1,48]{2,1,0:T(2,128)(2,1)}), bf16[16,1,48]{2,1,0:T(2,128)(2,1)S(1)}, u32[]{:S(2)}, u32[]{:S(2)}) async-start(bf16[16,1,48]{2,1,0:T(2,128)(2,1)} %convert_element_type.64), calls=%async_computation.1 | async-start | bytes 16384 | tf_op jit(solution)/shard_map/all_to_all | solution.py:98
  128.7 13.1 %collective-permute-start.1 = (bf16[16,48,768]{2,1,0:T(8,128)(2,1)S(1)}, bf16[16,48,768]{2,1,0:T(8,128)(2,1)S(1)}, u32[]{:S(2)}, u32[]{:S(2)}) collective-permute-start(bf16[16,48,768]{2,1,0:T(8,128)(2,1)S(1)} %get-tuple-element.24), channel_id=1, source_target_pairs={{0,1},{1,0},{2,3},{3,2},{4,5},{5,4},{6,7},{7,6},{8,9},{9,8},{10,11... | collective-permute-start | bytes 3538952 | tf_op jit(solution)/shard_map/ppermute | solution.py:8
  130.1 4.7 %copy-start.3 = (bf16[1,2048,768]{2,1,0:T(8,128)(2,1)S(1)}, bf16[1,2048,768]{2,1,0:T(8,128)(2,1)}, u32[]{:S(2)}) copy-start(bf16[1,2048,768]{2,1,0:T(8,128)(2,1)} %param.15) | copy-start | bytes 9437188
where the time goes:
time: 157 us; the launch traced here: 156 us
  blocking collectives  77.4 us (49%)
  local copies, waits for them, and re-layouts  34.2 us (22%)
  matrix products  24.6 us (16%)
  other arithmetic  7.65 us (5%)
  starting transfers between devices  5.73 us (4%)
  waiting for transfers between devices  3.55 us (2%)
  between operations  2.82 us (2%)
    all_to_all x1, blocking collectives, shards(): lax.all_to_all(send_rows, 'expert', split_axis=0, concat_axis=0, tiled=True)  77.4 us
    dot_general x2, matrix products, hidden_rows(): jnp.einsum('nsd,dh->nsh', slot_rows, w_up, preferred_element_type=jnp.flo...  10.2 us
    unnamed x16, local copies, waits for them, and re-layouts  10.2 us
    dot_general x2, matrix products, hidden_rows(): jnp.einsum('nsd,dh->nsh', slot_rows, w_gate, preferred_element_type=jnp.f...  9.42 us
    gather x1, local copies, waits for them, and re-layouts, shards(): padded_tokens[token_slot]  8.26 us
    gather x1, local copies, waits for them, and re-layouts, shards(): padded_weights[dispatch_sequence].astype(jnp.bfloat16)  5 us
    all_to_all x1, starting transfers between devices, shards(): lax.all_to_all(send_weights, 'expert', split_axis=0, concat_axis=0, tiled...  4.89 us
    another operation x3, other arithmetic  4.64 us
  transfers between devices with their start and end apart: 3, of which 1 were waited for; matrix products, arithmetic and copies ran while one was open for 19% of the time, Pallas kernels for 0%

commit v1 on v0

--- a/solution.py
+++ b/solution.py
@@ -1,6 +1,10 @@
+import functools
+
 import jax
 import jax.numpy as jnp
 from jax import lax
+from jax.experimental import pallas as pl
+from jax.experimental.pallas import tpu as pltpu
 from jax.sharding import PartitionSpec as P
 
 
@@ -129,6 +133,298 @@
     return (gram[None], self_cross[None], merge_cross[None])
 
 
+def route_table_kernel(quota_ref, pick_ref, entry_ref, coef_ref, out_ref):
+    tokens, top_count = pick_ref.shape
+    experts = out_ref.shape[0]
+    levels = coef_ref.shape[1]
+    picks = pick_ref[...]
+    entries = entry_ref[...]
+    coef = coef_ref[...].astype(jnp.float32)
+    expert_lane = lax.broadcasted_iota(jnp.int32, (tokens, experts), 1)
+    level_lane = lax.broadcasted_iota(jnp.int32, (tokens, levels), 1)
+    chosen = jnp.zeros((tokens, experts), jnp.float32)
+    weight = jnp.zeros((tokens, experts), jnp.float32)
+    for choice in range(top_count):
+        level = entries[:, choice : choice + 1] == level_lane
+        value = jnp.sum(jnp.where(level, coef, 0.0), axis=1, keepdims=True)
+        hit = picks[:, choice : choice + 1] == expert_lane
+        chosen = jnp.where(hit, 1.0, chosen)
+        weight = jnp.where(hit, value, weight)
+    row = lax.broadcasted_iota(jnp.int32, (tokens, tokens), 0)
+    col = lax.broadcasted_iota(jnp.int32, (tokens, tokens), 1)
+
+    def over_tokens(values, token_matrix):
+        return lax.dot_general(
+            values.astype(jnp.bfloat16),
+            token_matrix.astype(jnp.bfloat16),
+            (((0,), (0,)), ((), ())),
+            preferred_element_type=jnp.float32,
+        )
+
+    rank = over_tokens(chosen, jnp.where(row < col, 1.0, 0.0))
+    weight_rows = over_tokens(weight, jnp.where(row == col, 1.0, 0.0))
+    expert_row = lax.broadcasted_iota(jnp.int32, (experts, tokens), 0)
+    bound = jnp.zeros((experts, tokens), jnp.float32)
+    for expert in range(experts):
+        bound = jnp.where(expert_row == expert, quota_ref[expert].astype(jnp.float32), bound)
+    used = jnp.where(rank < bound, weight_rows, 0.0).astype(jnp.bfloat16)
+    one = lax.broadcasted_iota(jnp.int32, (experts, experts), 0)
+    two = lax.broadcasted_iota(jnp.int32, (experts, experts), 1)
+    partner = jnp.where(jnp.bitwise_xor(one, 1) == two, 1.0, 0.0).astype(jnp.bfloat16)
+    out_ref[:, :tokens] = used
+    out_ref[:, tokens:] = jnp.dot(partner, used, preferred_element_type=jnp.float32).astype(
+        jnp.bfloat16
+    )
+
+
+def route_table(picks, entries, coefficients, quotas):
+    experts = quotas.shape[0]
+    tokens = picks.shape[0]
+    vmem = pl.BlockSpec(memory_space=pltpu.VMEM)
+    return pl.pallas_call(
+        route_table_kernel,
+        out_shape=jax.ShapeDtypeStruct((experts, 2 * tokens), jnp.bfloat16),
+        in_specs=[pl.BlockSpec(memory_space=pltpu.SMEM), vmem, vmem, vmem],
+        out_specs=vmem,
+        name="route_table",
+    )(quotas, picks, entries, coefficients[None, :])
+
+
+def hidden_kernel(
+    pair_total, place_ref, table_ref, *refs
+):
+    block_refs = refs[: 2 * pair_total]
+    gate_ref, up_ref, lhs_ref, count_ref, weigh_ref, rows_ref, coef_ref = refs[2 * pair_total :]
+    tokens = block_refs[0].shape[0]
+
+    @pl.when(pl.program_id(0) == 0)
+    def _():
+        core = place_ref[0]
+        keep = place_ref[1].astype(jnp.float32)
+        merge = place_ref[2].astype(jnp.float32)
+        row = lax.broadcasted_iota(jnp.int32, (tokens, tokens), 0)
+        col = lax.broadcasted_iota(jnp.int32, (tokens, tokens), 1)
+        for pair in range(pair_total):
+            for side in range(2):
+                half = core if side == 0 else 1 - core
+                start = pl.multiple_of(2 * pair * tokens + half * tokens, tokens)
+                rows_ref[pl.ds(start, tokens), :] = block_refs[2 * pair + side][...]
+                table = table_ref[place_ref[3 + pair] + side]
+                own = jnp.where(row == col, table[0:1, :], 0.0)
+                partner = jnp.where(row == col, table[1:2, :], 0.0)
+                own = jnp.sum(own, axis=1, keepdims=True)
+                partner = jnp.sum(partner, axis=1, keepdims=True)
+                count = jnp.where(own > 0.0, keep, 0.0) + jnp.where(partner > 0.0, merge, 0.0)
+                fixed = (2 * pair + side) * tokens
+                coef_ref[0, fixed : fixed + tokens, :] = jnp.broadcast_to(count, (tokens, 128))
+                coef_ref[1, fixed : fixed + tokens, :] = jnp.broadcast_to(own, (tokens, 128))
+
+    gate = jnp.dot(rows_ref[...], gate_ref[...], preferred_element_type=jnp.float32)
+    upward = jnp.dot(rows_ref[...], up_ref[...], preferred_element_type=jnp.float32)
+    hidden = (gate / (1.0 + jnp.exp(-gate)) * upward).astype(jnp.bfloat16).astype(jnp.float32)
+    lhs_ref[...] = hidden.T.astype(jnp.bfloat16)
+    for lane in range(0, hidden.shape[1], 128):
+        part = hidden[:, lane : lane + 128]
+        count_ref[:, lane : lane + 128] = (part * coef_ref[0]).astype(jnp.bfloat16)
+        weigh_ref[:, lane : lane + 128] = (part * coef_ref[1]).astype(jnp.bfloat16)
+
+
+def hidden_parts(place, table, blocks, w_gate, w_up, name):
+    pair_total = len(blocks) // 2
+    tokens, width = blocks[0].shape
+    rows = len(blocks) * tokens
+    hidden_width = w_gate.shape[2]
+    tile = 256
+    whole = pl.BlockSpec((tokens, width), lambda j, place: (0, 0))
+    weights = pl.BlockSpec((None, width, tile), lambda j, place: (0, 0, j))
+    out_rows = pl.BlockSpec((rows, tile), lambda j, place: (0, j))
+    row_shape = jax.ShapeDtypeStruct((rows, hidden_width), jnp.bfloat16)
+    return pl.pallas_call(
+        functools.partial(hidden_kernel, pair_total),
+        out_shape=(
+            jax.ShapeDtypeStruct((hidden_width, rows), jnp.bfloat16),
+            row_shape,
+            row_shape,
+        ),
+        grid_spec=pltpu.PrefetchScalarGridSpec(
+            num_scalar_prefetch=1,
+            grid=(hidden_width // tile,),
+            in_specs=[
+                pl.BlockSpec(table.shape, lambda j, place: (0, 0, 0)),
+                *[whole] * len(blocks),
+                weights,
+                weights,
+            ],
+            out_specs=(
+                pl.BlockSpec((tile, rows), lambda j, place: (j, 0)),
+                out_rows,
+                out_rows,
+            ),
+            scratch_shapes=[
+                pltpu.VMEM((rows, width), jnp.bfloat16),
+                pltpu.VMEM((2, rows, 128), jnp.float32),
+            ],
+        ),
+        compiler_params=pltpu.CompilerParams(vmem_limit_bytes=40 << 20),
+        cost_estimate=pl.CostEstimate(
+            flops=4 * rows * width * hidden_width,
+            bytes_accessed=4 * width * hidden_width + 2 * rows * width + 6 * rows * hidden_width,
+            transcendentals=rows * hidden_width,
+        ),
+        name=name,
+    )(place, table, *blocks, w_gate, w_up)
+
+
+def sums_kernel(set_total, part_total, has_base, divisor, scaled, scale_ref, *refs):
+    lhs = refs[:part_total]
+    rest = refs[part_total:]
+    rhs = [rest[part_total * index : part_total * (index + 1)] for index in range(set_total)]
+    rest = rest[part_total * set_total :]
+    bases = rest[:set_total] if has_base else [None] * set_total
+    outs = rest[-set_total:]
+    for index in range(set_total):
+        total = bases[index][...] if has_base else None
+        for left, right in zip(lhs, rhs[index]):
+            term = jnp.dot(left[...], right[...], preferred_element_type=jnp.float32)
+            total = term if total is None else total + term
+        if scaled:
+            total = total * (scale_ref[index].astype(jnp.float32) / divisor)
+        outs[index][...] = total
+
+
+def sums(lhs, rhs_sets, bases, scales, divisor, name):
+    hidden_width = lhs[0].shape[0]
+    tile = 256
+    rows = sum(part.shape[1] for part in lhs)
+    scaled = scales is not None
+    if scaled:
+        shape, out_spec = (1, hidden_width, hidden_width), pl.BlockSpec(
+            (None, hidden_width, tile), lambda j, scale: (0, 0, j)
+        )
+    else:
+        scales = jnp.ones((len(rhs_sets),), jnp.int32)
+        shape, out_spec = (hidden_width, hidden_width), pl.BlockSpec(
+            (hidden_width, tile), lambda j, scale: (0, j)
+        )
+    operands = list(lhs)
+    in_specs = [pl.BlockSpec(part.shape, lambda j, scale: (0, 0)) for part in lhs]
+    for parts in rhs_sets:
+        operands += parts
+        in_specs += [
+            pl.BlockSpec((part.shape[0], tile), lambda j, scale: (0, j)) for part in parts
+        ]
+    for base in bases or ():
+        operands.append(base)
+        in_specs.append(pl.BlockSpec((hidden_width, tile), lambda j, scale: (0, j)))
+    total = len(rhs_sets)
+    return pl.pallas_call(
+        functools.partial(
+            sums_kernel, total, len(lhs), bool(bases), float(divisor), scaled
+        ),
+        out_shape=[jax.ShapeDtypeStruct(shape, jnp.float32)] * total,
+        grid_spec=pltpu.PrefetchScalarGridSpec(
+            num_scalar_prefetch=1,
+            grid=(hidden_width // tile,),
+            in_specs=in_specs,
+            out_specs=[out_spec] * total,
+        ),
+        compiler_params=pltpu.CompilerParams(vmem_limit_bytes=48 << 20),
+        cost_estimate=pl.CostEstimate(
+            flops=2 * total * rows * hidden_width * hidden_width,
+            bytes_accessed=2 * (1 + total) * rows * hidden_width
+            + 4 * total * (2 if bases else 1) * hidden_width * hidden_width,
+            transcendentals=0,
+        ),
+        name=name,
+    )(scales, *operands)
+
+
+def gathered_shards(
+    layer_inputs,
+    specialist_picks,
+    coefficient_lookup_entry,
+    dispatch_coefficients,
+    retained_specialist_flags,
+    specialist_quotas,
+    gating_projection,
+    raising_projection,
+):
+    experts = retained_specialist_flags.shape[0]
+    tok_rows, top_count = specialist_picks.shape
+    position_ordinal = max(4, 3 * tok_rows * top_count // (4 * experts))
+    me = lax.axis_index("expert")
+    core = jnp.bitwise_and(me, 1)
+    expert_lane = jnp.arange(experts, dtype=jnp.int32)
+    keep = jnp.sum(jnp.where(expert_lane == me, retained_specialist_flags, 0))
+    keep_partner = jnp.sum(
+        jnp.where(expert_lane == jnp.bitwise_xor(me, 1), retained_specialist_flags, 0)
+    )
+    merge = keep * (1 - keep_partner)
+    groups = experts // 4
+
+    def along(x):
+        return lax.ppermute(x, "expert", [(i, (i + 4) % experts) for i in range(experts)])
+
+    def back(steps):
+        return jnp.bitwise_and(jnp.remainder(me + experts - 4 * steps, experts), ~1)
+
+    def place(*firsts):
+        return jnp.stack([core, keep, merge, *firsts]).astype(jnp.int32)
+
+    def hidden(firsts, blocks, name):
+        return hidden_parts(
+            place(*firsts), table, blocks, gating_projection, raising_projection, name
+        )
+
+    table = route_table(
+        specialist_picks, coefficient_lookup_entry, dispatch_coefficients, specialist_quotas
+    )
+    line = [layer_inputs, along(layer_inputs)]
+    side = [swapped(layer_inputs, "expert", 1)]
+    other = swapped(layer_inputs, "expert", 0)
+    table = lax.all_to_all(table, "expert", split_axis=0, concat_axis=0, tiled=True)
+    table = table.astype(jnp.float32).reshape(experts, 2, tok_rows)
+    parts = [hidden([back(0)], [layer_inputs, other], "hidden_0")]
+    for step in range(1, groups):
+        if step < groups - 1:
+            line.append(along(line[step]))
+        side.append(swapped(line[step], "expert", 1))
+        blocks = [
+            side[step - 1],
+            swapped(side[step - 1], "expert", 0),
+            line[step],
+            swapped(line[step], "expert", 0),
+        ]
+        firsts = [jnp.bitwise_xor(back(step - 1), 2), back(step)]
+        parts.append(hidden(firsts, blocks, "hidden_%d" % step))
+    blocks = [side[groups - 1], swapped(side[groups - 1], "expert", 0)]
+    last = hidden([jnp.bitwise_xor(back(groups - 1), 2)], blocks, "hidden_last")
+    incoming = [swapped(part[2], "expert", 0) for part in parts]
+    early = sums(
+        [part[0] for part in parts],
+        [[part[1] for part in parts], [part[2] for part in parts], incoming],
+        None,
+        None,
+        1,
+        "early_sums",
+    )
+    divisor = experts * position_ordinal
+    arrived = swapped(last[2], "expert", 0)
+    one = jnp.ones((), jnp.int32)
+    gram, self_cross = sums(
+        [last[0]],
+        [[last[1]], [last[2]]],
+        early[:2],
+        jnp.stack([one, keep]).astype(jnp.int32),
+        divisor,
+        "own_sums",
+    )
+    (merge_cross,) = sums(
+        [last[0]], [[arrived]], early[2:], merge[None].astype(jnp.int32), divisor, "merge_sums"
+    )
+    return gram, self_cross, merge_cross
+
+
 def solution(mesh):
     in_specs = (
         P(("parts", "expert", "replica"), None),
@@ -145,4 +441,6 @@
         P(("parts", "expert"), "replica", None),
         P(("parts", "expert"), "replica", None),
     )
-    return jax.shard_map(shards, mesh=mesh, in_specs=in_specs, out_specs=out_specs, check_vma=False)
+    gather_fits = mesh.shape["replica"] == 1 and mesh.shape["expert"] == 16
+    body = gathered_shards if gather_fits else shards
+    return jax.shard_map(body, mesh=mesh, in_specs=in_specs, out_specs=out_specs, check_vma=False)

time: 157 us -> 126 us (0.80)
  blocking collectives: 77.4 us -> 0 us
  Pallas kernels: 0 us -> 50.6 us
  matrix products: 24.6 us -> 0 us
  waiting for transfers between devices: 3.55 us -> 27.5 us
  starting transfers between devices: 5.73 us -> 16.4 us
  local copies, waits for them, and re-layouts: 34.2 us -> 24.8 us
  other arithmetic: 7.65 us -> 3.98 us
    all_to_all x1 -> x0, blocking collectives: 77.4 us -> none  [shards(): lax.all_to_all(send_rows, 'expert', split_axis=0, concat_axis=0, tiled=True)]
    pallas_call x0 -> x9, Pallas kernels: none -> 50.6 us  [the longest x5 30.8 us: hidden_parts(): pl.pallas_call(functools.partial(hidden_kernel, pair_total), out_shape=(j...]
    ppermute x0 -> x3, waiting for transfers between devices: none -> 25.6 us  [along(): lax.ppermute(x, 'expert', [(i, (i + 4) % experts) for i in range(experts)])]
    dot_general x8 -> x0, matrix products: 24.6 us -> none  [the longest x2 10.2 us: hidden_rows(): jnp.einsum('nsd,dh->nsh', slot_rows, w_up, preferred_element_type=jnp.flo...]
    gather x2 -> x0, local copies, waits for them, and re-layouts: 13.3 us -> none  [the longest x1 8.26 us: shards(): padded_tokens[token_slot]]
    unnamed x16 -> x54, local copies, waits for them, and re-layouts: 10.2 us -> 21.2 us
    ppermute x2 -> x17, starting transfers between devices: 0.84 us -> 7.92 us  [swapped(): lax.ppermute(x, axis, [(i, i ^ 1 << stride) for i in range(lax.axis_size(...]
    scatter x1 -> x0, local copies, waits for them, and re-layouts: 4.31 us -> none  [dispatches_at_position(): empty_table.at[target]]
  transfers between devices with their start and end apart: 3 -> 21, of which waited for: 1 -> 3; matrix products, arithmetic and copies ran while one was open for 19% -> 9% of each run, Pallas kernels for 0% -> 38%
where the time goes in v1:
time: 126 us; the launch traced here: 125 us
  Pallas kernels  50.6 us (40%)
  waiting for transfers between devices  27.5 us (22%)
  local copies, waits for them, and re-layouts  24.8 us (20%)
  starting transfers between devices  16.4 us (13%)
  other arithmetic  3.98 us (3%)
  between operations  2.09 us (2%)
    pallas_call x5, Pallas kernels, hidden_parts(): pl.pallas_call(functools.partial(hidden_kernel, pair_total), out_shape=(j...  30.8 us
    ppermute x3, waiting for transfers between devices, along(): lax.ppermute(x, 'expert', [(i, (i + 4) % experts) for i in range(experts)])  25.6 us
    unnamed x54, local copies, waits for them, and re-layouts  21.2 us
    pallas_call x3, Pallas kernels, sums(): pl.pallas_call(functools.partial(sums_kernel, total, len(lhs), bool(bases...  16.7 us
    ppermute x17, starting transfers between devices, swapped(): lax.ppermute(x, axis, [(i, i ^ 1 << stride) for i in range(lax.axis_size(...  7.92 us
    all_to_all x1, starting transfers between devices, gathered_shards(): lax.all_to_all(table, 'expert', split_axis=0, concat_axis=0, tiled=True)  5.41 us
    ppermute x3, starting transfers between devices, along(): lax.ppermute(x, 'expert', [(i, (i + 4) % experts) for i in range(experts)])  3.08 us
    pallas_call x1, Pallas kernels, route_table(): pl.pallas_call(route_table_kernel, out_shape=jax.ShapeDtypeStruct((expert...  3 us
  transfers between devices with their start and end apart: 21, of which 3 were waited for; matrix products, arithmetic and copies ran while one was open for 9% of the time, Pallas kernels for 38%

profile of v1, /device:TPU:0, one launch (start us, length us, event | category | flops | bytes accessed | tf_op | source)
XLA Modules:
  0.0 125.3 jit_solution(15341918884366917206)
XLA Ops:
  0.6 3.1 %collective-permute-start = (bf16[128,2048]{1,0:T(8,128)(2,1)}, bf16[128,2048]{1,0:T(8,128)(2,1)S(1)}, u32[]{:S(2)}, u32[]{:S(2)}) collective-permute-start(bf16[128,2048]{1,0:T(8,128)(2,1)} %refs_0_.1), channel_id=1, source_target_pairs={{0,4},{1,5},{2,6},{3,7},{4,8},{5,9},{6,10},{7,11},{8,12},{9,13},{1... | collective-permute-start | bytes 1572872 | tf_op jit(solution)/shard_map/ppermute | solution.py:366
  3.7 1.5 %collective-permute-start.6 = (bf16[128,2048]{1,0:T(8,128)(2,1)}, bf16[128,2048]{1,0:T(8,128)(2,1)}, u32[]{:S(2)}, u32[]{:S(2)}) collective-permute-start(bf16[128,2048]{1,0:T(8,128)(2,1)} %refs_0_.1), channel_id=1, source_target_pairs={{0,2},{1,3},{2,0},{3,1},{4,6},{5,7},{6,4},{7,5},{8,10},{9,11},{10,... | collective-permute-start | bytes 1572872 | tf_op jit(solution)/shard_map/ppermute | solution.py:12
  5.2 12.7 %collective-permute-done.refs_2_ = bf16[128,2048]{1,0:T(8,128)(2,1)S(1)} collective-permute-done((bf16[128,2048]{1,0:T(8,128)(2,1)}, bf16[128,2048]{1,0:T(8,128)(2,1)S(1)}, u32[]{:S(2)}, u32[]{:S(2)}) %collective-permute-start) | collective-permute-done | bytes 524320 | tf_op jit(solution)/shard_map/ppermute | solution.py:366
  17.9 1.5 %collective-permute-start.9 = (bf16[128,2048]{1,0:T(8,128)(2,1)S(1)}, bf16[128,2048]{1,0:T(8,128)(2,1)S(1)}, u32[]{:S(2)}, u32[]{:S(2)}) collective-permute-start(bf16[128,2048]{1,0:T(8,128)(2,1)S(1)} %collective-permute-done.refs_2_), channel_id=1, source_target_pairs={{0,2},{1,3},{2,0},{3,1},{4,6},{5,7},{6,4},{7,5},{8,10},{9,11},{10,... | collective-permute-start | bytes 1572872 | tf_op jit(solution)/shard_map/ppermute | solution.py:12
  19.9 12.9 %collective-permute-done.1.refs_2_ = bf16[128,2048]{1,0:T(8,128)(2,1)S(1)} collective-permute-done((bf16[128,2048]{1,0:T(8,128)(2,1)S(1)}, bf16[128,2048]{1,0:T(8,128)(2,1)S(1)}, u32[]{:S(2)}, u32[]{:S(2)}) %collective-permute-start.1) | collective-permute-done | bytes 524320 | tf_op jit(solution)/shard_map/ppermute | solution.py:366
  35.3 1.4 %copy.13.pick_ref = s32[128,8]{1,0:T(8,128)} copy(s32[128,8]{0,1:T(8,128)} %param.9) | data formatting | bytes 8192 | tf_op args[1]
  36.8 1.4 %copy.14.entry_ref = s32[128,8]{1,0:T(8,128)} copy(s32[128,8]{0,1:T(8,128)} %param.10) | data formatting | bytes 8192 | tf_op args[2]
  39.4 3.0 %route_table.1 = bf16[16,256]{1,0:T(8,128)(2,1)} custom-call(s32[16]{0:T(128)} %quota_ref.1, s32[128,8]{1,0:T(8,128)} %copy.13.pick_ref, s32[128,8]{1,0:T(8,128)} %copy.14.entry_ref, bf16[1,256]{1,0:T(2,128)(2,1)} %broadcast_in_dim.10.coef_ref), custom_call_target="tpu_custom_call" | custom-call | tf_op jit(solution)/shard_map/route_table/pallas_call | solution.py:184
  42.9 1.3 %reduce = bf16[16,256]{1,0:T(8,128)(2,1)S(1)} reduce(bf16[16,1,256]{2,0,1:T(8,128)(2,1)} %bitcast.18, bf16[]{:T(256)} %broadcast.5), dimensions={1}, to_apply=%copy.15.reduce_sub_computation | reduce | bytes 16386 | tf_op jit(solution)/shard_map/all_to_all | solution.py:385
  44.8 5.4 %all-to-all-start = ((bf16[16,2,128]{2,1,0:T(2,128)(2,1)}), bf16[16,2,128]{2,1,0:T(2,128)(2,1)S(1)}, u32[]{:S(2)}, u32[]{:S(2)}) async-start(bf16[16,2,128]{2,1,0:T(2,128)(2,1)} %reshape.13), calls=%async_computation | async-start | bytes 16384 | tf_op jit(solution)/shard_map/all_to_all | solution.py:385
  54.7 1.9 %all-to-all-done = bf16[16,2,128]{2,1,0:T(2,128)(2,1)S(1)} async-done(((bf16[16,2,128]{2,1,0:T(2,128)(2,1)}), bf16[16,2,128]{2,1,0:T(2,128)(2,1)S(1)}, u32[]{:S(2)}, u32[]{:S(2)}) %all-to-all-start) | async-done | bytes 8224 | tf_op jit(solution)/shard_map/all_to_all | solution.py:385
  57.3 1.9 %copy-done = bf16[1,2048,768]{2,1,0:T(8,128)(2,1)S(1)} copy-done((bf16[1,2048,768]{2,1,0:T(8,128)(2,1)S(1)}, bf16[1,2048,768]{2,1,0:T(8,128)(2,1)}, u32[]{:S(2)}) %copy-start) | copy-done | bytes 3145752
  59.2 1.9 %copy-done.2 = bf16[1,2048,768]{2,1,0:T(8,128)(2,1)S(1)} copy-done((bf16[1,2048,768]{2,1,0:T(8,128)(2,1)S(1)}, bf16[1,2048,768]{2,1,0:T(8,128)(2,1)}, u32[]{:S(2)}) %copy-start.2) | copy-done | bytes 3145752
  62.1 7.4 %hidden_1.1 = (bf16[768,512]{1,0:T(8,128)(2,1)S(1)}, bf16[512,768]{1,0:T(8,128)(2,1)S(1)}, bf16[512,768]{1,0:T(8,128)(2,1)}) custom-call(s32[5]{0:T(128)S(1)} %stack.74.place_ref, f32[16,2,128]{2,1,0:T(2,128)S(1)} %bitcast.13, bf16[128,2048]{1,0:T(8,128)(2,1)} %collective-permute-done.6.refs_0_, bf16[128,2048]{1,0:T(8,128)(2,1)} %collective-permute-done.7.refs_1_, ...), custom_call_target="tpu_custom_call" | custom-call | flops 3221225472 | bytes 10747904 | tf_op jit(solution)/shard_map/hidden_1/pallas_call | solution.py:242
  72.3 7.4 %hidden_2.1 = (bf16[768,512]{1,0:T(8,128)(2,1)S(1)}, bf16[512,768]{1,0:T(8,128)(2,1)S(1)}, bf16[512,768]{1,0:T(8,128)(2,1)}) custom-call(s32[5]{0:T(128)S(1)} %stack.77.place_ref, f32[16,2,128]{2,1,0:T(2,128)S(1)} %bitcast.14, bf16[128,2048]{1,0:T(8,128)(2,1)S(1)} %collective-permute-done.9.refs_0_, bf16[128,2048]{1,0:T(8,128)(2,1)} %collective-permute-done.10.refs_1_, ...), custom_call_target="tpu_custom_call" | custom-call | flops 3221225472 | bytes 10747904 | tf_op jit(solution)/shard_map/hidden_2/pallas_call | solution.py:242
  81.5 6.4 %hidden_3.1 = (bf16[768,512]{1,0:T(8,128)(2,1)S(1)}, bf16[512,768]{1,0:T(8,128)(2,1)S(1)}, bf16[512,768]{1,0:T(8,128)(2,1)}) custom-call(s32[5]{0:T(128)S(1)} %stack.80.place_ref, f32[16,2,128]{2,1,0:T(2,128)S(1)} %bitcast.15, bf16[128,2048]{1,0:T(8,128)(2,1)S(1)} %collective-permute-done.12.refs_0_, bf16[128,2048]{1,0:T(8,128)(2,1)S(1)} %collective-permute-done.13.refs_1_, ...), custom_call_target="tpu_custom_call" | custom-call | flops 3221225472 | bytes 10747904 | tf_op jit(solution)/shard_map/hidden_3/pallas_call | solution.py:242
  90.8 4.4 %hidden_0.1 = (bf16[768,256]{1,0:T(8,128)(2,1)S(1)}, bf16[256,768]{1,0:T(8,128)(2,1)S(1)}, bf16[256,768]{1,0:T(8,128)(2,1)}) custom-call(s32[4]{0:T(128)S(1)} %get-tuple-element.45.place_ref, f32[16,2,128]{2,1,0:T(2,128)S(1)} %bitcast.16, bf16[128,2048]{1,0:T(8,128)(2,1)S(1)} %copy-done.7, bf16[128,2048]{1,0:T(8,128)(2,1)S(1)} %collective-permute-done.5.refs_1_, ...), custom_call_target="tpu_custom_call" | custom-call | flops 1610612736 | bytes 8519680 | tf_op jit(solution)/shard_map/hidden_0/pallas_call | solution.py:242
  97.9 1.9 %copy-done.3 = bf16[1,2048,768]{2,1,0:T(8,128)(2,1)S(1)} copy-done((bf16[1,2048,768]{2,1,0:T(8,128)(2,1)S(1)}, bf16[1,2048,768]{2,1,0:T(8,128)(2,1)}, u32[]{:S(2)}) %copy-start.3) | copy-done | bytes 3145752
  99.9 5.2 %hidden_last.1 = (bf16[768,256]{1,0:T(8,128)(2,1)S(1)}, bf16[256,768]{1,0:T(8,128)(2,1)S(1)}, bf16[256,768]{1,0:T(8,128)(2,1)S(1)}) custom-call(s32[4]{0:T(128)S(1)} %pad_add_fusion.1.place_ref, f32[16,2,128]{2,1,0:T(2,128)S(1)} %bitcast.17, bf16[128,2048]{1,0:T(8,128)(2,1)} %collective-permute-done.3.refs_0_, ...), custom_call_target="tpu_custom_call" | custom-call | flops 1610612736 | bytes 8519680 | tf_op jit(solution)/shard_map/hidden_last/pallas_call | solution.py:242
  105.3 10.4 %early_sums.1 = (f32[768,768]{1,0:T(8,128)}, f32[768,768]{1,0:T(8,128)}, f32[768,768]{1,0:T(8,128)}) custom-call(s32[3]{0:T(128)S(1)} %broadcast_1_scale_ref.2.scale_ref, bf16[768,256]{1,0:T(8,128)(2,1)S(1)} %copy-done.11, bf16[768,512]{1,0:T(8,128)(2,1)S(1)} %copy-done.15, bf16[768,512]{1,0:T(8,128)(2,1)S(1)} %copy-done.19, ...), custom_call_target="tpu_custom_call" | custom-call | flops 6341787648 | bytes 18087936 | tf_op jit(solution)/shard_map/early_sums/pallas_call | solution.py:320
  115.7 1.7 %copy-done.4 = f32[768,768]{1,0:T(8,128)S(1)} copy-done((f32[768,768]{1,0:T(8,128)S(1)}, f32[768,768]{1,0:T(8,128)}, u32[]{:S(2)}) %copy-start.4) | copy-done | bytes 2359320
  117.4 1.7 %copy-done.5 = f32[768,768]{1,0:T(8,128)S(1)} copy-done((f32[768,768]{1,0:T(8,128)S(1)}, f32[768,768]{1,0:T(8,128)}, u32[]{:S(2)}) %copy-start.5) | copy-done | bytes 2359320
  119.1 3.8 %own_sums.1 = (f32[1,768,768]{2,1,0:T(8,128)}, f32[1,768,768]{2,1,0:T(8,128)}) custom-call(s32[2]{0:T(128)S(1)} %pad_add_fusion.scale_ref, bf16[768,256]{1,0:T(8,128)(2,1)S(1)} %get-tuple-element.23.refs_0_, bf16[256,768]{1,0:T(8,128)(2,1)S(1)} %get-tuple-element.24.refs_1_, bf16[256,768]{1,0:T(8,128)(2,1)S(1)} %get-tuple-element.25.refs_2_, ...), custom_call_target="tpu_custom_call" | custom-call | flops 603979776 | bytes 10616832 | tf_op jit(solution)/shard_map/own_sums/pallas_call | solution.py:320
  122.9 2.4 %merge_sums.1 = f32[1,768,768]{2,1,0:T(8,128)} custom-call(s32[1]{0:T(128)} %bitcast.2.scale_ref, bf16[768,256]{1,0:T(8,128)(2,1)S(1)} %get-tuple-element.23.refs_0_, bf16[256,768]{1,0:T(8,128)(2,1)S(1)} %collective-permute-done.19.refs_1_, f32[768,768]{1,0:T(8,128)S(1)} %copy-done.6), custom_call_target="tpu_custom_call" | custom-call | flops 301989888 | bytes 5505024 | tf_op jit(solution)/shard_map/merge_sums/pallas_call | solution.py:320
  (93 shorter events, 20.6 us)
Async XLA Ops:
  0.6 17.2 %collective-permute-start = (bf16[128,2048]{1,0:T(8,128)(2,1)}, bf16[128,2048]{1,0:T(8,128)(2,1)S(1)}, u32[]{:S(2)}, u32[]{:S(2)}) collective-permute-start(bf16[128,2048]{1,0:T(8,128)(2,1)} %refs_0_.1), channel_id=1, source_target_pairs={{0,4},{1,5},{2,6},{3,7},{4,8},{5,9},{6,10},{7,11},{8,12},{9,13},{1... | collective-permute-start | bytes 1572872 | tf_op jit(solution)/shard_map/ppermute | solution.py:366
  3.7 15.7 %collective-permute-start.6 = (bf16[128,2048]{1,0:T(8,128)(2,1)}, bf16[128,2048]{1,0:T(8,128)(2,1)}, u32[]{:S(2)}, u32[]{:S(2)}) collective-permute-start(bf16[128,2048]{1,0:T(8,128)(2,1)} %refs_0_.1), channel_id=1, source_target_pairs={{0,2},{1,3},{2,0},{3,1},{4,6},{5,7},{6,4},{7,5},{8,10},{9,11},{10,... | collective-permute-start | bytes 1572872 | tf_op jit(solution)/shard_map/ppermute | solution.py:12
  17.9 14.9 %collective-permute-start.1 = (bf16[128,2048]{1,0:T(8,128)(2,1)S(1)}, bf16[128,2048]{1,0:T(8,128)(2,1)S(1)}, u32[]{:S(2)}, u32[]{:S(2)}) collective-permute-start(bf16[128,2048]{1,0:T(8,128)(2,1)S(1)} %collective-permute-done.refs_2_), channel_id=1, source_target_pairs={{0,4},{1,5},{2,6},{3,7},{4,8},{5,9},{6,10},{7,11},{8,12},{9,13},{1... | collective-permute-start | bytes 1572872 | tf_op jit(solution)/shard_map/ppermute | solution.py:366
  17.9 16.2 %collective-permute-start.9 = (bf16[128,2048]{1,0:T(8,128)(2,1)S(1)}, bf16[128,2048]{1,0:T(8,128)(2,1)S(1)}, u32[]{:S(2)}, u32[]{:S(2)}) collective-permute-start(bf16[128,2048]{1,0:T(8,128)(2,1)S(1)} %collective-permute-done.refs_2_), channel_id=1, source_target_pairs={{0,2},{1,3},{2,0},{3,1},{4,6},{5,7},{6,4},{7,5},{8,10},{9,11},{10,... | collective-permute-start | bytes 1572872 | tf_op jit(solution)/shard_map/ppermute | solution.py:12
  19.4 14.7 %collective-permute-start.8 = (bf16[128,2048]{1,0:T(8,128)(2,1)S(1)}, bf16[128,2048]{1,0:T(8,128)(2,1)S(1)}, u32[]{:S(2)}, u32[]{:S(2)}) collective-permute-start(bf16[128,2048]{1,0:T(8,128)(2,1)S(1)} %collective-permute-done.refs_2_), channel_id=1, source_target_pairs={{0,1},{1,0},{2,3},{3,2},{4,5},{5,4},{6,7},{7,6},{8,9},{9,8},{10,11... | collective-permute-start | bytes 1572872 | tf_op jit(solution)/shard_map/ppermute | solution.py:12
  19.4 37.3 %collective-permute-start.7 = (bf16[128,2048]{1,0:T(8,128)(2,1)}, bf16[128,2048]{1,0:T(8,128)(2,1)}, u32[]{:S(2)}, u32[]{:S(2)}) collective-permute-start(bf16[128,2048]{1,0:T(8,128)(2,1)} %collective-permute-done.6.refs_0_), channel_id=1, source_target_pairs={{0,1},{1,0},{2,3},{3,2},{4,5},{5,4},{6,7},{7,6},{8,9},{9,8},{10,11... | collective-permute-start | bytes 1572872 | tf_op jit(solution)/shard_map/ppermute | solution.py:12
  32.8 24.0 %collective-permute-start.2 = (bf16[128,2048]{1,0:T(8,128)(2,1)S(1)}, bf16[128,2048]{1,0:T(8,128)(2,1)S(1)}, u32[]{:S(2)}, u32[]{:S(2)}) collective-permute-start(bf16[128,2048]{1,0:T(8,128)(2,1)S(1)} %collective-permute-done.1.refs_2_), channel_id=1, source_target_pairs={{0,4},{1,5},{2,6},{3,7},{4,8},{5,9},{6,10},{7,11},{8,12},{9,13},{1... | collective-permute-start | bytes 1572872 | tf_op jit(solution)/shard_map/ppermute | solution.py:366
  32.8 24.4 %collective-permute-start.12 = (bf16[128,2048]{1,0:T(8,128)(2,1)S(1)}, bf16[128,2048]{1,0:T(8,128)(2,1)S(1)}, u32[]{:S(2)}, u32[]{:S(2)}) collective-permute-start(bf16[128,2048]{1,0:T(8,128)(2,1)S(1)} %collective-permute-done.1.refs_2_), channel_id=1, source_target_pairs={{0,2},{1,3},{2,0},{3,1},{4,6},{5,7},{6,4},{7,5},{8,10},{9,11},{10,... | collective-permute-start | bytes 1572872 | tf_op jit(solution)/shard_map/ppermute | solution.py:12
  34.0 37.3 %collective-permute-start.11 = (bf16[128,2048]{1,0:T(8,128)(2,1)S(1)}, bf16[128,2048]{1,0:T(8,128)(2,1)}, u32[]{:S(2)}, u32[]{:S(2)}) collective-permute-start(bf16[128,2048]{1,0:T(8,128)(2,1)S(1)} %collective-permute-done.1.refs_2_), channel_id=1, source_target_pairs={{0,1},{1,0},{2,3},{3,2},{4,5},{5,4},{6,7},{7,6},{8,9},{9,8},{10,11... | collective-permute-start | bytes 1572872 | tf_op jit(solution)/shard_map/ppermute | solution.py:12
  34.8 36.9 %collective-permute-start.10 = (bf16[128,2048]{1,0:T(8,128)(2,1)S(1)}, bf16[128,2048]{1,0:T(8,128)(2,1)}, u32[]{:S(2)}, u32[]{:S(2)}) collective-permute-start(bf16[128,2048]{1,0:T(8,128)(2,1)S(1)} %collective-permute-done.9.refs_0_), channel_id=1, source_target_pairs={{0,1},{1,0},{2,3},{3,2},{4,5},{5,4},{6,7},{7,6},{8,9},{9,8},{10,11... | collective-permute-start | bytes 1572872 | tf_op jit(solution)/shard_map/ppermute | solution.py:12
  44.8 11.8 %all-to-all-start = ((bf16[16,2,128]{2,1,0:T(2,128)(2,1)}), bf16[16,2,128]{2,1,0:T(2,128)(2,1)S(1)}, u32[]{:S(2)}, u32[]{:S(2)}) async-start(bf16[16,2,128]{2,1,0:T(2,128)(2,1)} %reshape.13), calls=%async_computation | async-start | bytes 16384 | tf_op jit(solution)/shard_map/all_to_all | solution.py:385
  56.6 34.2 %collective-permute-start.5 = (bf16[128,2048]{1,0:T(8,128)(2,1)}, bf16[128,2048]{1,0:T(8,128)(2,1)S(1)}, u32[]{:S(2)}, u32[]{:S(2)}) collective-permute-start(bf16[128,2048]{1,0:T(8,128)(2,1)} %refs_0_.1), channel_id=1, source_target_pairs={{0,1},{1,0},{2,3},{3,2},{4,5},{5,4},{6,7},{7,6},{8,9},{9,8},{10,11... | collective-permute-start | bytes 1572872 | tf_op jit(solution)/shard_map/ppermute | solution.py:12
  56.7 24.7 %collective-permute-start.14 = (bf16[128,2048]{1,0:T(8,128)(2,1)S(1)}, bf16[128,2048]{1,0:T(8,128)(2,1)S(1)}, u32[]{:S(2)}, u32[]{:S(2)}) collective-permute-start(bf16[128,2048]{1,0:T(8,128)(2,1)S(1)} %collective-permute-done.2.refs_2_), channel_id=1, source_target_pairs={{0,1},{1,0},{2,3},{3,2},{4,5},{5,4},{6,7},{7,6},{8,9},{9,8},{10,11... | collective-permute-start | bytes 1572872 | tf_op jit(solution)/shard_map/ppermute | solution.py:12
  57.2 24.3 %collective-permute-start.13 = (bf16[128,2048]{1,0:T(8,128)(2,1)S(1)}, bf16[128,2048]{1,0:T(8,128)(2,1)S(1)}, u32[]{:S(2)}, u32[]{:S(2)}) collective-permute-start(bf16[128,2048]{1,0:T(8,128)(2,1)S(1)} %collective-permute-done.12.refs_0_), channel_id=1, source_target_pairs={{0,1},{1,0},{2,3},{3,2},{4,5},{5,4},{6,7},{7,6},{8,9},{9,8},{10,11... | collective-permute-start | bytes 1572872 | tf_op jit(solution)/shard_map/ppermute | solution.py:12
  71.3 33.8 %collective-permute-start.16 = (bf16[512,768]{1,0:T(8,128)(2,1)}, bf16[512,768]{1,0:T(8,128)(2,1)}, u32[]{:S(2)}, u32[]{:S(2)}) collective-permute-start(bf16[512,768]{1,0:T(8,128)(2,1)} %get-tuple-element.35.refs_9_), channel_id=1, source_target_pairs={{0,1},{1,0},{2,3},{3,2},{4,5},{5,4},{6,7},{7,6},{8,9},{9,8},{10,11... | collective-permute-start | bytes 2359304 | tf_op jit(solution)/shard_map/ppermute | solution.py:12
  71.8 18.4 %collective-permute-start.3 = (bf16[128,2048]{1,0:T(8,128)(2,1)S(1)}, bf16[128,2048]{1,0:T(8,128)(2,1)}, u32[]{:S(2)}, u32[]{:S(2)}) collective-permute-start(bf16[128,2048]{1,0:T(8,128)(2,1)S(1)} %collective-permute-done.2.refs_2_), channel_id=1, source_target_pairs={{0,2},{1,3},{2,0},{3,1},{4,6},{5,7},{6,4},{7,5},{8,10},{9,11},{10,... | collective-permute-start | bytes 1572872 | tf_op jit(solution)/shard_map/ppermute | solution.py:12
  81.5 9.3 %copy-start.7 = (bf16[128,2048]{1,0:T(8,128)(2,1)S(1)}, bf16[128,2048]{1,0:T(8,128)(2,1)}, u32[]{:S(2)}) copy-start(bf16[128,2048]{1,0:T(8,128)(2,1)} %refs_0_.1) | copy-start | bytes 1572868
  81.5 23.7 %collective-permute-start.17 = (bf16[512,768]{1,0:T(8,128)(2,1)}, bf16[512,768]{1,0:T(8,128)(2,1)}, u32[]{:S(2)}, u32[]{:S(2)}) collective-permute-start(bf16[512,768]{1,0:T(8,128)(2,1)} %get-tuple-element.36.refs_10_), channel_id=1, source_target_pairs={{0,1},{1,0},{2,3},{3,2},{4,5},{5,4},{6,7},{7,6},{8,9},{9,8},{10,11... | collective-permute-start | bytes 2359304 | tf_op jit(solution)/shard_map/ppermute | solution.py:12
  89.7 15.5 %collective-permute-start.18 = (bf16[512,768]{1,0:T(8,128)(2,1)}, bf16[512,768]{1,0:T(8,128)(2,1)}, u32[]{:S(2)}, u32[]{:S(2)}) collective-permute-start(bf16[512,768]{1,0:T(8,128)(2,1)} %get-tuple-element.37.refs_11_), channel_id=1, source_target_pairs={{0,1},{1,0},{2,3},{3,2},{4,5},{5,4},{6,7},{7,6},{8,9},{9,8},{10,11... | collective-permute-start | bytes 2359304 | tf_op jit(solution)/shard_map/ppermute | solution.py:12
  90.2 7.8 %collective-permute-start.4 = (bf16[128,2048]{1,0:T(8,128)(2,1)}, bf16[128,2048]{1,0:T(8,128)(2,1)}, u32[]{:S(2)}, u32[]{:S(2)}) collective-permute-start(bf16[128,2048]{1,0:T(8,128)(2,1)} %collective-permute-done.3.refs_0_), channel_id=1, source_target_pairs={{0,1},{1,0},{2,3},{3,2},{4,5},{5,4},{6,7},{7,6},{8,9},{9,8},{10,11... | collective-permute-start | bytes 1572872 | tf_op jit(solution)/shard_map/ppermute | solution.py:12
  90.8 7.1 %copy-start.1 = (bf16[1,2048,768]{2,1,0:T(8,128)(2,1)S(1)}, bf16[1,2048,768]{2,1,0:T(8,128)(2,1)}, u32[]{:S(2)}) copy-start(bf16[1,2048,768]{2,1,0:T(8,128)(2,1)} %refs_4_.5) | copy-start | bytes 9437188
  96.7 8.4 %collective-permute-start.15 = (bf16[256,768]{1,0:T(8,128)(2,1)}, bf16[256,768]{1,0:T(8,128)(2,1)}, u32[]{:S(2)}, u32[]{:S(2)}) collective-permute-start(bf16[256,768]{1,0:T(8,128)(2,1)} %get-tuple-element.34.refs_8_), channel_id=1, source_target_pairs={{0,1},{1,0},{2,3},{3,2},{4,5},{5,4},{6,7},{7,6},{8,9},{9,8},{10,11... | collective-permute-start | bytes 1179656 | tf_op jit(solution)/shard_map/ppermute | solution.py:12
  99.8 5.4 %copy-start.19 = (bf16[768,512]{1,0:T(8,128)(2,1)S(1)}, bf16[768,512]{1,0:T(8,128)(2,1)}, u32[]{:S(2)}) copy-start(bf16[768,512]{1,0:T(8,128)(2,1)} %copy-done.18) | copy-start | bytes 2359300
  105.1 17.8 %collective-permute-start.19 = (bf16[256,768]{1,0:T(8,128)(2,1)S(1)}, bf16[256,768]{1,0:T(8,128)(2,1)S(1)}, u32[]{:S(2)}, u32[]{:S(2)}) collective-permute-start(bf16[256,768]{1,0:T(8,128)(2,1)S(1)} %get-tuple-element.25.refs_2_), channel_id=1, source_target_pairs={{0,1},{1,0},{2,3},{3,2},{4,5},{5,4},{6,7},{7,6},{8,9},{9,8},{10,11... | collective-permute-start | bytes 1179656 | tf_op jit(solution)/shard_map/ppermute | solution.py:12
  (22 other events, 53.9 us)

commit v2 on v1

--- a/solution.py
+++ b/solution.py
@@ -133,41 +133,34 @@
     return (gram[None], self_cross[None], merge_cross[None])
 
 
+VMEM_GRANT = 60 << 20
+
+
 def route_table_kernel(quota_ref, pick_ref, entry_ref, coef_ref, out_ref):
-    tokens, top_count = pick_ref.shape
+    top_count, tokens = pick_ref.shape
     experts = out_ref.shape[0]
     levels = coef_ref.shape[1]
     picks = pick_ref[...]
     entries = entry_ref[...]
-    coef = coef_ref[...].astype(jnp.float32)
-    expert_lane = lax.broadcasted_iota(jnp.int32, (tokens, experts), 1)
-    level_lane = lax.broadcasted_iota(jnp.int32, (tokens, levels), 1)
-    chosen = jnp.zeros((tokens, experts), jnp.float32)
-    weight = jnp.zeros((tokens, experts), jnp.float32)
+    coef = coef_ref[...]
+    expert_row = lax.broadcasted_iota(jnp.int32, (experts, tokens), 0)
+    level_row = lax.broadcasted_iota(jnp.int32, (levels, tokens), 0)
+    chosen = jnp.zeros((experts, tokens), jnp.float32)
+    weight = jnp.zeros((experts, tokens), jnp.float32)
     for choice in range(top_count):
-        level = entries[:, choice : choice + 1] == level_lane
-        value = jnp.sum(jnp.where(level, coef, 0.0), axis=1, keepdims=True)
-        hit = picks[:, choice : choice + 1] == expert_lane
+        level = jnp.where(entries[choice : choice + 1, :] == level_row, 1.0, 0.0)
+        value = jnp.dot(coef, level.astype(jnp.bfloat16), preferred_element_type=jnp.float32)
+        hit = picks[choice : choice + 1, :] == expert_row
         chosen = jnp.where(hit, 1.0, chosen)
         weight = jnp.where(hit, value, weight)
     row = lax.broadcasted_iota(jnp.int32, (tokens, tokens), 0)
     col = lax.broadcasted_iota(jnp.int32, (tokens, tokens), 1)
-
-    def over_tokens(values, token_matrix):
-        return lax.dot_general(
-            values.astype(jnp.bfloat16),
-            token_matrix.astype(jnp.bfloat16),
-            (((0,), (0,)), ((), ())),
-            preferred_element_type=jnp.float32,
-        )
-
-    rank = over_tokens(chosen, jnp.where(row < col, 1.0, 0.0))
-    weight_rows = over_tokens(weight, jnp.where(row == col, 1.0, 0.0))
-    expert_row = lax.broadcasted_iota(jnp.int32, (experts, tokens), 0)
+    earlier = jnp.where(row < col, 1.0, 0.0).astype(jnp.bfloat16)
+    rank = jnp.dot(chosen.astype(jnp.bfloat16), earlier, preferred_element_type=jnp.float32)
     bound = jnp.zeros((experts, tokens), jnp.float32)
     for expert in range(experts):
         bound = jnp.where(expert_row == expert, quota_ref[expert].astype(jnp.float32), bound)
-    used = jnp.where(rank < bound, weight_rows, 0.0).astype(jnp.bfloat16)
+    used = jnp.where(rank < bound, weight, 0.0).astype(jnp.bfloat16)
     one = lax.broadcasted_iota(jnp.int32, (experts, experts), 0)
     two = lax.broadcasted_iota(jnp.int32, (experts, experts), 1)
     partner = jnp.where(jnp.bitwise_xor(one, 1) == two, 1.0, 0.0).astype(jnp.bfloat16)
@@ -187,12 +180,10 @@
         in_specs=[pl.BlockSpec(memory_space=pltpu.SMEM), vmem, vmem, vmem],
         out_specs=vmem,
         name="route_table",
-    )(quotas, picks, entries, coefficients[None, :])
-
-
-def hidden_kernel(
-    pair_total, place_ref, table_ref, *refs
-):
+    )(quotas, picks.T, entries.T, coefficients[None, :])
+
+
+def hidden_kernel(pair_total, first_slot, place_ref, table_ref, *refs):
     block_refs = refs[: 2 * pair_total]
     gate_ref, up_ref, lhs_ref, count_ref, weigh_ref, rows_ref, coef_ref = refs[2 * pair_total :]
     tokens = block_refs[0].shape[0]
@@ -204,14 +195,17 @@
         merge = place_ref[2].astype(jnp.float32)
         row = lax.broadcasted_iota(jnp.int32, (tokens, tokens), 0)
         col = lax.broadcasted_iota(jnp.int32, (tokens, tokens), 1)
+        table_row = lax.broadcasted_iota(jnp.int32, table_ref.shape, 0)
         for pair in range(pair_total):
             for side in range(2):
                 half = core if side == 0 else 1 - core
                 start = pl.multiple_of(2 * pair * tokens + half * tokens, tokens)
                 rows_ref[pl.ds(start, tokens), :] = block_refs[2 * pair + side][...]
-                table = table_ref[place_ref[3 + pair] + side]
-                own = jnp.where(row == col, table[0:1, :], 0.0)
-                partner = jnp.where(row == col, table[1:2, :], 0.0)
+                source = place_ref[first_slot + pair] + side
+                weights = jnp.where(table_row == source, table_ref[...].astype(jnp.float32), 0.0)
+                weights = jnp.sum(weights, axis=0, keepdims=True)
+                own = jnp.where(row == col, weights[:, :tokens], 0.0)
+                partner = jnp.where(row == col, weights[:, tokens:], 0.0)
                 own = jnp.sum(own, axis=1, keepdims=True)
                 partner = jnp.sum(partner, axis=1, keepdims=True)
                 count = jnp.where(own > 0.0, keep, 0.0) + jnp.where(partner > 0.0, merge, 0.0)
@@ -229,7 +223,7 @@
         weigh_ref[:, lane : lane + 128] = (part * coef_ref[1]).astype(jnp.bfloat16)
 
 
-def hidden_parts(place, table, blocks, w_gate, w_up, name):
+def hidden_parts(place, first_slot, table, blocks, w_gate, w_up, name):
     pair_total = len(blocks) // 2
     tokens, width = blocks[0].shape
     rows = len(blocks) * tokens
@@ -240,7 +234,7 @@
     out_rows = pl.BlockSpec((rows, tile), lambda j, place: (0, j))
     row_shape = jax.ShapeDtypeStruct((rows, hidden_width), jnp.bfloat16)
     return pl.pallas_call(
-        functools.partial(hidden_kernel, pair_total),
+        functools.partial(hidden_kernel, pair_total, first_slot),
         out_shape=(
             jax.ShapeDtypeStruct((hidden_width, rows), jnp.bfloat16),
             row_shape,
@@ -250,7 +244,7 @@
             num_scalar_prefetch=1,
             grid=(hidden_width // tile,),
             in_specs=[
-                pl.BlockSpec(table.shape, lambda j, place: (0, 0, 0)),
+                pl.BlockSpec(table.shape, lambda j, place: (0, 0)),
                 *[whole] * len(blocks),
                 weights,
                 weights,
@@ -265,7 +259,7 @@
                 pltpu.VMEM((2, rows, 128), jnp.float32),
             ],
         ),
-        compiler_params=pltpu.CompilerParams(vmem_limit_bytes=40 << 20),
+        compiler_params=pltpu.CompilerParams(vmem_limit_bytes=VMEM_GRANT),
         cost_estimate=pl.CostEstimate(
             flops=4 * rows * width * hidden_width,
             bytes_accessed=4 * width * hidden_width + 2 * rows * width + 6 * rows * hidden_width,
@@ -275,7 +269,7 @@
     )(place, table, *blocks, w_gate, w_up)
 
 
-def sums_kernel(set_total, part_total, has_base, divisor, scaled, scale_ref, *refs):
+def sums_kernel(set_total, part_total, has_base, divisor, slots, scale_ref, *refs):
     lhs = refs[:part_total]
     rest = refs[part_total:]
     rhs = [rest[part_total * index : part_total * (index + 1)] for index in range(set_total)]
@@ -287,22 +281,21 @@
         for left, right in zip(lhs, rhs[index]):
             term = jnp.dot(left[...], right[...], preferred_element_type=jnp.float32)
             total = term if total is None else total + term
-        if scaled:
-            total = total * (scale_ref[index].astype(jnp.float32) / divisor)
+        if slots is not None:
+            factor = 1.0 if slots[index] is None else scale_ref[slots[index]].astype(jnp.float32)
+            total = total * (factor / divisor)
         outs[index][...] = total
 
 
-def sums(lhs, rhs_sets, bases, scales, divisor, name):
+def sums(place, lhs, rhs_sets, bases, slots, divisor, name):
     hidden_width = lhs[0].shape[0]
     tile = 256
     rows = sum(part.shape[1] for part in lhs)
-    scaled = scales is not None
-    if scaled:
+    if slots is not None:
         shape, out_spec = (1, hidden_width, hidden_width), pl.BlockSpec(
             (None, hidden_width, tile), lambda j, scale: (0, 0, j)
         )
     else:
-        scales = jnp.ones((len(rhs_sets),), jnp.int32)
         shape, out_spec = (hidden_width, hidden_width), pl.BlockSpec(
             (hidden_width, tile), lambda j, scale: (0, j)
         )
@@ -319,7 +312,7 @@
     total = len(rhs_sets)
     return pl.pallas_call(
         functools.partial(
-            sums_kernel, total, len(lhs), bool(bases), float(divisor), scaled
+            sums_kernel, total, len(lhs), bool(bases), float(divisor), slots
         ),
         out_shape=[jax.ShapeDtypeStruct(shape, jnp.float32)] * total,
         grid_spec=pltpu.PrefetchScalarGridSpec(
@@ -328,7 +321,7 @@
             in_specs=in_specs,
             out_specs=[out_spec] * total,
         ),
-        compiler_params=pltpu.CompilerParams(vmem_limit_bytes=48 << 20),
+        compiler_params=pltpu.CompilerParams(vmem_limit_bytes=VMEM_GRANT),
         cost_estimate=pl.CostEstimate(
             flops=2 * total * rows * hidden_width * hidden_width,
             bytes_accessed=2 * (1 + total) * rows * hidden_width
@@ -336,7 +329,7 @@
             transcendentals=0,
         ),
         name=name,
-    )(scales, *operands)
+    )(place, *operands)
 
 
 def gathered_shards(
@@ -361,6 +354,7 @@
     )
     merge = keep * (1 - keep_partner)
     groups = experts // 4
+    divisor = experts * position_ordinal
 
     def along(x):
         return lax.ppermute(x, "expert", [(i, (i + 4) % experts) for i in range(experts)])
@@ -368,59 +362,62 @@
     def back(steps):
         return jnp.bitwise_and(jnp.remainder(me + experts - 4 * steps, experts), ~1)
 
-    def place(*firsts):
-        return jnp.stack([core, keep, merge, *firsts]).astype(jnp.int32)
-
-    def hidden(firsts, blocks, name):
+    firsts = [back(0)]
+    for step in range(1, groups):
+        firsts += [jnp.bitwise_xor(back(step - 1), 2), back(step)]
+    firsts.append(jnp.bitwise_xor(back(groups - 1), 2))
+    place = jnp.stack([core, keep, merge, *firsts]).astype(jnp.int32)
+
+    def hidden(slot, blocks, name):
         return hidden_parts(
-            place(*firsts), table, blocks, gating_projection, raising_projection, name
+            place, 3 + slot, table, blocks, gating_projection, raising_projection, name
         )
 
+    def other(x):
+        return swapped(x, "expert", 0)
+
+    def totals(parts, bases, name):
+        return sums(
+            place,
+            [part[0] for part in parts],
+            [[part[index] for part in parts] for index in (1, 2, 3)],
+            bases,
+            None,
+            1,
+            name,
+        )
+
+    line, side = along(layer_inputs), swapped(layer_inputs, "expert", 1)
+    near = other(layer_inputs)
     table = route_table(
         specialist_picks, coefficient_lookup_entry, dispatch_coefficients, specialist_quotas
     )
-    line = [layer_inputs, along(layer_inputs)]
-    side = [swapped(layer_inputs, "expert", 1)]
-    other = swapped(layer_inputs, "expert", 0)
     table = lax.all_to_all(table, "expert", split_axis=0, concat_axis=0, tiled=True)
-    table = table.astype(jnp.float32).reshape(experts, 2, tok_rows)
-    parts = [hidden([back(0)], [layer_inputs, other], "hidden_0")]
+    part = hidden(0, [layer_inputs, near], "hidden_0")
+    waiting, bases = [], None
     for step in range(1, groups):
-        if step < groups - 1:
-            line.append(along(line[step]))
-        side.append(swapped(line[step], "expert", 1))
-        blocks = [
-            side[step - 1],
-            swapped(side[step - 1], "expert", 0),
-            line[step],
-            swapped(line[step], "expert", 0),
-        ]
-        firsts = [jnp.bitwise_xor(back(step - 1), 2), back(step)]
-        parts.append(hidden(firsts, blocks, "hidden_%d" % step))
-    blocks = [side[groups - 1], swapped(side[groups - 1], "expert", 0)]
-    last = hidden([jnp.bitwise_xor(back(groups - 1), 2)], blocks, "hidden_last")
-    incoming = [swapped(part[2], "expert", 0) for part in parts]
-    early = sums(
-        [part[0] for part in parts],
-        [[part[1] for part in parts], [part[2] for part in parts], incoming],
-        None,
-        None,
-        1,
-        "early_sums",
-    )
-    divisor = experts * position_ordinal
-    arrived = swapped(last[2], "expert", 0)
-    one = jnp.ones((), jnp.int32)
+        part, line, side = lax.optimization_barrier((part, line, side))
+        part = (*part, other(part[2]))
+        next_line = along(line) if step < groups - 1 else None
+        next_side = swapped(line, "expert", 1)
+        blocks = [side, other(side), line, other(line)]
+        new = hidden(2 * step - 1, blocks, "hidden_%d" % step)
+        waiting.append(part)
+        if step >= 2:
+            bases = totals(waiting, bases, "totals_%d" % step)
+            waiting = []
+            new, bases = lax.optimization_barrier((new, bases))
+        part, line, side = new, next_line, next_side
+    waiting.append((*part, other(part[2])))
+    bases = totals(waiting, bases, "totals_last")
+    side, bases = lax.optimization_barrier((side, bases))
+    last = hidden(2 * groups - 1, [side, other(side)], "hidden_last")
+    arrived = other(last[2])
     gram, self_cross = sums(
-        [last[0]],
-        [[last[1]], [last[2]]],
-        early[:2],
-        jnp.stack([one, keep]).astype(jnp.int32),
-        divisor,
-        "own_sums",
+        place, [last[0]], [[last[1]], [last[2]]], bases[:2], (None, 1), divisor, "own_sums"
     )
     (merge_cross,) = sums(
-        [last[0]], [[arrived]], early[2:], merge[None].astype(jnp.int32), divisor, "merge_sums"
+        place, [last[0]], [[arrived]], bases[2:], (2,), divisor, "merge_sums"
     )
     return gram, self_cross, merge_cross
 

time: 126 us -> 128 us (1.016)
  Pallas kernels: 50.6 us -> 79.9 us
  local copies, waits for them, and re-layouts: 24.8 us -> 11 us
  waiting for transfers between devices: 27.5 us -> 17.6 us
  starting transfers between devices: 16.4 us -> 13.4 us
  other arithmetic: 3.98 us -> 2.65 us
    pallas_call x3 -> x5, Pallas kernels: 16.7 us -> 38.7 us  [sums(): pl.pallas_call(functools.partial(sums_kernel, total, len(lhs), bool(bases...]
    ppermute x3, waiting for transfers between devices: 25.6 us -> 4.01 us  [along(): lax.ppermute(x, 'expert', [(i, (i + 4) % experts) for i in range(experts)])]
    unnamed x54 -> x45, local copies, waits for them, and re-layouts: 21.2 us -> 8 us
    ppermute x17, waiting for transfers between devices: 0.04 us -> 11.1 us  [swapped(): lax.ppermute(x, axis, [(i, i ^ 1 << stride) for i in range(lax.axis_size(...]
    pallas_call x5, Pallas kernels: 30.8 us -> 39.5 us  [hidden_parts(): pl.pallas_call(functools.partial(hidden_kernel, pair_total, first_slot),...]
    ppermute x17, starting transfers between devices: 7.92 us -> 6.31 us  [swapped(): lax.ppermute(x, axis, [(i, i ^ 1 << stride) for i in range(lax.axis_size(...]
    all_to_all x1, starting transfers between devices: 5.41 us -> 3.97 us  [gathered_shards(): lax.all_to_all(table, 'expert', split_axis=0, concat_axis=0, tiled=True)]
    another operation x3 -> x0, other arithmetic: 1.32 us -> none  [the longest x2 0.7 us: place(): return jnp.stack([core, keep, merge, *firsts]).astype(jnp.int32)]
  transfers between devices with their start and end apart: 21 -> 21, of which waited for: 3 -> 11; matrix products, arithmetic and copies ran while one was open for 9% -> 5% of each run, Pallas kernels for 38% -> 46%
where the time goes in v2:
time: 128 us; the launch traced here: 127 us
  Pallas kernels  79.9 us (62%)
  waiting for transfers between devices  17.6 us (14%)
  starting transfers between devices  13.4 us (10%)
  local copies, waits for them, and re-layouts  11 us (9%)
  other arithmetic  2.65 us (2%)
  between operations  2.1 us (2%)
    pallas_call x5, Pallas kernels, hidden_parts(): pl.pallas_call(functools.partial(hidden_kernel, pair_total, first_slot),...  39.5 us
    pallas_call x5, Pallas kernels, sums(): pl.pallas_call(functools.partial(sums_kernel, total, len(lhs), bool(bases...  38.7 us
    ppermute x17, waiting for transfers between devices, swapped(): lax.ppermute(x, axis, [(i, i ^ 1 << stride) for i in range(lax.axis_size(...  11.1 us
    unnamed x45, local copies, waits for them, and re-layouts  8 us
    ppermute x17, starting transfers between devices, swapped(): lax.ppermute(x, axis, [(i, i ^ 1 << stride) for i in range(lax.axis_size(...  6.31 us
    ppermute x3, waiting for transfers between devices, along(): lax.ppermute(x, 'expert', [(i, (i + 4) % experts) for i in range(experts)])  4.01 us
    all_to_all x1, starting transfers between devices, gathered_shards(): lax.all_to_all(table, 'expert', split_axis=0, concat_axis=0, tiled=True)  3.97 us
    ppermute x3, starting transfers between devices, along(): lax.ppermute(x, 'expert', [(i, (i + 4) % experts) for i in range(experts)])  3.15 us
  transfers between devices with their start and end apart: 21, of which 11 were waited for; matrix products, arithmetic and copies ran while one was open for 5% of the time, Pallas kernels for 46%

profile of v2, /device:TPU:0, one launch (start us, length us, event | category | flops | bytes accessed | tf_op | source)
XLA Modules:
  0.0 126.7 jit_solution(16936456092995437982)
XLA Ops:
  1.1 2.6 %collective-permute-start.1 = (bf16[128,2048]{1,0:T(8,128)(2,1)}, bf16[128,2048]{1,0:T(8,128)(2,1)S(1)}, u32[]{:S(2)}, u32[]{:S(2)}) collective-permute-start(bf16[128,2048]{1,0:T(8,128)(2,1)} %refs_0_.1), channel_id=1, source_target_pairs={{0,4},{1,5},{2,6},{3,7},{4,8},{5,9},{6,10},{7,11},{8,12},{9,13},{1... | collective-permute-start | bytes 1572872 | tf_op jit(solution)/shard_map/ppermute | solution.py:360
  3.8 1.5 %collective-permute-start.2 = (bf16[128,2048]{1,0:T(8,128)(2,1)}, bf16[128,2048]{1,0:T(8,128)(2,1)S(1)}, u32[]{:S(2)}, u32[]{:S(2)}) collective-permute-start(bf16[128,2048]{1,0:T(8,128)(2,1)} %refs_0_.1), channel_id=1, source_target_pairs={{0,2},{1,3},{2,0},{3,1},{4,6},{5,7},{6,4},{7,5},{8,10},{9,11},{10,... | collective-permute-start | bytes 1572872 | tf_op jit(solution)/shard_map/ppermute | solution.py:12
  6.5 1.7 %route_table.1 = bf16[16,256]{1,0:T(8,128)(2,1)} custom-call(s32[16]{0:T(128)} %quota_ref.1, s32[8,128]{1,0:T(8,128)} %bitcast.23, s32[8,128]{1,0:T(8,128)} %bitcast.24, bf16[1,256]{1,0:T(2,128)(2,1)} %broadcast_in_dim.9.coef_ref), custom_call_target="tpu_custom_call" | custom-call | tf_op jit(solution)/shard_map/route_table/pallas_call | solution.py:177
  8.7 1.3 %reduce = bf16[16,256]{1,0:T(8,128)(2,1)S(1)} reduce(bf16[16,1,256]{2,0,1:T(8,128)(2,1)} %bitcast.22, bf16[]{:T(256)} %broadcast.4), dimensions={1}, to_apply=%copy.12.reduce_sub_computation | reduce | bytes 16386 | tf_op jit(solution)/shard_map/all_to_all | solution.py:395
  10.7 4.0 %all-to-all-start = ((bf16[16,2,128]{2,1,0:T(2,128)(2,1)}), bf16[16,2,128]{2,1,0:T(2,128)(2,1)S(1)}, u32[]{:S(2)}, u32[]{:S(2)}) async-start(bf16[16,2,128]{2,1,0:T(2,128)(2,1)} %reshape.8), calls=%async_computation | async-start | bytes 16384 | tf_op jit(solution)/shard_map/all_to_all | solution.py:395
  14.7 1.3 %fusion.1 = (s32[]{:T(128)}, s32[]{:T(128)}) fusion(s32[16]{0:T(128)} %param.12, s32[]{:T(128)S(6)} %xor.15, s32[]{:T(128)S(6)} %axis_index.12), kind=kLoop, calls=%fused_computation.4 | loop fusion | flops 94 | bytes 80 | tf_op jit(solution)/shard_map/reduce_sum | solution.py:352
  17.2 1.3 %stack.47.place_ref.scale_ref = s32[11]{0:T(128)} concatenate(s32[1]{0:T(128)} %bitcast, s32[1]{0:T(128)} %bitcast.1, s32[1]{0:T(128)} %bitcast.2, s32[1]{0:T(128)} %bitcast.3, s32[1]{0:T(128)} %bitcast.4, s32[1]{0:T(128)} %bitcast.5, s32[1]{0:T(128)} %bitcast.6, s32[1]{0:T(128)} %bitcast.7, s32[1]{0:T(128)} %bitcast.8, s32[1]{0:T(128)} %bitcast.9, s32[1]{0:T(128)} %bitcast.10), dimensions={0} | concatenate | bytes 88 | tf_op jit(solution)/shard_map/stack | solution.py:369
  18.5 2.5 %all-to-all-done = bf16[16,2,128]{2,1,0:T(2,128)(2,1)S(1)} async-done(((bf16[16,2,128]{2,1,0:T(2,128)(2,1)}), bf16[16,2,128]{2,1,0:T(2,128)(2,1)S(1)}, u32[]{:S(2)}, u32[]{:S(2)}) %all-to-all-start) | async-done | bytes 8224 | tf_op jit(solution)/shard_map/all_to_all | solution.py:395
  22.4 6.7 %hidden_0.1 = (bf16[768,256]{1,0:T(8,128)(2,1)}, bf16[256,768]{1,0:T(8,128)(2,1)}, bf16[256,768]{1,0:T(8,128)(2,1)}) custom-call(s32[11]{0:T(128)} %stack.47.place_ref.scale_ref, bf16[16,256]{1,0:T(8,128)(2,1)} %bitcast.17, bf16[128,2048]{1,0:T(8,128)(2,1)} %refs_0_.1, bf16[128,2048]{1,0:T(8,128)(2,1)} %copy-done.4, bf16[1,2048,768]{2,1,0:T(8,128)(2,1)} %refs_2_.3, ...), custom_call_target="tpu_custom_call" | custom-call | flops 1610612736 | bytes 8519680 | tf_op jit(solution)/shard_map/hidden_0/pallas_call | solution.py:236
  32.7 8.7 %hidden_1.1 = (bf16[768,512]{1,0:T(8,128)(2,1)}, bf16[512,768]{1,0:T(8,128)(2,1)}, bf16[512,768]{1,0:T(8,128)(2,1)}) custom-call(s32[11]{0:T(128)} %stack.47.place_ref.scale_ref, bf16[16,256]{1,0:T(8,128)(2,1)} %bitcast.18, bf16[128,2048]{1,0:T(8,128)(2,1)} %copy-done.10, bf16[128,2048]{1,0:T(8,128)(2,1)} %copy-done.17, bf16[128,2048]{1,0:T(8,128)(2,1)} %copy-done.9, ...), custom_call_target="tpu_custom_call" | custom-call | flops 3221225472 | bytes 10747904 | tf_op jit(solution)/shard_map/hidden_1/pallas_call | solution.py:236
  41.5 4.0 %collective-permute-done.5.refs_2_ = bf16[128,2048]{1,0:T(8,128)(2,1)S(1)} collective-permute-done((bf16[128,2048]{1,0:T(8,128)(2,1)S(1)}, bf16[128,2048]{1,0:T(8,128)(2,1)S(1)}, u32[]{:S(2)}, u32[]{:S(2)}) %collective-permute-start.5) | collective-permute-done | bytes 524320 | tf_op jit(solution)/shard_map/ppermute | solution.py:360
  47.9 1.7 %collective-permute-done.8.refs_3_ = bf16[128,2048]{1,0:T(8,128)(2,1)} collective-permute-done((bf16[128,2048]{1,0:T(8,128)(2,1)S(1)}, bf16[128,2048]{1,0:T(8,128)(2,1)}, u32[]{:S(2)}, u32[]{:S(2)}) %collective-permute-start.8) | collective-permute-done | bytes 524320 | tf_op jit(solution)/shard_map/ppermute | solution.py:12
  49.6 8.7 %hidden_2.1 = (bf16[768,512]{1,0:T(8,128)(2,1)}, bf16[512,768]{1,0:T(8,128)(2,1)}, bf16[512,768]{1,0:T(8,128)(2,1)}) custom-call(s32[11]{0:T(128)} %stack.47.place_ref.scale_ref, bf16[16,256]{1,0:T(8,128)(2,1)} %bitcast.19, bf16[128,2048]{1,0:T(8,128)(2,1)} %copy-done.15, bf16[128,2048]{1,0:T(8,128)(2,1)} %copy-done.16, bf16[128,2048]{1,0:T(8,128)(2,1)} %copy-done.13, ...), custom_call_target="tpu_custom_call" | custom-call | flops 3221225472 | bytes 10747904 | tf_op jit(solution)/shard_map/hidden_2/pallas_call | solution.py:236
  59.3 8.0 %totals_2.1 = (f32[768,768]{1,0:T(8,128)}, f32[768,768]{1,0:T(8,128)}, f32[768,768]{1,0:T(8,128)}) custom-call(s32[11]{0:T(128)} %stack.47.place_ref.scale_ref, bf16[768,256]{1,0:T(8,128)(2,1)} %get-tuple-element.73.refs_0_, bf16[768,512]{1,0:T(8,128)(2,1)} %get-tuple-element.74.refs_1_, bf16[256,768]{1,0:T(8,128)(2,1)} %get-tuple-element.75.refs_2_, ...), custom_call_target="tpu_custom_call" | custom-call | flops 2717908992 | bytes 11796480 | tf_op jit(solution)/shard_map/totals_2/pallas_call | solution.py:313
  68.0 1.3 collective-permute-done.14.refs_1_
  70.9 8.7 %hidden_3.1 = (bf16[768,512]{1,0:T(8,128)(2,1)}, bf16[512,768]{1,0:T(8,128)(2,1)}, bf16[512,768]{1,0:T(8,128)(2,1)}) custom-call(s32[11]{0:T(128)} %stack.47.place_ref.scale_ref, bf16[16,256]{1,0:T(8,128)(2,1)} %bitcast.20, bf16[128,2048]{1,0:T(8,128)(2,1)} %copy-done.14, bf16[128,2048]{1,0:T(8,128)(2,1)} %copy-done.19, bf16[128,2048]{1,0:T(8,128)(2,1)} %copy-done.11, ...), custom_call_target="tpu_custom_call" | custom-call | flops 3221225472 | bytes 10747904 | tf_op jit(solution)/shard_map/hidden_3/pallas_call | solution.py:236
  80.5 9.3 %totals_3.1 = (f32[768,768]{1,0:T(8,128)}, f32[768,768]{1,0:T(8,128)}, f32[768,768]{1,0:T(8,128)}) custom-call(s32[11]{0:T(128)} %stack.47.place_ref.scale_ref, bf16[768,512]{1,0:T(8,128)(2,1)} %get-tuple-element.90.refs_0_, bf16[512,768]{1,0:T(8,128)(2,1)} %get-tuple-element.91.refs_1_, bf16[512,768]{1,0:T(8,128)(2,1)} %get-tuple-element.92.refs_2_, ...), custom_call_target="tpu_custom_call" | custom-call | flops 1811939328 | bytes 17301504 | tf_op jit(solution)/shard_map/totals_3/pallas_call | solution.py:313
  90.5 1.6 %collective-permute-done.17.refs_3_ = bf16[512,768]{1,0:T(8,128)(2,1)S(1)} collective-permute-done((bf16[512,768]{1,0:T(8,128)(2,1)S(1)}, bf16[512,768]{1,0:T(8,128)(2,1)S(1)}, u32[]{:S(2)}, u32[]{:S(2)}) %collective-permute-start.17) | collective-permute-done | bytes 786464 | tf_op jit(solution)/shard_map/ppermute | solution.py:12
  93.0 9.3 %totals_last.1 = (f32[768,768]{1,0:T(8,128)}, f32[768,768]{1,0:T(8,128)}, f32[768,768]{1,0:T(8,128)}) custom-call(s32[11]{0:T(128)} %stack.47.place_ref.scale_ref, bf16[768,512]{1,0:T(8,128)(2,1)} %get-tuple-element.99.refs_0_, bf16[512,768]{1,0:T(8,128)(2,1)} %get-tuple-element.100.refs_1_, bf16[512,768]{1,0:T(8,128)(2,1)} %get-tuple-element.101.refs_2_, ...), custom_call_target="tpu_custom_call" | custom-call | flops 1811939328 | bytes 17301504 | tf_op jit(solution)/shard_map/totals_last/pallas_call | solution.py:313
  102.3 1.9 %collective-permute-done.13.refs_0_ = bf16[128,2048]{1,0:T(8,128)(2,1)S(1)} collective-permute-done((bf16[128,2048]{1,0:T(8,128)(2,1)S(1)}, bf16[128,2048]{1,0:T(8,128)(2,1)S(1)}, u32[]{:S(2)}, u32[]{:S(2)}) %collective-permute-start.13) | collective-permute-done | bytes 524320 | tf_op jit(solution)/shard_map/ppermute | solution.py:12
  104.2 1.9 %collective-permute-done.18.refs_1_ = bf16[128,2048]{1,0:T(8,128)(2,1)S(1)} collective-permute-done((bf16[128,2048]{1,0:T(8,128)(2,1)S(1)}, bf16[128,2048]{1,0:T(8,128)(2,1)S(1)}, u32[]{:S(2)}, u32[]{:S(2)}) %collective-permute-start.18) | collective-permute-done | bytes 524320 | tf_op jit(solution)/shard_map/ppermute | solution.py:12
  106.9 6.7 %hidden_last.1 = (bf16[768,256]{1,0:T(8,128)(2,1)}, bf16[256,768]{1,0:T(8,128)(2,1)}, bf16[256,768]{1,0:T(8,128)(2,1)}) custom-call(s32[11]{0:T(128)} %stack.47.place_ref.scale_ref, bf16[16,256]{1,0:T(8,128)(2,1)} %bitcast.21, bf16[128,2048]{1,0:T(8,128)(2,1)} %copy-done.5, bf16[128,2048]{1,0:T(8,128)(2,1)} %copy-done.6, bf16[1,2048,768]{2,1,0:T(8,128)(2,1)} %refs_2_.3, ...), custom_call_target="tpu_custom_call" | custom-call | flops 1610612736 | bytes 8519680 | tf_op jit(solution)/shard_map/hidden_last/pallas_call | solution.py:236
  113.8 6.9 %own_sums.1 = (f32[1,768,768]{2,1,0:T(8,128)}, f32[1,768,768]{2,1,0:T(8,128)}) custom-call(s32[11]{0:T(128)} %stack.47.place_ref.scale_ref, bf16[768,256]{1,0:T(8,128)(2,1)} %get-tuple-element.109.refs_0_, bf16[256,768]{1,0:T(8,128)(2,1)} %get-tuple-element.110.refs_1_, bf16[256,768]{1,0:T(8,128)(2,1)} %get-tuple-element.111.refs_2_, ...), custom_call_target="tpu_custom_call" | custom-call | flops 603979776 | bytes 10616832 | tf_op jit(solution)/shard_map/own_sums/pallas_call | solution.py:313
  121.4 5.2 %merge_sums.1 = f32[1,768,768]{2,1,0:T(8,128)} custom-call(s32[11]{0:T(128)} %stack.47.place_ref.scale_ref, bf16[768,256]{1,0:T(8,128)(2,1)} %get-tuple-element.109.refs_0_, bf16[256,768]{1,0:T(8,128)(2,1)} %copy-done.7, f32[768,768]{1,0:T(8,128)} %get-tuple-element.116.refs_2_), custom_call_target="tpu_custom_call" | custom-call | flops 301989888 | bytes 5505024 | tf_op jit(solution)/shard_map/merge_sums/pallas_call | solution.py:313
  (79 shorter events, 17.8 us)
Async XLA Ops:
  0.6 21.0 %collective-permute-start = (bf16[128,2048]{1,0:T(8,128)(2,1)}, bf16[128,2048]{1,0:T(8,128)(2,1)S(1)}, u32[]{:S(2)}, u32[]{:S(2)}) collective-permute-start(bf16[128,2048]{1,0:T(8,128)(2,1)} %refs_0_.1), channel_id=1, source_target_pairs={{0,1},{1,0},{2,3},{3,2},{4,5},{5,4},{6,7},{7,6},{8,9},{9,8},{10,11... | collective-permute-start | bytes 1572872 | tf_op jit(solution)/shard_map/ppermute | solution.py:12
  1.1 28.0 %collective-permute-start.1 = (bf16[128,2048]{1,0:T(8,128)(2,1)}, bf16[128,2048]{1,0:T(8,128)(2,1)S(1)}, u32[]{:S(2)}, u32[]{:S(2)}) collective-permute-start(bf16[128,2048]{1,0:T(8,128)(2,1)} %refs_0_.1), channel_id=1, source_target_pairs={{0,4},{1,5},{2,6},{3,7},{4,8},{5,9},{6,10},{7,11},{8,12},{9,13},{1... | collective-permute-start | bytes 1572872 | tf_op jit(solution)/shard_map/ppermute | solution.py:360
  3.8 25.4 %collective-permute-start.2 = (bf16[128,2048]{1,0:T(8,128)(2,1)}, bf16[128,2048]{1,0:T(8,128)(2,1)S(1)}, u32[]{:S(2)}, u32[]{:S(2)}) collective-permute-start(bf16[128,2048]{1,0:T(8,128)(2,1)} %refs_0_.1), channel_id=1, source_target_pairs={{0,2},{1,3},{2,0},{3,1},{4,6},{5,7},{6,4},{7,5},{8,10},{9,11},{10,... | collective-permute-start | bytes 1572872 | tf_op jit(solution)/shard_map/ppermute | solution.py:12
  10.7 10.3 %all-to-all-start = ((bf16[16,2,128]{2,1,0:T(2,128)(2,1)}), bf16[16,2,128]{2,1,0:T(2,128)(2,1)S(1)}, u32[]{:S(2)}, u32[]{:S(2)}) async-start(bf16[16,2,128]{2,1,0:T(2,128)(2,1)} %reshape.8), calls=%async_computation | async-start | bytes 16384 | tf_op jit(solution)/shard_map/all_to_all | solution.py:395
  29.2 2.0 %collective-permute-start.3 = (bf16[128,2048]{1,0:T(8,128)(2,1)S(1)}, bf16[128,2048]{1,0:T(8,128)(2,1)S(1)}, u32[]{:S(2)}, u32[]{:S(2)}) collective-permute-start(bf16[128,2048]{1,0:T(8,128)(2,1)S(1)} %collective-permute-done.2.refs_0_), channel_id=1, source_target_pairs={{0,1},{1,0},{2,3},{3,2},{4,5},{5,4},{6,7},{7,6},{8,9},{9,8},{10,11... | collective-permute-start | bytes 1572872 | tf_op jit(solution)/shard_map/ppermute | solution.py:12
  29.3 2.6 %collective-permute-start.4 = (bf16[128,2048]{1,0:T(8,128)(2,1)S(1)}, bf16[128,2048]{1,0:T(8,128)(2,1)S(1)}, u32[]{:S(2)}, u32[]{:S(2)}) collective-permute-start(bf16[128,2048]{1,0:T(8,128)(2,1)S(1)} %collective-permute-done.1.refs_2_), channel_id=1, source_target_pairs={{0,1},{1,0},{2,3},{3,2},{4,5},{5,4},{6,7},{7,6},{8,9},{9,8},{10,11... | collective-permute-start | bytes 1572872 | tf_op jit(solution)/shard_map/ppermute | solution.py:12
  29.8 15.7 %collective-permute-start.5 = (bf16[128,2048]{1,0:T(8,128)(2,1)S(1)}, bf16[128,2048]{1,0:T(8,128)(2,1)S(1)}, u32[]{:S(2)}, u32[]{:S(2)}) collective-permute-start(bf16[128,2048]{1,0:T(8,128)(2,1)S(1)} %collective-permute-done.1.refs_2_), channel_id=1, source_target_pairs={{0,4},{1,5},{2,6},{3,7},{4,8},{5,9},{6,10},{7,11},{8,12},{9,13},{1... | collective-permute-start | bytes 1572872 | tf_op jit(solution)/shard_map/ppermute | solution.py:360
  30.3 15.2 %collective-permute-start.6 = (bf16[128,2048]{1,0:T(8,128)(2,1)S(1)}, bf16[128,2048]{1,0:T(8,128)(2,1)S(1)}, u32[]{:S(2)}, u32[]{:S(2)}) collective-permute-start(bf16[128,2048]{1,0:T(8,128)(2,1)S(1)} %collective-permute-done.1.refs_2_), channel_id=1, source_target_pairs={{0,2},{1,3},{2,0},{3,1},{4,6},{5,7},{6,4},{7,5},{8,10},{9,11},{10,... | collective-permute-start | bytes 1572872 | tf_op jit(solution)/shard_map/ppermute | solution.py:12
  45.5 2.0 %collective-permute-start.7 = (bf16[128,2048]{1,0:T(8,128)(2,1)S(1)}, bf16[128,2048]{1,0:T(8,128)(2,1)S(1)}, u32[]{:S(2)}, u32[]{:S(2)}) collective-permute-start(bf16[128,2048]{1,0:T(8,128)(2,1)S(1)} %collective-permute-done.6.refs_0_), channel_id=1, source_target_pairs={{0,1},{1,0},{2,3},{3,2},{4,5},{5,4},{6,7},{7,6},{8,9},{9,8},{10,11... | collective-permute-start | bytes 1572872 | tf_op jit(solution)/shard_map/ppermute | solution.py:12
  45.5 4.1 %collective-permute-start.8 = (bf16[128,2048]{1,0:T(8,128)(2,1)S(1)}, bf16[128,2048]{1,0:T(8,128)(2,1)}, u32[]{:S(2)}, u32[]{:S(2)}) collective-permute-start(bf16[128,2048]{1,0:T(8,128)(2,1)S(1)} %collective-permute-done.5.refs_2_), channel_id=1, source_target_pairs={{0,1},{1,0},{2,3},{3,2},{4,5},{5,4},{6,7},{7,6},{8,9},{9,8},{10,11... | collective-permute-start | bytes 1572872 | tf_op jit(solution)/shard_map/ppermute | solution.py:12
  46.0 12.3 %collective-permute-start.10 = (bf16[512,768]{1,0:T(8,128)(2,1)}, bf16[512,768]{1,0:T(8,128)(2,1)S(1)}, u32[]{:S(2)}, u32[]{:S(2)}) collective-permute-start(bf16[512,768]{1,0:T(8,128)(2,1)} %get-tuple-element.78.refs_5_), channel_id=1, source_target_pairs={{0,1},{1,0},{2,3},{3,2},{4,5},{5,4},{6,7},{7,6},{8,9},{9,8},{10,11... | collective-permute-start | bytes 2359304 | tf_op jit(solution)/shard_map/ppermute | solution.py:12
  46.1 12.2 %collective-permute-start.9 = (bf16[256,768]{1,0:T(8,128)(2,1)}, bf16[256,768]{1,0:T(8,128)(2,1)}, u32[]{:S(2)}, u32[]{:S(2)}) collective-permute-start(bf16[256,768]{1,0:T(8,128)(2,1)} %get-tuple-element.77.refs_4_), channel_id=1, source_target_pairs={{0,1},{1,0},{2,3},{3,2},{4,5},{5,4},{6,7},{7,6},{8,9},{9,8},{10,11... | collective-permute-start | bytes 1179656 | tf_op jit(solution)/shard_map/ppermute | solution.py:12
  46.5 20.7 %collective-permute-start.11 = (bf16[128,2048]{1,0:T(8,128)(2,1)S(1)}, bf16[128,2048]{1,0:T(8,128)(2,1)S(1)}, u32[]{:S(2)}, u32[]{:S(2)}) collective-permute-start(bf16[128,2048]{1,0:T(8,128)(2,1)S(1)} %collective-permute-done.5.refs_2_), channel_id=1, source_target_pairs={{0,4},{1,5},{2,6},{3,7},{4,8},{5,9},{6,10},{7,11},{8,12},{9,13},{1... | collective-permute-start | bytes 1572872 | tf_op jit(solution)/shard_map/ppermute | solution.py:360
  47.4 19.9 %collective-permute-start.12 = (bf16[128,2048]{1,0:T(8,128)(2,1)S(1)}, bf16[128,2048]{1,0:T(8,128)(2,1)S(1)}, u32[]{:S(2)}, u32[]{:S(2)}) collective-permute-start(bf16[128,2048]{1,0:T(8,128)(2,1)S(1)} %collective-permute-done.5.refs_2_), channel_id=1, source_target_pairs={{0,2},{1,3},{2,0},{3,1},{4,6},{5,7},{6,4},{7,5},{8,10},{9,11},{10,... | collective-permute-start | bytes 1572872 | tf_op jit(solution)/shard_map/ppermute | solution.py:12
  58.3 9.6 %copy-start = (bf16[512,768]{1,0:T(8,128)(2,1)S(1)}, bf16[512,768]{1,0:T(8,128)(2,1)}, u32[]{:S(2)}) copy-start(bf16[512,768]{1,0:T(8,128)(2,1)} %get-tuple-element.92.refs_2_) | copy-start | bytes 2359300
  67.3 2.0 %collective-permute-start.14 = (bf16[128,2048]{1,0:T(8,128)(2,1)S(1)}, bf16[128,2048]{1,0:T(8,128)(2,1)S(1)}, u32[]{:S(2)}, u32[]{:S(2)}) collective-permute-start(bf16[128,2048]{1,0:T(8,128)(2,1)S(1)} %collective-permute-done.12.refs_0_), channel_id=1, source_target_pairs={{0,1},{1,0},{2,3},{3,2},{4,5},{5,4},{6,7},{7,6},{8,9},{9,8},{10,11... | collective-permute-start | bytes 1572872 | tf_op jit(solution)/shard_map/ppermute | solution.py:12
  67.5 2.5 %collective-permute-start.15 = (bf16[128,2048]{1,0:T(8,128)(2,1)S(1)}, bf16[128,2048]{1,0:T(8,128)(2,1)S(1)}, u32[]{:S(2)}, u32[]{:S(2)}) collective-permute-start(bf16[128,2048]{1,0:T(8,128)(2,1)S(1)} %collective-permute-done.11.refs_2_), channel_id=1, source_target_pairs={{0,1},{1,0},{2,3},{3,2},{4,5},{5,4},{6,7},{7,6},{8,9},{9,8},{10,11... | collective-permute-start | bytes 1572872 | tf_op jit(solution)/shard_map/ppermute | solution.py:12
  67.9 11.7 %collective-permute-start.16 = (bf16[512,768]{1,0:T(8,128)(2,1)S(1)}, bf16[512,768]{1,0:T(8,128)(2,1)S(1)}, u32[]{:S(2)}, u32[]{:S(2)}) collective-permute-start(bf16[512,768]{1,0:T(8,128)(2,1)S(1)} %copy-done), channel_id=1, source_target_pairs={{0,1},{1,0},{2,3},{3,2},{4,5},{5,4},{6,7},{7,6},{8,9},{9,8},{10,11... | collective-permute-start | bytes 2359304 | tf_op jit(solution)/shard_map/ppermute | solution.py:12
  79.6 10.2 %copy-start.1 = (bf16[512,768]{1,0:T(8,128)(2,1)S(1)}, bf16[512,768]{1,0:T(8,128)(2,1)}, u32[]{:S(2)}) copy-start(bf16[512,768]{1,0:T(8,128)(2,1)} %get-tuple-element.101.refs_2_) | copy-start | bytes 2359300
  79.6 10.4 %copy-start.12 = (bf16[128,2048]{1,0:T(8,128)(2,1)S(1)}, bf16[128,2048]{1,0:T(8,128)(2,1)}, u32[]{:S(2)}) copy-start(bf16[128,2048]{1,0:T(8,128)(2,1)} %copy-done.11) | copy-start | bytes 1572868
  89.8 2.4 %collective-permute-start.17 = (bf16[512,768]{1,0:T(8,128)(2,1)S(1)}, bf16[512,768]{1,0:T(8,128)(2,1)S(1)}, u32[]{:S(2)}, u32[]{:S(2)}) collective-permute-start(bf16[512,768]{1,0:T(8,128)(2,1)S(1)} %copy-done.1), channel_id=1, source_target_pairs={{0,1},{1,0},{2,3},{3,2},{4,5},{5,4},{6,7},{7,6},{8,9},{9,8},{10,11... | collective-permute-start | bytes 2359304 | tf_op jit(solution)/shard_map/ppermute | solution.py:12
  90.0 14.2 %collective-permute-start.13 = (bf16[128,2048]{1,0:T(8,128)(2,1)S(1)}, bf16[128,2048]{1,0:T(8,128)(2,1)S(1)}, u32[]{:S(2)}, u32[]{:S(2)}) collective-permute-start(bf16[128,2048]{1,0:T(8,128)(2,1)S(1)} %copy-done.12), channel_id=1, source_target_pairs={{0,2},{1,3},{2,0},{3,1},{4,6},{5,7},{6,4},{7,5},{8,10},{9,11},{10,... | collective-permute-start | bytes 1572872 | tf_op jit(solution)/shard_map/ppermute | solution.py:12
  104.2 1.9 %collective-permute-start.18 = (bf16[128,2048]{1,0:T(8,128)(2,1)S(1)}, bf16[128,2048]{1,0:T(8,128)(2,1)S(1)}, u32[]{:S(2)}, u32[]{:S(2)}) collective-permute-start(bf16[128,2048]{1,0:T(8,128)(2,1)S(1)} %collective-permute-done.13.refs_0_), channel_id=1, source_target_pairs={{0,1},{1,0},{2,3},{3,2},{4,5},{5,4},{6,7},{7,6},{8,9},{9,8},{10,11... | collective-permute-start | bytes 1572872 | tf_op jit(solution)/shard_map/ppermute | solution.py:12
  113.6 7.0 %collective-permute-start.19 = (bf16[256,768]{1,0:T(8,128)(2,1)}, bf16[256,768]{1,0:T(8,128)(2,1)S(1)}, u32[]{:S(2)}, u32[]{:S(2)}) collective-permute-start(bf16[256,768]{1,0:T(8,128)(2,1)} %get-tuple-element.111.refs_2_), channel_id=1, source_target_pairs={{0,1},{1,0},{2,3},{3,2},{4,5},{5,4},{6,7},{7,6},{8,9},{9,8},{10,11... | collective-permute-start | bytes 1179656 | tf_op jit(solution)/shard_map/ppermute | solution.py:12
  (18 other events, 31.7 us)

commit v3 on v0

--- a/solution.py
+++ b/solution.py
@@ -1,6 +1,10 @@
+import functools
+
 import jax
 import jax.numpy as jnp
 from jax import lax
+from jax.experimental import pallas as pl
+from jax.experimental.pallas import tpu as pltpu
 from jax.sharding import PartitionSpec as P
 
 
@@ -129,6 +133,370 @@
     return (gram[None], self_cross[None], merge_cross[None])
 
 
+VMEM_GRANT = 16 << 20
+
+
+def route_table_kernel(quota_ref, pick_ref, entry_ref, coef_ref, out_ref):
+    top_count, tokens = pick_ref.shape
+    experts = out_ref.shape[0]
+    levels = coef_ref.shape[1]
+    picks = pick_ref[...]
+    entries = entry_ref[...]
+    coef = coef_ref[...]
+    expert_row = lax.broadcasted_iota(jnp.int32, (experts, tokens), 0)
+    level_row = lax.broadcasted_iota(jnp.int32, (levels, tokens), 0)
+    chosen = jnp.zeros((experts, tokens), jnp.float32)
+    weight = jnp.zeros((experts, tokens), jnp.float32)
+    for choice in range(top_count):
+        level = jnp.where(entries[choice : choice + 1, :] == level_row, 1.0, 0.0)
+        value = jnp.dot(coef, level.astype(jnp.bfloat16), preferred_element_type=jnp.float32)
+        hit = picks[choice : choice + 1, :] == expert_row
+        chosen = jnp.where(hit, 1.0, chosen)
+        weight = jnp.where(hit, value, weight)
+    row = lax.broadcasted_iota(jnp.int32, (tokens, tokens), 0)
+    col = lax.broadcasted_iota(jnp.int32, (tokens, tokens), 1)
+    earlier = jnp.where(row < col, 1.0, 0.0).astype(jnp.bfloat16)
+    rank = jnp.dot(chosen.astype(jnp.bfloat16), earlier, preferred_element_type=jnp.float32)
+    bound = jnp.zeros((experts, tokens), jnp.float32)
+    for expert in range(experts):
+        bound = jnp.where(expert_row == expert, quota_ref[expert].astype(jnp.float32), bound)
+    used = jnp.where(rank < bound, weight, 0.0).astype(jnp.bfloat16)
+    one = lax.broadcasted_iota(jnp.int32, (experts, experts), 0)
+    two = lax.broadcasted_iota(jnp.int32, (experts, experts), 1)
+    partner = jnp.where(jnp.bitwise_xor(one, 1) == two, 1.0, 0.0).astype(jnp.bfloat16)
+    out_ref[:, :tokens] = used
+    out_ref[:, tokens:] = jnp.dot(partner, used, preferred_element_type=jnp.float32).astype(
+        jnp.bfloat16
+    )
+
+
+def route_table(picks, entries, coefficients, quotas):
+    experts = quotas.shape[0]
+    tokens = picks.shape[0]
+    vmem = pl.BlockSpec(memory_space=pltpu.VMEM)
+    return pl.pallas_call(
+        route_table_kernel,
+        out_shape=jax.ShapeDtypeStruct((experts, 2 * tokens), jnp.bfloat16),
+        in_specs=[pl.BlockSpec(memory_space=pltpu.SMEM), vmem, vmem, vmem],
+        out_specs=vmem,
+        compiler_params=pltpu.CompilerParams(vmem_limit_bytes=VMEM_GRANT),
+        name="route_table",
+    )(quotas, picks.T, entries.T, coefficients[None, :])
+
+
+def hidden_kernel(block_total, source_slot, place_ref, table_ref, *refs):
+    block_refs = refs[:block_total]
+    gate_ref, up_ref, lhs_ref, count_ref, weigh_ref, send_ref = refs[block_total : block_total + 6]
+    rows_ref, coef_ref, arrive = refs[block_total + 6 :]
+    tokens = block_refs[0].shape[0]
+    hidden_width = gate_ref.shape[1]
+    copies = []
+    for block in range(block_total):
+        target = rows_ref.at[block * tokens : (block + 1) * tokens]
+        copies.append(pltpu.make_async_copy(block_refs[block], target, arrive.at[block]))
+        copies[-1].start()
+    keep = place_ref[1].astype(jnp.float32)
+    merge = place_ref[2].astype(jnp.float32)
+    row = lax.broadcasted_iota(jnp.int32, (tokens, tokens), 0)
+    col = lax.broadcasted_iota(jnp.int32, (tokens, tokens), 1)
+    table = table_ref[...].astype(jnp.float32)
+    table_row = lax.broadcasted_iota(jnp.int32, table.shape, 0)
+    for block in range(block_total):
+        source = place_ref[source_slot + block]
+        weights = jnp.sum(jnp.where(table_row == source, table, 0.0), axis=0, keepdims=True)
+        own = jnp.where(row == col, weights[:, :tokens], 0.0)
+        partner = jnp.where(row == col, weights[:, tokens:], 0.0)
+        own = jnp.sum(own, axis=1, keepdims=True)
+        partner = jnp.sum(partner, axis=1, keepdims=True)
+        count = jnp.where(own > 0.0, keep, 0.0) + jnp.where(partner > 0.0, merge, 0.0)
+        span = slice(block * tokens, (block + 1) * tokens)
+        coef_ref[0, span, :] = jnp.broadcast_to(count, (tokens, 128))
+        coef_ref[1, span, :] = jnp.broadcast_to(own, (tokens, 128))
+    tile = 256
+    for pair in range(0, block_total, 2):
+        copies[pair].wait()
+        copies[pair + 1].wait()
+        span = slice(pair * tokens, (pair + 2) * tokens)
+        rows = rows_ref[span, :]
+        for start in range(0, hidden_width, tile):
+            lanes = slice(start, start + tile)
+            gate = jnp.dot(rows, gate_ref[:, lanes], preferred_element_type=jnp.float32)
+            upward = jnp.dot(rows, up_ref[:, lanes], preferred_element_type=jnp.float32)
+            hidden = (gate / (1.0 + jnp.exp(-gate)) * upward).astype(jnp.bfloat16)
+            lhs_ref[lanes, span] = hidden.T
+            hidden = hidden.astype(jnp.float32)
+            for lane in range(0, tile, 128):
+                part = hidden[:, lane : lane + 128]
+                to = slice(start + lane, start + lane + 128)
+                count_ref[span, to] = (part * coef_ref[0, span, :]).astype(jnp.bfloat16)
+                weighed = (part * coef_ref[1, span, :]).astype(jnp.bfloat16)
+                weigh_ref[span, to] = weighed
+                middle = (pair + 1) * tokens
+                send_ref[pair * tokens : middle, to] = weighed[tokens:]
+                send_ref[middle : (pair + 2) * tokens, to] = weighed[:tokens]
+
+
+def in_vmem(x):
+    return pltpu.with_memory_space_constraint(x, pltpu.VMEM)
+
+
+def hidden_parts(place, source_slot, table, blocks, w_gate, w_up, name):
+    tokens, width = blocks[0].shape
+    block_total = len(blocks)
+    rows = block_total * tokens
+    hidden_width = w_gate.shape[1]
+    vmem = pl.BlockSpec(memory_space=pltpu.VMEM)
+    outside = pl.BlockSpec(memory_space=pl.ANY)
+    return pl.pallas_call(
+        functools.partial(hidden_kernel, block_total, source_slot),
+        out_shape=(
+            pltpu.VMEM((hidden_width, rows), jnp.bfloat16),
+            pltpu.VMEM((rows, hidden_width), jnp.bfloat16),
+            pltpu.VMEM((rows, hidden_width), jnp.bfloat16),
+            jax.ShapeDtypeStruct((rows, hidden_width), jnp.bfloat16),
+        ),
+        in_specs=[
+            pl.BlockSpec(memory_space=pltpu.SMEM),
+            vmem,
+            *[outside] * block_total,
+            vmem,
+            vmem,
+        ],
+        out_specs=(vmem, vmem, vmem, vmem),
+        scratch_shapes=[
+            pltpu.VMEM((rows, width), jnp.bfloat16),
+            pltpu.VMEM((2, rows, 128), jnp.float32),
+            pltpu.SemaphoreType.DMA((block_total,)),
+        ],
+        compiler_params=pltpu.CompilerParams(vmem_limit_bytes=VMEM_GRANT),
+        cost_estimate=pl.CostEstimate(
+            flops=4 * rows * width * hidden_width,
+            bytes_accessed=2 * rows * width + 2 * rows * hidden_width,
+            transcendentals=rows * hidden_width,
+        ),
+        name=name,
+    )(place, table, *blocks, in_vmem(w_gate), in_vmem(w_up))
+
+
+def resident_kernel(gate_ref, up_ref, gate_out, up_out, arrive):
+    copies = [
+        pltpu.make_async_copy(gate_ref.at[0], gate_out, arrive.at[0]),
+        pltpu.make_async_copy(up_ref.at[0], up_out, arrive.at[1]),
+    ]
+    for copy in copies:
+        copy.start()
+    for copy in copies:
+        copy.wait()
+
+
+def resident(w_gate, w_up):
+    shape = w_gate.shape[1:]
+    outside = pl.BlockSpec(memory_space=pl.ANY)
+    vmem = pl.BlockSpec(memory_space=pltpu.VMEM)
+    return pl.pallas_call(
+        resident_kernel,
+        out_shape=(pltpu.VMEM(shape, w_gate.dtype), pltpu.VMEM(shape, w_up.dtype)),
+        in_specs=[outside, outside],
+        out_specs=(vmem, vmem),
+        scratch_shapes=[pltpu.SemaphoreType.DMA((2,))],
+        compiler_params=pltpu.CompilerParams(vmem_limit_bytes=VMEM_GRANT),
+        name="resident_weights",
+    )(w_gate, w_up)
+
+
+def totals_kernel(part_total, has_base, *refs):
+    parts = [refs[4 * index : 4 * index + 4] for index in range(part_total)]
+    rest = refs[4 * part_total :]
+    bases = rest[:3] if has_base else None
+    rest = rest[3:] if has_base else rest
+    outs, landed, arrive = rest[:3], rest[3 : 3 + part_total], rest[3 + part_total]
+    copies = []
+    for index in range(part_total):
+        copies.append(
+            pltpu.make_async_copy(parts[index][3], landed[index], arrive.at[index])
+        )
+        copies[-1].start()
+    hidden_width = outs[0].shape[1]
+    tile = 256
+    for which in range(3):
+        if which == 2:
+            for copy in copies:
+                copy.wait()
+        for start in range(0, hidden_width, tile):
+            lanes = slice(start, start + tile)
+            total = bases[which][:, lanes] if has_base else None
+            for index, part in enumerate(parts):
+                right = landed[index] if which == 2 else part[1 + which]
+                term = jnp.dot(
+                    part[0][...], right[:, lanes], preferred_element_type=jnp.float32
+                )
+                total = term if total is None else total + term
+            outs[which][:, lanes] = total
+
+
+def add_totals(parts, bases, name):
+    hidden_width = parts[0][0].shape[0]
+    vmem = pl.BlockSpec(memory_space=pltpu.VMEM)
+    outside = pl.BlockSpec(memory_space=pl.ANY)
+    operands, in_specs = [], []
+    rows = 0
+    for part in parts:
+        rows += part[0].shape[1]
+        operands += [in_vmem(part[0]), in_vmem(part[1]), in_vmem(part[2]), part[3]]
+        in_specs += [vmem, vmem, vmem, outside]
+    aliases = {}
+    if bases is not None:
+        aliases = {len(operands) + index: index for index in range(3)}
+        operands += [in_vmem(base) for base in bases]
+        in_specs += [vmem] * 3
+    return pl.pallas_call(
+        functools.partial(totals_kernel, len(parts), bases is not None),
+        out_shape=[pltpu.VMEM((hidden_width, hidden_width), jnp.float32)] * 3,
+        in_specs=in_specs,
+        out_specs=[vmem] * 3,
+        input_output_aliases=aliases,
+        scratch_shapes=[
+            *[pltpu.VMEM(part[3].shape, jnp.bfloat16) for part in parts],
+            pltpu.SemaphoreType.DMA((len(parts),)),
+        ],
+        compiler_params=pltpu.CompilerParams(vmem_limit_bytes=VMEM_GRANT),
+        cost_estimate=pl.CostEstimate(
+            flops=6 * rows * hidden_width * hidden_width,
+            bytes_accessed=2 * rows * hidden_width,
+            transcendentals=0,
+        ),
+        name=name,
+    )(*operands)
+
+
+def final_kernel(set_total, slots, divisor, place_ref, lhs_ref, *refs):
+    rhs, bases = refs[:set_total], refs[set_total : 2 * set_total]
+    outs, done_ref, leave = refs[2 * set_total : 3 * set_total], refs[-2], refs[-1]
+    hidden_width = lhs_ref.shape[0]
+    tile = 256
+    copies = []
+    for index in range(set_total):
+        factor = 1.0 if slots[index] is None else place_ref[slots[index]].astype(jnp.float32)
+        factor = factor / divisor
+        for start in range(0, hidden_width, tile):
+            span = slice(start, start + tile)
+            total = bases[index][span, :] + jnp.dot(
+                lhs_ref[span, :], rhs[index][...], preferred_element_type=jnp.float32
+            )
+            done_ref[index, span, :] = total * factor
+            copies.append(
+                pltpu.make_async_copy(
+                    done_ref.at[index, span],
+                    outs[index].at[0, span],
+                    leave.at[index, start // tile],
+                )
+            )
+            copies[-1].start()
+    for copy in copies:
+        copy.wait()
+
+
+def final_sums(place, lhs, rhs, bases, slots, divisor, name):
+    hidden_width, rows = lhs.shape
+    total = len(rhs)
+    vmem = pl.BlockSpec(memory_space=pltpu.VMEM)
+    outside = pl.BlockSpec(memory_space=pl.ANY)
+    return pl.pallas_call(
+        functools.partial(final_kernel, total, slots, float(divisor)),
+        out_shape=[jax.ShapeDtypeStruct((1, hidden_width, hidden_width), jnp.float32)] * total,
+        in_specs=[pl.BlockSpec(memory_space=pltpu.SMEM)] + [vmem] * (1 + 2 * total),
+        out_specs=[outside] * total,
+        scratch_shapes=[
+            pltpu.VMEM((total, hidden_width, hidden_width), jnp.float32),
+            pltpu.SemaphoreType.DMA((total, hidden_width // 256)),
+        ],
+        compiler_params=pltpu.CompilerParams(vmem_limit_bytes=VMEM_GRANT),
+        cost_estimate=pl.CostEstimate(
+            flops=2 * total * rows * hidden_width * hidden_width,
+            bytes_accessed=4 * total * hidden_width * hidden_width,
+            transcendentals=0,
+        ),
+        name=name,
+    )(place, in_vmem(lhs), *rhs, *[in_vmem(base) for base in bases])
+
+
+def gathered_shards(
+    layer_inputs,
+    specialist_picks,
+    coefficient_lookup_entry,
+    dispatch_coefficients,
+    retained_specialist_flags,
+    specialist_quotas,
+    gating_projection,
+    raising_projection,
+):
+    experts = retained_specialist_flags.shape[0]
+    tok_rows, top_count = specialist_picks.shape
+    position_ordinal = max(4, 3 * tok_rows * top_count // (4 * experts))
+    me = lax.axis_index("expert")
+    core = jnp.bitwise_and(me, 1)
+    expert_lane = jnp.arange(experts, dtype=jnp.int32)
+    keep = jnp.sum(jnp.where(expert_lane == me, retained_specialist_flags, 0))
+    keep_partner = jnp.sum(
+        jnp.where(expert_lane == jnp.bitwise_xor(me, 1), retained_specialist_flags, 0)
+    )
+    merge = keep * (1 - keep_partner)
+    groups = experts // 4
+    divisor = experts * position_ordinal
+
+    def along(x):
+        return lax.ppermute(x, "expert", [(i, (i + 4) % experts) for i in range(experts)])
+
+    def back(steps):
+        return jnp.bitwise_and(jnp.remainder(me + experts - 4 * steps, experts), ~1)
+
+    firsts = [back(0)]
+    for step in range(1, groups):
+        firsts += [jnp.bitwise_xor(back(step - 1), 2), back(step)]
+    firsts.append(jnp.bitwise_xor(back(groups - 1), 2))
+    sources = []
+    for first in firsts:
+        sources += [first + core, first + 1 - core]
+    place = jnp.stack([core, keep, merge, *sources]).astype(jnp.int32)
+    w_gate, w_up = resident(gating_projection, raising_projection)
+
+    def hidden(slot, blocks, name):
+        return hidden_parts(place, 3 + 2 * slot, table, blocks, w_gate, w_up, name)
+
+    def other(x):
+        return swapped(x, "expert", 0)
+
+    line, side = along(layer_inputs), swapped(layer_inputs, "expert", 1)
+    near = other(layer_inputs)
+    table = route_table(
+        specialist_picks, coefficient_lookup_entry, dispatch_coefficients, specialist_quotas
+    )
+    table = lax.all_to_all(table, "expert", split_axis=0, concat_axis=0, tiled=True)
+    part = hidden(0, [layer_inputs, near], "hidden_0")
+    bases = None
+    for step in range(1, groups):
+        part, line, side = lax.optimization_barrier((part, line, side))
+        part = (*part[:3], other(part[3]))
+        next_line = along(line) if step < groups - 1 else None
+        next_side = swapped(line, "expert", 1)
+        blocks = [side, other(side), line, other(line)]
+        new = hidden(2 * step - 1, blocks, "hidden_%d" % step)
+        bases = add_totals([part], bases, "totals_%d" % step)
+        new, bases = lax.optimization_barrier((new, bases))
+        part, line, side = new, next_line, next_side
+    bases = add_totals([(*part[:3], other(part[3]))], bases, "totals_last")
+    side, bases = lax.optimization_barrier((side, bases))
+    last = hidden(2 * groups - 1, [side, other(side)], "hidden_last")
+    arrived = other(last[3])
+    gram, self_cross = final_sums(
+        place, last[0], [in_vmem(last[1]), in_vmem(last[2])], bases[:2], (None, 1), divisor, "own_sums"
+    )
+    (merge_cross,) = final_sums(
+        place, last[0], [arrived], bases[2:], (2,), divisor, "merge_sums"
+    )
+    return gram, self_cross, merge_cross
+
+
 def solution(mesh):
     in_specs = (
         P(("parts", "expert", "replica"), None),
@@ -145,4 +513,6 @@
         P(("parts", "expert"), "replica", None),
         P(("parts", "expert"), "replica", None),
     )
-    return jax.shard_map(shards, mesh=mesh, in_specs=in_specs, out_specs=out_specs, check_vma=False)
+    gather_fits = mesh.shape["replica"] == 1 and mesh.shape["expert"] == 16
+    body = gathered_shards if gather_fits else shards
+    return jax.shard_map(body, mesh=mesh, in_specs=in_specs, out_specs=out_specs, check_vma=False)

time: 157 us -> 100 us (0.64)
  blocking collectives: 77.4 us -> 0 us
  Pallas kernels: 0 us -> 39.4 us
  matrix products: 24.6 us -> 0 us
  local copies, waits for them, and re-layouts: 34.2 us -> 12.8 us
  waiting for transfers between devices: 3.55 us -> 24.5 us
  starting transfers between devices: 5.73 us -> 18.5 us
  other arithmetic: 7.65 us -> 1.94 us
    all_to_all x1 -> x0, blocking collectives: 77.4 us -> none  [shards(): lax.all_to_all(send_rows, 'expert', split_axis=0, concat_axis=0, tiled=True)]
    pallas_call x0 -> x13, Pallas kernels: none -> 39.4 us  [the longest x5 21.9 us: hidden_parts(): pl.pallas_call(functools.partial(hidden_kernel, block_total, source_slot)...]
    dot_general x8 -> x0, matrix products: 24.6 us -> none  [the longest x2 10.2 us: hidden_rows(): jnp.einsum('nsd,dh->nsh', slot_rows, w_up, preferred_element_type=jnp.flo...]
    ppermute x2 -> x17, waiting for transfers between devices: 0.01 us -> 13.3 us  [swapped(): lax.ppermute(x, axis, [(i, i ^ 1 << stride) for i in range(lax.axis_size(...]
    gather x2 -> x0, local copies, waits for them, and re-layouts: 13.3 us -> none  [the longest x1 8.26 us: shards(): padded_tokens[token_slot]]
    ppermute x0 -> x3, waiting for transfers between devices: none -> 11.2 us  [along(): lax.ppermute(x, 'expert', [(i, (i + 4) % experts) for i in range(experts)])]
    ppermute x2 -> x17, starting transfers between devices: 0.84 us -> 9.1 us  [swapped(): lax.ppermute(x, axis, [(i, i ^ 1 << stride) for i in range(lax.axis_size(...]
    ppermute x0 -> x3, starting transfers between devices: none -> 5.44 us  [along(): lax.ppermute(x, 'expert', [(i, (i + 4) % experts) for i in range(experts)])]
  transfers between devices with their start and end apart: 3 -> 21, of which waited for: 1 -> 7; matrix products, arithmetic and copies ran while one was open for 19% -> 4% of each run, Pallas kernels for 0% -> 31%
where the time goes in v3:
time: 100 us; the launch traced here: 99.5 us
  Pallas kernels  39.4 us (39%)
  waiting for transfers between devices  24.5 us (24%)
  starting transfers between devices  18.5 us (18%)
  local copies, waits for them, and re-layouts  12.8 us (13%)
  between operations  2.29 us (2%)
  other arithmetic  1.94 us (2%)
    pallas_call x5, Pallas kernels, hidden_parts(): pl.pallas_call(functools.partial(hidden_kernel, block_total, source_slot)...  21.9 us
    ppermute x17, waiting for transfers between devices, swapped(): lax.ppermute(x, axis, [(i, i ^ 1 << stride) for i in range(lax.axis_size(...  13.3 us
    ppermute x3, waiting for transfers between devices, along(): lax.ppermute(x, 'expert', [(i, (i + 4) % experts) for i in range(experts)])  11.2 us
    unnamed x21, local copies, waits for them, and re-layouts  11 us
    pallas_call x4, Pallas kernels, add_totals(): pl.pallas_call(functools.partial(totals_kernel, len(parts), bases is not...  10.9 us
    ppermute x17, starting transfers between devices, swapped(): lax.ppermute(x, axis, [(i, i ^ 1 << stride) for i in range(lax.axis_size(...  9.1 us
    ppermute x3, starting transfers between devices, along(): lax.ppermute(x, 'expert', [(i, (i + 4) % experts) for i in range(experts)])  5.44 us
    pallas_call x2, Pallas kernels, final_sums(): pl.pallas_call(functools.partial(final_kernel, total, slots, float(diviso...  5.33 us
  transfers between devices with their start and end apart: 21, of which 7 were waited for; matrix products, arithmetic and copies ran while one was open for 4% of the time, Pallas kernels for 31%

profile of v3, /device:TPU:0, one launch (start us, length us, event | category | flops | bytes accessed | tf_op | source)
XLA Modules:
  0.0 99.5 jit_solution(10056833608975030397)
XLA Ops:
  1.1 2.6 %collective-permute-start.1 = (bf16[128,2048]{1,0:T(8,128)(2,1)}, bf16[128,2048]{1,0:T(8,128)(2,1)}, u32[]{:S(2)}, u32[]{:S(2)}) collective-permute-start(bf16[128,2048]{1,0:T(8,128)(2,1)} %refs_0_.1), channel_id=1, source_target_pairs={{0,4},{1,5},{2,6},{3,7},{4,8},{5,9},{6,10},{7,11},{8,12},{9,13},{1... | collective-permute-start | bytes 1572872 | tf_op jit(solution)/shard_map/ppermute | solution.py:448
  3.8 1.5 %collective-permute-start.2 = (bf16[128,2048]{1,0:T(8,128)(2,1)}, bf16[128,2048]{1,0:T(8,128)(2,1)}, u32[]{:S(2)}, u32[]{:S(2)}) collective-permute-start(bf16[128,2048]{1,0:T(8,128)(2,1)} %refs_0_.1), channel_id=1, source_target_pairs={{0,2},{1,3},{2,0},{3,1},{4,6},{5,7},{6,4},{7,5},{8,10},{9,11},{10,... | collective-permute-start | bytes 1572872 | tf_op jit(solution)/shard_map/ppermute | solution.py:12
  10.6 4.0 %all-to-all-start = ((bf16[16,2,128]{2,1,0:T(2,128)(2,1)}), bf16[16,2,128]{2,1,0:T(2,128)(2,1)S(1)}, u32[]{:S(2)}, u32[]{:S(2)}) async-start(bf16[16,2,128]{2,1,0:T(2,128)(2,1)} %reshape.8), calls=%async_computation | async-start | bytes 16384 | tf_op jit(solution)/shard_map/all_to_all | solution.py:474
  17.1 1.9 %copy-done.3 = bf16[1,2048,768]{2,1,0:T(8,128)(2,1)S(1)} copy-done((bf16[1,2048,768]{2,1,0:T(8,128)(2,1)S(1)}, bf16[1,2048,768]{2,1,0:T(8,128)(2,1)}, u32[]{:S(2)}) %copy-start.3) | copy-done | bytes 3145752
  19.0 1.9 %copy-done.4 = bf16[1,2048,768]{2,1,0:T(8,128)(2,1)S(1)} copy-done((bf16[1,2048,768]{2,1,0:T(8,128)(2,1)S(1)}, bf16[1,2048,768]{2,1,0:T(8,128)(2,1)}, u32[]{:S(2)}) %copy-start.4) | copy-done | bytes 3145752
  21.3 1.6 %copy-done = bf16[2048,768]{1,0:T(8,128)(2,1)} copy-done((bf16[2048,768]{1,0:T(8,128)(2,1)}, bf16[2048,768]{1,0:T(8,128)(2,1)S(1)}, u32[]{:S(2)}) %copy-start) | copy-done | bytes 3145752
  23.7 1.9 %copy-done.1 = bf16[2048,768]{1,0:T(8,128)(2,1)S(1)} copy-done((bf16[2048,768]{1,0:T(8,128)(2,1)S(1)}, bf16[2048,768]{1,0:T(8,128)(2,1)}, u32[]{:S(2)}) %copy-start.1) | copy-done | bytes 3145752
  26.6 3.6 %hidden_0.1 = (bf16[768,256]{1,0:T(8,128)(2,1)S(1)}, bf16[256,768]{1,0:T(8,128)(2,1)S(1)}, bf16[256,768]{1,0:T(8,128)(2,1)S(1)}, bf16[256,768]{1,0:T(8,128)(2,1)S(1)}) custom-call(s32[19]{0:T(128)S(1)} %stack.79.place_ref, bf16[16,256]{1,0:T(8,128)(2,1)S(1)} %bitcast.25, bf16[128,2048]{1,0:T(8,128)(2,1)S(1)} %copy-done.5, ...), custom_call_target="tpu_custom_call" | custom-call | flops 1610612736 | bytes 1441792 | tf_op jit(solution)/shard_map/hidden_0/pallas_call | solution.py:250
  31.2 1.7 %collective-permute-start.6 = (bf16[128,2048]{1,0:T(8,128)(2,1)}, bf16[128,2048]{1,0:T(8,128)(2,1)S(1)}, u32[]{:S(2)}, u32[]{:S(2)}) collective-permute-start(bf16[128,2048]{1,0:T(8,128)(2,1)} %collective-permute-done.1.refs_2_), channel_id=1, source_target_pairs={{0,4},{1,5},{2,6},{3,7},{4,8},{5,9},{6,10},{7,11},{8,12},{9,13},{1... | collective-permute-start | bytes 1572872 | tf_op jit(solution)/shard_map/ppermute | solution.py:448
  34.3 1.6 %totals_1.1 = (f32[768,768]{1,0:T(8,128)S(1)}, f32[768,768]{1,0:T(8,128)S(1)}, f32[768,768]{1,0:T(8,128)S(1)}) custom-call(bf16[768,256]{1,0:T(8,128)(2,1)S(1)} %get-tuple-element.94.refs_0_, bf16[256,768]{1,0:T(8,128)(2,1)S(1)} %get-tuple-element.95.refs_1_, bf16[256,768]{1,0:T(8,128)(2,1)S(1)} %get-tuple-element.96.refs_2_, ...), custom_call_target="tpu_custom_call" | custom-call | flops 905969664 | bytes 393216 | tf_op jit(solution)/shard_map/totals_1/pallas_call | solution.py:352
  36.0 5.6 %hidden_1.1 = (bf16[768,512]{1,0:T(8,128)(2,1)S(1)}, bf16[512,768]{1,0:T(8,128)(2,1)S(1)}, bf16[512,768]{1,0:T(8,128)(2,1)S(1)}, bf16[512,768]{1,0:T(8,128)(2,1)S(1)}) custom-call(s32[19]{0:T(128)S(1)} %stack.79.place_ref, bf16[16,256]{1,0:T(8,128)(2,1)S(1)} %bitcast.26, bf16[128,2048]{1,0:T(8,128)(2,1)} %collective-permute-done.2.refs_0_, ...), custom_call_target="tpu_custom_call" | custom-call | flops 3221225472 | bytes 2883584 | tf_op jit(solution)/shard_map/hidden_1/pallas_call | solution.py:250
  41.6 5.7 %collective-permute-done.6.refs_2_ = bf16[128,2048]{1,0:T(8,128)(2,1)S(1)} collective-permute-done((bf16[128,2048]{1,0:T(8,128)(2,1)}, bf16[128,2048]{1,0:T(8,128)(2,1)S(1)}, u32[]{:S(2)}, u32[]{:S(2)}) %collective-permute-start.6) | collective-permute-done | bytes 524320 | tf_op jit(solution)/shard_map/ppermute | solution.py:448
  50.4 4.9 %hidden_2.1 = (bf16[768,512]{1,0:T(8,128)(2,1)S(1)}, bf16[512,768]{1,0:T(8,128)(2,1)S(1)}, bf16[512,768]{1,0:T(8,128)(2,1)S(1)}, bf16[512,768]{1,0:T(8,128)(2,1)S(1)}) custom-call(s32[19]{0:T(128)S(1)} %stack.79.place_ref, bf16[16,256]{1,0:T(8,128)(2,1)S(1)} %bitcast.27, bf16[128,2048]{1,0:T(8,128)(2,1)S(1)} %collective-permute-done.7.refs_0_, ...), custom_call_target="tpu_custom_call" | custom-call | flops 3221225472 | bytes 2883584 | tf_op jit(solution)/shard_map/hidden_2/pallas_call | solution.py:250
  55.4 3.0 %totals_2.1 = (f32[768,768]{1,0:T(8,128)S(1)}, f32[768,768]{1,0:T(8,128)S(1)}, f32[768,768]{1,0:T(8,128)S(1)}) custom-call(bf16[768,512]{1,0:T(8,128)(2,1)S(1)} %get-tuple-element.111.refs_0_, bf16[512,768]{1,0:T(8,128)(2,1)S(1)} %get-tuple-element.112.refs_1_, ...), custom_call_target="tpu_custom_call", output_to_operand_aliasing={{0}: (4, {}), {1}: (5, {}), {2}: (6, {})} | custom-call | flops 1811939328 | bytes 786432 | tf_op jit(solution)/shard_map/totals_2/pallas_call | solution.py:352
  58.4 5.5 %collective-permute-done.11.refs_2_ = bf16[128,2048]{1,0:T(8,128)(2,1)S(1)} collective-permute-done((bf16[128,2048]{1,0:T(8,128)(2,1)S(1)}, bf16[128,2048]{1,0:T(8,128)(2,1)S(1)}, u32[]{:S(2)}, u32[]{:S(2)}) %collective-permute-start.11) | collective-permute-done | bytes 524320 | tf_op jit(solution)/shard_map/ppermute | solution.py:448
  66.6 4.9 %hidden_3.1 = (bf16[768,512]{1,0:T(8,128)(2,1)S(1)}, bf16[512,768]{1,0:T(8,128)(2,1)S(1)}, bf16[512,768]{1,0:T(8,128)(2,1)S(1)}, bf16[512,768]{1,0:T(8,128)(2,1)S(1)}) custom-call(s32[19]{0:T(128)S(1)} %stack.79.place_ref, bf16[16,256]{1,0:T(8,128)(2,1)S(1)} %bitcast.28, bf16[128,2048]{1,0:T(8,128)(2,1)S(1)} %collective-permute-done.12.refs_0_, ...), custom_call_target="tpu_custom_call" | custom-call | flops 3221225472 | bytes 2883584 | tf_op jit(solution)/shard_map/hidden_3/pallas_call | solution.py:250
  71.6 3.0 %totals_3.1 = (f32[768,768]{1,0:T(8,128)S(1)}, f32[768,768]{1,0:T(8,128)S(1)}, f32[768,768]{1,0:T(8,128)S(1)}) custom-call(bf16[768,512]{1,0:T(8,128)(2,1)S(1)} %get-tuple-element.131.refs_0_, bf16[512,768]{1,0:T(8,128)(2,1)S(1)} %get-tuple-element.132.refs_1_, ...), custom_call_target="tpu_custom_call", output_to_operand_aliasing={{0}: (4, {}), {1}: (5, {}), {2}: (6, {})} | custom-call | flops 1811939328 | bytes 786432 | tf_op jit(solution)/shard_map/totals_3/pallas_call | solution.py:352
  74.8 1.8 %collective-permute-start.13 = (bf16[128,2048]{1,0:T(8,128)(2,1)S(1)}, bf16[128,2048]{1,0:T(8,128)(2,1)S(1)}, u32[]{:S(2)}, u32[]{:S(2)}) collective-permute-start(bf16[128,2048]{1,0:T(8,128)(2,1)S(1)} %collective-permute-done.11.refs_2_), channel_id=1, source_target_pairs={{0,2},{1,3},{2,0},{3,1},{4,6},{5,7},{6,4},{7,5},{8,10},{9,11},{10,... | collective-permute-start | bytes 1572872 | tf_op jit(solution)/shard_map/ppermute | solution.py:12
  77.0 3.2 %totals_last.1 = (f32[768,768]{1,0:T(8,128)S(1)}, f32[768,768]{1,0:T(8,128)S(1)}, f32[768,768]{1,0:T(8,128)S(1)}) custom-call(bf16[768,512]{1,0:T(8,128)(2,1)S(1)} %get-tuple-element.141.refs_0_, bf16[512,768]{1,0:T(8,128)(2,1)S(1)} %get-tuple-element.142.refs_1_, ...), custom_call_target="tpu_custom_call", output_to_operand_aliasing={{0}: (4, {}), {1}: (5, {}), {2}: (6, {})} | custom-call | flops 1811939328 | bytes 786432 | tf_op jit(solution)/shard_map/totals_last/pallas_call | solution.py:352
  80.2 8.8 %collective-permute-done.13.refs_0_ = bf16[128,2048]{1,0:T(8,128)(2,1)S(1)} collective-permute-done((bf16[128,2048]{1,0:T(8,128)(2,1)S(1)}, bf16[128,2048]{1,0:T(8,128)(2,1)S(1)}, u32[]{:S(2)}, u32[]{:S(2)}) %collective-permute-start.13) | collective-permute-done | bytes 524320 | tf_op jit(solution)/shard_map/ppermute | solution.py:12
  89.1 1.9 %collective-permute-done.18.refs_1_ = bf16[128,2048]{1,0:T(8,128)(2,1)S(1)} collective-permute-done((bf16[128,2048]{1,0:T(8,128)(2,1)S(1)}, bf16[128,2048]{1,0:T(8,128)(2,1)S(1)}, u32[]{:S(2)}, u32[]{:S(2)}) %collective-permute-start.18) | collective-permute-done | bytes 524320 | tf_op jit(solution)/shard_map/ppermute | solution.py:12
  91.0 2.8 %hidden_last.1 = (bf16[768,256]{1,0:T(8,128)(2,1)S(1)}, bf16[256,768]{1,0:T(8,128)(2,1)S(1)}, bf16[256,768]{1,0:T(8,128)(2,1)S(1)}, bf16[256,768]{1,0:T(8,128)(2,1)S(1)}) custom-call(s32[19]{0:T(128)S(1)} %stack.79.place_ref, bf16[16,256]{1,0:T(8,128)(2,1)S(1)} %bitcast.29, bf16[128,2048]{1,0:T(8,128)(2,1)S(1)} %collective-permute-done.13.refs_0_, ...), custom_call_target="tpu_custom_call" | custom-call | flops 1610612736 | bytes 1441792 | tf_op jit(solution)/shard_map/hidden_last/pallas_call | solution.py:250
  94.0 3.1 %own_sums.1 = (f32[1,768,768]{2,1,0:T(8,128)}, f32[1,768,768]{2,1,0:T(8,128)}) custom-call(s32[19]{0:T(128)S(1)} %stack.79.place_ref, bf16[768,256]{1,0:T(8,128)(2,1)S(1)} %get-tuple-element.152.lhs_ref, bf16[256,768]{1,0:T(8,128)(2,1)S(1)} %get-tuple-element.153.refs_0_, bf16[256,768]{1,0:T(8,128)(2,1)S(1)} %get-tuple-element.154.refs_1_, ...), custom_call_target="tpu_custom_call" | custom-call | flops 603979776 | bytes 4718592 | tf_op jit(solution)/shard_map/own_sums/pallas_call | solution.py:404
  97.0 2.3 %merge_sums.1 = f32[1,768,768]{2,1,0:T(8,128)} custom-call(s32[19]{0:T(128)S(1)} %stack.79.place_ref, bf16[768,256]{1,0:T(8,128)(2,1)S(1)} %get-tuple-element.152.lhs_ref, bf16[256,768]{1,0:T(8,128)(2,1)S(1)} %collective-permute-done.19.refs_0_, f32[768,768]{1,0:T(8,128)S(1)} %get-tuple-element.160.refs_1_), custom_call_target="tpu_custom_call" | custom-call | flops 301989888 | bytes 2359296 | tf_op jit(solution)/shard_map/merge_sums/pallas_call | solution.py:404
  (57 shorter events, 18.3 us)
Async XLA Ops:
  0.6 23.0 %collective-permute-start = (bf16[128,2048]{1,0:T(8,128)(2,1)}, bf16[128,2048]{1,0:T(8,128)(2,1)}, u32[]{:S(2)}, u32[]{:S(2)}) collective-permute-start(bf16[128,2048]{1,0:T(8,128)(2,1)} %refs_0_.1), channel_id=1, source_target_pairs={{0,1},{1,0},{2,3},{3,2},{4,5},{5,4},{6,7},{7,6},{8,9},{9,8},{10,11... | collective-permute-start | bytes 1572872 | tf_op jit(solution)/shard_map/ppermute | solution.py:12
  1.1 29.1 %collective-permute-start.1 = (bf16[128,2048]{1,0:T(8,128)(2,1)}, bf16[128,2048]{1,0:T(8,128)(2,1)}, u32[]{:S(2)}, u32[]{:S(2)}) collective-permute-start(bf16[128,2048]{1,0:T(8,128)(2,1)} %refs_0_.1), channel_id=1, source_target_pairs={{0,4},{1,5},{2,6},{3,7},{4,8},{5,9},{6,10},{7,11},{8,12},{9,13},{1... | collective-permute-start | bytes 1572872 | tf_op jit(solution)/shard_map/ppermute | solution.py:448
  3.8 26.4 %collective-permute-start.2 = (bf16[128,2048]{1,0:T(8,128)(2,1)}, bf16[128,2048]{1,0:T(8,128)(2,1)}, u32[]{:S(2)}, u32[]{:S(2)}) collective-permute-start(bf16[128,2048]{1,0:T(8,128)(2,1)} %refs_0_.1), channel_id=1, source_target_pairs={{0,2},{1,3},{2,0},{3,1},{4,6},{5,7},{6,4},{7,5},{8,10},{9,11},{10,... | collective-permute-start | bytes 1572872 | tf_op jit(solution)/shard_map/ppermute | solution.py:12
  10.6 13.0 %all-to-all-start = ((bf16[16,2,128]{2,1,0:T(2,128)(2,1)}), bf16[16,2,128]{2,1,0:T(2,128)(2,1)S(1)}, u32[]{:S(2)}, u32[]{:S(2)}) async-start(bf16[16,2,128]{2,1,0:T(2,128)(2,1)} %reshape.8), calls=%async_computation | async-start | bytes 16384 | tf_op jit(solution)/shard_map/all_to_all | solution.py:474
  17.1 1.9 %copy-start.3 = (bf16[1,2048,768]{2,1,0:T(8,128)(2,1)S(1)}, bf16[1,2048,768]{2,1,0:T(8,128)(2,1)}, u32[]{:S(2)}) copy-start(bf16[1,2048,768]{2,1,0:T(8,128)(2,1)} %gate_ref.1) | copy-start | bytes 9437188
  23.7 1.9 %copy-start.1 = (bf16[2048,768]{1,0:T(8,128)(2,1)S(1)}, bf16[2048,768]{1,0:T(8,128)(2,1)}, u32[]{:S(2)}) copy-start(bf16[2048,768]{1,0:T(8,128)(2,1)} %copy-done) | copy-start | bytes 9437188
  30.2 5.8 %copy-start.2 = (bf16[2048,768]{1,0:T(8,128)(2,1)S(1)}, bf16[2048,768]{1,0:T(8,128)(2,1)}, u32[]{:S(2)}) copy-start(bf16[2048,768]{1,0:T(8,128)(2,1)} %copy-done) | copy-start | bytes 9437188
  30.2 5.8 %collective-permute-start.3 = (bf16[128,2048]{1,0:T(8,128)(2,1)}, bf16[128,2048]{1,0:T(8,128)(2,1)S(1)}, u32[]{:S(2)}, u32[]{:S(2)}) collective-permute-start(bf16[128,2048]{1,0:T(8,128)(2,1)} %collective-permute-done.2.refs_0_), channel_id=1, source_target_pairs={{0,1},{1,0},{2,3},{3,2},{4,5},{5,4},{6,7},{7,6},{8,9},{9,8},{10,11... | collective-permute-start | bytes 1572872 | tf_op jit(solution)/shard_map/ppermute | solution.py:12
  30.7 5.3 %collective-permute-start.4 = (bf16[128,2048]{1,0:T(8,128)(2,1)}, bf16[128,2048]{1,0:T(8,128)(2,1)S(1)}, u32[]{:S(2)}, u32[]{:S(2)}) collective-permute-start(bf16[128,2048]{1,0:T(8,128)(2,1)} %collective-permute-done.1.refs_2_), channel_id=1, source_target_pairs={{0,1},{1,0},{2,3},{3,2},{4,5},{5,4},{6,7},{7,6},{8,9},{9,8},{10,11... | collective-permute-start | bytes 1572872 | tf_op jit(solution)/shard_map/ppermute | solution.py:12
  30.8 3.6 %collective-permute-start.5 = (bf16[256,768]{1,0:T(8,128)(2,1)S(1)}, bf16[256,768]{1,0:T(8,128)(2,1)S(1)}, u32[]{:S(2)}, u32[]{:S(2)}) collective-permute-start(bf16[256,768]{1,0:T(8,128)(2,1)S(1)} %get-tuple-element.97), channel_id=1, source_target_pairs={{0,1},{1,0},{2,3},{3,2},{4,5},{5,4},{6,7},{7,6},{8,9},{9,8},{10,11... | collective-permute-start | bytes 1179656 | tf_op jit(solution)/shard_map/ppermute | solution.py:12
  31.2 16.1 %collective-permute-start.6 = (bf16[128,2048]{1,0:T(8,128)(2,1)}, bf16[128,2048]{1,0:T(8,128)(2,1)S(1)}, u32[]{:S(2)}, u32[]{:S(2)}) collective-permute-start(bf16[128,2048]{1,0:T(8,128)(2,1)} %collective-permute-done.1.refs_2_), channel_id=1, source_target_pairs={{0,4},{1,5},{2,6},{3,7},{4,8},{5,9},{6,10},{7,11},{8,12},{9,13},{1... | collective-permute-start | bytes 1572872 | tf_op jit(solution)/shard_map/ppermute | solution.py:448
  32.9 14.4 %collective-permute-start.7 = (bf16[128,2048]{1,0:T(8,128)(2,1)}, bf16[128,2048]{1,0:T(8,128)(2,1)S(1)}, u32[]{:S(2)}, u32[]{:S(2)}) collective-permute-start(bf16[128,2048]{1,0:T(8,128)(2,1)} %collective-permute-done.1.refs_2_), channel_id=1, source_target_pairs={{0,2},{1,3},{2,0},{3,1},{4,6},{5,7},{6,4},{7,5},{8,10},{9,11},{10,... | collective-permute-start | bytes 1572872 | tf_op jit(solution)/shard_map/ppermute | solution.py:12
  47.3 3.1 %collective-permute-start.8 = (bf16[128,2048]{1,0:T(8,128)(2,1)S(1)}, bf16[128,2048]{1,0:T(8,128)(2,1)S(1)}, u32[]{:S(2)}, u32[]{:S(2)}) collective-permute-start(bf16[128,2048]{1,0:T(8,128)(2,1)S(1)} %collective-permute-done.7.refs_0_), channel_id=1, source_target_pairs={{0,1},{1,0},{2,3},{3,2},{4,5},{5,4},{6,7},{7,6},{8,9},{9,8},{10,11... | collective-permute-start | bytes 1572872 | tf_op jit(solution)/shard_map/ppermute | solution.py:12
  47.3 3.1 %collective-permute-start.9 = (bf16[128,2048]{1,0:T(8,128)(2,1)S(1)}, bf16[128,2048]{1,0:T(8,128)(2,1)S(1)}, u32[]{:S(2)}, u32[]{:S(2)}) collective-permute-start(bf16[128,2048]{1,0:T(8,128)(2,1)S(1)} %collective-permute-done.6.refs_2_), channel_id=1, source_target_pairs={{0,1},{1,0},{2,3},{3,2},{4,5},{5,4},{6,7},{7,6},{8,9},{9,8},{10,11... | collective-permute-start | bytes 1572872 | tf_op jit(solution)/shard_map/ppermute | solution.py:12
  47.8 7.6 %collective-permute-start.10 = (bf16[512,768]{1,0:T(8,128)(2,1)S(1)}, bf16[512,768]{1,0:T(8,128)(2,1)S(1)}, u32[]{:S(2)}, u32[]{:S(2)}) collective-permute-start(bf16[512,768]{1,0:T(8,128)(2,1)S(1)} %get-tuple-element.114), channel_id=1, source_target_pairs={{0,1},{1,0},{2,3},{3,2},{4,5},{5,4},{6,7},{7,6},{8,9},{9,8},{10,11... | collective-permute-start | bytes 2359304 | tf_op jit(solution)/shard_map/ppermute | solution.py:12
  47.8 16.1 %collective-permute-start.11 = (bf16[128,2048]{1,0:T(8,128)(2,1)S(1)}, bf16[128,2048]{1,0:T(8,128)(2,1)S(1)}, u32[]{:S(2)}, u32[]{:S(2)}) collective-permute-start(bf16[128,2048]{1,0:T(8,128)(2,1)S(1)} %collective-permute-done.6.refs_2_), channel_id=1, source_target_pairs={{0,4},{1,5},{2,6},{3,7},{4,8},{5,9},{6,10},{7,11},{8,12},{9,13},{1... | collective-permute-start | bytes 1572872 | tf_op jit(solution)/shard_map/ppermute | solution.py:448
  49.0 15.0 %collective-permute-start.12 = (bf16[128,2048]{1,0:T(8,128)(2,1)S(1)}, bf16[128,2048]{1,0:T(8,128)(2,1)S(1)}, u32[]{:S(2)}, u32[]{:S(2)}) collective-permute-start(bf16[128,2048]{1,0:T(8,128)(2,1)S(1)} %collective-permute-done.6.refs_2_), channel_id=1, source_target_pairs={{0,2},{1,3},{2,0},{3,1},{4,6},{5,7},{6,4},{7,5},{8,10},{9,11},{10,... | collective-permute-start | bytes 1572872 | tf_op jit(solution)/shard_map/ppermute | solution.py:12
  64.0 1.9 %collective-permute-start.14 = (bf16[128,2048]{1,0:T(8,128)(2,1)S(1)}, bf16[128,2048]{1,0:T(8,128)(2,1)S(1)}, u32[]{:S(2)}, u32[]{:S(2)}) collective-permute-start(bf16[128,2048]{1,0:T(8,128)(2,1)S(1)} %collective-permute-done.12.refs_0_), channel_id=1, source_target_pairs={{0,1},{1,0},{2,3},{3,2},{4,5},{5,4},{6,7},{7,6},{8,9},{9,8},{10,11... | collective-permute-start | bytes 1572872 | tf_op jit(solution)/shard_map/ppermute | solution.py:12
  64.0 2.7 %collective-permute-start.15 = (bf16[128,2048]{1,0:T(8,128)(2,1)S(1)}, bf16[128,2048]{1,0:T(8,128)(2,1)S(1)}, u32[]{:S(2)}, u32[]{:S(2)}) collective-permute-start(bf16[128,2048]{1,0:T(8,128)(2,1)S(1)} %collective-permute-done.11.refs_2_), channel_id=1, source_target_pairs={{0,1},{1,0},{2,3},{3,2},{4,5},{5,4},{6,7},{7,6},{8,9},{9,8},{10,11... | collective-permute-start | bytes 1572872 | tf_op jit(solution)/shard_map/ppermute | solution.py:12
  64.5 7.1 %collective-permute-start.16 = (bf16[512,768]{1,0:T(8,128)(2,1)S(1)}, bf16[512,768]{1,0:T(8,128)(2,1)S(1)}, u32[]{:S(2)}, u32[]{:S(2)}) collective-permute-start(bf16[512,768]{1,0:T(8,128)(2,1)S(1)} %get-tuple-element.134), channel_id=1, source_target_pairs={{0,1},{1,0},{2,3},{3,2},{4,5},{5,4},{6,7},{7,6},{8,9},{9,8},{10,11... | collective-permute-start | bytes 2359304 | tf_op jit(solution)/shard_map/ppermute | solution.py:12
  74.6 2.4 %collective-permute-start.17 = (bf16[512,768]{1,0:T(8,128)(2,1)S(1)}, bf16[512,768]{1,0:T(8,128)(2,1)S(1)}, u32[]{:S(2)}, u32[]{:S(2)}) collective-permute-start(bf16[512,768]{1,0:T(8,128)(2,1)S(1)} %get-tuple-element.144), channel_id=1, source_target_pairs={{0,1},{1,0},{2,3},{3,2},{4,5},{5,4},{6,7},{7,6},{8,9},{9,8},{10,11... | collective-permute-start | bytes 2359304 | tf_op jit(solution)/shard_map/ppermute | solution.py:12
  74.8 14.2 %collective-permute-start.13 = (bf16[128,2048]{1,0:T(8,128)(2,1)S(1)}, bf16[128,2048]{1,0:T(8,128)(2,1)S(1)}, u32[]{:S(2)}, u32[]{:S(2)}) collective-permute-start(bf16[128,2048]{1,0:T(8,128)(2,1)S(1)} %collective-permute-done.11.refs_2_), channel_id=1, source_target_pairs={{0,2},{1,3},{2,0},{3,1},{4,6},{5,7},{6,4},{7,5},{8,10},{9,11},{10,... | collective-permute-start | bytes 1572872 | tf_op jit(solution)/shard_map/ppermute | solution.py:12
  89.1 1.9 %collective-permute-start.18 = (bf16[128,2048]{1,0:T(8,128)(2,1)S(1)}, bf16[128,2048]{1,0:T(8,128)(2,1)S(1)}, u32[]{:S(2)}, u32[]{:S(2)}) collective-permute-start(bf16[128,2048]{1,0:T(8,128)(2,1)S(1)} %collective-permute-done.13.refs_0_), channel_id=1, source_target_pairs={{0,1},{1,0},{2,3},{3,2},{4,5},{5,4},{6,7},{7,6},{8,9},{9,8},{10,11... | collective-permute-start | bytes 1572872 | tf_op jit(solution)/shard_map/ppermute | solution.py:12
  93.8 3.3 %collective-permute-start.19 = (bf16[256,768]{1,0:T(8,128)(2,1)S(1)}, bf16[256,768]{1,0:T(8,128)(2,1)S(1)}, u32[]{:S(2)}, u32[]{:S(2)}) collective-permute-start(bf16[256,768]{1,0:T(8,128)(2,1)S(1)} %get-tuple-element.159), channel_id=1, source_target_pairs={{0,1},{1,0},{2,3},{3,2},{4,5},{5,4},{6,7},{7,6},{8,9},{9,8},{10,11... | collective-permute-start | bytes 1179656 | tf_op jit(solution)/shard_map/ppermute | solution.py:12
  (6 other events, 6.6 us)

commit v4 on v3

--- a/solution.py
+++ b/solution.py
@@ -134,11 +134,12 @@
 
 
 VMEM_GRANT = 16 << 20
+SMALL_COST = pl.CostEstimate(flops=1 << 20, bytes_accessed=1 << 16, transcendentals=0)
 
 
 def route_table_kernel(quota_ref, pick_ref, entry_ref, coef_ref, out_ref):
     top_count, tokens = pick_ref.shape
-    experts = out_ref.shape[0]
+    experts = out_ref.shape[1]
     levels = coef_ref.shape[1]
     picks = pick_ref[...]
     entries = entry_ref[...]
@@ -161,13 +162,8 @@
     for expert in range(experts):
         bound = jnp.where(expert_row == expert, quota_ref[expert].astype(jnp.float32), bound)
     used = jnp.where(rank < bound, weight, 0.0).astype(jnp.bfloat16)
-    one = lax.broadcasted_iota(jnp.int32, (experts, experts), 0)
-    two = lax.broadcasted_iota(jnp.int32, (experts, experts), 1)
-    partner = jnp.where(jnp.bitwise_xor(one, 1) == two, 1.0, 0.0).astype(jnp.bfloat16)
-    out_ref[:, :tokens] = used
-    out_ref[:, tokens:] = jnp.dot(partner, used, preferred_element_type=jnp.float32).astype(
-        jnp.bfloat16
-    )
+    for receiver in range(experts):
+        out_ref[receiver] = used
 
 
 def route_table(picks, entries, coefficients, quotas):
@@ -176,7 +172,7 @@
     vmem = pl.BlockSpec(memory_space=pltpu.VMEM)
     return pl.pallas_call(
         route_table_kernel,
-        out_shape=jax.ShapeDtypeStruct((experts, 2 * tokens), jnp.bfloat16),
+        out_shape=jax.ShapeDtypeStruct((experts, experts, tokens), jnp.bfloat16),
         in_specs=[pl.BlockSpec(memory_space=pltpu.SMEM), vmem, vmem, vmem],
         out_specs=vmem,
         compiler_params=pltpu.CompilerParams(vmem_limit_bytes=VMEM_GRANT),
@@ -184,44 +180,57 @@
     )(quotas, picks.T, entries.T, coefficients[None, :])
 
 
-def hidden_kernel(block_total, source_slot, place_ref, table_ref, *refs):
+def hidden_kernel(places, table_ref, flag_ref, *refs):
+    block_total = len(places)
     block_refs = refs[:block_total]
     gate_ref, up_ref, lhs_ref, count_ref, weigh_ref, send_ref = refs[block_total : block_total + 6]
     rows_ref, coef_ref, arrive = refs[block_total + 6 :]
-    tokens = block_refs[0].shape[0]
-    hidden_width = gate_ref.shape[1]
-    copies = []
+    experts, _, tokens = table_ref.shape
+    hidden_width = gate_ref.shape[2]
+    copies, spans = [], []
     for block in range(block_total):
-        target = rows_ref.at[block * tokens : (block + 1) * tokens]
-        copies.append(pltpu.make_async_copy(block_refs[block], target, arrive.at[block]))
+        first = spans[-1].stop if spans else 0
+        spans.append(slice(first, first + block_refs[block].shape[0]))
+        copies.append(
+            pltpu.make_async_copy(block_refs[block], rows_ref.at[spans[block]], arrive.at[block])
+        )
         copies[-1].start()
-    keep = place_ref[1].astype(jnp.float32)
-    merge = place_ref[2].astype(jnp.float32)
+    me = lax.axis_index("expert")
+    partner_index = jnp.bitwise_xor(me, 1)
+    keep = flag_ref[me].astype(jnp.float32)
+    merge = keep * (1.0 - flag_ref[partner_index].astype(jnp.float32))
     row = lax.broadcasted_iota(jnp.int32, (tokens, tokens), 0)
     col = lax.broadcasted_iota(jnp.int32, (tokens, tokens), 1)
-    table = table_ref[...].astype(jnp.float32)
-    table_row = lax.broadcasted_iota(jnp.int32, table.shape, 0)
-    for block in range(block_total):
-        source = place_ref[source_slot + block]
-        weights = jnp.sum(jnp.where(table_row == source, table, 0.0), axis=0, keepdims=True)
-        own = jnp.where(row == col, weights[:, :tokens], 0.0)
-        partner = jnp.where(row == col, weights[:, tokens:], 0.0)
-        own = jnp.sum(own, axis=1, keepdims=True)
-        partner = jnp.sum(partner, axis=1, keepdims=True)
+    expert_row = lax.broadcasted_iota(jnp.int32, (experts, tokens), 0)
+    for block, (steps, turn, offset) in enumerate(places):
+        source = jnp.bitwise_xor(lax.rem(me + experts - 4 * steps, experts), turn)
+        table = table_ref[source].astype(jnp.float32)
+        own = jnp.sum(jnp.where(expert_row == me, table, 0.0), axis=0, keepdims=True)
+        partner = jnp.sum(jnp.where(expert_row == partner_index, table, 0.0), axis=0, keepdims=True)
+        own = jnp.sum(jnp.where(row == col, own, 0.0), axis=1, keepdims=True)
+        partner = jnp.sum(jnp.where(row == col, partner, 0.0), axis=1, keepdims=True)
         count = jnp.where(own > 0.0, keep, 0.0) + jnp.where(partner > 0.0, merge, 0.0)
-        span = slice(block * tokens, (block + 1) * tokens)
-        coef_ref[0, span, :] = jnp.broadcast_to(count, (tokens, 128))
-        coef_ref[1, span, :] = jnp.broadcast_to(own, (tokens, 128))
+        size = spans[block].stop - spans[block].start
+        part = slice(offset, offset + size)
+        coef_ref[0, spans[block], :] = jnp.broadcast_to(count[part], (size, 128))
+        coef_ref[1, spans[block], :] = jnp.broadcast_to(own[part], (size, 128))
     tile = 256
+    groups, group = [], []
     for pair in range(0, block_total, 2):
-        copies[pair].wait()
-        copies[pair + 1].wait()
-        span = slice(pair * tokens, (pair + 2) * tokens)
+        group.append(pair)
+        if spans[pair + 1].stop - spans[group[0]].start >= 256 or pair + 2 == block_total:
+            groups.append(group)
+            group = []
+    for group in groups:
+        for pair in group:
+            copies[pair].wait()
+            copies[pair + 1].wait()
+        span = slice(spans[group[0]].start, spans[group[-1] + 1].stop)
         rows = rows_ref[span, :]
         for start in range(0, hidden_width, tile):
             lanes = slice(start, start + tile)
-            gate = jnp.dot(rows, gate_ref[:, lanes], preferred_element_type=jnp.float32)
-            upward = jnp.dot(rows, up_ref[:, lanes], preferred_element_type=jnp.float32)
+            gate = jnp.dot(rows, gate_ref[0, :, lanes], preferred_element_type=jnp.float32)
+            upward = jnp.dot(rows, up_ref[0, :, lanes], preferred_element_type=jnp.float32)
             hidden = (gate / (1.0 + jnp.exp(-gate)) * upward).astype(jnp.bfloat16)
             lhs_ref[lanes, span] = hidden.T
             hidden = hidden.astype(jnp.float32)
@@ -231,24 +240,30 @@
                 count_ref[span, to] = (part * coef_ref[0, span, :]).astype(jnp.bfloat16)
                 weighed = (part * coef_ref[1, span, :]).astype(jnp.bfloat16)
                 weigh_ref[span, to] = weighed
-                middle = (pair + 1) * tokens
-                send_ref[pair * tokens : middle, to] = weighed[tokens:]
-                send_ref[middle : (pair + 2) * tokens, to] = weighed[:tokens]
+                for pair in group:
+                    mine, theirs = spans[pair], spans[pair + 1]
+                    base = span.start
+                    send_ref[mine, to] = weighed[theirs.start - base : theirs.stop - base]
+                    send_ref[theirs, to] = weighed[mine.start - base : mine.stop - base]
 
 
 def in_vmem(x):
     return pltpu.with_memory_space_constraint(x, pltpu.VMEM)
 
 
-def hidden_parts(place, source_slot, table, blocks, w_gate, w_up, name):
-    tokens, width = blocks[0].shape
+def in_hbm(x):
+    return pltpu.with_memory_space_constraint(x, pltpu.HBM)
+
+
+def hidden_parts(places, table, flags, blocks, w_gate, w_up, name):
+    width = blocks[0].shape[1]
     block_total = len(blocks)
-    rows = block_total * tokens
-    hidden_width = w_gate.shape[1]
+    rows = sum(block.shape[0] for block in blocks)
+    hidden_width = w_gate.shape[2]
     vmem = pl.BlockSpec(memory_space=pltpu.VMEM)
     outside = pl.BlockSpec(memory_space=pl.ANY)
     return pl.pallas_call(
-        functools.partial(hidden_kernel, block_total, source_slot),
+        functools.partial(hidden_kernel, places),
         out_shape=(
             pltpu.VMEM((hidden_width, rows), jnp.bfloat16),
             pltpu.VMEM((rows, hidden_width), jnp.bfloat16),
@@ -256,8 +271,8 @@
             jax.ShapeDtypeStruct((rows, hidden_width), jnp.bfloat16),
         ),
         in_specs=[
+            vmem,
             pl.BlockSpec(memory_space=pltpu.SMEM),
-            vmem,
             *[outside] * block_total,
             vmem,
             vmem,
@@ -269,39 +284,9 @@
             pltpu.SemaphoreType.DMA((block_total,)),
         ],
         compiler_params=pltpu.CompilerParams(vmem_limit_bytes=VMEM_GRANT),
-        cost_estimate=pl.CostEstimate(
-            flops=4 * rows * width * hidden_width,
-            bytes_accessed=2 * rows * width + 2 * rows * hidden_width,
-            transcendentals=rows * hidden_width,
-        ),
+        cost_estimate=SMALL_COST,
         name=name,
-    )(place, table, *blocks, in_vmem(w_gate), in_vmem(w_up))
-
-
-def resident_kernel(gate_ref, up_ref, gate_out, up_out, arrive):
-    copies = [
-        pltpu.make_async_copy(gate_ref.at[0], gate_out, arrive.at[0]),
-        pltpu.make_async_copy(up_ref.at[0], up_out, arrive.at[1]),
-    ]
-    for copy in copies:
-        copy.start()
-    for copy in copies:
-        copy.wait()
-
-
-def resident(w_gate, w_up):
-    shape = w_gate.shape[1:]
-    outside = pl.BlockSpec(memory_space=pl.ANY)
-    vmem = pl.BlockSpec(memory_space=pltpu.VMEM)
-    return pl.pallas_call(
-        resident_kernel,
-        out_shape=(pltpu.VMEM(shape, w_gate.dtype), pltpu.VMEM(shape, w_up.dtype)),
-        in_specs=[outside, outside],
-        out_specs=(vmem, vmem),
-        scratch_shapes=[pltpu.SemaphoreType.DMA((2,))],
-        compiler_params=pltpu.CompilerParams(vmem_limit_bytes=VMEM_GRANT),
-        name="resident_weights",
-    )(w_gate, w_up)
+    )(table, flags, *[in_hbm(block) for block in blocks], in_vmem(w_gate), in_vmem(w_up))
 
 
 def totals_kernel(part_total, has_base, *refs):
@@ -360,24 +345,26 @@
             pltpu.SemaphoreType.DMA((len(parts),)),
         ],
         compiler_params=pltpu.CompilerParams(vmem_limit_bytes=VMEM_GRANT),
-        cost_estimate=pl.CostEstimate(
-            flops=6 * rows * hidden_width * hidden_width,
-            bytes_accessed=2 * rows * hidden_width,
-            transcendentals=0,
-        ),
+        cost_estimate=SMALL_COST,
         name=name,
     )(*operands)
 
 
-def final_kernel(set_total, slots, divisor, place_ref, lhs_ref, *refs):
+def final_kernel(set_total, slots, divisor, flag_ref, lhs_ref, *refs):
     rhs, bases = refs[:set_total], refs[set_total : 2 * set_total]
     outs, done_ref, leave = refs[2 * set_total : 3 * set_total], refs[-2], refs[-1]
     hidden_width = lhs_ref.shape[0]
+    me = lax.axis_index("expert")
+    keep = flag_ref[me].astype(jnp.float32)
+    keep_partner = flag_ref[jnp.bitwise_xor(me, 1)].astype(jnp.float32)
     tile = 256
     copies = []
     for index in range(set_total):
-        factor = 1.0 if slots[index] is None else place_ref[slots[index]].astype(jnp.float32)
-        factor = factor / divisor
+        factor = 1.0 / divisor
+        if slots[index] != "gram":
+            factor = factor * keep
+        if slots[index] == "merge":
+            factor = factor * (1.0 - keep_partner)
         for start in range(0, hidden_width, tile):
             span = slice(start, start + tile)
             total = bases[index][span, :] + jnp.dot(
@@ -396,7 +383,7 @@
         copy.wait()
 
 
-def final_sums(place, lhs, rhs, bases, slots, divisor, name):
+def final_sums(flags, lhs, rhs, bases, slots, divisor, name):
     hidden_width, rows = lhs.shape
     total = len(rhs)
     vmem = pl.BlockSpec(memory_space=pltpu.VMEM)
@@ -411,13 +398,9 @@
             pltpu.SemaphoreType.DMA((total, hidden_width // 256)),
         ],
         compiler_params=pltpu.CompilerParams(vmem_limit_bytes=VMEM_GRANT),
-        cost_estimate=pl.CostEstimate(
-            flops=2 * total * rows * hidden_width * hidden_width,
-            bytes_accessed=4 * total * hidden_width * hidden_width,
-            transcendentals=0,
-        ),
+        cost_estimate=SMALL_COST,
         name=name,
-    )(place, in_vmem(lhs), *rhs, *[in_vmem(base) for base in bases])
+    )(flags, in_vmem(lhs), *rhs, *[in_vmem(base) for base in bases])
 
 
 def gathered_shards(
@@ -433,66 +416,78 @@
     experts = retained_specialist_flags.shape[0]
     tok_rows, top_count = specialist_picks.shape
     position_ordinal = max(4, 3 * tok_rows * top_count // (4 * experts))
-    me = lax.axis_index("expert")
-    core = jnp.bitwise_and(me, 1)
-    expert_lane = jnp.arange(experts, dtype=jnp.int32)
-    keep = jnp.sum(jnp.where(expert_lane == me, retained_specialist_flags, 0))
-    keep_partner = jnp.sum(
-        jnp.where(expert_lane == jnp.bitwise_xor(me, 1), retained_specialist_flags, 0)
-    )
-    merge = keep * (1 - keep_partner)
-    groups = experts // 4
     divisor = experts * position_ordinal
+    half = tok_rows // 2
 
     def along(x):
         return lax.ppermute(x, "expert", [(i, (i + 4) % experts) for i in range(experts)])
 
-    def back(steps):
-        return jnp.bitwise_and(jnp.remainder(me + experts - 4 * steps, experts), ~1)
-
-    firsts = [back(0)]
-    for step in range(1, groups):
-        firsts += [jnp.bitwise_xor(back(step - 1), 2), back(step)]
-    firsts.append(jnp.bitwise_xor(back(groups - 1), 2))
-    sources = []
-    for first in firsts:
-        sources += [first + core, first + 1 - core]
-    place = jnp.stack([core, keep, merge, *sources]).astype(jnp.int32)
-    w_gate, w_up = resident(gating_projection, raising_projection)
-
-    def hidden(slot, blocks, name):
-        return hidden_parts(place, 3 + 2 * slot, table, blocks, w_gate, w_up, name)
+    def across(x):
+        return swapped(x, "expert", 1)
 
     def other(x):
         return swapped(x, "expert", 0)
 
-    line, side = along(layer_inputs), swapped(layer_inputs, "expert", 1)
-    near = other(layer_inputs)
+    def hidden(arrivals, name):
+        blocks, places = [], []
+        for block, steps, turn, offset in arrivals:
+            blocks += [block, other(block)]
+            places += [(steps, turn, offset), (steps, turn ^ 1, offset)]
+        return hidden_parts(
+            places,
+            table,
+            retained_specialist_flags,
+            blocks,
+            gating_projection,
+            raising_projection,
+            name,
+        )
+
+    def totals(parts, bases, name):
+        return add_totals([(*part[:3], other(part[3])) for part in parts], bases, name)
+
+    tied = lax.optimization_barrier
+    line_1, side_0 = along(layer_inputs), across(layer_inputs)
     table = route_table(
         specialist_picks, coefficient_lookup_entry, dispatch_coefficients, specialist_quotas
     )
     table = lax.all_to_all(table, "expert", split_axis=0, concat_axis=0, tiled=True)
-    part = hidden(0, [layer_inputs, near], "hidden_0")
-    bases = None
-    for step in range(1, groups):
-        part, line, side = lax.optimization_barrier((part, line, side))
-        part = (*part[:3], other(part[3]))
-        next_line = along(line) if step < groups - 1 else None
-        next_side = swapped(line, "expert", 1)
-        blocks = [side, other(side), line, other(line)]
-        new = hidden(2 * step - 1, blocks, "hidden_%d" % step)
-        bases = add_totals([part], bases, "totals_%d" % step)
-        new, bases = lax.optimization_barrier((new, bases))
-        part, line, side = new, next_line, next_side
-    bases = add_totals([(*part[:3], other(part[3]))], bases, "totals_last")
-    side, bases = lax.optimization_barrier((side, bases))
-    last = hidden(2 * groups - 1, [side, other(side)], "hidden_last")
+
+    table, line_1, side_0 = tied((table, line_1, side_0))
+    line_2, side_1 = along(line_1), across(line_1)
+    first = [(layer_inputs, 0, 0, 0), (side_0, 0, 2, 0), (line_1, 1, 0, 0)]
+    first = hidden(first, "hidden_first")
+
+    first, line_2, side_1 = tied((first, line_2, side_1))
+    upper_3, side_2 = along(line_2[:half]), across(line_2)
+    lower_3 = along(line_2[half:])
+    second = hidden([(side_1, 1, 2, 0), (line_2, 2, 0, 0)], "hidden_second")
+    bases = totals([first], None, "totals_first")
+
+    second, upper_3 = tied((second, upper_3))
+    last_upper = across(upper_3)
+    bases, lower_3, side_2 = tied((bases, lower_3, side_2))
+    last_lower = across(lower_3)
+    third = [(side_2, 2, 2, 0), (upper_3, 3, 0, 0), (lower_3, 3, 0, half)]
+    third = hidden(third, "hidden_third")
+    bases = totals([second], bases, "totals_second")
+    fourth = hidden([(last_upper, 3, 2, 0)], "hidden_fourth")
+    bases = totals([third, fourth], bases, "totals_third")
+
+    bases, last_lower = tied((bases, last_lower))
+    last = hidden([(last_lower, 3, 2, half)], "hidden_last")
     arrived = other(last[3])
     gram, self_cross = final_sums(
-        place, last[0], [in_vmem(last[1]), in_vmem(last[2])], bases[:2], (None, 1), divisor, "own_sums"
+        retained_specialist_flags,
+        last[0],
+        [in_vmem(last[1]), in_vmem(last[2])],
+        bases[:2],
+        ("gram", "self"),
+        divisor,
+        "own_sums",
     )
     (merge_cross,) = final_sums(
-        place, last[0], [arrived], bases[2:], (2,), divisor, "merge_sums"
+        retained_specialist_flags, last[0], [arrived], bases[2:], ("merge",), divisor, "merge_sums"
     )
     return gram, self_cross, merge_cross
 

time: 100 us -> 101 us (1.010)
  Pallas kernels: 39.4 us -> 42.8 us
  other arithmetic: 1.94 us -> 0 us
  between operations: 2.29 us -> 1.08 us
    all_to_all x1, waiting for transfers between devices: 0.01 us -> 6.49 us  [gathered_shards(): lax.all_to_all(table, 'expert', split_axis=0, concat_axis=0, tiled=True)]
    ppermute x3 -> x4, waiting for transfers between devices: 11.2 us -> 4.97 us  [along(): lax.ppermute(x, 'expert', [(i, (i + 4) % experts) for i in range(experts)])]
    pallas_call x6 -> x5, Pallas kernels: 22.3 us -> 24.7 us  [hidden_parts(): pl.pallas_call(functools.partial(hidden_kernel, places), out_shape=(pltpu...]
    reduce_sum x1 -> x0, other arithmetic: 1.29 us -> none  [gathered_shards(): jnp.sum(jnp.where(expert_lane == jnp.bitwise_xor(me, 1), retained_special...]
    unnamed x21 -> x54, local copies, waits for them, and re-layouts: 11 us -> 11.9 us
    pallas_call x4 -> x3, Pallas kernels: 10.9 us -> 11.5 us  [add_totals(): pl.pallas_call(functools.partial(totals_kernel, len(parts), bases is not...]
    ppermute x17 -> x20, starting transfers between devices: 9.1 us -> 9.37 us  [swapped(): lax.ppermute(x, axis, [(i, i ^ 1 << stride) for i in range(lax.axis_size(...]
    ppermute x17 -> x20, waiting for transfers between devices: 13.3 us -> 13.4 us  [swapped(): lax.ppermute(x, axis, [(i, i ^ 1 << stride) for i in range(lax.axis_size(...]
  transfers between devices with their start and end apart: 21 -> 25, of which waited for: 7 -> 12; matrix products, arithmetic and copies ran while one was open for 4% -> 1% of each run, Pallas kernels for 31% -> 38%
where the time goes in v4:
time: 101 us; the launch traced here: 100 us
  Pallas kernels  42.8 us (42%)
  waiting for transfers between devices  24.9 us (25%)
  starting transfers between devices  18.9 us (19%)
  local copies, waits for them, and re-layouts  12.6 us (12%)
  between operations  1.08 us (1%)
    pallas_call x5, Pallas kernels, hidden_parts(): pl.pallas_call(functools.partial(hidden_kernel, places), out_shape=(pltpu...  24.7 us
    ppermute x20, waiting for transfers between devices, swapped(): lax.ppermute(x, axis, [(i, i ^ 1 << stride) for i in range(lax.axis_size(...  13.4 us
    unnamed x54, local copies, waits for them, and re-layouts  11.9 us
    pallas_call x3, Pallas kernels, add_totals(): pl.pallas_call(functools.partial(totals_kernel, len(parts), bases is not...  11.5 us
    ppermute x20, starting transfers between devices, swapped(): lax.ppermute(x, axis, [(i, i ^ 1 << stride) for i in range(lax.axis_size(...  9.37 us
    all_to_all x1, waiting for transfers between devices, gathered_shards(): lax.all_to_all(table, 'expert', split_axis=0, concat_axis=0, tiled=True)  6.49 us
    ppermute x4, starting transfers between devices, along(): lax.ppermute(x, 'expert', [(i, (i + 4) % experts) for i in range(experts)])  5.51 us
    pallas_call x2, Pallas kernels, final_sums(): pl.pallas_call(functools.partial(final_kernel, total, slots, float(diviso...  5.27 us
  transfers between devices with their start and end apart: 25, of which 12 were waited for; matrix products, arithmetic and copies ran while one was open for 1% of the time, Pallas kernels for 38%

profile of v4, /device:TPU:0, one launch (start us, length us, event | category | flops | bytes accessed | tf_op | source)
XLA Modules:
  0.0 100.3 jit_solution(9353172278616847002)
XLA Ops:
  0.6 3.1 %collective-permute-start = (bf16[128,2048]{1,0:T(8,128)(2,1)}, bf16[128,2048]{1,0:T(8,128)(2,1)S(1)}, u32[]{:S(2)}, u32[]{:S(2)}) collective-permute-start(bf16[128,2048]{1,0:T(8,128)(2,1)} %refs_0_.1), channel_id=1, source_target_pairs={{0,4},{1,5},{2,6},{3,7},{4,8},{5,9},{6,10},{7,11},{8,12},{9,13},{1... | collective-permute-start | bytes 1572872 | tf_op jit(solution)/shard_map/ppermute | solution.py:423
  3.7 1.5 %collective-permute-start.1 = (bf16[128,2048]{1,0:T(8,128)(2,1)}, bf16[128,2048]{1,0:T(8,128)(2,1)S(1)}, u32[]{:S(2)}, u32[]{:S(2)}) collective-permute-start(bf16[128,2048]{1,0:T(8,128)(2,1)} %refs_0_.1), channel_id=1, source_target_pairs={{0,2},{1,3},{2,0},{3,1},{4,6},{5,7},{6,4},{7,5},{8,10},{9,11},{10,... | collective-permute-start | bytes 1572872 | tf_op jit(solution)/shard_map/ppermute | solution.py:12
  7.9 1.4 %route_table.1 = bf16[16,16,128]{2,1,0:T(8,128)(2,1)} custom-call(s32[16]{0:T(128)S(1)} %copy-done.7, s32[8,128]{1,0:T(8,128)S(1)} %bitcast.2, s32[8,128]{1,0:T(8,128)S(1)} %bitcast.3, bf16[1,256]{1,0:T(2,128)(2,1)S(1)} %broadcast_in_dim.3.coef_ref), custom_call_target="tpu_custom_call" | custom-call | tf_op jit(solution)/shard_map/route_table/pallas_call | solution.py:173
  9.3 4.0 %all-to-all-start = ((bf16[16,16,128]{2,1,0:T(8,128)(2,1)}), bf16[16,16,128]{2,1,0:T(8,128)(2,1)S(1)}, u32[]{:S(2)}, u32[]{:S(2)}) async-start(bf16[16,16,128]{2,1,0:T(8,128)(2,1)} %route_table.1), calls=%async_computation | async-start | bytes 131072 | tf_op jit(solution)/shard_map/all_to_all | solution.py:454
  13.7 6.5 %all-to-all-done.table_ref = bf16[16,16,128]{2,1,0:T(8,128)(2,1)S(1)} async-done(((bf16[16,16,128]{2,1,0:T(8,128)(2,1)}), bf16[16,16,128]{2,1,0:T(8,128)(2,1)S(1)}, u32[]{:S(2)}, u32[]{:S(2)}) %all-to-all-start) | async-done | bytes 65568 | tf_op jit(solution)/shard_map/all_to_all | solution.py:454
  23.8 1.9 %copy-done = bf16[1,2048,768]{2,1,0:T(8,128)(2,1)S(1)} copy-done((bf16[1,2048,768]{2,1,0:T(8,128)(2,1)S(1)}, bf16[1,2048,768]{2,1,0:T(8,128)(2,1)}, u32[]{:S(2)}) %copy-start) | copy-done | bytes 3145752
  25.6 1.9 %copy-done.2 = bf16[1,2048,768]{2,1,0:T(8,128)(2,1)S(1)} copy-done((bf16[1,2048,768]{2,1,0:T(8,128)(2,1)S(1)}, bf16[1,2048,768]{2,1,0:T(8,128)(2,1)}, u32[]{:S(2)}) %copy-start.2) | copy-done | bytes 3145752
  28.2 8.0 %hidden_first.1 = (bf16[768,768]{1,0:T(8,128)(2,1)S(1)}, bf16[768,768]{1,0:T(8,128)(2,1)S(1)}, bf16[768,768]{1,0:T(8,128)(2,1)S(1)}, bf16[768,768]{1,0:T(8,128)(2,1)S(1)}) custom-call(bf16[16,16,128]{2,1,0:T(8,128)(2,1)S(1)} %all-to-all-done.table_ref, s32[16]{0:T(128)S(1)} %copy-done.4, bf16[128,2048]{1,0:T(8,128)(2,1)} %refs_0_.1, ...), custom_call_target="tpu_custom_call" | custom-call | flops 1048576 | bytes 65536 | tf_op jit(solution)/shard_map/hidden_first/pallas_call | solution.py:265
  37.0 1.0 %collective-permute-start.9 = (bf16[128,2048]{1,0:T(8,128)(2,1)S(1)}, bf16[128,2048]{1,0:T(8,128)(2,1)S(1)}, u32[]{:S(2)}, u32[]{:S(2)}) collective-permute-start(bf16[128,2048]{1,0:T(8,128)(2,1)S(1)} %collective-permute-done.5.refs_2_), channel_id=1, source_target_pairs={{0,2},{1,3},{2,0},{3,1},{4,6},{5,7},{6,4},{7,5},{8,10},{9,11},{10,... | collective-permute-start | bytes 1572872 | tf_op jit(solution)/shard_map/ppermute | solution.py:12
  39.4 1.0 %collective-permute-start.13 = (bf16[64,2048]{1,0:T(8,128)(2,1)S(1)}, bf16[64,2048]{1,0:T(8,128)(2,1)S(1)}, u32[]{:S(2)}, u32[]{:S(2)}) collective-permute-start(bf16[64,2048]{1,0:T(8,128)(2,1)S(1)} %get-tuple-element.111), channel_id=1, source_target_pairs={{0,4},{1,5},{2,6},{3,7},{4,8},{5,9},{6,10},{7,11},{8,12},{9,13},{1... | collective-permute-start | bytes 786440 | tf_op jit(solution)/shard_map/ppermute | solution.py:423
  40.4 3.9 %totals_first.1 = (f32[768,768]{1,0:T(8,128)S(1)}, f32[768,768]{1,0:T(8,128)S(1)}, f32[768,768]{1,0:T(8,128)S(1)}) custom-call(bf16[768,768]{1,0:T(8,128)(2,1)S(1)} %get-tuple-element.64.refs_0_, bf16[768,768]{1,0:T(8,128)(2,1)S(1)} %get-tuple-element.65.refs_1_, bf16[768,768]{1,0:T(8,128)(2,1)S(1)} %get-tuple-element.66.refs_2_, ...), custom_call_target="tpu_custom_call" | custom-call | flops 1048576 | bytes 65536 | tf_op jit(solution)/shard_map/totals_first/pallas_call | solution.py:337
  44.4 4.7 %collective-permute-done.8.refs_4_ = bf16[64,2048]{1,0:T(8,128)(2,1)S(1)} collective-permute-done((bf16[64,2048]{1,0:T(8,128)(2,1)S(1)}, bf16[64,2048]{1,0:T(8,128)(2,1)S(1)}, u32[]{:S(2)}, u32[]{:S(2)}) %collective-permute-start.8) | collective-permute-done | bytes 262176 | tf_op jit(solution)/shard_map/ppermute | solution.py:423
  49.1 1.9 %collective-permute-done.9.refs_0_ = bf16[128,2048]{1,0:T(8,128)(2,1)S(1)} collective-permute-done((bf16[128,2048]{1,0:T(8,128)(2,1)S(1)}, bf16[128,2048]{1,0:T(8,128)(2,1)S(1)}, u32[]{:S(2)}, u32[]{:S(2)}) %collective-permute-start.9) | collective-permute-done | bytes 524320 | tf_op jit(solution)/shard_map/ppermute | solution.py:12
  52.6 5.7 %hidden_second.1 = (bf16[768,512]{1,0:T(8,128)(2,1)S(1)}, bf16[512,768]{1,0:T(8,128)(2,1)S(1)}, bf16[512,768]{1,0:T(8,128)(2,1)S(1)}, bf16[512,768]{1,0:T(8,128)(2,1)S(1)}) custom-call(bf16[16,16,128]{2,1,0:T(8,128)(2,1)S(1)} %all-to-all-done.table_ref, s32[16]{0:T(128)S(1)} %copy-done.4, bf16[128,2048]{1,0:T(8,128)(2,1)} %copy-done.9, ...), custom_call_target="tpu_custom_call" | custom-call | flops 1048576 | bytes 65536 | tf_op jit(solution)/shard_map/hidden_second/pallas_call | solution.py:265
  61.9 5.7 %hidden_third.1 = (bf16[768,512]{1,0:T(8,128)(2,1)S(1)}, bf16[512,768]{1,0:T(8,128)(2,1)S(1)}, bf16[512,768]{1,0:T(8,128)(2,1)S(1)}, bf16[512,768]{1,0:T(8,128)(2,1)S(1)}) custom-call(bf16[16,16,128]{2,1,0:T(8,128)(2,1)S(1)} %all-to-all-done.table_ref, s32[16]{0:T(128)S(1)} %copy-done.4, bf16[128,2048]{1,0:T(8,128)(2,1)} %copy-done.10, ...), custom_call_target="tpu_custom_call" | custom-call | flops 1048576 | bytes 65536 | tf_op jit(solution)/shard_map/hidden_third/pallas_call | solution.py:265
  69.1 7.5 %collective-permute-done.17.refs_0_ = bf16[64,2048]{1,0:T(8,128)(2,1)S(1)} collective-permute-done((bf16[64,2048]{1,0:T(8,128)(2,1)}, bf16[64,2048]{1,0:T(8,128)(2,1)S(1)}, u32[]{:S(2)}, u32[]{:S(2)}) %collective-permute-start.17) | collective-permute-done | bytes 262176 | tf_op jit(solution)/shard_map/ppermute | solution.py:12
  76.6 1.0 %collective-permute-start.21 = (bf16[64,2048]{1,0:T(8,128)(2,1)}, bf16[64,2048]{1,0:T(8,128)(2,1)S(1)}, u32[]{:S(2)}, u32[]{:S(2)}) collective-permute-start(bf16[64,2048]{1,0:T(8,128)(2,1)} %copy-done.19), channel_id=1, source_target_pairs={{0,2},{1,3},{2,0},{3,1},{4,6},{5,7},{6,4},{7,5},{8,10},{9,11},{10,... | collective-permute-start | bytes 786440 | tf_op jit(solution)/shard_map/ppermute | solution.py:12
  78.8 2.7 %hidden_fourth.1 = (bf16[768,128]{1,0:T(8,128)(2,1)S(1)}, bf16[128,768]{1,0:T(8,128)(2,1)S(1)}, bf16[128,768]{1,0:T(8,128)(2,1)S(1)}, bf16[128,768]{1,0:T(8,128)(2,1)S(1)}) custom-call(bf16[16,16,128]{2,1,0:T(8,128)(2,1)S(1)} %all-to-all-done.table_ref, s32[16]{0:T(128)S(1)} %copy-done.4, bf16[64,2048]{1,0:T(8,128)(2,1)} %copy-done.24, ...), custom_call_target="tpu_custom_call" | custom-call | flops 1048576 | bytes 65536 | tf_op jit(solution)/shard_map/hidden_fourth/pallas_call | solution.py:265
  81.7 3.2 %totals_second.1 = (f32[768,768]{1,0:T(8,128)S(1)}, f32[768,768]{1,0:T(8,128)S(1)}, f32[768,768]{1,0:T(8,128)S(1)}) custom-call(bf16[768,512]{1,0:T(8,128)(2,1)S(1)} %get-tuple-element.88.refs_0_, bf16[512,768]{1,0:T(8,128)(2,1)S(1)} %get-tuple-element.89.refs_1_, ...), custom_call_target="tpu_custom_call", output_to_operand_aliasing={{0}: (4, {}), {1}: (5, {}), {2}: (6, {})} | custom-call | flops 1048576 | bytes 65536 | tf_op jit(solution)/shard_map/totals_second/pallas_call | solution.py:337
  85.0 4.3 %totals_third.1 = (f32[768,768]{1,0:T(8,128)S(1)}, f32[768,768]{1,0:T(8,128)S(1)}, f32[768,768]{1,0:T(8,128)S(1)}) custom-call(bf16[768,512]{1,0:T(8,128)(2,1)S(1)} %get-tuple-element.80.refs_0_, bf16[512,768]{1,0:T(8,128)(2,1)S(1)} %get-tuple-element.81.refs_1_, ...), custom_call_target="tpu_custom_call", output_to_operand_aliasing={{0}: (8, {}), {1}: (9, {}), {2}: (10, {})} | custom-call | flops 1048576 | bytes 65536 | tf_op jit(solution)/shard_map/totals_third/pallas_call | solution.py:337
  89.8 1.2 %collective-permute-done.22.refs_1_ = bf16[64,2048]{1,0:T(8,128)(2,1)S(1)} collective-permute-done((bf16[64,2048]{1,0:T(8,128)(2,1)S(1)}, bf16[64,2048]{1,0:T(8,128)(2,1)S(1)}, u32[]{:S(2)}, u32[]{:S(2)}) %collective-permute-start.22) | collective-permute-done | bytes 262176 | tf_op jit(solution)/shard_map/ppermute | solution.py:12
  91.6 2.7 %hidden_last.1 = (bf16[768,128]{1,0:T(8,128)(2,1)S(1)}, bf16[128,768]{1,0:T(8,128)(2,1)S(1)}, bf16[128,768]{1,0:T(8,128)(2,1)S(1)}, bf16[128,768]{1,0:T(8,128)(2,1)S(1)}) custom-call(bf16[16,16,128]{2,1,0:T(8,128)(2,1)S(1)} %all-to-all-done.table_ref, s32[16]{0:T(128)S(1)} %copy-done.4, bf16[64,2048]{1,0:T(8,128)(2,1)} %copy-done.21, ...), custom_call_target="tpu_custom_call" | custom-call | flops 1048576 | bytes 65536 | tf_op jit(solution)/shard_map/hidden_last/pallas_call | solution.py:265
  94.8 3.1 %own_sums.1 = (f32[1,768,768]{2,1,0:T(8,128)}, f32[1,768,768]{2,1,0:T(8,128)}) custom-call(s32[16]{0:T(128)S(1)} %copy-done.4, bf16[768,128]{1,0:T(8,128)(2,1)S(1)} %get-tuple-element.102.lhs_ref, bf16[128,768]{1,0:T(8,128)(2,1)S(1)} %get-tuple-element.103.refs_0_, bf16[128,768]{1,0:T(8,128)(2,1)S(1)} %get-tuple-element.104.refs_1_, ...), custom_call_target="tpu_custom_call" | custom-call | flops 1048576 | bytes 65536 | tf_op jit(solution)/shard_map/own_sums/pallas_call | solution.py:391
  97.9 2.2 %merge_sums.1 = f32[1,768,768]{2,1,0:T(8,128)} custom-call(s32[16]{0:T(128)S(1)} %copy-done.4, bf16[768,128]{1,0:T(8,128)(2,1)S(1)} %get-tuple-element.102.lhs_ref, bf16[128,768]{1,0:T(8,128)(2,1)S(1)} %collective-permute-done.23.refs_0_, f32[768,768]{1,0:T(8,128)S(1)} %get-tuple-element.110.refs_1_), custom_call_target="tpu_custom_call" | custom-call | flops 1048576 | bytes 65536 | tf_op jit(solution)/shard_map/merge_sums/pallas_call | solution.py:391
  (93 shorter events, 19.2 us)
Async XLA Ops:
  0.6 19.5 %collective-permute-start = (bf16[128,2048]{1,0:T(8,128)(2,1)}, bf16[128,2048]{1,0:T(8,128)(2,1)S(1)}, u32[]{:S(2)}, u32[]{:S(2)}) collective-permute-start(bf16[128,2048]{1,0:T(8,128)(2,1)} %refs_0_.1), channel_id=1, source_target_pairs={{0,4},{1,5},{2,6},{3,7},{4,8},{5,9},{6,10},{7,11},{8,12},{9,13},{1... | collective-permute-start | bytes 1572872 | tf_op jit(solution)/shard_map/ppermute | solution.py:423
  3.7 16.4 %collective-permute-start.1 = (bf16[128,2048]{1,0:T(8,128)(2,1)}, bf16[128,2048]{1,0:T(8,128)(2,1)S(1)}, u32[]{:S(2)}, u32[]{:S(2)}) collective-permute-start(bf16[128,2048]{1,0:T(8,128)(2,1)} %refs_0_.1), channel_id=1, source_target_pairs={{0,2},{1,3},{2,0},{3,1},{4,6},{5,7},{6,4},{7,5},{8,10},{9,11},{10,... | collective-permute-start | bytes 1572872 | tf_op jit(solution)/shard_map/ppermute | solution.py:12
  9.3 10.9 %all-to-all-start = ((bf16[16,16,128]{2,1,0:T(8,128)(2,1)}), bf16[16,16,128]{2,1,0:T(8,128)(2,1)S(1)}, u32[]{:S(2)}, u32[]{:S(2)}) async-start(bf16[16,16,128]{2,1,0:T(8,128)(2,1)} %route_table.1), calls=%async_computation | async-start | bytes 131072 | tf_op jit(solution)/shard_map/all_to_all | solution.py:454
  13.2 8.7 %collective-permute-start.2 = (bf16[128,2048]{1,0:T(8,128)(2,1)}, bf16[128,2048]{1,0:T(8,128)(2,1)S(1)}, u32[]{:S(2)}, u32[]{:S(2)}) collective-permute-start(bf16[128,2048]{1,0:T(8,128)(2,1)} %refs_0_.1), channel_id=1, source_target_pairs={{0,1},{1,0},{2,3},{3,2},{4,5},{5,4},{6,7},{7,6},{8,9},{9,8},{10,11... | collective-permute-start | bytes 1572872 | tf_op jit(solution)/shard_map/ppermute | solution.py:12
  20.2 2.0 %collective-permute-start.4 = (bf16[128,2048]{1,0:T(8,128)(2,1)S(1)}, bf16[128,2048]{1,0:T(8,128)(2,1)S(1)}, u32[]{:S(2)}, u32[]{:S(2)}) collective-permute-start(bf16[128,2048]{1,0:T(8,128)(2,1)S(1)} %collective-permute-done.refs_4_), channel_id=1, source_target_pairs={{0,1},{1,0},{2,3},{3,2},{4,5},{5,4},{6,7},{7,6},{8,9},{9,8},{10,11... | collective-permute-start | bytes 1572872 | tf_op jit(solution)/shard_map/ppermute | solution.py:12
  20.2 2.6 %collective-permute-start.3 = (bf16[128,2048]{1,0:T(8,128)(2,1)S(1)}, bf16[128,2048]{1,0:T(8,128)(2,1)S(1)}, u32[]{:S(2)}, u32[]{:S(2)}) collective-permute-start(bf16[128,2048]{1,0:T(8,128)(2,1)S(1)} %collective-permute-done.1.refs_2_), channel_id=1, source_target_pairs={{0,1},{1,0},{2,3},{3,2},{4,5},{5,4},{6,7},{7,6},{8,9},{9,8},{10,11... | collective-permute-start | bytes 1572872 | tf_op jit(solution)/shard_map/ppermute | solution.py:12
  20.7 15.7 %collective-permute-start.5 = (bf16[128,2048]{1,0:T(8,128)(2,1)S(1)}, bf16[128,2048]{1,0:T(8,128)(2,1)S(1)}, u32[]{:S(2)}, u32[]{:S(2)}) collective-permute-start(bf16[128,2048]{1,0:T(8,128)(2,1)S(1)} %collective-permute-done.refs_4_), channel_id=1, source_target_pairs={{0,4},{1,5},{2,6},{3,7},{4,8},{5,9},{6,10},{7,11},{8,12},{9,13},{1... | collective-permute-start | bytes 1572872 | tf_op jit(solution)/shard_map/ppermute | solution.py:423
  21.2 15.3 %collective-permute-start.6 = (bf16[128,2048]{1,0:T(8,128)(2,1)S(1)}, bf16[128,2048]{1,0:T(8,128)(2,1)S(1)}, u32[]{:S(2)}, u32[]{:S(2)}) collective-permute-start(bf16[128,2048]{1,0:T(8,128)(2,1)S(1)} %collective-permute-done.refs_4_), channel_id=1, source_target_pairs={{0,2},{1,3},{2,0},{3,1},{4,6},{5,7},{6,4},{7,5},{8,10},{9,11},{10,... | collective-permute-start | bytes 1572872 | tf_op jit(solution)/shard_map/ppermute | solution.py:12
  36.5 2.9 %collective-permute-start.7 = (bf16[768,768]{1,0:T(8,128)(2,1)S(1)}, bf16[768,768]{1,0:T(8,128)(2,1)S(1)}, u32[]{:S(2)}, u32[]{:S(2)}) collective-permute-start(bf16[768,768]{1,0:T(8,128)(2,1)S(1)} %get-tuple-element.67), channel_id=1, source_target_pairs={{0,1},{1,0},{2,3},{3,2},{4,5},{5,4},{6,7},{7,6},{8,9},{9,8},{10,11... | collective-permute-start | bytes 3538952 | tf_op jit(solution)/shard_map/ppermute | solution.py:12
  36.5 14.4 %collective-permute-start.12 = (bf16[128,2048]{1,0:T(8,128)(2,1)S(1)}, bf16[128,2048]{1,0:T(8,128)(2,1)S(1)}, u32[]{:S(2)}, u32[]{:S(2)}) collective-permute-start(bf16[128,2048]{1,0:T(8,128)(2,1)S(1)} %collective-permute-done.5.refs_2_), channel_id=1, source_target_pairs={{0,1},{1,0},{2,3},{3,2},{4,5},{5,4},{6,7},{7,6},{8,9},{9,8},{10,11... | collective-permute-start | bytes 1572872 | tf_op jit(solution)/shard_map/ppermute | solution.py:12
  37.0 13.9 %collective-permute-start.9 = (bf16[128,2048]{1,0:T(8,128)(2,1)S(1)}, bf16[128,2048]{1,0:T(8,128)(2,1)S(1)}, u32[]{:S(2)}, u32[]{:S(2)}) collective-permute-start(bf16[128,2048]{1,0:T(8,128)(2,1)S(1)} %collective-permute-done.5.refs_2_), channel_id=1, source_target_pairs={{0,2},{1,3},{2,0},{3,1},{4,6},{5,7},{6,4},{7,5},{8,10},{9,11},{10,... | collective-permute-start | bytes 1572872 | tf_op jit(solution)/shard_map/ppermute | solution.py:12
  38.1 12.9 %collective-permute-start.11 = (bf16[128,2048]{1,0:T(8,128)(2,1)S(1)}, bf16[128,2048]{1,0:T(8,128)(2,1)S(1)}, u32[]{:S(2)}, u32[]{:S(2)}) collective-permute-start(bf16[128,2048]{1,0:T(8,128)(2,1)S(1)} %collective-permute-done.6.refs_0_), channel_id=1, source_target_pairs={{0,1},{1,0},{2,3},{3,2},{4,5},{5,4},{6,7},{7,6},{8,9},{9,8},{10,11... | collective-permute-start | bytes 1572872 | tf_op jit(solution)/shard_map/ppermute | solution.py:12
  38.1 11.0 %collective-permute-start.8 = (bf16[64,2048]{1,0:T(8,128)(2,1)S(1)}, bf16[64,2048]{1,0:T(8,128)(2,1)S(1)}, u32[]{:S(2)}, u32[]{:S(2)}) collective-permute-start(bf16[64,2048]{1,0:T(8,128)(2,1)S(1)} %get-tuple-element.112), channel_id=1, source_target_pairs={{0,4},{1,5},{2,6},{3,7},{4,8},{5,9},{6,10},{7,11},{8,12},{9,13},{1... | collective-permute-start | bytes 786440 | tf_op jit(solution)/shard_map/ppermute | solution.py:423
  39.4 18.9 %collective-permute-start.13 = (bf16[64,2048]{1,0:T(8,128)(2,1)S(1)}, bf16[64,2048]{1,0:T(8,128)(2,1)S(1)}, u32[]{:S(2)}, u32[]{:S(2)}) collective-permute-start(bf16[64,2048]{1,0:T(8,128)(2,1)S(1)} %get-tuple-element.111), channel_id=1, source_target_pairs={{0,4},{1,5},{2,6},{3,7},{4,8},{5,9},{6,10},{7,11},{8,12},{9,13},{1... | collective-permute-start | bytes 786440 | tf_op jit(solution)/shard_map/ppermute | solution.py:423
  50.9 9.4 %collective-permute-start.10 = (bf16[128,2048]{1,0:T(8,128)(2,1)S(1)}, bf16[128,2048]{1,0:T(8,128)(2,1)S(1)}, u32[]{:S(2)}, u32[]{:S(2)}) collective-permute-start(bf16[128,2048]{1,0:T(8,128)(2,1)S(1)} %collective-permute-done.9.refs_0_), channel_id=1, source_target_pairs={{0,1},{1,0},{2,3},{3,2},{4,5},{5,4},{6,7},{7,6},{8,9},{9,8},{10,11... | collective-permute-start | bytes 1572872 | tf_op jit(solution)/shard_map/ppermute | solution.py:12
  58.3 1.7 %collective-permute-start.14 = (bf16[64,2048]{1,0:T(8,128)(2,1)S(1)}, bf16[64,2048]{1,0:T(8,128)(2,1)S(1)}, u32[]{:S(2)}, u32[]{:S(2)}) collective-permute-start(bf16[64,2048]{1,0:T(8,128)(2,1)S(1)} %collective-permute-done.13.refs_2_), channel_id=1, source_target_pairs={{0,1},{1,0},{2,3},{3,2},{4,5},{5,4},{6,7},{7,6},{8,9},{9,8},{10,11... | collective-permute-start | bytes 786440 | tf_op jit(solution)/shard_map/ppermute | solution.py:12
  58.8 1.5 %collective-permute-start.15 = (bf16[64,2048]{1,0:T(8,128)(2,1)S(1)}, bf16[64,2048]{1,0:T(8,128)(2,1)S(1)}, u32[]{:S(2)}, u32[]{:S(2)}) collective-permute-start(bf16[64,2048]{1,0:T(8,128)(2,1)S(1)} %collective-permute-done.8.refs_4_), channel_id=1, source_target_pairs={{0,1},{1,0},{2,3},{3,2},{4,5},{5,4},{6,7},{7,6},{8,9},{9,8},{10,11... | collective-permute-start | bytes 786440 | tf_op jit(solution)/shard_map/ppermute | solution.py:12
  58.9 22.8 %collective-permute-start.20 = (bf16[512,768]{1,0:T(8,128)(2,1)S(1)}, bf16[512,768]{1,0:T(8,128)(2,1)S(1)}, u32[]{:S(2)}, u32[]{:S(2)}) collective-permute-start(bf16[512,768]{1,0:T(8,128)(2,1)S(1)} %get-tuple-element.91), channel_id=1, source_target_pairs={{0,1},{1,0},{2,3},{3,2},{4,5},{5,4},{6,7},{7,6},{8,9},{9,8},{10,11... | collective-permute-start | bytes 2359304 | tf_op jit(solution)/shard_map/ppermute | solution.py:12
  67.6 17.4 %collective-permute-start.16 = (bf16[512,768]{1,0:T(8,128)(2,1)S(1)}, bf16[512,768]{1,0:T(8,128)(2,1)S(1)}, u32[]{:S(2)}, u32[]{:S(2)}) collective-permute-start(bf16[512,768]{1,0:T(8,128)(2,1)S(1)} %get-tuple-element.83), channel_id=1, source_target_pairs={{0,1},{1,0},{2,3},{3,2},{4,5},{5,4},{6,7},{7,6},{8,9},{9,8},{10,11... | collective-permute-start | bytes 2359304 | tf_op jit(solution)/shard_map/ppermute | solution.py:12
  68.0 8.6 %collective-permute-start.17 = (bf16[64,2048]{1,0:T(8,128)(2,1)}, bf16[64,2048]{1,0:T(8,128)(2,1)S(1)}, u32[]{:S(2)}, u32[]{:S(2)}) collective-permute-start(bf16[64,2048]{1,0:T(8,128)(2,1)} %copy-done.20), channel_id=1, source_target_pairs={{0,2},{1,3},{2,0},{3,1},{4,6},{5,7},{6,4},{7,5},{8,10},{9,11},{10,... | collective-permute-start | bytes 786440 | tf_op jit(solution)/shard_map/ppermute | solution.py:12
  76.6 12.7 %collective-permute-start.21 = (bf16[64,2048]{1,0:T(8,128)(2,1)}, bf16[64,2048]{1,0:T(8,128)(2,1)S(1)}, u32[]{:S(2)}, u32[]{:S(2)}) collective-permute-start(bf16[64,2048]{1,0:T(8,128)(2,1)} %copy-done.19), channel_id=1, source_target_pairs={{0,2},{1,3},{2,0},{3,1},{4,6},{5,7},{6,4},{7,5},{8,10},{9,11},{10,... | collective-permute-start | bytes 786440 | tf_op jit(solution)/shard_map/ppermute | solution.py:12
  81.5 3.4 %collective-permute-start.19 = (bf16[128,768]{1,0:T(8,128)(2,1)S(1)}, bf16[128,768]{1,0:T(8,128)(2,1)S(1)}, u32[]{:S(2)}, u32[]{:S(2)}) collective-permute-start(bf16[128,768]{1,0:T(8,128)(2,1)S(1)} %get-tuple-element.87), channel_id=1, source_target_pairs={{0,1},{1,0},{2,3},{3,2},{4,5},{5,4},{6,7},{7,6},{8,9},{9,8},{10,11... | collective-permute-start | bytes 589832 | tf_op jit(solution)/shard_map/ppermute | solution.py:12
  89.3 1.6 %collective-permute-start.22 = (bf16[64,2048]{1,0:T(8,128)(2,1)S(1)}, bf16[64,2048]{1,0:T(8,128)(2,1)S(1)}, u32[]{:S(2)}, u32[]{:S(2)}) collective-permute-start(bf16[64,2048]{1,0:T(8,128)(2,1)S(1)} %collective-permute-done.21.refs_0_), channel_id=1, source_target_pairs={{0,1},{1,0},{2,3},{3,2},{4,5},{5,4},{6,7},{7,6},{8,9},{9,8},{10,11... | collective-permute-start | bytes 786440 | tf_op jit(solution)/shard_map/ppermute | solution.py:12
  94.3 3.5 %collective-permute-start.23 = (bf16[128,768]{1,0:T(8,128)(2,1)S(1)}, bf16[128,768]{1,0:T(8,128)(2,1)S(1)}, u32[]{:S(2)}, u32[]{:S(2)}) collective-permute-start(bf16[128,768]{1,0:T(8,128)(2,1)S(1)} %get-tuple-element.109), channel_id=1, source_target_pairs={{0,1},{1,0},{2,3},{3,2},{4,5},{5,4},{6,7},{7,6},{8,9},{9,8},{10,11... | collective-permute-start | bytes 589832 | tf_op jit(solution)/shard_map/ppermute | solution.py:12
  (28 other events, 98.8 us)

commit v5 on v4

--- a/solution.py
+++ b/solution.py
@@ -133,13 +133,27 @@
     return (gram[None], self_cross[None], merge_cross[None])
 
 
-VMEM_GRANT = 16 << 20
-SMALL_COST = pl.CostEstimate(flops=1 << 20, bytes_accessed=1 << 16, transcendentals=0)
-
-
-def route_table_kernel(quota_ref, pick_ref, entry_ref, coef_ref, out_ref):
+def kernel_cost(flops):
+    return pl.CostEstimate(flops=flops, bytes_accessed=1 << 16, transcendentals=0)
+
+
+def in_hbm(x):
+    return pltpu.with_memory_space_constraint(x, pltpu.HBM)
+
+
+def route_table_kernel(
+    quota_ref, pick_in, entry_in, coef_ref, out_ref, pick_ref, entry_ref, arrive
+):
+    copies = [
+        pltpu.make_async_copy(pick_in, pick_ref, arrive.at[0]),
+        pltpu.make_async_copy(entry_in, entry_ref, arrive.at[1]),
+    ]
+    for copy in copies:
+        copy.start()
+    for copy in copies:
+        copy.wait()
     top_count, tokens = pick_ref.shape
-    experts = out_ref.shape[1]
+    experts = out_ref.shape[0]
     levels = coef_ref.shape[1]
     picks = pick_ref[...]
     entries = entry_ref[...]
@@ -163,52 +177,81 @@
         bound = jnp.where(expert_row == expert, quota_ref[expert].astype(jnp.float32), bound)
     used = jnp.where(rank < bound, weight, 0.0).astype(jnp.bfloat16)
     for receiver in range(experts):
-        out_ref[receiver] = used
+        out_ref[receiver, 0:1, :] = used[receiver : receiver + 1]
+        out_ref[receiver, 1:2, :] = used[receiver ^ 1 : (receiver ^ 1) + 1]
 
 
 def route_table(picks, entries, coefficients, quotas):
     experts = quotas.shape[0]
     tokens = picks.shape[0]
     vmem = pl.BlockSpec(memory_space=pltpu.VMEM)
+    outside = pl.BlockSpec(memory_space=pl.ANY)
     return pl.pallas_call(
         route_table_kernel,
-        out_shape=jax.ShapeDtypeStruct((experts, experts, tokens), jnp.bfloat16),
-        in_specs=[pl.BlockSpec(memory_space=pltpu.SMEM), vmem, vmem, vmem],
+        out_shape=jax.ShapeDtypeStruct((experts, 2, tokens), jnp.bfloat16),
+        in_specs=[pl.BlockSpec(memory_space=pltpu.SMEM), outside, outside, vmem],
         out_specs=vmem,
-        compiler_params=pltpu.CompilerParams(vmem_limit_bytes=VMEM_GRANT),
+        scratch_shapes=[
+            pltpu.VMEM(picks.shape[::-1], jnp.int32),
+            pltpu.VMEM(entries.shape[::-1], jnp.int32),
+            pltpu.SemaphoreType.DMA((2,)),
+        ],
+        compiler_params=pltpu.CompilerParams(vmem_limit_bytes=4 << 20),
         name="route_table",
-    )(quotas, picks.T, entries.T, coefficients[None, :])
-
-
-def hidden_kernel(places, table_ref, flag_ref, *refs):
+    )(quotas, in_hbm(picks.T), in_hbm(entries.T), coefficients[None, :])
+
+
+def stage_kernel(places, with_part, with_base, *refs):
+    taken = iter(refs)
+
+    def take(count):
+        return [next(taken) for _ in range(count)]
+
+    table_ref, flag_ref = take(2)
+    blocks = take(len(places))
+    weights = take(2)
+    part = take(4) if with_part else None
+    bases = take(3) if with_base else None
+    hidden_outs = take(4)
+    sums = take(3) if with_part else None
+    scratch = take(2)
+    if with_part:
+        totals_body([part], bases, sums)
+    hidden_body(places, table_ref, flag_ref, blocks, *weights, *hidden_outs, *scratch)
+
+
+def hidden_body(
+    places,
+    table_ref,
+    flag_ref,
+    block_refs,
+    gate_ref,
+    up_ref,
+    lhs_ref,
+    count_ref,
+    weigh_ref,
+    send_ref,
+    rows_ref,
+    coef_ref,
+):
     block_total = len(places)
-    block_refs = refs[:block_total]
-    gate_ref, up_ref, lhs_ref, count_ref, weigh_ref, send_ref = refs[block_total : block_total + 6]
-    rows_ref, coef_ref, arrive = refs[block_total + 6 :]
     experts, _, tokens = table_ref.shape
     hidden_width = gate_ref.shape[2]
-    copies, spans = [], []
+    spans = []
     for block in range(block_total):
         first = spans[-1].stop if spans else 0
         spans.append(slice(first, first + block_refs[block].shape[0]))
-        copies.append(
-            pltpu.make_async_copy(block_refs[block], rows_ref.at[spans[block]], arrive.at[block])
-        )
-        copies[-1].start()
+        rows_ref[spans[block], :] = block_refs[block][...]
     me = lax.axis_index("expert")
-    partner_index = jnp.bitwise_xor(me, 1)
     keep = flag_ref[me].astype(jnp.float32)
-    merge = keep * (1.0 - flag_ref[partner_index].astype(jnp.float32))
+    merge = keep * (1.0 - flag_ref[jnp.bitwise_xor(me, 1)].astype(jnp.float32))
     row = lax.broadcasted_iota(jnp.int32, (tokens, tokens), 0)
     col = lax.broadcasted_iota(jnp.int32, (tokens, tokens), 1)
-    expert_row = lax.broadcasted_iota(jnp.int32, (experts, tokens), 0)
     for block, (steps, turn, offset) in enumerate(places):
         source = jnp.bitwise_xor(lax.rem(me + experts - 4 * steps, experts), turn)
         table = table_ref[source].astype(jnp.float32)
-        own = jnp.sum(jnp.where(expert_row == me, table, 0.0), axis=0, keepdims=True)
-        partner = jnp.sum(jnp.where(expert_row == partner_index, table, 0.0), axis=0, keepdims=True)
-        own = jnp.sum(jnp.where(row == col, own, 0.0), axis=1, keepdims=True)
-        partner = jnp.sum(jnp.where(row == col, partner, 0.0), axis=1, keepdims=True)
+        own = jnp.sum(jnp.where(row == col, table[0:1], 0.0), axis=1, keepdims=True)
+        partner = jnp.sum(jnp.where(row == col, table[1:2], 0.0), axis=1, keepdims=True)
         count = jnp.where(own > 0.0, keep, 0.0) + jnp.where(partner > 0.0, merge, 0.0)
         size = spans[block].stop - spans[block].start
         part = slice(offset, offset + size)
@@ -222,9 +265,6 @@
             groups.append(group)
             group = []
     for group in groups:
-        for pair in group:
-            copies[pair].wait()
-            copies[pair + 1].wait()
         span = slice(spans[group[0]].start, spans[group[-1] + 1].stop)
         rows = rows_ref[span, :]
         for start in range(0, hidden_width, tile):
@@ -251,103 +291,100 @@
     return pltpu.with_memory_space_constraint(x, pltpu.VMEM)
 
 
-def in_hbm(x):
-    return pltpu.with_memory_space_constraint(x, pltpu.HBM)
-
-
-def hidden_parts(places, table, flags, blocks, w_gate, w_up, name):
+def run_stage(places, table, flags, blocks, w_gate, w_up, part, bases, name):
     width = blocks[0].shape[1]
-    block_total = len(blocks)
     rows = sum(block.shape[0] for block in blocks)
     hidden_width = w_gate.shape[2]
     vmem = pl.BlockSpec(memory_space=pltpu.VMEM)
-    outside = pl.BlockSpec(memory_space=pl.ANY)
-    return pl.pallas_call(
-        functools.partial(hidden_kernel, places),
-        out_shape=(
-            pltpu.VMEM((hidden_width, rows), jnp.bfloat16),
-            pltpu.VMEM((rows, hidden_width), jnp.bfloat16),
-            pltpu.VMEM((rows, hidden_width), jnp.bfloat16),
-            jax.ShapeDtypeStruct((rows, hidden_width), jnp.bfloat16),
-        ),
-        in_specs=[
-            vmem,
-            pl.BlockSpec(memory_space=pltpu.SMEM),
-            *[outside] * block_total,
-            vmem,
-            vmem,
-        ],
-        out_specs=(vmem, vmem, vmem, vmem),
+    operands = [in_vmem(table), flags, *map(in_vmem, blocks), in_vmem(w_gate), in_vmem(w_up)]
+    out_shape = [
+        pltpu.VMEM((hidden_width, rows), jnp.bfloat16),
+        pltpu.VMEM((rows, hidden_width), jnp.bfloat16),
+        pltpu.VMEM((rows, hidden_width), jnp.bfloat16),
+        jax.ShapeDtypeStruct((rows, hidden_width), jnp.bfloat16),
+    ]
+    aliases = {}
+    if part is not None:
+        operands += map(in_vmem, part)
+        out_shape += [pltpu.VMEM((hidden_width, hidden_width), jnp.float32)] * 3
+    if bases is not None:
+        aliases = {len(operands) + index: 4 + index for index in range(3)}
+        operands += map(in_vmem, bases)
+    in_specs = [vmem] * len(operands)
+    in_specs[1] = pl.BlockSpec(memory_space=pltpu.SMEM)
+    outs = pl.pallas_call(
+        functools.partial(stage_kernel, places, part is not None, bases is not None),
+        out_shape=out_shape,
+        in_specs=in_specs,
+        out_specs=[vmem] * len(out_shape),
+        input_output_aliases=aliases,
         scratch_shapes=[
             pltpu.VMEM((rows, width), jnp.bfloat16),
             pltpu.VMEM((2, rows, 128), jnp.float32),
-            pltpu.SemaphoreType.DMA((block_total,)),
         ],
-        compiler_params=pltpu.CompilerParams(vmem_limit_bytes=VMEM_GRANT),
-        cost_estimate=SMALL_COST,
+        compiler_params=pltpu.CompilerParams(vmem_limit_bytes=10 << 20),
+        cost_estimate=kernel_cost(4 * rows * width * hidden_width),
         name=name,
-    )(table, flags, *[in_hbm(block) for block in blocks], in_vmem(w_gate), in_vmem(w_up))
-
-
-def totals_kernel(part_total, has_base, *refs):
-    parts = [refs[4 * index : 4 * index + 4] for index in range(part_total)]
-    rest = refs[4 * part_total :]
-    bases = rest[:3] if has_base else None
-    rest = rest[3:] if has_base else rest
-    outs, landed, arrive = rest[:3], rest[3 : 3 + part_total], rest[3 + part_total]
-    copies = []
-    for index in range(part_total):
-        copies.append(
-            pltpu.make_async_copy(parts[index][3], landed[index], arrive.at[index])
-        )
-        copies[-1].start()
+    )(*operands)
+    return tuple(outs[:4]), tuple(outs[4:])
+
+
+def totals_body(parts, bases, outs):
     hidden_width = outs[0].shape[1]
     tile = 256
     for which in range(3):
-        if which == 2:
-            for copy in copies:
-                copy.wait()
         for start in range(0, hidden_width, tile):
             lanes = slice(start, start + tile)
-            total = bases[which][:, lanes] if has_base else None
-            for index, part in enumerate(parts):
-                right = landed[index] if which == 2 else part[1 + which]
+            total = None if bases is None else bases[which][:, lanes]
+            for part in parts:
                 term = jnp.dot(
-                    part[0][...], right[:, lanes], preferred_element_type=jnp.float32
+                    part[0][...], part[1 + which][:, lanes], preferred_element_type=jnp.float32
                 )
                 total = term if total is None else total + term
             outs[which][:, lanes] = total
 
 
-def add_totals(parts, bases, name):
-    hidden_width = parts[0][0].shape[0]
+def totals_kernel(*refs):
+    totals_body([refs[:4]], refs[4:7], refs[7:])
+
+
+def add_totals(part, bases, name):
+    hidden_width, rows = part[0].shape
     vmem = pl.BlockSpec(memory_space=pltpu.VMEM)
-    outside = pl.BlockSpec(memory_space=pl.ANY)
-    operands, in_specs = [], []
-    rows = 0
-    for part in parts:
-        rows += part[0].shape[1]
-        operands += [in_vmem(part[0]), in_vmem(part[1]), in_vmem(part[2]), part[3]]
-        in_specs += [vmem, vmem, vmem, outside]
-    aliases = {}
-    if bases is not None:
-        aliases = {len(operands) + index: index for index in range(3)}
-        operands += [in_vmem(base) for base in bases]
-        in_specs += [vmem] * 3
     return pl.pallas_call(
-        functools.partial(totals_kernel, len(parts), bases is not None),
+        totals_kernel,
         out_shape=[pltpu.VMEM((hidden_width, hidden_width), jnp.float32)] * 3,
-        in_specs=in_specs,
+        in_specs=[vmem] * 7,
         out_specs=[vmem] * 3,
-        input_output_aliases=aliases,
-        scratch_shapes=[
-            *[pltpu.VMEM(part[3].shape, jnp.bfloat16) for part in parts],
-            pltpu.SemaphoreType.DMA((len(parts),)),
-        ],
-        compiler_params=pltpu.CompilerParams(vmem_limit_bytes=VMEM_GRANT),
-        cost_estimate=SMALL_COST,
+        input_output_aliases={4: 0, 5: 1, 6: 2},
+        compiler_params=pltpu.CompilerParams(vmem_limit_bytes=6 << 20),
+        cost_estimate=kernel_cost(6 * rows * hidden_width * hidden_width),
         name=name,
-    )(*operands)
+    )(*map(in_vmem, part), *map(in_vmem, bases))
+
+
+def pick_kernel(even_ref, odd_ref, out_ref):
+    core = jnp.bitwise_and(lax.axis_index("expert"), 1)
+
+    @pl.when(core == 0)
+    def _():
+        out_ref[...] = even_ref[...]
+
+    @pl.when(core == 1)
+    def _():
+        out_ref[...] = odd_ref[...]
+
+
+def pick_by_core(even, odd):
+    vmem = pl.BlockSpec(memory_space=pltpu.VMEM)
+    return pl.pallas_call(
+        pick_kernel,
+        out_shape=pltpu.VMEM(even.shape, even.dtype),
+        in_specs=[vmem, vmem],
+        out_specs=vmem,
+        compiler_params=pltpu.CompilerParams(vmem_limit_bytes=4 << 20),
+        name="pick_by_core",
+    )(in_vmem(even), in_vmem(odd))
 
 
 def final_kernel(set_total, slots, divisor, flag_ref, lhs_ref, *refs):
@@ -397,8 +434,8 @@
             pltpu.VMEM((total, hidden_width, hidden_width), jnp.float32),
             pltpu.SemaphoreType.DMA((total, hidden_width // 256)),
         ],
-        compiler_params=pltpu.CompilerParams(vmem_limit_bytes=VMEM_GRANT),
-        cost_estimate=SMALL_COST,
+        compiler_params=pltpu.CompilerParams(vmem_limit_bytes=8 << 20),
+        cost_estimate=kernel_cost(1 << 20),
         name=name,
     )(flags, in_vmem(lhs), *rhs, *[in_vmem(base) for base in bases])
 
@@ -417,7 +454,6 @@
     tok_rows, top_count = specialist_picks.shape
     position_ordinal = max(4, 3 * tok_rows * top_count // (4 * experts))
     divisor = experts * position_ordinal
-    half = tok_rows // 2
 
     def along(x):
         return lax.ppermute(x, "expert", [(i, (i + 4) % experts) for i in range(experts)])
@@ -428,23 +464,22 @@
     def other(x):
         return swapped(x, "expert", 0)
 
-    def hidden(arrivals, name):
+    def stage(arrivals, part, bases, name):
         blocks, places = [], []
         for block, steps, turn, offset in arrivals:
             blocks += [block, other(block)]
             places += [(steps, turn, offset), (steps, turn ^ 1, offset)]
-        return hidden_parts(
+        return run_stage(
             places,
             table,
             retained_specialist_flags,
             blocks,
             gating_projection,
             raising_projection,
+            None if part is None else (*part[:3], other(part[3])),
+            bases,
             name,
         )
-
-    def totals(parts, bases, name):
-        return add_totals([(*part[:3], other(part[3])) for part in parts], bases, name)
 
     tied = lax.optimization_barrier
     line_1, side_0 = along(layer_inputs), across(layer_inputs)
@@ -456,26 +491,22 @@
     table, line_1, side_0 = tied((table, line_1, side_0))
     line_2, side_1 = along(line_1), across(line_1)
     first = [(layer_inputs, 0, 0, 0), (side_0, 0, 2, 0), (line_1, 1, 0, 0)]
-    first = hidden(first, "hidden_first")
+    first, _ = stage(first, None, None, "stage_first")
 
     first, line_2, side_1 = tied((first, line_2, side_1))
-    upper_3, side_2 = along(line_2[:half]), across(line_2)
-    lower_3 = along(line_2[half:])
-    second = hidden([(side_1, 1, 2, 0), (line_2, 2, 0, 0)], "hidden_second")
-    bases = totals([first], None, "totals_first")
-
-    second, upper_3 = tied((second, upper_3))
-    last_upper = across(upper_3)
-    bases, lower_3, side_2 = tied((bases, lower_3, side_2))
-    last_lower = across(lower_3)
-    third = [(side_2, 2, 2, 0), (upper_3, 3, 0, 0), (lower_3, 3, 0, half)]
-    third = hidden(third, "hidden_third")
-    bases = totals([second], bases, "totals_second")
-    fourth = hidden([(last_upper, 3, 2, 0)], "hidden_fourth")
-    bases = totals([third, fourth], bases, "totals_third")
-
-    bases, last_lower = tied((bases, last_lower))
-    last = hidden([(last_lower, 3, 2, half)], "hidden_last")
+    line_3, side_2 = along(line_2), across(line_2)
+    second = [(side_1, 1, 2, 0), (line_2, 2, 0, 0)]
+    second, bases = stage(second, first, None, "stage_second")
+
+    second, bases, line_3, side_2 = tied((second, bases, line_3, side_2))
+    fourth = [(i, i ^ 2) if i % 2 == 0 else (i, (i + 4) % experts) for i in range(experts)]
+    side_3 = lax.ppermute(pick_by_core(line_3, side_2), "expert", fourth)
+    third = [(side_2, 2, 2, 0), (line_3, 3, 0, 0)]
+    third, bases = stage(third, second, bases, "stage_third")
+
+    third, bases, side_3 = tied((third, bases, side_3))
+    bases = add_totals((*third[:3], other(third[3])), bases, "totals_third")
+    last, _ = stage([(side_3, 3, 2, 0)], None, None, "stage_last")
     arrived = other(last[3])
     gram, self_cross = final_sums(
         retained_specialist_flags,

time: 101 us -> 75.5 us (0.75)
  Pallas kernels: 42.8 us -> 31.8 us
  local copies, waits for them, and re-layouts: 12.6 us -> 6.79 us
  waiting for transfers between devices: 24.9 us -> 20.5 us
  starting transfers between devices: 18.9 us -> 15.1 us
    pallas_call x8 -> x6, Pallas kernels: 36.2 us -> 24.4 us  [the longest x4 22.2 us: run_stage(): pl.pallas_call(functools.partial(stage_kernel, places, part is not None,...]
    ppermute x20 -> x15, waiting for transfers between devices: 13.4 us -> 7.28 us  [swapped(): lax.ppermute(x, axis, [(i, i ^ 1 << stride) for i in range(lax.axis_size(...]
    unnamed x54 -> x14, local copies, waits for them, and re-layouts: 11.9 us -> 6.14 us
    ppermute x20 -> x15, starting transfers between devices: 9.37 us -> 6.69 us  [swapped(): lax.ppermute(x, axis, [(i, i ^ 1 << stride) for i in range(lax.axis_size(...]
    ppermute x4 -> x3, waiting for transfers between devices: 4.97 us -> 7.26 us  [along(): lax.ppermute(x, 'expert', [(i, (i + 4) % experts) for i in range(experts)])]
    ppermute x4 -> x3, starting transfers between devices: 5.51 us -> 3.61 us  [along(): lax.ppermute(x, 'expert', [(i, (i + 4) % experts) for i in range(experts)])]
  transfers between devices with their start and end apart: 25 -> 20, of which waited for: 12 -> 9; matrix products, arithmetic and copies ran while one was open for 1% -> 1% of each run, Pallas kernels for 38% -> 39%
where the time goes in v5:
time: 75.5 us; the launch traced here: 75.1 us
  Pallas kernels  31.8 us (42%)
  waiting for transfers between devices  20.5 us (27%)
  starting transfers between devices  15.1 us (20%)
  local copies, waits for them, and re-layouts  6.79 us (9%)
  between operations  0.91 us (1%)
    pallas_call x4, Pallas kernels, run_stage(): pl.pallas_call(functools.partial(stage_kernel, places, part is not None,...  22.2 us
    ppermute x15, waiting for transfers between devices, swapped(): lax.ppermute(x, axis, [(i, i ^ 1 << stride) for i in range(lax.axis_size(...  7.28 us
    ppermute x3, waiting for transfers between devices, along(): lax.ppermute(x, 'expert', [(i, (i + 4) % experts) for i in range(experts)])  7.26 us
    ppermute x15, starting transfers between devices, swapped(): lax.ppermute(x, axis, [(i, i ^ 1 << stride) for i in range(lax.axis_size(...  6.69 us
    unnamed x14, local copies, waits for them, and re-layouts  6.14 us
    all_to_all x1, waiting for transfers between devices, gathered_shards(): lax.all_to_all(table, 'expert', split_axis=0, concat_axis=0, tiled=True)  5.94 us
    pallas_call x2, Pallas kernels, final_sums(): pl.pallas_call(functools.partial(final_kernel, total, slots, float(diviso...  5.33 us
    all_to_all x1, starting transfers between devices, gathered_shards(): lax.all_to_all(table, 'expert', split_axis=0, concat_axis=0, tiled=True)  3.98 us
  transfers between devices with their start and end apart: 20, of which 9 were waited for; matrix products, arithmetic and copies ran while one was open for 1% of the time, Pallas kernels for 39%

profile of v5, /device:TPU:0, one launch (start us, length us, event | category | flops | bytes accessed | tf_op | source)
XLA Modules:
  0.0 75.1 jit_solution(6250857773432772819)
XLA Ops:
  0.6 3.1 %collective-permute-start = (bf16[128,2048]{1,0:T(8,128)(2,1)}, bf16[128,2048]{1,0:T(8,128)(2,1)S(1)}, u32[]{:S(2)}, u32[]{:S(2)}) collective-permute-start(bf16[128,2048]{1,0:T(8,128)(2,1)} %refs_2_.1), channel_id=1, source_target_pairs={{0,4},{1,5},{2,6},{3,7},{4,8},{5,9},{6,10},{7,11},{8,12},{9,13},{1... | collective-permute-start | bytes 1572872 | tf_op jit(solution)/shard_map/ppermute | solution.py:459
  3.7 1.5 %collective-permute-start.1 = (bf16[128,2048]{1,0:T(8,128)(2,1)}, bf16[128,2048]{1,0:T(8,128)(2,1)S(1)}, u32[]{:S(2)}, u32[]{:S(2)}) collective-permute-start(bf16[128,2048]{1,0:T(8,128)(2,1)} %refs_2_.1), channel_id=1, source_target_pairs={{0,2},{1,3},{2,0},{3,1},{4,6},{5,7},{6,4},{7,5},{8,10},{9,11},{10,... | collective-permute-start | bytes 1572872 | tf_op jit(solution)/shard_map/ppermute | solution.py:12
  6.5 2.1 %route_table.1 = bf16[16,2,128]{2,1,0:T(2,128)(2,1)} custom-call(s32[16]{0:T(128)S(1)} %copy-done.5, s32[8,128]{1,0:T(8,128)} %bitcast.2, s32[8,128]{1,0:T(8,128)} %bitcast.3, bf16[1,256]{1,0:T(2,128)(2,1)S(1)} %broadcast_in_dim.3.coef_ref), custom_call_target="tpu_custom_call" | custom-call | tf_op jit(solution)/shard_map/route_table/pallas_call | solution.py:189
  8.6 4.0 %all-to-all-start = ((bf16[16,2,128]{2,1,0:T(2,128)(2,1)}), bf16[16,2,128]{2,1,0:T(2,128)(2,1)S(1)}, u32[]{:S(2)}, u32[]{:S(2)}) async-start(bf16[16,2,128]{2,1,0:T(2,128)(2,1)} %route_table.1), calls=%async_computation | async-start | bytes 16384 | tf_op jit(solution)/shard_map/all_to_all | solution.py:489
  13.0 5.9 %all-to-all-done.refs_0_ = bf16[16,2,128]{2,1,0:T(2,128)(2,1)S(1)} async-done(((bf16[16,2,128]{2,1,0:T(2,128)(2,1)}), bf16[16,2,128]{2,1,0:T(2,128)(2,1)S(1)}, u32[]{:S(2)}, u32[]{:S(2)}) %all-to-all-start) | async-done | bytes 8224 | tf_op jit(solution)/shard_map/all_to_all | solution.py:489
  20.0 1.0 %collective-permute-start.6 = (bf16[128,2048]{1,0:T(8,128)(2,1)S(1)}, bf16[128,2048]{1,0:T(8,128)(2,1)S(1)}, u32[]{:S(2)}, u32[]{:S(2)}) collective-permute-start(bf16[128,2048]{1,0:T(8,128)(2,1)S(1)} %collective-permute-done.refs_6_), channel_id=1, source_target_pairs={{0,2},{1,3},{2,0},{3,1},{4,6},{5,7},{6,4},{7,5},{8,10},{9,11},{10,... | collective-permute-start | bytes 1572872 | tf_op jit(solution)/shard_map/ppermute | solution.py:12
  21.6 1.9 %copy-done = bf16[1,2048,768]{2,1,0:T(8,128)(2,1)S(1)} copy-done((bf16[1,2048,768]{2,1,0:T(8,128)(2,1)S(1)}, bf16[1,2048,768]{2,1,0:T(8,128)(2,1)}, u32[]{:S(2)}) %copy-start) | copy-done | bytes 3145752
  23.5 1.9 %copy-done.2 = bf16[1,2048,768]{2,1,0:T(8,128)(2,1)S(1)} copy-done((bf16[1,2048,768]{2,1,0:T(8,128)(2,1)S(1)}, bf16[1,2048,768]{2,1,0:T(8,128)(2,1)}, u32[]{:S(2)}) %copy-start.2) | copy-done | bytes 3145752
  26.1 1.0 %copy-done.6 = bf16[128,2048]{1,0:T(8,128)(2,1)S(1)} copy-done((bf16[128,2048]{1,0:T(8,128)(2,1)S(1)}, bf16[128,2048]{1,0:T(8,128)(2,1)}, u32[]{:S(2)}) %copy-start.6) | copy-done | bytes 524312
  27.1 6.0 %stage_first.1 = (bf16[768,768]{1,0:T(8,128)(2,1)S(1)}, bf16[768,768]{1,0:T(8,128)(2,1)S(1)}, bf16[768,768]{1,0:T(8,128)(2,1)S(1)}, bf16[768,768]{1,0:T(8,128)(2,1)S(1)}) custom-call(bf16[16,2,128]{2,1,0:T(2,128)(2,1)S(1)} %all-to-all-done.refs_0_, s32[16]{0:T(128)S(1)} %copy-done.3, bf16[128,2048]{1,0:T(8,128)(2,1)S(1)} %copy-done.6, ...), custom_call_target="tpu_custom_call" | custom-call | flops 4831838208 | bytes 65536 | tf_op jit(solution)/shard_map/stage_first/pallas_call | solution.py:315
  33.1 2.0 %collective-permute-done.5.refs_4_ = bf16[128,2048]{1,0:T(8,128)(2,1)S(1)} collective-permute-done((bf16[128,2048]{1,0:T(8,128)(2,1)S(1)}, bf16[128,2048]{1,0:T(8,128)(2,1)S(1)}, u32[]{:S(2)}, u32[]{:S(2)}) %collective-permute-start.5) | collective-permute-done | bytes 524320 | tf_op jit(solution)/shard_map/ppermute | solution.py:459
  35.8 1.0 %collective-permute-start.11 = (bf16[128,2048]{1,0:T(8,128)(2,1)S(1)}, bf16[128,2048]{1,0:T(8,128)(2,1)S(1)}, u32[]{:S(2)}, u32[]{:S(2)}) collective-permute-start(bf16[128,2048]{1,0:T(8,128)(2,1)S(1)} %collective-permute-done.5.refs_4_), channel_id=1, source_target_pairs={{0,2},{1,3},{2,0},{3,1},{4,6},{5,7},{6,4},{7,5},{8,10},{9,11},{10,... | collective-permute-start | bytes 1572872 | tf_op jit(solution)/shard_map/ppermute | solution.py:12
  36.7 2.0 %collective-permute-done.7.refs_3_ = bf16[128,2048]{1,0:T(8,128)(2,1)S(1)} collective-permute-done((bf16[128,2048]{1,0:T(8,128)(2,1)S(1)}, bf16[128,2048]{1,0:T(8,128)(2,1)S(1)}, u32[]{:S(2)}, u32[]{:S(2)}) %collective-permute-start.7) | collective-permute-done | bytes 524320 | tf_op jit(solution)/shard_map/ppermute | solution.py:12
  39.5 7.1 %stage_second.1 = (bf16[768,512]{1,0:T(8,128)(2,1)S(1)}, bf16[512,768]{1,0:T(8,128)(2,1)S(1)}, bf16[512,768]{1,0:T(8,128)(2,1)S(1)}, bf16[512,768]{1,0:T(8,128)(...) custom-call(bf16[16,2,128]{2,1,0:T(2,128)(2,1)S(1)} %all-to-all-done.refs_0_, ...), custom_call_target="tpu_custom_call" | custom-call | flops 3221225472 | bytes 65536 | tf_op jit(solution)/shard_map/stage_second/pallas_call | solution.py:315
  46.6 5.2 %collective-permute-done.10.refs_4_.even_ref = bf16[128,2048]{1,0:T(8,128)(2,1)S(1)} collective-permute-done((bf16[128,2048]{1,0:T(8,128)(2,1)S(1)}, bf16[128,2048]{1,0:T(8,128)(2,1)S(1)}, u32[]{:S(2)}, u32[]{:S(2)}) %collective-permute-start.10) | collective-permute-done | bytes 524320 | tf_op jit(solution)/shard_map/ppermute | solution.py:459
  52.4 0.8 %collective-permute-start.15 = (bf16[128,2048]{1,0:T(8,128)(2,1)S(1)}, bf16[128,2048]{1,0:T(8,128)(2,1)S(1)}, u32[]{:S(2)}, u32[]{:S(2)}) collective-permute-start(bf16[128,2048]{1,0:T(8,128)(2,1)S(1)} %pick_by_core.1), channel_id=1, source_target_pairs={{0,2},{1,5},{2,0},{3,7},{4,6},{5,9},{6,4},{7,11},{8,10},{9,13},{10... | collective-permute-start | bytes 1572872 | tf_op jit(solution)/shard_map/ppermute | solution.py:503
  53.2 1.6 %collective-permute-done.12.refs_3_ = bf16[128,2048]{1,0:T(8,128)(2,1)S(1)} collective-permute-done((bf16[128,2048]{1,0:T(8,128)(2,1)S(1)}, bf16[128,2048]{1,0:T(8,128)(2,1)S(1)}, u32[]{:S(2)}, u32[]{:S(2)}) %collective-permute-start.12) | collective-permute-done | bytes 524320 | tf_op jit(solution)/shard_map/ppermute | solution.py:12
  54.9 0.7 collective-permute-done.13.refs_5_
  55.6 6.6 %stage_third.1 = (bf16[768,512]{1,0:T(8,128)(2,1)S(1)}, bf16[512,768]{1,0:T(8,128)(2,1)S(1)}, bf16[512,768]{1,0:T(8,128)(2,1)S(1)}, bf16[512,768]{1,0:T(8,128)(2...) custom-call(bf16[16,2,128]{2,1,0:T(2,128)(2,1)S(1)} %all-to-all-done, ...), custom_call_target="tpu_custom_call", output_to_operand_aliasing={{4}: (12, {}), {5}: (13, {}), {6}: (14, {})} | custom-call | flops 3221225472 | bytes 65536 | tf_op jit(solution)/shard_map/stage_third/pallas_call | solution.py:315
  62.9 1.5 %collective-permute-done.16.refs_3_ = bf16[128,2048]{1,0:T(8,128)(2,1)S(1)} collective-permute-done((bf16[128,2048]{1,0:T(8,128)(2,1)S(1)}, bf16[128,2048]{1,0:T(8,128)(2,1)S(1)}, u32[]{:S(2)}, u32[]{:S(2)}) %collective-permute-start.16) | collective-permute-done | bytes 524320 | tf_op jit(solution)/shard_map/ppermute | solution.py:12
  64.5 2.5 %stage_last.1 = (bf16[768,256]{1,0:T(8,128)(2,1)S(1)}, bf16[256,768]{1,0:T(8,128)(2,1)S(1)}, bf16[256,768]{1,0:T(8,128)(2,1)S(1)}, bf16[256,768]{1,0:T(8,128)(2,1)S(1)}) custom-call(bf16[16,2,128]{2,1,0:T(2,128)(2,1)S(1)} %all-to-all-done.refs_0_, s32[16]{0:T(128)S(1)} %copy-done.4, bf16[128,2048]{1,0:T(8,128)(2,1)S(1)} %collective-permute-done.15.refs_2_, ...), custom_call_target="tpu_custom_call" | custom-call | flops 1610612736 | bytes 65536 | tf_op jit(solution)/shard_map/stage_last/pallas_call | solution.py:315
  67.4 2.2 %totals_third.1 = (f32[768,768]{1,0:T(8,128)S(1)}, f32[768,768]{1,0:T(8,128)S(1)}, f32[768,768]{1,0:T(8,128)S(1)}) custom-call(bf16[768,512]{1,0:T(8,128)(2,1)S(1)} %get-tuple-element.96.refs_0_, bf16[512,768]{1,0:T(8,128)(2,1)S(1)} %get-tuple-element.97.refs_1_, ...), custom_call_target="tpu_custom_call", output_to_operand_aliasing={{0}: (4, {}), {1}: (5, {}), {2}: (6, {})} | custom-call | flops 1811939328 | bytes 65536 | tf_op jit(solution)/shard_map/totals_third/pallas_call | solution.py:354
  69.6 3.1 %own_sums.1 = (f32[1,768,768]{2,1,0:T(8,128)}, f32[1,768,768]{2,1,0:T(8,128)}) custom-call(s32[16]{0:T(128)S(1)} %copy-done.4, bf16[768,256]{1,0:T(8,128)(2,1)S(1)} %get-tuple-element.93.lhs_ref, bf16[256,768]{1,0:T(8,128)(2,1)S(1)} %get-tuple-element.94.refs_0_, bf16[256,768]{1,0:T(8,128)(2,1)S(1)} %get-tuple-element.95.refs_1_, ...), custom_call_target="tpu_custom_call" | custom-call | flops 1048576 | bytes 65536 | tf_op jit(solution)/shard_map/own_sums/pallas_call | solution.py:428
  72.7 2.3 %merge_sums.1 = f32[1,768,768]{2,1,0:T(8,128)} custom-call(s32[16]{0:T(128)S(1)} %copy-done.4, bf16[768,256]{1,0:T(8,128)(2,1)S(1)} %get-tuple-element.93.lhs_ref, bf16[256,768]{1,0:T(8,128)(2,1)S(1)} %collective-permute-done.18.refs_0_, f32[768,768]{1,0:T(8,128)S(1)} %get-tuple-element.108.refs_1_), custom_call_target="tpu_custom_call" | custom-call | flops 1048576 | bytes 65536 | tf_op jit(solution)/shard_map/merge_sums/pallas_call | solution.py:428
  (40 shorter events, 7.1 us)
Async XLA Ops:
  0.6 18.3 %collective-permute-start = (bf16[128,2048]{1,0:T(8,128)(2,1)}, bf16[128,2048]{1,0:T(8,128)(2,1)S(1)}, u32[]{:S(2)}, u32[]{:S(2)}) collective-permute-start(bf16[128,2048]{1,0:T(8,128)(2,1)} %refs_2_.1), channel_id=1, source_target_pairs={{0,4},{1,5},{2,6},{3,7},{4,8},{5,9},{6,10},{7,11},{8,12},{9,13},{1... | collective-permute-start | bytes 1572872 | tf_op jit(solution)/shard_map/ppermute | solution.py:459
  3.7 15.2 %collective-permute-start.1 = (bf16[128,2048]{1,0:T(8,128)(2,1)}, bf16[128,2048]{1,0:T(8,128)(2,1)S(1)}, u32[]{:S(2)}, u32[]{:S(2)}) collective-permute-start(bf16[128,2048]{1,0:T(8,128)(2,1)} %refs_2_.1), channel_id=1, source_target_pairs={{0,2},{1,3},{2,0},{3,1},{4,6},{5,7},{6,4},{7,5},{8,10},{9,11},{10,... | collective-permute-start | bytes 1572872 | tf_op jit(solution)/shard_map/ppermute | solution.py:12
  8.6 10.3 %all-to-all-start = ((bf16[16,2,128]{2,1,0:T(2,128)(2,1)}), bf16[16,2,128]{2,1,0:T(2,128)(2,1)S(1)}, u32[]{:S(2)}, u32[]{:S(2)}) async-start(bf16[16,2,128]{2,1,0:T(2,128)(2,1)} %route_table.1), calls=%async_computation | async-start | bytes 16384 | tf_op jit(solution)/shard_map/all_to_all | solution.py:489
  12.6 8.4 %collective-permute-start.2 = (bf16[128,2048]{1,0:T(8,128)(2,1)}, bf16[128,2048]{1,0:T(8,128)(2,1)S(1)}, u32[]{:S(2)}, u32[]{:S(2)}) collective-permute-start(bf16[128,2048]{1,0:T(8,128)(2,1)} %refs_2_.1), channel_id=1, source_target_pairs={{0,1},{1,0},{2,3},{3,2},{4,5},{5,4},{6,7},{7,6},{8,9},{9,8},{10,11... | collective-permute-start | bytes 1572872 | tf_op jit(solution)/shard_map/ppermute | solution.py:12
  18.9 2.1 %collective-permute-start.3 = (bf16[128,2048]{1,0:T(8,128)(2,1)S(1)}, bf16[128,2048]{1,0:T(8,128)(2,1)S(1)}, u32[]{:S(2)}, u32[]{:S(2)}) collective-permute-start(bf16[128,2048]{1,0:T(8,128)(2,1)S(1)} %collective-permute-done.1.refs_4_), channel_id=1, source_target_pairs={{0,1},{1,0},{2,3},{3,2},{4,5},{5,4},{6,7},{7,6},{8,9},{9,8},{10,11... | collective-permute-start | bytes 1572872 | tf_op jit(solution)/shard_map/ppermute | solution.py:12
  19.0 2.7 %collective-permute-start.4 = (bf16[128,2048]{1,0:T(8,128)(2,1)S(1)}, bf16[128,2048]{1,0:T(8,128)(2,1)S(1)}, u32[]{:S(2)}, u32[]{:S(2)}) collective-permute-start(bf16[128,2048]{1,0:T(8,128)(2,1)S(1)} %collective-permute-done.refs_6_), channel_id=1, source_target_pairs={{0,1},{1,0},{2,3},{3,2},{4,5},{5,4},{6,7},{7,6},{8,9},{9,8},{10,11... | collective-permute-start | bytes 1572872 | tf_op jit(solution)/shard_map/ppermute | solution.py:12
  19.5 15.7 %collective-permute-start.5 = (bf16[128,2048]{1,0:T(8,128)(2,1)S(1)}, bf16[128,2048]{1,0:T(8,128)(2,1)S(1)}, u32[]{:S(2)}, u32[]{:S(2)}) collective-permute-start(bf16[128,2048]{1,0:T(8,128)(2,1)S(1)} %collective-permute-done.refs_6_), channel_id=1, source_target_pairs={{0,4},{1,5},{2,6},{3,7},{4,8},{5,9},{6,10},{7,11},{8,12},{9,13},{1... | collective-permute-start | bytes 1572872 | tf_op jit(solution)/shard_map/ppermute | solution.py:459
  20.0 15.2 %collective-permute-start.6 = (bf16[128,2048]{1,0:T(8,128)(2,1)S(1)}, bf16[128,2048]{1,0:T(8,128)(2,1)S(1)}, u32[]{:S(2)}, u32[]{:S(2)}) collective-permute-start(bf16[128,2048]{1,0:T(8,128)(2,1)S(1)} %collective-permute-done.refs_6_), channel_id=1, source_target_pairs={{0,2},{1,3},{2,0},{3,1},{4,6},{5,7},{6,4},{7,5},{8,10},{9,11},{10,... | collective-permute-start | bytes 1572872 | tf_op jit(solution)/shard_map/ppermute | solution.py:12
  21.6 1.9 %copy-start = (bf16[1,2048,768]{2,1,0:T(8,128)(2,1)S(1)}, bf16[1,2048,768]{2,1,0:T(8,128)(2,1)}, u32[]{:S(2)}) copy-start(bf16[1,2048,768]{2,1,0:T(8,128)(2,1)} %refs_4_.1) | copy-start | bytes 9437188
  23.5 1.9 %copy-start.2 = (bf16[1,2048,768]{2,1,0:T(8,128)(2,1)S(1)}, bf16[1,2048,768]{2,1,0:T(8,128)(2,1)}, u32[]{:S(2)}) copy-start(bf16[1,2048,768]{2,1,0:T(8,128)(2,1)} %refs_5_.1) | copy-start | bytes 9437188
  35.2 20.4 %copy-start.4 = (s32[16]{0:T(128)S(1)}, s32[16]{0:T(128)}, u32[]{:S(2)}) copy-start(s32[16]{0:T(128)} %flag_ref.3) | copy-start | bytes 196
  35.2 4.4 %collective-permute-start.9 = (bf16[768,768]{1,0:T(8,128)(2,1)S(1)}, bf16[768,768]{1,0:T(8,128)(2,1)S(1)}, u32[]{:S(2)}, u32[]{:S(2)}) collective-permute-start(bf16[768,768]{1,0:T(8,128)(2,1)S(1)} %get-tuple-element.68), channel_id=1, source_target_pairs={{0,1},{1,0},{2,3},{3,2},{4,5},{5,4},{6,7},{7,6},{8,9},{9,8},{10,11... | collective-permute-start | bytes 3538952 | tf_op jit(solution)/shard_map/ppermute | solution.py:12
  35.2 3.6 %collective-permute-start.7 = (bf16[128,2048]{1,0:T(8,128)(2,1)S(1)}, bf16[128,2048]{1,0:T(8,128)(2,1)S(1)}, u32[]{:S(2)}, u32[]{:S(2)}) collective-permute-start(bf16[128,2048]{1,0:T(8,128)(2,1)S(1)} %collective-permute-done.6.refs_2_), channel_id=1, source_target_pairs={{0,1},{1,0},{2,3},{3,2},{4,5},{5,4},{6,7},{7,6},{8,9},{9,8},{10,11... | collective-permute-start | bytes 1572872 | tf_op jit(solution)/shard_map/ppermute | solution.py:12
  35.7 3.8 %collective-permute-start.8 = (bf16[128,2048]{1,0:T(8,128)(2,1)S(1)}, bf16[128,2048]{1,0:T(8,128)(2,1)S(1)}, u32[]{:S(2)}, u32[]{:S(2)}) collective-permute-start(bf16[128,2048]{1,0:T(8,128)(2,1)S(1)} %collective-permute-done.5.refs_4_), channel_id=1, source_target_pairs={{0,1},{1,0},{2,3},{3,2},{4,5},{5,4},{6,7},{7,6},{8,9},{9,8},{10,11... | collective-permute-start | bytes 1572872 | tf_op jit(solution)/shard_map/ppermute | solution.py:12
  35.7 16.1 %collective-permute-start.10 = (bf16[128,2048]{1,0:T(8,128)(2,1)S(1)}, bf16[128,2048]{1,0:T(8,128)(2,1)S(1)}, u32[]{:S(2)}, u32[]{:S(2)}) collective-permute-start(bf16[128,2048]{1,0:T(8,128)(2,1)S(1)} %collective-permute-done.5.refs_4_), channel_id=1, source_target_pairs={{0,4},{1,5},{2,6},{3,7},{4,8},{5,9},{6,10},{7,11},{8,12},{9,13},{1... | collective-permute-start | bytes 1572872 | tf_op jit(solution)/shard_map/ppermute | solution.py:459
  35.8 16.1 %collective-permute-start.11 = (bf16[128,2048]{1,0:T(8,128)(2,1)S(1)}, bf16[128,2048]{1,0:T(8,128)(2,1)S(1)}, u32[]{:S(2)}, u32[]{:S(2)}) collective-permute-start(bf16[128,2048]{1,0:T(8,128)(2,1)S(1)} %collective-permute-done.5.refs_4_), channel_id=1, source_target_pairs={{0,2},{1,3},{2,0},{3,1},{4,6},{5,7},{6,4},{7,5},{8,10},{9,11},{10,... | collective-permute-start | bytes 1572872 | tf_op jit(solution)/shard_map/ppermute | solution.py:12
  39.5 16.1 %copy-start.1 = (bf16[1,2048,768]{2,1,0:T(8,128)(2,1)S(1)}, bf16[1,2048,768]{2,1,0:T(8,128)(2,1)}, u32[]{:S(2)}) copy-start(bf16[1,2048,768]{2,1,0:T(8,128)(2,1)} %refs_4_.1) | copy-start | bytes 9437188
  51.8 3.8 %collective-permute-start.14 = (bf16[512,768]{1,0:T(8,128)(2,1)S(1)}, bf16[512,768]{1,0:T(8,128)(2,1)S(1)}, u32[]{:S(2)}, u32[]{:S(2)}) collective-permute-start(bf16[512,768]{1,0:T(8,128)(2,1)S(1)} %get-tuple-element.81), channel_id=1, source_target_pairs={{0,1},{1,0},{2,3},{3,2},{4,5},{5,4},{6,7},{7,6},{8,9},{9,8},{10,11... | collective-permute-start | bytes 2359304 | tf_op jit(solution)/shard_map/ppermute | solution.py:12
  51.8 3.0 %collective-permute-start.12 = (bf16[128,2048]{1,0:T(8,128)(2,1)S(1)}, bf16[128,2048]{1,0:T(8,128)(2,1)S(1)}, u32[]{:S(2)}, u32[]{:S(2)}) collective-permute-start(bf16[128,2048]{1,0:T(8,128)(2,1)S(1)} %collective-permute-done.11.refs_2_.odd_ref), channel_id=1, source_target_pairs={{0,1},{1,0},{2,3},{3,2},{4,5},{5,4},{6,7},{7,6},{8,9},{9,8},{10,11... | collective-permute-start | bytes 1572872 | tf_op jit(solution)/shard_map/ppermute | solution.py:12
  52.3 3.3 %collective-permute-start.13 = (bf16[128,2048]{1,0:T(8,128)(2,1)S(1)}, bf16[128,2048]{1,0:T(8,128)(2,1)S(1)}, u32[]{:S(2)}, u32[]{:S(2)}) collective-permute-start(bf16[128,2048]{1,0:T(8,128)(2,1)S(1)} %collective-permute-done.10.refs_4_.even_ref), channel_id=1, source_target_pairs={{0,1},{1,0},{2,3},{3,2},{4,5},{5,4},{6,7},{7,6},{8,9},{9,8},{10,11... | collective-permute-start | bytes 1572872 | tf_op jit(solution)/shard_map/ppermute | solution.py:12
  52.4 9.8 %collective-permute-start.15 = (bf16[128,2048]{1,0:T(8,128)(2,1)S(1)}, bf16[128,2048]{1,0:T(8,128)(2,1)S(1)}, u32[]{:S(2)}, u32[]{:S(2)}) collective-permute-start(bf16[128,2048]{1,0:T(8,128)(2,1)S(1)} %pick_by_core.1), channel_id=1, source_target_pairs={{0,2},{1,5},{2,0},{3,7},{4,6},{5,9},{6,4},{7,11},{8,10},{9,13},{10... | collective-permute-start | bytes 1572872 | tf_op jit(solution)/shard_map/ppermute | solution.py:503
  62.2 2.3 %collective-permute-start.16 = (bf16[128,2048]{1,0:T(8,128)(2,1)S(1)}, bf16[128,2048]{1,0:T(8,128)(2,1)S(1)}, u32[]{:S(2)}, u32[]{:S(2)}) collective-permute-start(bf16[128,2048]{1,0:T(8,128)(2,1)S(1)} %collective-permute-done.15.refs_2_), channel_id=1, source_target_pairs={{0,1},{1,0},{2,3},{3,2},{4,5},{5,4},{6,7},{7,6},{8,9},{9,8},{10,11... | collective-permute-start | bytes 1572872 | tf_op jit(solution)/shard_map/ppermute | solution.py:12
  62.9 4.5 %collective-permute-start.17 = (bf16[512,768]{1,0:T(8,128)(2,1)S(1)}, bf16[512,768]{1,0:T(8,128)(2,1)S(1)}, u32[]{:S(2)}, u32[]{:S(2)}) collective-permute-start(bf16[512,768]{1,0:T(8,128)(2,1)S(1)} %get-tuple-element.99), channel_id=1, source_target_pairs={{0,1},{1,0},{2,3},{3,2},{4,5},{5,4},{6,7},{7,6},{8,9},{9,8},{10,11... | collective-permute-start | bytes 2359304 | tf_op jit(solution)/shard_map/ppermute | solution.py:12
  67.0 5.7 %collective-permute-start.18 = (bf16[256,768]{1,0:T(8,128)(2,1)S(1)}, bf16[256,768]{1,0:T(8,128)(2,1)S(1)}, u32[]{:S(2)}, u32[]{:S(2)}) collective-permute-start(bf16[256,768]{1,0:T(8,128)(2,1)S(1)} %get-tuple-element.107), channel_id=1, source_target_pairs={{0,1},{1,0},{2,3},{3,2},{4,5},{5,4},{6,7},{7,6},{8,9},{9,8},{10,11... | collective-permute-start | bytes 1179656 | tf_op jit(solution)/shard_map/ppermute | solution.py:12
  (3 other events, 2.4 us)

commit v6 on v5

--- a/solution.py
+++ b/solution.py
@@ -142,11 +142,12 @@
 
 
 def route_table_kernel(
-    quota_ref, pick_in, entry_in, coef_ref, out_ref, pick_ref, entry_ref, arrive
+    quota_ref, pick_in, entry_in, coef_in, out_ref, pick_ref, entry_ref, coef_ref, arrive
 ):
     copies = [
         pltpu.make_async_copy(pick_in, pick_ref, arrive.at[0]),
         pltpu.make_async_copy(entry_in, entry_ref, arrive.at[1]),
+        pltpu.make_async_copy(coef_in, coef_ref, arrive.at[2]),
     ]
     for copy in copies:
         copy.start()
@@ -154,10 +155,10 @@
         copy.wait()
     top_count, tokens = pick_ref.shape
     experts = out_ref.shape[0]
-    levels = coef_ref.shape[1]
+    levels = coef_ref.shape[0]
     picks = pick_ref[...]
     entries = entry_ref[...]
-    coef = coef_ref[...]
+    coef = coef_ref[...].reshape(1, levels)
     expert_row = lax.broadcasted_iota(jnp.int32, (experts, tokens), 0)
     level_row = lax.broadcasted_iota(jnp.int32, (levels, tokens), 0)
     chosen = jnp.zeros((experts, tokens), jnp.float32)
@@ -189,19 +190,40 @@
     return pl.pallas_call(
         route_table_kernel,
         out_shape=jax.ShapeDtypeStruct((experts, 2, tokens), jnp.bfloat16),
-        in_specs=[pl.BlockSpec(memory_space=pltpu.SMEM), outside, outside, vmem],
+        in_specs=[pl.BlockSpec(memory_space=pltpu.SMEM), outside, outside, outside],
         out_specs=vmem,
         scratch_shapes=[
             pltpu.VMEM(picks.shape[::-1], jnp.int32),
             pltpu.VMEM(entries.shape[::-1], jnp.int32),
-            pltpu.SemaphoreType.DMA((2,)),
+            pltpu.VMEM(coefficients.shape, coefficients.dtype),
+            pltpu.SemaphoreType.DMA((3,)),
         ],
         compiler_params=pltpu.CompilerParams(vmem_limit_bytes=4 << 20),
         name="route_table",
-    )(quotas, in_hbm(picks.T), in_hbm(entries.T), coefficients[None, :])
-
-
-def stage_kernel(places, with_part, with_base, *refs):
+    )(quotas, in_hbm(picks.T), in_hbm(entries.T), in_hbm(coefficients))
+
+
+def ring_neighbour(me, experts, steps, turn):
+    rows = experts // 4
+    row, side, core = me // 4, jnp.bitwise_and(me // 2, 1), jnp.bitwise_and(me, 1)
+    position = jnp.where(side == 0, row, 2 * rows - 1 - row)
+    position = lax.rem(position + steps + 2 * rows, 2 * rows)
+    far = position >= rows
+    row = jnp.where(far, 2 * rows - 1 - position, position)
+    return 4 * row + jnp.where(far, 2, 0) + jnp.bitwise_xor(core, turn)
+
+
+def ring_pairs(experts, directions):
+    rows = experts // 4
+    chips = [2 * row for row in range(rows)] + [2 * row + 1 for row in reversed(range(rows))]
+    return [
+        (2 * chip + core, 2 * chips[(position + directions[core]) % len(chips)] + core)
+        for position, chip in enumerate(chips)
+        for core in range(2)
+    ]
+
+
+def stage_kernel(places, before, after, with_base, *refs):
     taken = iter(refs)
 
     def take(count):
@@ -210,14 +232,26 @@
     table_ref, flag_ref = take(2)
     blocks = take(len(places))
     weights = take(2)
-    part = take(4) if with_part else None
-    bases = take(3) if with_base else None
+    part = take(4) if before else None
+    bases = take(3) if with_base else [None] * 3
     hidden_outs = take(4)
-    sums = take(3) if with_part else None
+    sums = take(3) if before or after else [None] * 3
     scratch = take(2)
-    if with_part:
-        totals_body([part], bases, sums)
+    for which in before:
+        add_product(sums[which], bases[which], part[0], part[1 + which])
     hidden_body(places, table_ref, flag_ref, blocks, *weights, *hidden_outs, *scratch)
+    for which in after:
+        base = sums[which] if which in before else bases[which]
+        add_product(sums[which], base, hidden_outs[0], hidden_outs[1 + which])
+
+
+def add_product(out_ref, base_ref, lhs_ref, rhs_ref):
+    hidden_width = out_ref.shape[1]
+    tile = 256
+    for start in range(0, hidden_width, tile):
+        lanes = slice(start, start + tile)
+        total = jnp.dot(lhs_ref[...], rhs_ref[:, lanes], preferred_element_type=jnp.float32)
+        out_ref[:, lanes] = total if base_ref is None else base_ref[:, lanes] + total
 
 
 def hidden_body(
@@ -248,7 +282,7 @@
     row = lax.broadcasted_iota(jnp.int32, (tokens, tokens), 0)
     col = lax.broadcasted_iota(jnp.int32, (tokens, tokens), 1)
     for block, (steps, turn, offset) in enumerate(places):
-        source = jnp.bitwise_xor(lax.rem(me + experts - 4 * steps, experts), turn)
+        source = ring_neighbour(me, experts, steps, turn)
         table = table_ref[source].astype(jnp.float32)
         own = jnp.sum(jnp.where(row == col, table[0:1], 0.0), axis=1, keepdims=True)
         partner = jnp.sum(jnp.where(row == col, table[1:2], 0.0), axis=1, keepdims=True)
@@ -258,14 +292,15 @@
         coef_ref[0, spans[block], :] = jnp.broadcast_to(count[part], (size, 128))
         coef_ref[1, spans[block], :] = jnp.broadcast_to(own[part], (size, 128))
     tile = 256
+    units = [(0,)] if block_total == 1 else [(i, i + 1) for i in range(0, block_total, 2)]
     groups, group = [], []
-    for pair in range(0, block_total, 2):
-        group.append(pair)
-        if spans[pair + 1].stop - spans[group[0]].start >= 256 or pair + 2 == block_total:
+    for unit in units:
+        group.append(unit)
+        if spans[unit[-1]].stop - spans[group[0][0]].start >= 256 or unit == units[-1]:
             groups.append(group)
             group = []
     for group in groups:
-        span = slice(spans[group[0]].start, spans[group[-1] + 1].stop)
+        span = slice(spans[group[0][0]].start, spans[group[-1][-1]].stop)
         rows = rows_ref[span, :]
         for start in range(0, hidden_width, tile):
             lanes = slice(start, start + tile)
@@ -280,18 +315,18 @@
                 count_ref[span, to] = (part * coef_ref[0, span, :]).astype(jnp.bfloat16)
                 weighed = (part * coef_ref[1, span, :]).astype(jnp.bfloat16)
                 weigh_ref[span, to] = weighed
-                for pair in group:
-                    mine, theirs = spans[pair], spans[pair + 1]
-                    base = span.start
-                    send_ref[mine, to] = weighed[theirs.start - base : theirs.stop - base]
-                    send_ref[theirs, to] = weighed[mine.start - base : mine.stop - base]
+                for unit in group:
+                    for block, source in zip(unit, unit[::-1]):
+                        base = span.start
+                        piece = slice(spans[source].start - base, spans[source].stop - base)
+                        send_ref[spans[block], to] = weighed[piece]
 
 
 def in_vmem(x):
     return pltpu.with_memory_space_constraint(x, pltpu.VMEM)
 
 
-def run_stage(places, table, flags, blocks, w_gate, w_up, part, bases, name):
+def run_stage(places, table, flags, blocks, w_gate, w_up, part, bases, before, after, name):
     width = blocks[0].shape[1]
     rows = sum(block.shape[0] for block in blocks)
     hidden_width = w_gate.shape[2]
@@ -304,8 +339,9 @@
         jax.ShapeDtypeStruct((rows, hidden_width), jnp.bfloat16),
     ]
     aliases = {}
-    if part is not None:
+    if before:
         operands += map(in_vmem, part)
+    if before or after:
         out_shape += [pltpu.VMEM((hidden_width, hidden_width), jnp.float32)] * 3
     if bases is not None:
         aliases = {len(operands) + index: 4 + index for index in range(3)}
@@ -313,7 +349,7 @@
     in_specs = [vmem] * len(operands)
     in_specs[1] = pl.BlockSpec(memory_space=pltpu.SMEM)
     outs = pl.pallas_call(
-        functools.partial(stage_kernel, places, part is not None, bases is not None),
+        functools.partial(stage_kernel, places, before, after, bases is not None),
         out_shape=out_shape,
         in_specs=in_specs,
         out_specs=[vmem] * len(out_shape),
@@ -329,40 +365,6 @@
     return tuple(outs[:4]), tuple(outs[4:])
 
 
-def totals_body(parts, bases, outs):
-    hidden_width = outs[0].shape[1]
-    tile = 256
-    for which in range(3):
-        for start in range(0, hidden_width, tile):
-            lanes = slice(start, start + tile)
-            total = None if bases is None else bases[which][:, lanes]
-            for part in parts:
-                term = jnp.dot(
-                    part[0][...], part[1 + which][:, lanes], preferred_element_type=jnp.float32
-                )
-                total = term if total is None else total + term
-            outs[which][:, lanes] = total
-
-
-def totals_kernel(*refs):
-    totals_body([refs[:4]], refs[4:7], refs[7:])
-
-
-def add_totals(part, bases, name):
-    hidden_width, rows = part[0].shape
-    vmem = pl.BlockSpec(memory_space=pltpu.VMEM)
-    return pl.pallas_call(
-        totals_kernel,
-        out_shape=[pltpu.VMEM((hidden_width, hidden_width), jnp.float32)] * 3,
-        in_specs=[vmem] * 7,
-        out_specs=[vmem] * 3,
-        input_output_aliases={4: 0, 5: 1, 6: 2},
-        compiler_params=pltpu.CompilerParams(vmem_limit_bytes=6 << 20),
-        cost_estimate=kernel_cost(6 * rows * hidden_width * hidden_width),
-        name=name,
-    )(*map(in_vmem, part), *map(in_vmem, bases))
-
-
 def pick_kernel(even_ref, odd_ref, out_ref):
     core = jnp.bitwise_and(lax.axis_index("expert"), 1)
 
@@ -387,10 +389,14 @@
     )(in_vmem(even), in_vmem(odd))
 
 
-def final_kernel(set_total, slots, divisor, flag_ref, lhs_ref, *refs):
-    rhs, bases = refs[:set_total], refs[set_total : 2 * set_total]
-    outs, done_ref, leave = refs[2 * set_total : 3 * set_total], refs[-2], refs[-1]
-    hidden_width = lhs_ref.shape[0]
+def final_kernel(kinds, part_total, divisor, flag_ref, *refs):
+    set_total = len(kinds)
+    lhs, rest = refs[:part_total], refs[part_total:]
+    rhs = [rest[part_total * index : part_total * (index + 1)] for index in range(set_total)]
+    rest = rest[part_total * set_total :]
+    bases, outs = rest[:set_total], rest[set_total : 2 * set_total]
+    done_ref, leave = rest[2 * set_total :]
+    hidden_width = lhs[0].shape[0]
     me = lax.axis_index("expert")
     keep = flag_ref[me].astype(jnp.float32)
     keep_partner = flag_ref[jnp.bitwise_xor(me, 1)].astype(jnp.float32)
@@ -398,15 +404,17 @@
     copies = []
     for index in range(set_total):
         factor = 1.0 / divisor
-        if slots[index] != "gram":
+        if kinds[index] != "gram":
             factor = factor * keep
-        if slots[index] == "merge":
+        if kinds[index] == "merge":
             factor = factor * (1.0 - keep_partner)
         for start in range(0, hidden_width, tile):
             span = slice(start, start + tile)
-            total = bases[index][span, :] + jnp.dot(
-                lhs_ref[span, :], rhs[index][...], preferred_element_type=jnp.float32
-            )
+            total = bases[index][span, :]
+            for left, right in zip(lhs, rhs[index]):
+                total = total + jnp.dot(
+                    left[span, :], right[...], preferred_element_type=jnp.float32
+                )
             done_ref[index, span, :] = total * factor
             copies.append(
                 pltpu.make_async_copy(
@@ -420,15 +428,19 @@
         copy.wait()
 
 
-def final_sums(flags, lhs, rhs, bases, slots, divisor, name):
-    hidden_width, rows = lhs.shape
+def final_sums(flags, lhs, rhs, bases, kinds, divisor, name):
+    hidden_width = lhs[0].shape[0]
     total = len(rhs)
     vmem = pl.BlockSpec(memory_space=pltpu.VMEM)
     outside = pl.BlockSpec(memory_space=pl.ANY)
+    operands = [*lhs]
+    for parts in rhs:
+        operands += parts
+    operands += bases
     return pl.pallas_call(
-        functools.partial(final_kernel, total, slots, float(divisor)),
+        functools.partial(final_kernel, kinds, len(lhs), float(divisor)),
         out_shape=[jax.ShapeDtypeStruct((1, hidden_width, hidden_width), jnp.float32)] * total,
-        in_specs=[pl.BlockSpec(memory_space=pltpu.SMEM)] + [vmem] * (1 + 2 * total),
+        in_specs=[pl.BlockSpec(memory_space=pltpu.SMEM)] + [vmem] * len(operands),
         out_specs=[outside] * total,
         scratch_shapes=[
             pltpu.VMEM((total, hidden_width, hidden_width), jnp.float32),
@@ -437,7 +449,7 @@
         compiler_params=pltpu.CompilerParams(vmem_limit_bytes=8 << 20),
         cost_estimate=kernel_cost(1 << 20),
         name=name,
-    )(flags, in_vmem(lhs), *rhs, *[in_vmem(base) for base in bases])
+    )(flags, *map(in_vmem, operands))
 
 
 def gathered_shards(
@@ -455,20 +467,23 @@
     position_ordinal = max(4, 3 * tok_rows * top_count // (4 * experts))
     divisor = experts * position_ordinal
 
-    def along(x):
-        return lax.ppermute(x, "expert", [(i, (i + 4) % experts) for i in range(experts)])
-
-    def across(x):
-        return swapped(x, "expert", 1)
+    def onward(x):
+        return lax.ppermute(x, "expert", ring_pairs(experts, (1, 1)))
+
+    def backward(x):
+        return lax.ppermute(x, "expert", ring_pairs(experts, (-1, -1)))
 
     def other(x):
         return swapped(x, "expert", 0)
 
-    def stage(arrivals, part, bases, name):
+    def stage(arrivals, part, bases, before, after, name):
         blocks, places = [], []
         for block, steps, turn, offset in arrivals:
-            blocks += [block, other(block)]
-            places += [(steps, turn, offset), (steps, turn ^ 1, offset)]
+            blocks.append(block)
+            places.append((steps, turn, offset))
+            if len(arrivals) > 1:
+                blocks.append(other(block))
+                places.append((steps, turn ^ 1, offset))
         return run_stage(
             places,
             table,
@@ -478,47 +493,56 @@
             raising_projection,
             None if part is None else (*part[:3], other(part[3])),
             bases,
+            before,
+            after,
             name,
         )
 
     tied = lax.optimization_barrier
-    line_1, side_0 = along(layer_inputs), across(layer_inputs)
+    left_1, right_1 = onward(layer_inputs), backward(layer_inputs)
     table = route_table(
         specialist_picks, coefficient_lookup_entry, dispatch_coefficients, specialist_quotas
     )
     table = lax.all_to_all(table, "expert", split_axis=0, concat_axis=0, tiled=True)
 
-    table, line_1, side_0 = tied((table, line_1, side_0))
-    line_2, side_1 = along(line_1), across(line_1)
-    first = [(layer_inputs, 0, 0, 0), (side_0, 0, 2, 0), (line_1, 1, 0, 0)]
-    first, _ = stage(first, None, None, "stage_first")
-
-    first, line_2, side_1 = tied((first, line_2, side_1))
-    line_3, side_2 = along(line_2), across(line_2)
-    second = [(side_1, 1, 2, 0), (line_2, 2, 0, 0)]
-    second, bases = stage(second, first, None, "stage_second")
-
-    second, bases, line_3, side_2 = tied((second, bases, line_3, side_2))
-    fourth = [(i, i ^ 2) if i % 2 == 0 else (i, (i + 4) % experts) for i in range(experts)]
-    side_3 = lax.ppermute(pick_by_core(line_3, side_2), "expert", fourth)
-    third = [(side_2, 2, 2, 0), (line_3, 3, 0, 0)]
-    third, bases = stage(third, second, bases, "stage_third")
-
-    third, bases, side_3 = tied((third, bases, side_3))
-    bases = add_totals((*third[:3], other(third[3])), bases, "totals_third")
-    last, _ = stage([(side_3, 3, 2, 0)], None, None, "stage_last")
-    arrived = other(last[3])
+    table, left_1, right_1 = tied((table, left_1, right_1))
+    left_2, right_2 = onward(left_1), backward(right_1)
+    first = [(layer_inputs, 0, 0, 0), (left_1, -1, 0, 0), (right_1, 1, 0, 0)]
+    first, _ = stage(first, None, None, (), (), "stage_first")
+
+    first, left_2, right_2 = tied((first, left_2, right_2))
+    left_3, right_3 = onward(left_2), backward(right_2)
+    second = [(left_2, -2, 0, 0), (right_2, 2, 0, 0)]
+    second, bases = stage(second, first, None, (0, 1, 2), (0, 1), "stage_second")
+
+    second, bases, left_3, right_3 = tied((second, bases, left_3, right_3))
+    far = lax.ppermute(pick_by_core(left_3, right_3), "expert", ring_pairs(experts, (1, -1)))
+    third = [(left_3, -3, 0, 0), (right_3, 3, 0, 0)]
+    third, bases = stage(third, second, bases, (2,), (0, 1), "stage_third")
+
+    third, bases, far = tied((third, bases, far))
+    near_far = other(far)
+    mine, _ = stage([(far, 4, 0, 0)], None, None, (), (), "stage_mine")
+    mine, near_far = tied((mine, near_far))
+    theirs, _ = stage([(near_far, 4, 1, 0)], None, None, (), (), "stage_theirs")
+    last = [mine, theirs]
     gram, self_cross = final_sums(
         retained_specialist_flags,
-        last[0],
-        [in_vmem(last[1]), in_vmem(last[2])],
+        [part[0] for part in last],
+        [[part[1] for part in last], [part[2] for part in last]],
         bases[:2],
         ("gram", "self"),
         divisor,
         "own_sums",
     )
     (merge_cross,) = final_sums(
-        retained_specialist_flags, last[0], [arrived], bases[2:], ("merge",), divisor, "merge_sums"
+        retained_specialist_flags,
+        [third[0], mine[0], theirs[0]],
+        [[other(third[3]), other(theirs[3]), other(mine[3])]],
+        bases[2:],
+        ("merge",),
+        divisor,
+        "merge_sums",
     )
     return gram, self_cross, merge_cross
 

time: 75.5 us -> 70.6 us (0.935)
  waiting for transfers between devices: 20.5 us -> 12.8 us
  starting transfers between devices: 15.1 us -> 18.3 us
    ppermute x4 -> x7, starting transfers between devices: 4.45 us -> 8.88 us  [the longest x3 4.31 us: onward(): return lax.ppermute(x, 'expert', ring_pairs(experts, (1, 1)))]
    ppermute x4 -> x7, waiting for transfers between devices: 7.26 us -> 3.3 us  [the longest x3 2.62 us: onward(): return lax.ppermute(x, 'expert', ring_pairs(experts, (1, 1)))]
    ppermute x15 -> x13, waiting for transfers between devices: 7.28 us -> 3.42 us  [swapped(): lax.ppermute(x, axis, [(i, i ^ 1 << stride) for i in range(lax.axis_size(...]
    ppermute x15 -> x13, starting transfers between devices: 6.69 us -> 3.09 us  [swapped(): lax.ppermute(x, axis, [(i, i ^ 1 << stride) for i in range(lax.axis_size(...]
    all_to_all x1, starting transfers between devices: 3.98 us -> 6.37 us  [gathered_shards(): lax.all_to_all(table, 'expert', split_axis=0, concat_axis=0, tiled=True)]
  transfers between devices with their start and end apart: 20 -> 21, of which waited for: 9 -> 10; matrix products, arithmetic and copies ran while one was open for 1% -> 0% of each run, Pallas kernels for 39% -> 42%
where the time goes in v6:
time: 70.6 us; the launch traced here: 70.3 us
  Pallas kernels  32 us (45%)
  starting transfers between devices  18.3 us (26%)
  waiting for transfers between devices  12.8 us (18%)
  local copies, waits for them, and re-layouts  6.14 us (9%)
  between operations  0.95 us (1%)
    pallas_call x5, Pallas kernels, run_stage(): pl.pallas_call(functools.partial(stage_kernel, places, before, after, bas...  23.9 us
    all_to_all x1, starting transfers between devices, gathered_shards(): lax.all_to_all(table, 'expert', split_axis=0, concat_axis=0, tiled=True)  6.37 us
    unnamed x14, local copies, waits for them, and re-layouts  6.14 us
    all_to_all x1, waiting for transfers between devices, gathered_shards(): lax.all_to_all(table, 'expert', split_axis=0, concat_axis=0, tiled=True)  6.12 us
    pallas_call x2, Pallas kernels, final_sums(): pl.pallas_call(functools.partial(final_kernel, kinds, len(lhs), float(div...  6.05 us
    ppermute x3, starting transfers between devices, onward(): return lax.ppermute(x, 'expert', ring_pairs(experts, (1, 1)))  4.31 us
    ppermute x13, waiting for transfers between devices, swapped(): lax.ppermute(x, axis, [(i, i ^ 1 << stride) for i in range(lax.axis_size(...  3.42 us
    ppermute x13, starting transfers between devices, swapped(): lax.ppermute(x, axis, [(i, i ^ 1 << stride) for i in range(lax.axis_size(...  3.09 us
  transfers between devices with their start and end apart: 21, of which 10 were waited for; matrix products, arithmetic and copies ran while one was open for 0% of the time, Pallas kernels for 42%

profile of v6, /device:TPU:0, one launch (start us, length us, event | category | flops | bytes accessed | tf_op | source)
XLA Modules:
  0.0 70.3 jit_solution(12132530835280418094)
XLA Ops:
  0.6 3.1 %collective-permute-start = (bf16[128,2048]{1,0:T(8,128)(2,1)}, bf16[128,2048]{1,0:T(8,128)(2,1)S(1)}, u32[]{:S(2)}, u32[]{:S(2)}) collective-permute-start(bf16[128,2048]{1,0:T(8,128)(2,1)} %refs_2_.1), channel_id=1, source_target_pairs={{0,4},{1,5},{4,8},{5,9},{8,12},{9,13},{12,14},{13,15},{14,10},{15,... | collective-permute-start | bytes 1572872 | tf_op jit(solution)/shard_map/ppermute | solution.py:471
  3.7 0.7 copy-done.5
  4.4 2.1 %route_table.1 = bf16[16,2,128]{2,1,0:T(2,128)(2,1)} custom-call(s32[16]{0:T(128)S(1)} %copy-done.5, s32[8,128]{1,0:T(8,128)} %bitcast.2, s32[8,128]{1,0:T(8,128)} %bitcast.3, bf16[256]{0:T(256)(128)(2,1)} %coef_in.1), custom_call_target="tpu_custom_call" | custom-call | tf_op jit(solution)/shard_map/route_table/pallas_call | solution.py:190
  6.5 6.4 %all-to-all-start = ((bf16[16,2,128]{2,1,0:T(2,128)(2,1)}), bf16[16,2,128]{2,1,0:T(2,128)(2,1)S(1)}, u32[]{:S(2)}, u32[]{:S(2)}) async-start(bf16[16,2,128]{2,1,0:T(2,128)(2,1)} %route_table.1), calls=%async_computation | async-start | bytes 16384 | tf_op jit(solution)/shard_map/all_to_all | solution.py:506
  13.3 6.1 %all-to-all-done.refs_0_ = bf16[16,2,128]{2,1,0:T(2,128)(2,1)S(1)} async-done(((bf16[16,2,128]{2,1,0:T(2,128)(2,1)}), bf16[16,2,128]{2,1,0:T(2,128)(2,1)S(1)}, u32[]{:S(2)}, u32[]{:S(2)}) %all-to-all-start) | async-done | bytes 8224 | tf_op jit(solution)/shard_map/all_to_all | solution.py:506
  20.5 1.5 %collective-permute-start.6 = (bf16[128,2048]{1,0:T(8,128)(2,1)S(1)}, bf16[128,2048]{1,0:T(8,128)(2,1)S(1)}, u32[]{:S(2)}, u32[]{:S(2)}) collective-permute-start(bf16[128,2048]{1,0:T(8,128)(2,1)S(1)} %collective-permute-done.1.refs_6_), channel_id=1, source_target_pairs={{0,2},{1,3},{4,0},{5,1},{8,4},{9,5},{12,8},{13,9},{14,12},{15,13},... | collective-permute-start | bytes 1572872 | tf_op jit(solution)/shard_map/ppermute | solution.py:474
  22.0 1.9 %copy-done = bf16[1,2048,768]{2,1,0:T(8,128)(2,1)S(1)} copy-done((bf16[1,2048,768]{2,1,0:T(8,128)(2,1)S(1)}, bf16[1,2048,768]{2,1,0:T(8,128)(2,1)}, u32[]{:S(2)}) %copy-start) | copy-done | bytes 3145752
  23.9 1.9 %copy-done.2 = bf16[1,2048,768]{2,1,0:T(8,128)(2,1)S(1)} copy-done((bf16[1,2048,768]{2,1,0:T(8,128)(2,1)S(1)}, bf16[1,2048,768]{2,1,0:T(8,128)(2,1)}, u32[]{:S(2)}) %copy-start.2) | copy-done | bytes 3145752
  26.5 1.0 %copy-done.6 = bf16[128,2048]{1,0:T(8,128)(2,1)S(1)} copy-done((bf16[128,2048]{1,0:T(8,128)(2,1)S(1)}, bf16[128,2048]{1,0:T(8,128)(2,1)}, u32[]{:S(2)}) %copy-start.6) | copy-done | bytes 524312
  27.5 6.0 %stage_first.1 = (bf16[768,768]{1,0:T(8,128)(2,1)S(1)}, bf16[768,768]{1,0:T(8,128)(2,1)S(1)}, bf16[768,768]{1,0:T(8,128)(2,1)S(1)}, bf16[768,768]{1,0:T(8,128)(2,1)S(1)}) custom-call(bf16[16,2,128]{2,1,0:T(2,128)(2,1)S(1)} %all-to-all-done.refs_0_, s32[16]{0:T(128)S(1)} %copy-done.3, bf16[128,2048]{1,0:T(8,128)(2,1)S(1)} %copy-done.6, ...), custom_call_target="tpu_custom_call" | custom-call | flops 4831838208 | bytes 65536 | tf_op jit(solution)/shard_map/stage_first/pallas_call | solution.py:351
  34.6 0.7 collective-permute-start.10
  35.3 1.4 %collective-permute-start.11 = (bf16[128,2048]{1,0:T(8,128)(2,1)S(1)}, bf16[128,2048]{1,0:T(8,128)(2,1)S(1)}, u32[]{:S(2)}, u32[]{:S(2)}) collective-permute-start(bf16[128,2048]{1,0:T(8,128)(2,1)S(1)} %collective-permute-done.6.refs_4_), channel_id=1, source_target_pairs={{0,2},{1,3},{4,0},{5,1},{8,4},{9,5},{12,8},{13,9},{14,12},{15,13},... | collective-permute-start | bytes 1572872 | tf_op jit(solution)/shard_map/ppermute | solution.py:474
  36.6 1.1 %collective-permute-done.7.refs_3_ = bf16[128,2048]{1,0:T(8,128)(2,1)S(1)} collective-permute-done((bf16[128,2048]{1,0:T(8,128)(2,1)S(1)}, bf16[128,2048]{1,0:T(8,128)(2,1)S(1)}, u32[]{:S(2)}, u32[]{:S(2)}) %collective-permute-start.7) | collective-permute-done | bytes 524320 | tf_op jit(solution)/shard_map/ppermute | solution.py:12
  37.7 0.7 %collective-permute-done.8.refs_5_ = bf16[128,2048]{1,0:T(8,128)(2,1)S(1)} collective-permute-done((bf16[128,2048]{1,0:T(8,128)(2,1)S(1)}, bf16[128,2048]{1,0:T(8,128)(2,1)S(1)}, u32[]{:S(2)}, u32[]{:S(2)}) %collective-permute-start.8) | collective-permute-done | bytes 524320 | tf_op jit(solution)/shard_map/ppermute | solution.py:12
  38.4 8.1 %stage_second.1 = (bf16[768,512]{1,0:T(8,128)(2,1)S(1)}, bf16[512,768]{1,0:T(8,128)(2,1)S(1)}, bf16[512,768]{1,0:T(8,128)(2,1)S(1)}, bf16[512,768]{1,0:T(8,128)(...) custom-call(bf16[16,2,128]{2,1,0:T(2,128)(2,1)S(1)} %all-to-all-done.refs_0_, ...), custom_call_target="tpu_custom_call" | custom-call | flops 3221225472 | bytes 65536 | tf_op jit(solution)/shard_map/stage_second/pallas_call | solution.py:351
  46.6 2.4 %collective-permute-done.10.refs_2_.even_ref = bf16[128,2048]{1,0:T(8,128)(2,1)S(1)} collective-permute-done((bf16[128,2048]{1,0:T(8,128)(2,1)S(1)}, bf16[128,2048]{1,0:T(8,128)(2,1)S(1)}, u32[]{:S(2)}, u32[]{:S(2)}) %collective-permute-start.10) | collective-permute-done | bytes 524320 | tf_op jit(solution)/shard_map/ppermute | solution.py:471
  49.9 1.8 %collective-permute-start.15 = (bf16[128,2048]{1,0:T(8,128)(2,1)S(1)}, bf16[128,2048]{1,0:T(8,128)(2,1)S(1)}, u32[]{:S(2)}, u32[]{:S(2)}) collective-permute-start(bf16[128,2048]{1,0:T(8,128)(2,1)S(1)} %pick_by_core.1), channel_id=1, source_target_pairs={{0,4},{1,3},{4,8},{5,1},{8,12},{9,5},{12,14},{13,9},{14,10},{15,13... | collective-permute-start | bytes 1572872 | tf_op jit(solution)/shard_map/ppermute | solution.py:519
  51.6 0.7 %collective-permute-done.12.refs_3_ = bf16[128,2048]{1,0:T(8,128)(2,1)S(1)} collective-permute-done((bf16[128,2048]{1,0:T(8,128)(2,1)S(1)}, bf16[128,2048]{1,0:T(8,128)(2,1)S(1)}, u32[]{:S(2)}, u32[]{:S(2)}) %collective-permute-start.12) | collective-permute-done | bytes 524320 | tf_op jit(solution)/shard_map/ppermute | solution.py:12
  52.4 0.7 %collective-permute-done.13.refs_5_ = bf16[128,2048]{1,0:T(8,128)(2,1)S(1)} collective-permute-done((bf16[128,2048]{1,0:T(8,128)(2,1)S(1)}, bf16[128,2048]{1,0:T(8,128)(2,1)S(1)}, u32[]{:S(2)}, u32[]{:S(2)}) %collective-permute-start.13) | collective-permute-done | bytes 524320 | tf_op jit(solution)/shard_map/ppermute | solution.py:12
  53.1 6.4 %stage_third.1 = (bf16[768,512]{1,0:T(8,128)(2,1)S(1)}, bf16[512,768]{1,0:T(8,128)(2,1)}, bf16[512,768]{1,0:T(8,128)(2,1)}, bf16[512,768]{1,0:T(8,128)(2,1)S(1)}...) custom-call(bf16[16,2,128]{2,1,0:T(2,128)(2,1)S(1)} %all-to-all-done, ...), custom_call_target="tpu_custom_call", output_to_operand_aliasing={{4}: (12, {}), {5}: (13, {}), {6}: (14, {})} | custom-call | flops 3221225472 | bytes 65536 | tf_op jit(solution)/shard_map/stage_third/pallas_call | solution.py:351
  60.1 1.7 %stage_mine.1 = (bf16[768,128]{1,0:T(8,128)(2,1)S(1)}, bf16[128,768]{1,0:T(8,128)(2,1)S(1)}, bf16[128,768]{1,0:T(8,128)(2,1)S(1)}, bf16[128,768]{1,0:T(8,128)(2,1)S(1)}) custom-call(bf16[16,2,128]{2,1,0:T(2,128)(2,1)S(1)} %all-to-all-done.refs_0_, s32[16]{0:T(128)S(1)} %copy-done.4, bf16[128,2048]{1,0:T(8,128)(2,1)S(1)} %collective-permute-done.15.refs_2_, ...), custom_call_target="tpu_custom_call" | custom-call | flops 805306368 | bytes 65536 | tf_op jit(solution)/shard_map/stage_mine/pallas_call | solution.py:351
  61.8 1.7 %stage_theirs.1 = (bf16[768,128]{1,0:T(8,128)(2,1)S(1)}, bf16[128,768]{1,0:T(8,128)(2,1)S(1)}, bf16[128,768]{1,0:T(8,128)(2,1)S(1)}, bf16[128,768]{1,0:T(8,128)(2,1)S(1)}) custom-call(bf16[16,2,128]{2,1,0:T(2,128)(2,1)S(1)} %all-to-all-done.refs_0_, s32[16]{0:T(128)S(1)} %copy-done.4, bf16[128,2048]{1,0:T(8,128)(2,1)S(1)} %collective-permute-done.16.refs_2_, ...), custom_call_target="tpu_custom_call" | custom-call | flops 805306368 | bytes 65536 | tf_op jit(solution)/shard_map/stage_theirs/pallas_call | solution.py:351
  64.0 3.2 %own_sums.1 = (f32[1,768,768]{2,1,0:T(8,128)}, f32[1,768,768]{2,1,0:T(8,128)}) custom-call(s32[16]{0:T(128)S(1)} %copy-done.4, bf16[768,128]{1,0:T(8,128)(2,1)S(1)} %get-tuple-element.97.refs_0_.refs_1_, bf16[768,128]{1,0:T(8,128)(2,1)S(1)} %get-tuple-element.99.refs_1_.refs_2_, bf16[128,768]{1,0:T(8,128)(2,1)S(1)} %get-tuple-element.100.refs_2_, ...), custom_call_target="tpu_custom_call" | custom-call | flops 1048576 | bytes 65536 | tf_op jit(solution)/shard_map/own_sums/pallas_call | solution.py:440
  67.3 2.9 %merge_sums.1 = f32[1,768,768]{2,1,0:T(8,128)} custom-call(s32[16]{0:T(128)S(1)} %copy-done.4, bf16[768,512]{1,0:T(8,128)(2,1)S(1)} %get-tuple-element.108.refs_0_, bf16[768,128]{1,0:T(8,128)(2,1)S(1)} %get-tuple-element.97.refs_0_.refs_1_, bf16[768,128]{1,0:T(8,128)(2,1)S(1)} %get-tuple-element.99.refs_1_.refs_2_, ...), custom_call_target="tpu_custom_call" | custom-call | flops 1048576 | bytes 65536 | tf_op jit(solution)/shard_map/merge_sums/pallas_call | solution.py:440
  (41 shorter events, 5.4 us)
Async XLA Ops:
  0.6 18.7 %collective-permute-start = (bf16[128,2048]{1,0:T(8,128)(2,1)}, bf16[128,2048]{1,0:T(8,128)(2,1)S(1)}, u32[]{:S(2)}, u32[]{:S(2)}) collective-permute-start(bf16[128,2048]{1,0:T(8,128)(2,1)} %refs_2_.1), channel_id=1, source_target_pairs={{0,4},{1,5},{4,8},{5,9},{8,12},{9,13},{12,14},{13,15},{14,10},{15,... | collective-permute-start | bytes 1572872 | tf_op jit(solution)/shard_map/ppermute | solution.py:471
  3.7 15.7 %collective-permute-start.1 = (bf16[128,2048]{1,0:T(8,128)(2,1)}, bf16[128,2048]{1,0:T(8,128)(2,1)S(1)}, u32[]{:S(2)}, u32[]{:S(2)}) collective-permute-start(bf16[128,2048]{1,0:T(8,128)(2,1)} %refs_2_.1), channel_id=1, source_target_pairs={{0,2},{1,3},{4,0},{5,1},{8,4},{9,5},{12,8},{13,9},{14,12},{15,13},... | collective-permute-start | bytes 1572872 | tf_op jit(solution)/shard_map/ppermute | solution.py:474
  6.5 12.9 %all-to-all-start = ((bf16[16,2,128]{2,1,0:T(2,128)(2,1)}), bf16[16,2,128]{2,1,0:T(2,128)(2,1)S(1)}, u32[]{:S(2)}, u32[]{:S(2)}) async-start(bf16[16,2,128]{2,1,0:T(2,128)(2,1)} %route_table.1), calls=%async_computation | async-start | bytes 16384 | tf_op jit(solution)/shard_map/all_to_all | solution.py:506
  12.8 9.1 %collective-permute-start.2 = (bf16[128,2048]{1,0:T(8,128)(2,1)}, bf16[128,2048]{1,0:T(8,128)(2,1)S(1)}, u32[]{:S(2)}, u32[]{:S(2)}) collective-permute-start(bf16[128,2048]{1,0:T(8,128)(2,1)} %refs_2_.1), channel_id=1, source_target_pairs={{0,1},{1,0},{2,3},{3,2},{4,5},{5,4},{6,7},{7,6},{8,9},{9,8},{10,11... | collective-permute-start | bytes 1572872 | tf_op jit(solution)/shard_map/ppermute | solution.py:12
  19.4 2.5 %collective-permute-start.3 = (bf16[128,2048]{1,0:T(8,128)(2,1)S(1)}, bf16[128,2048]{1,0:T(8,128)(2,1)S(1)}, u32[]{:S(2)}, u32[]{:S(2)}) collective-permute-start(bf16[128,2048]{1,0:T(8,128)(2,1)S(1)} %collective-permute-done.refs_4_), channel_id=1, source_target_pairs={{0,1},{1,0},{2,3},{3,2},{4,5},{5,4},{6,7},{7,6},{8,9},{9,8},{10,11... | collective-permute-start | bytes 1572872 | tf_op jit(solution)/shard_map/ppermute | solution.py:12
  19.4 2.7 %collective-permute-start.4 = (bf16[128,2048]{1,0:T(8,128)(2,1)S(1)}, bf16[128,2048]{1,0:T(8,128)(2,1)S(1)}, u32[]{:S(2)}, u32[]{:S(2)}) collective-permute-start(bf16[128,2048]{1,0:T(8,128)(2,1)S(1)} %collective-permute-done.1.refs_6_), channel_id=1, source_target_pairs={{0,1},{1,0},{2,3},{3,2},{4,5},{5,4},{6,7},{7,6},{8,9},{9,8},{10,11... | collective-permute-start | bytes 1572872 | tf_op jit(solution)/shard_map/ppermute | solution.py:12
  19.9 13.9 %collective-permute-start.5 = (bf16[128,2048]{1,0:T(8,128)(2,1)S(1)}, bf16[128,2048]{1,0:T(8,128)(2,1)S(1)}, u32[]{:S(2)}, u32[]{:S(2)}) collective-permute-start(bf16[128,2048]{1,0:T(8,128)(2,1)S(1)} %collective-permute-done.refs_4_), channel_id=1, source_target_pairs={{0,4},{1,5},{4,8},{5,9},{8,12},{9,13},{12,14},{13,15},{14,10},{15,... | collective-permute-start | bytes 1572872 | tf_op jit(solution)/shard_map/ppermute | solution.py:471
  20.5 13.6 %collective-permute-start.6 = (bf16[128,2048]{1,0:T(8,128)(2,1)S(1)}, bf16[128,2048]{1,0:T(8,128)(2,1)S(1)}, u32[]{:S(2)}, u32[]{:S(2)}) collective-permute-start(bf16[128,2048]{1,0:T(8,128)(2,1)S(1)} %collective-permute-done.1.refs_6_), channel_id=1, source_target_pairs={{0,2},{1,3},{4,0},{5,1},{8,4},{9,5},{12,8},{13,9},{14,12},{15,13},... | collective-permute-start | bytes 1572872 | tf_op jit(solution)/shard_map/ppermute | solution.py:474
  22.0 1.9 %copy-start = (bf16[1,2048,768]{2,1,0:T(8,128)(2,1)S(1)}, bf16[1,2048,768]{2,1,0:T(8,128)(2,1)}, u32[]{:S(2)}) copy-start(bf16[1,2048,768]{2,1,0:T(8,128)(2,1)} %refs_3_.3) | copy-start | bytes 9437188
  34.1 19.0 %copy-start.4 = (s32[16]{0:T(128)S(1)}, s32[16]{0:T(128)}, u32[]{:S(2)}) copy-start(s32[16]{0:T(128)} %flag_ref.3) | copy-start | bytes 196
  34.1 4.4 %collective-permute-start.9 = (bf16[768,768]{1,0:T(8,128)(2,1)S(1)}, bf16[768,768]{1,0:T(8,128)(2,1)S(1)}, u32[]{:S(2)}, u32[]{:S(2)}) collective-permute-start(bf16[768,768]{1,0:T(8,128)(2,1)S(1)} %get-tuple-element.70), channel_id=1, source_target_pairs={{0,1},{1,0},{2,3},{3,2},{4,5},{5,4},{6,7},{7,6},{8,9},{9,8},{10,11... | collective-permute-start | bytes 3538952 | tf_op jit(solution)/shard_map/ppermute | solution.py:12
  34.1 3.6 %collective-permute-start.7 = (bf16[128,2048]{1,0:T(8,128)(2,1)S(1)}, bf16[128,2048]{1,0:T(8,128)(2,1)S(1)}, u32[]{:S(2)}, u32[]{:S(2)}) collective-permute-start(bf16[128,2048]{1,0:T(8,128)(2,1)S(1)} %collective-permute-done.5.refs_2_), channel_id=1, source_target_pairs={{0,1},{1,0},{2,3},{3,2},{4,5},{5,4},{6,7},{7,6},{8,9},{9,8},{10,11... | collective-permute-start | bytes 1572872 | tf_op jit(solution)/shard_map/ppermute | solution.py:12
  34.6 3.8 %collective-permute-start.8 = (bf16[128,2048]{1,0:T(8,128)(2,1)S(1)}, bf16[128,2048]{1,0:T(8,128)(2,1)S(1)}, u32[]{:S(2)}, u32[]{:S(2)}) collective-permute-start(bf16[128,2048]{1,0:T(8,128)(2,1)S(1)} %collective-permute-done.6.refs_4_), channel_id=1, source_target_pairs={{0,1},{1,0},{2,3},{3,2},{4,5},{5,4},{6,7},{7,6},{8,9},{9,8},{10,11... | collective-permute-start | bytes 1572872 | tf_op jit(solution)/shard_map/ppermute | solution.py:12
  34.6 14.3 %collective-permute-start.10 = (bf16[128,2048]{1,0:T(8,128)(2,1)S(1)}, bf16[128,2048]{1,0:T(8,128)(2,1)S(1)}, u32[]{:S(2)}, u32[]{:S(2)}) collective-permute-start(bf16[128,2048]{1,0:T(8,128)(2,1)S(1)} %collective-permute-done.5.refs_2_), channel_id=1, source_target_pairs={{0,4},{1,5},{4,8},{5,9},{8,12},{9,13},{12,14},{13,15},{14,10},{15,... | collective-permute-start | bytes 1572872 | tf_op jit(solution)/shard_map/ppermute | solution.py:471
  35.3 14.1 %collective-permute-start.11 = (bf16[128,2048]{1,0:T(8,128)(2,1)S(1)}, bf16[128,2048]{1,0:T(8,128)(2,1)S(1)}, u32[]{:S(2)}, u32[]{:S(2)}) collective-permute-start(bf16[128,2048]{1,0:T(8,128)(2,1)S(1)} %collective-permute-done.6.refs_4_), channel_id=1, source_target_pairs={{0,2},{1,3},{4,0},{5,1},{8,4},{9,5},{12,8},{13,9},{14,12},{15,13},... | collective-permute-start | bytes 1572872 | tf_op jit(solution)/shard_map/ppermute | solution.py:474
  38.4 14.7 %copy-start.1 = (bf16[1,2048,768]{2,1,0:T(8,128)(2,1)S(1)}, bf16[1,2048,768]{2,1,0:T(8,128)(2,1)}, u32[]{:S(2)}) copy-start(bf16[1,2048,768]{2,1,0:T(8,128)(2,1)} %refs_3_.3) | copy-start | bytes 9437188
  49.3 3.8 %collective-permute-start.14 = (bf16[512,768]{1,0:T(8,128)(2,1)S(1)}, bf16[512,768]{1,0:T(8,128)(2,1)S(1)}, u32[]{:S(2)}, u32[]{:S(2)}) collective-permute-start(bf16[512,768]{1,0:T(8,128)(2,1)S(1)} %get-tuple-element.83), channel_id=1, source_target_pairs={{0,1},{1,0},{2,3},{3,2},{4,5},{5,4},{6,7},{7,6},{8,9},{9,8},{10,11... | collective-permute-start | bytes 2359304 | tf_op jit(solution)/shard_map/ppermute | solution.py:12
  49.3 3.0 %collective-permute-start.12 = (bf16[128,2048]{1,0:T(8,128)(2,1)S(1)}, bf16[128,2048]{1,0:T(8,128)(2,1)S(1)}, u32[]{:S(2)}, u32[]{:S(2)}) collective-permute-start(bf16[128,2048]{1,0:T(8,128)(2,1)S(1)} %collective-permute-done.10.refs_2_.even_ref), channel_id=1, source_target_pairs={{0,1},{1,0},{2,3},{3,2},{4,5},{5,4},{6,7},{7,6},{8,9},{9,8},{10,11... | collective-permute-start | bytes 1572872 | tf_op jit(solution)/shard_map/ppermute | solution.py:12
  49.8 3.3 %collective-permute-start.13 = (bf16[128,2048]{1,0:T(8,128)(2,1)S(1)}, bf16[128,2048]{1,0:T(8,128)(2,1)S(1)}, u32[]{:S(2)}, u32[]{:S(2)}) collective-permute-start(bf16[128,2048]{1,0:T(8,128)(2,1)S(1)} %collective-permute-done.11.refs_4_.odd_ref), channel_id=1, source_target_pairs={{0,1},{1,0},{2,3},{3,2},{4,5},{5,4},{6,7},{7,6},{8,9},{9,8},{10,11... | collective-permute-start | bytes 1572872 | tf_op jit(solution)/shard_map/ppermute | solution.py:12
  49.9 9.7 %collective-permute-start.15 = (bf16[128,2048]{1,0:T(8,128)(2,1)S(1)}, bf16[128,2048]{1,0:T(8,128)(2,1)S(1)}, u32[]{:S(2)}, u32[]{:S(2)}) collective-permute-start(bf16[128,2048]{1,0:T(8,128)(2,1)S(1)} %pick_by_core.1), channel_id=1, source_target_pairs={{0,4},{1,3},{4,8},{5,1},{8,12},{9,5},{12,14},{13,9},{14,10},{15,13... | collective-permute-start | bytes 1572872 | tf_op jit(solution)/shard_map/ppermute | solution.py:519
  59.6 2.2 %collective-permute-start.16 = (bf16[128,2048]{1,0:T(8,128)(2,1)S(1)}, bf16[128,2048]{1,0:T(8,128)(2,1)S(1)}, u32[]{:S(2)}, u32[]{:S(2)}) collective-permute-start(bf16[128,2048]{1,0:T(8,128)(2,1)S(1)} %collective-permute-done.15.refs_2_), channel_id=1, source_target_pairs={{0,1},{1,0},{2,3},{3,2},{4,5},{5,4},{6,7},{7,6},{8,9},{9,8},{10,11... | collective-permute-start | bytes 1572872 | tf_op jit(solution)/shard_map/ppermute | solution.py:12
  59.8 7.5 %collective-permute-start.17 = (bf16[512,768]{1,0:T(8,128)(2,1)S(1)}, bf16[512,768]{1,0:T(8,128)(2,1)S(1)}, u32[]{:S(2)}, u32[]{:S(2)}) collective-permute-start(bf16[512,768]{1,0:T(8,128)(2,1)S(1)} %get-tuple-element.109), channel_id=1, source_target_pairs={{0,1},{1,0},{2,3},{3,2},{4,5},{5,4},{6,7},{7,6},{8,9},{9,8},{10,11... | collective-permute-start | bytes 2359304 | tf_op jit(solution)/shard_map/ppermute | solution.py:12
  63.5 3.8 %collective-permute-start.18 = (bf16[128,768]{1,0:T(8,128)(2,1)S(1)}, bf16[128,768]{1,0:T(8,128)(2,1)S(1)}, u32[]{:S(2)}, u32[]{:S(2)}) collective-permute-start(bf16[128,768]{1,0:T(8,128)(2,1)S(1)} %get-tuple-element.110), channel_id=1, source_target_pairs={{0,1},{1,0},{2,3},{3,2},{4,5},{5,4},{6,7},{7,6},{8,9},{9,8},{10,11... | collective-permute-start | bytes 589832 | tf_op jit(solution)/shard_map/ppermute | solution.py:12
  63.7 3.6 %collective-permute-start.19 = (bf16[128,768]{1,0:T(8,128)(2,1)S(1)}, bf16[128,768]{1,0:T(8,128)(2,1)S(1)}, u32[]{:S(2)}, u32[]{:S(2)}) collective-permute-start(bf16[128,768]{1,0:T(8,128)(2,1)S(1)} %get-tuple-element.111), channel_id=1, source_target_pairs={{0,1},{1,0},{2,3},{3,2},{4,5},{5,4},{6,7},{7,6},{8,9},{9,8},{10,11... | collective-permute-start | bytes 589832 | tf_op jit(solution)/shard_map/ppermute | solution.py:12
  (4 other events, 4.2 us)

commit v7 on v6

--- a/solution.py
+++ b/solution.py
@@ -199,6 +199,7 @@
             pltpu.SemaphoreType.DMA((3,)),
         ],
         compiler_params=pltpu.CompilerParams(vmem_limit_bytes=4 << 20),
+        cost_estimate=kernel_cost(1 << 34),
         name="route_table",
     )(quotas, in_hbm(picks.T), in_hbm(entries.T), in_hbm(coefficients))
 
@@ -223,7 +224,7 @@
     ]
 
 
-def stage_kernel(places, before, after, with_base, *refs):
+def stage_kernel(places, before, after, with_base, rows_at, *refs):
     taken = iter(refs)
 
     def take(count):
@@ -233,29 +234,35 @@
     blocks = take(len(places))
     weights = take(2)
     part = take(4) if before else None
-    bases = take(3) if with_base else [None] * 3
+    sum_total = max((*before, *after), default=-1) + 1
+    bases = take(sum_total) if with_base else [None] * 3
+    take(4 if rows_at else 0)
     hidden_outs = take(4)
-    sums = take(3) if before or after else [None] * 3
+    sums = take(sum_total)
     scratch = take(2)
     for which in before:
-        add_product(sums[which], bases[which], part[0], part[1 + which])
-    hidden_body(places, table_ref, flag_ref, blocks, *weights, *hidden_outs, *scratch)
+        add_product(sums[which], bases[which], [(part[0], part[1 + which])])
+    hidden_body(places, rows_at, table_ref, flag_ref, blocks, *weights, *hidden_outs, *scratch)
     for which in after:
         base = sums[which] if which in before else bases[which]
-        add_product(sums[which], base, hidden_outs[0], hidden_outs[1 + which])
-
-
-def add_product(out_ref, base_ref, lhs_ref, rhs_ref):
+        add_product(sums[which], base, [(hidden_outs[0], hidden_outs[1 + which])])
+
+
+def add_product(out_ref, base_ref, pairs):
     hidden_width = out_ref.shape[1]
     tile = 256
     for start in range(0, hidden_width, tile):
         lanes = slice(start, start + tile)
-        total = jnp.dot(lhs_ref[...], rhs_ref[:, lanes], preferred_element_type=jnp.float32)
-        out_ref[:, lanes] = total if base_ref is None else base_ref[:, lanes] + total
+        total = None if base_ref is None else base_ref[:, lanes]
+        for lhs_ref, rhs_ref in pairs:
+            term = jnp.dot(lhs_ref[...], rhs_ref[:, lanes], preferred_element_type=jnp.float32)
+            total = term if total is None else total + term
+        out_ref[:, lanes] = total
 
 
 def hidden_body(
     places,
+    rows_at,
     table_ref,
     flag_ref,
     block_refs,
@@ -307,14 +314,19 @@
             gate = jnp.dot(rows, gate_ref[0, :, lanes], preferred_element_type=jnp.float32)
             upward = jnp.dot(rows, up_ref[0, :, lanes], preferred_element_type=jnp.float32)
             hidden = (gate / (1.0 + jnp.exp(-gate)) * upward).astype(jnp.bfloat16)
-            lhs_ref[lanes, span] = hidden.T
+            out_span = slice(span.start + rows_at, span.stop + rows_at)
+            lhs_ref[lanes, out_span] = hidden.T
             hidden = hidden.astype(jnp.float32)
             for lane in range(0, tile, 128):
                 part = hidden[:, lane : lane + 128]
                 to = slice(start + lane, start + lane + 128)
-                count_ref[span, to] = (part * coef_ref[0, span, :]).astype(jnp.bfloat16)
+                count_ref[out_span, to] = (part * coef_ref[0, span, :]).astype(jnp.bfloat16)
                 weighed = (part * coef_ref[1, span, :]).astype(jnp.bfloat16)
-                weigh_ref[span, to] = weighed
+                weigh_ref[out_span, to] = weighed
+                if block_total == 1:
+                    send_at = send_ref.shape[0] - span.stop - rows_at
+                    send_ref[send_at : send_at + span.stop, to] = weighed
+                    continue
                 for unit in group:
                     for block, source in zip(unit, unit[::-1]):
                         base = span.start
@@ -326,30 +338,37 @@
     return pltpu.with_memory_space_constraint(x, pltpu.VMEM)
 
 
-def run_stage(places, table, flags, blocks, w_gate, w_up, part, bases, before, after, name):
+def run_stage(
+    places, table, flags, blocks, w_gate, w_up, part, bases, before, after, name, room=1, filled=None
+):
     width = blocks[0].shape[1]
     rows = sum(block.shape[0] for block in blocks)
     hidden_width = w_gate.shape[2]
     vmem = pl.BlockSpec(memory_space=pltpu.VMEM)
     operands = [in_vmem(table), flags, *map(in_vmem, blocks), in_vmem(w_gate), in_vmem(w_up)]
     out_shape = [
-        pltpu.VMEM((hidden_width, rows), jnp.bfloat16),
-        pltpu.VMEM((rows, hidden_width), jnp.bfloat16),
-        pltpu.VMEM((rows, hidden_width), jnp.bfloat16),
-        jax.ShapeDtypeStruct((rows, hidden_width), jnp.bfloat16),
+        pltpu.VMEM((hidden_width, room * rows), jnp.bfloat16),
+        pltpu.VMEM((room * rows, hidden_width), jnp.bfloat16),
+        pltpu.VMEM((room * rows, hidden_width), jnp.bfloat16),
+        pltpu.VMEM((room * rows, hidden_width), jnp.bfloat16),
     ]
     aliases = {}
     if before:
         operands += map(in_vmem, part)
-    if before or after:
-        out_shape += [pltpu.VMEM((hidden_width, hidden_width), jnp.float32)] * 3
+    sum_total = max((*before, *after), default=-1) + 1
+    out_shape += [pltpu.VMEM((hidden_width, hidden_width), jnp.float32)] * sum_total
     if bases is not None:
-        aliases = {len(operands) + index: 4 + index for index in range(3)}
+        aliases = {len(operands) + index: 4 + index for index in range(sum_total)}
         operands += map(in_vmem, bases)
+    if filled is not None:
+        aliases |= {len(operands) + index: index for index in range(4)}
+        operands += map(in_vmem, filled)
     in_specs = [vmem] * len(operands)
     in_specs[1] = pl.BlockSpec(memory_space=pltpu.SMEM)
     outs = pl.pallas_call(
-        functools.partial(stage_kernel, places, before, after, bases is not None),
+        functools.partial(
+            stage_kernel, places, before, after, bases is not None, 0 if filled is None else rows
+        ),
         out_shape=out_shape,
         in_specs=in_specs,
         out_specs=[vmem] * len(out_shape),
@@ -389,8 +408,12 @@
     )(in_vmem(even), in_vmem(odd))
 
 
-def final_kernel(kinds, part_total, divisor, flag_ref, *refs):
+def final_kernel(kinds, part_total, late_total, divisor, flag_ref, *refs):
     set_total = len(kinds)
+    if late_total:
+        late, refs = refs[: 2 * late_total + 1], refs[2 * late_total + 1 :]
+        late_out = refs[-3]
+        refs = refs[:-3] + refs[-2:]
     lhs, rest = refs[:part_total], refs[part_total:]
     rhs = [rest[part_total * index : part_total * (index + 1)] for index in range(set_total)]
     rest = rest[part_total * set_total :]
@@ -424,24 +447,37 @@
                 )
             )
             copies[-1].start()
+    if late_total:
+        pairs = [(late[index], late[late_total + index]) for index in range(late_total)]
+        add_product(late_out, late[-1], pairs)
     for copy in copies:
         copy.wait()
 
 
-def final_sums(flags, lhs, rhs, bases, kinds, divisor, name):
+def final_sums(flags, lhs, rhs, bases, kinds, divisor, name, late=None):
     hidden_width = lhs[0].shape[0]
     total = len(rhs)
     vmem = pl.BlockSpec(memory_space=pltpu.VMEM)
     outside = pl.BlockSpec(memory_space=pl.ANY)
-    operands = [*lhs]
+    operands = [] if late is None else [*late[0], *late[1], late[2]]
+    late_total = 0 if late is None else len(late[0])
+    operands += lhs
     for parts in rhs:
         operands += parts
     operands += bases
+    out_shape = [jax.ShapeDtypeStruct((1, hidden_width, hidden_width), jnp.float32)] * total
+    out_specs = [outside] * total
+    aliases = {}
+    if late is not None:
+        out_shape.append(pltpu.VMEM((hidden_width, hidden_width), jnp.float32))
+        out_specs.append(vmem)
+        aliases = {1 + 2 * late_total: total}
     return pl.pallas_call(
-        functools.partial(final_kernel, kinds, len(lhs), float(divisor)),
-        out_shape=[jax.ShapeDtypeStruct((1, hidden_width, hidden_width), jnp.float32)] * total,
+        functools.partial(final_kernel, kinds, len(lhs), late_total, float(divisor)),
+        out_shape=out_shape,
         in_specs=[pl.BlockSpec(memory_space=pltpu.SMEM)] + [vmem] * len(operands),
-        out_specs=[outside] * total,
+        out_specs=out_specs,
+        input_output_aliases=aliases,
         scratch_shapes=[
             pltpu.VMEM((total, hidden_width, hidden_width), jnp.float32),
             pltpu.SemaphoreType.DMA((total, hidden_width // 256)),
@@ -476,7 +512,7 @@
     def other(x):
         return swapped(x, "expert", 0)
 
-    def stage(arrivals, part, bases, before, after, name):
+    def stage(arrivals, part, bases, before, after, name, **options):
         blocks, places = [], []
         for block, steps, turn, offset in arrivals:
             blocks.append(block)
@@ -496,6 +532,7 @@
             before,
             after,
             name,
+            **options,
         )
 
     tied = lax.optimization_barrier
@@ -522,24 +559,25 @@
 
     third, bases, far = tied((third, bases, far))
     near_far = other(far)
-    mine, _ = stage([(far, 4, 0, 0)], None, None, (), (), "stage_mine")
+    mine, _ = stage([(far, 4, 0, 0)], None, None, (), (), "stage_mine", room=2)
     mine, near_far = tied((mine, near_far))
-    theirs, _ = stage([(near_far, 4, 1, 0)], None, None, (), (), "stage_theirs")
-    last = [mine, theirs]
-    gram, self_cross = final_sums(
+    theirs = [(near_far, 4, 1, 0)]
+    last, _ = stage(theirs, None, None, (), (), "stage_theirs", room=2, filled=mine)
+    gram, self_cross, merge_base = final_sums(
         retained_specialist_flags,
-        [part[0] for part in last],
-        [[part[1] for part in last], [part[2] for part in last]],
+        [last[0]],
+        [[last[1]], [last[2]]],
         bases[:2],
         ("gram", "self"),
         divisor,
         "own_sums",
+        ([third[0]], [other(third[3])], bases[2]),
     )
     (merge_cross,) = final_sums(
         retained_specialist_flags,
-        [third[0], mine[0], theirs[0]],
-        [[other(third[3]), other(theirs[3]), other(mine[3])]],
-        bases[2:],
+        [last[0]],
+        [[other(last[3])]],
+        [merge_base],
         ("merge",),
         divisor,
         "merge_sums",

time: 70.6 us -> 69.8 us (0.989)
  local copies, waits for them, and re-layouts: 6.14 us -> 3.59 us
  waiting for transfers between devices: 12.8 us -> 14.6 us
    unnamed x14 -> x10, local copies, waits for them, and re-layouts: 6.14 us -> 3.59 us
    ppermute x3, waiting for transfers between devices: 2.62 us -> 4.38 us  [onward(): return lax.ppermute(x, 'expert', ring_pairs(experts, (1, 1)))]
    pallas_call x5, Pallas kernels: 23.9 us -> 24.7 us  [run_stage(): pl.pallas_call(functools.partial(stage_kernel, places, before, after, bas...]
    ppermute x13 -> x12, starting transfers between devices: 3.09 us -> 2.72 us  [swapped(): lax.ppermute(x, axis, [(i, i ^ 1 << stride) for i in range(lax.axis_size(...]
    ppermute x13 -> x12, waiting for transfers between devices: 3.42 us -> 3.62 us  [swapped(): lax.ppermute(x, axis, [(i, i ^ 1 << stride) for i in range(lax.axis_size(...]
  transfers between devices with their start and end apart: 21 -> 20, of which waited for: 10 -> 10; matrix products, arithmetic and copies ran while one was open for 0% -> 0% of each run, Pallas kernels for 42% -> 43%
where the time goes in v7:
time: 69.8 us; the launch traced here: 69.5 us
  Pallas kernels  32.4 us (46%)
  starting transfers between devices  18 us (26%)
  waiting for transfers between devices  14.6 us (21%)
  local copies, waits for them, and re-layouts  3.59 us (5%)
  between operations  0.93 us (1%)
    pallas_call x5, Pallas kernels, run_stage(): pl.pallas_call(functools.partial(stage_kernel, places, before, after, bas...  24.7 us
    all_to_all x1, starting transfers between devices, gathered_shards(): lax.all_to_all(table, 'expert', split_axis=0, concat_axis=0, tiled=True)  6.37 us
    all_to_all x1, waiting for transfers between devices, gathered_shards(): lax.all_to_all(table, 'expert', split_axis=0, concat_axis=0, tiled=True)  5.92 us
    pallas_call x2, Pallas kernels, final_sums(): pl.pallas_call(functools.partial(final_kernel, kinds, len(lhs), late_tota...  5.35 us
    ppermute x3, waiting for transfers between devices, onward(): return lax.ppermute(x, 'expert', ring_pairs(experts, (1, 1)))  4.38 us
    ppermute x3, starting transfers between devices, onward(): return lax.ppermute(x, 'expert', ring_pairs(experts, (1, 1)))  4.3 us
    ppermute x12, waiting for transfers between devices, swapped(): lax.ppermute(x, axis, [(i, i ^ 1 << stride) for i in range(lax.axis_size(...  3.62 us
    unnamed x10, local copies, waits for them, and re-layouts  3.59 us
  transfers between devices with their start and end apart: 20, of which 10 were waited for; matrix products, arithmetic and copies ran while one was open for 0% of the time, Pallas kernels for 43%

profile of v7, /device:TPU:0, one launch (start us, length us, event | category | flops | bytes accessed | tf_op | source)
XLA Modules:
  0.0 69.5 jit_solution(17304320907070828020)
XLA Ops:
  0.6 3.1 %collective-permute-start = (bf16[128,2048]{1,0:T(8,128)(2,1)}, bf16[128,2048]{1,0:T(8,128)(2,1)}, u32[]{:S(2)}, u32[]{:S(2)}) collective-permute-start(bf16[128,2048]{1,0:T(8,128)(2,1)} %refs_2_.1), channel_id=1, source_target_pairs={{0,4},{1,5},{4,8},{5,9},{8,12},{9,13},{12,14},{13,15},{14,10},{15,... | collective-permute-start | bytes 1572872 | tf_op jit(solution)/shard_map/ppermute | solution.py:507
  3.7 0.7 copy-done.4
  4.4 2.4 %route_table.1 = bf16[16,2,128]{2,1,0:T(2,128)(2,1)} custom-call(s32[16]{0:T(128)S(1)} %copy-done.4, s32[8,128]{1,0:T(8,128)} %bitcast.2, s32[8,128]{1,0:T(8,128)} %bitcast.3, bf16[256]{0:T(256)(128)(2,1)} %coef_in.1), custom_call_target="tpu_custom_call" | custom-call | flops 17179869184 | bytes 65536 | tf_op jit(solution)/shard_map/route_table/pallas_call | solution.py:190
  6.7 6.4 %all-to-all-start = ((bf16[16,2,128]{2,1,0:T(2,128)(2,1)}), bf16[16,2,128]{2,1,0:T(2,128)(2,1)S(1)}, u32[]{:S(2)}, u32[]{:S(2)}) async-start(bf16[16,2,128]{2,1,0:T(2,128)(2,1)} %route_table.1), calls=%async_computation | async-start | bytes 16384 | tf_op jit(solution)/shard_map/all_to_all | solution.py:543
  13.5 5.9 %all-to-all-done.refs_0_ = bf16[16,2,128]{2,1,0:T(2,128)(2,1)S(1)} async-done(((bf16[16,2,128]{2,1,0:T(2,128)(2,1)}), bf16[16,2,128]{2,1,0:T(2,128)(2,1)S(1)}, u32[]{:S(2)}, u32[]{:S(2)}) %all-to-all-start) | async-done | bytes 8224 | tf_op jit(solution)/shard_map/all_to_all | solution.py:543
  20.5 1.5 %collective-permute-start.6 = (bf16[128,2048]{1,0:T(8,128)(2,1)}, bf16[128,2048]{1,0:T(8,128)(2,1)S(1)}, u32[]{:S(2)}, u32[]{:S(2)}) collective-permute-start(bf16[128,2048]{1,0:T(8,128)(2,1)} %collective-permute-done.1.refs_6_), channel_id=1, source_target_pairs={{0,2},{1,3},{4,0},{5,1},{8,4},{9,5},{12,8},{13,9},{14,12},{15,13},... | collective-permute-start | bytes 1572872 | tf_op jit(solution)/shard_map/ppermute | solution.py:510
  22.3 1.9 %copy-done.1 = bf16[1,2048,768]{2,1,0:T(8,128)(2,1)S(1)} copy-done((bf16[1,2048,768]{2,1,0:T(8,128)(2,1)S(1)}, bf16[1,2048,768]{2,1,0:T(8,128)(2,1)}, u32[]{:S(2)}) %copy-start.1) | copy-done | bytes 3145752
  24.2 1.0 %copy-done.3 = bf16[128,2048]{1,0:T(8,128)(2,1)S(1)} copy-done((bf16[128,2048]{1,0:T(8,128)(2,1)S(1)}, bf16[128,2048]{1,0:T(8,128)(2,1)}, u32[]{:S(2)}) %copy-start.3) | copy-done | bytes 524312
  25.3 6.8 %stage_first.1 = (bf16[768,768]{1,0:T(8,128)(2,1)S(1)}, bf16[768,768]{1,0:T(8,128)(2,1)S(1)}, bf16[768,768]{1,0:T(8,128)(2,1)S(1)}, bf16[768,768]{1,0:T(8,128)(2,1)S(1)}) custom-call(bf16[16,2,128]{2,1,0:T(2,128)(2,1)S(1)} %all-to-all-done.refs_0_, s32[16]{0:T(128)S(1)} %copy-done.2, bf16[128,2048]{1,0:T(8,128)(2,1)S(1)} %copy-done.3, ...), custom_call_target="tpu_custom_call" | custom-call | flops 4831838208 | bytes 65536 | tf_op jit(solution)/shard_map/stage_first/pallas_call | solution.py:368
  32.1 2.0 %collective-permute-done.5.refs_2_ = bf16[128,2048]{1,0:T(8,128)(2,1)S(1)} collective-permute-done((bf16[128,2048]{1,0:T(8,128)(2,1)}, bf16[128,2048]{1,0:T(8,128)(2,1)S(1)}, u32[]{:S(2)}, u32[]{:S(2)}) %collective-permute-start.5) | collective-permute-done | bytes 524320 | tf_op jit(solution)/shard_map/ppermute | solution.py:507
  34.8 0.7 %collective-permute-start.10 = (bf16[128,2048]{1,0:T(8,128)(2,1)S(1)}, bf16[128,2048]{1,0:T(8,128)(2,1)S(1)}, u32[]{:S(2)}, u32[]{:S(2)}) collective-permute-start(bf16[128,2048]{1,0:T(8,128)(2,1)S(1)} %collective-permute-done.5.refs_2_), channel_id=1, source_target_pairs={{0,4},{1,5},{4,8},{5,9},{8,12},{9,13},{12,14},{13,15},{14,10},{15,... | collective-permute-start | bytes 1572872 | tf_op jit(solution)/shard_map/ppermute | solution.py:507
  35.5 1.3 %collective-permute-start.11 = (bf16[128,2048]{1,0:T(8,128)(2,1)S(1)}, bf16[128,2048]{1,0:T(8,128)(2,1)S(1)}, u32[]{:S(2)}, u32[]{:S(2)}) collective-permute-start(bf16[128,2048]{1,0:T(8,128)(2,1)S(1)} %collective-permute-done.6.refs_4_), channel_id=1, source_target_pairs={{0,2},{1,3},{4,0},{5,1},{8,4},{9,5},{12,8},{13,9},{14,12},{15,13},... | collective-permute-start | bytes 1572872 | tf_op jit(solution)/shard_map/ppermute | solution.py:510
  36.8 1.1 %collective-permute-done.7.refs_3_ = bf16[128,2048]{1,0:T(8,128)(2,1)S(1)} collective-permute-done((bf16[128,2048]{1,0:T(8,128)(2,1)S(1)}, bf16[128,2048]{1,0:T(8,128)(2,1)S(1)}, u32[]{:S(2)}, u32[]{:S(2)}) %collective-permute-start.7) | collective-permute-done | bytes 524320 | tf_op jit(solution)/shard_map/ppermute | solution.py:12
  37.9 0.7 %collective-permute-done.8.refs_5_ = bf16[128,2048]{1,0:T(8,128)(2,1)S(1)} collective-permute-done((bf16[128,2048]{1,0:T(8,128)(2,1)S(1)}, bf16[128,2048]{1,0:T(8,128)(2,1)S(1)}, u32[]{:S(2)}, u32[]{:S(2)}) %collective-permute-start.8) | collective-permute-done | bytes 524320 | tf_op jit(solution)/shard_map/ppermute | solution.py:12
  38.7 8.1 %stage_second.1 = (bf16[768,512]{1,0:T(8,128)(2,1)S(1)}, bf16[512,768]{1,0:T(8,128)(2,1)S(1)}, bf16[512,768]{1,0:T(8,128)(2,1)S(1)}, bf16[512,768]{1,0:T(8,128)(...) custom-call(bf16[16,2,128]{2,1,0:T(2,128)(2,1)S(1)} %all-to-all-done.refs_0_, ...), custom_call_target="tpu_custom_call" | custom-call | flops 3221225472 | bytes 65536 | tf_op jit(solution)/shard_map/stage_second/pallas_call | solution.py:368
  46.8 2.4 %collective-permute-done.10.refs_2_.even_ref = bf16[128,2048]{1,0:T(8,128)(2,1)S(1)} collective-permute-done((bf16[128,2048]{1,0:T(8,128)(2,1)S(1)}, bf16[128,2048]{1,0:T(8,128)(2,1)S(1)}, u32[]{:S(2)}, u32[]{:S(2)}) %collective-permute-start.10) | collective-permute-done | bytes 524320 | tf_op jit(solution)/shard_map/ppermute | solution.py:507
  50.2 1.8 %collective-permute-start.15 = (bf16[128,2048]{1,0:T(8,128)(2,1)S(1)}, bf16[128,2048]{1,0:T(8,128)(2,1)S(1)}, u32[]{:S(2)}, u32[]{:S(2)}) collective-permute-start(bf16[128,2048]{1,0:T(8,128)(2,1)S(1)} %pick_by_core.1), channel_id=1, source_target_pairs={{0,4},{1,3},{4,8},{5,1},{8,12},{9,5},{12,14},{13,9},{14,10},{15,13... | collective-permute-start | bytes 1572872 | tf_op jit(solution)/shard_map/ppermute | solution.py:556
  51.9 0.7 %collective-permute-done.12.refs_3_ = bf16[128,2048]{1,0:T(8,128)(2,1)S(1)} collective-permute-done((bf16[128,2048]{1,0:T(8,128)(2,1)S(1)}, bf16[128,2048]{1,0:T(8,128)(2,1)S(1)}, u32[]{:S(2)}, u32[]{:S(2)}) %collective-permute-start.12) | collective-permute-done | bytes 524320 | tf_op jit(solution)/shard_map/ppermute | solution.py:12
  52.6 0.7 %collective-permute-done.13.refs_5_ = bf16[128,2048]{1,0:T(8,128)(2,1)S(1)} collective-permute-done((bf16[128,2048]{1,0:T(8,128)(2,1)S(1)}, bf16[128,2048]{1,0:T(8,128)(2,1)S(1)}, u32[]{:S(2)}, u32[]{:S(2)}) %collective-permute-start.13) | collective-permute-done | bytes 524320 | tf_op jit(solution)/shard_map/ppermute | solution.py:12
  53.4 6.4 %stage_third.1 = (bf16[768,512]{1,0:T(8,128)(2,1)S(1)}, bf16[512,768]{1,0:T(8,128)(2,1)}, bf16[512,768]{1,0:T(8,128)(2,1)}, bf16[512,768]{1,0:T(8,128)(2,1)S(1)}...) custom-call(bf16[16,2,128]{2,1,0:T(2,128)(2,1)S(1)} %all-to-all-done, ...), custom_call_target="tpu_custom_call", output_to_operand_aliasing={{4}: (12, {}), {5}: (13, {}), {6}: (14, {})} | custom-call | flops 3221225472 | bytes 65536 | tf_op jit(solution)/shard_map/stage_third/pallas_call | solution.py:368
  60.4 1.7 %stage_mine.1 = (bf16[768,256]{1,0:T(8,128)(2,1)S(1)}, bf16[256,768]{1,0:T(8,128)(2,1)S(1)}, bf16[256,768]{1,0:T(8,128)(2,1)S(1)}, bf16[256,768]{1,0:T(8,128)(2,1)S(1)}) custom-call(bf16[16,2,128]{2,1,0:T(2,128)(2,1)S(1)} %all-to-all-done.refs_0_, s32[16]{0:T(128)S(1)} %copy-done.2, bf16[128,2048]{1,0:T(8,128)(2,1)S(1)} %collective-permute-done.15.refs_2_, ...), custom_call_target="tpu_custom_call" | custom-call | flops 805306368 | bytes 65536 | tf_op jit(solution)/shard_map/stage_mine/pallas_call | solution.py:368
  62.1 1.7 %stage_theirs.1 = (bf16[768,256]{1,0:T(8,128)(2,1)S(1)}, bf16[256,768]{1,0:T(8,128)(2,1)S(1)}, bf16[256,768]{1,0:T(8,128)(2,1)S(1)}, bf16[256,768]{1,0:T(8,128)(2,1)S(1)}) custom-call(bf16[16,2,128]{2,1,0:T(2,128)(2,1)S(1)} %all-to-all-done.refs_0_, s32[16]{0:T(128)S(1)} %copy-done.2, ...), custom_call_target="tpu_custom_call", output_to_operand_aliasing={{0}: (5, {}), {1}: (6, {}), {2}: (7, {}), {3}: (8, {})} | custom-call | flops 805306368 | bytes 65536 | tf_op jit(solution)/shard_map/stage_theirs/pallas_call | solution.py:368
  63.9 3.1 %own_sums.1 = (f32[1,768,768]{2,1,0:T(8,128)}, f32[1,768,768]{2,1,0:T(8,128)}, f32[768,768]{1,0:T(8,128)S(1)}) custom-call(s32[16]{0:T(128)S(1)} %copy-done.2, bf16[768,512]{1,0:T(8,128)(2,1)S(1)} %get-tuple-element.93.refs_0_, bf16[512,768]{1,0:T(8,128)(2,1)S(1)} %collective-permute-done.16.refs_1_, ...), custom_call_target="tpu_custom_call", output_to_operand_aliasing={{2}: (3, {})} | custom-call | flops 1048576 | bytes 65536 | tf_op jit(solution)/shard_map/own_sums/pallas_call | solution.py:475
  67.0 2.3 %merge_sums.1 = f32[1,768,768]{2,1,0:T(8,128)} custom-call(s32[16]{0:T(128)S(1)} %copy-done.2, bf16[768,256]{1,0:T(8,128)(2,1)S(1)} %get-tuple-element.106.refs_3_.refs_0_, bf16[256,768]{1,0:T(8,128)(2,1)S(1)} %collective-permute-done.18.refs_1_, f32[768,768]{1,0:T(8,128)S(1)} %get-tuple-element.114.refs_2_), custom_call_target="tpu_custom_call" | custom-call | flops 1048576 | bytes 65536 | tf_op jit(solution)/shard_map/merge_sums/pallas_call | solution.py:475
  (35 shorter events, 4.3 us)
Async XLA Ops:
  0.6 18.8 %collective-permute-start = (bf16[128,2048]{1,0:T(8,128)(2,1)}, bf16[128,2048]{1,0:T(8,128)(2,1)}, u32[]{:S(2)}, u32[]{:S(2)}) collective-permute-start(bf16[128,2048]{1,0:T(8,128)(2,1)} %refs_2_.1), channel_id=1, source_target_pairs={{0,4},{1,5},{4,8},{5,9},{8,12},{9,13},{12,14},{13,15},{14,10},{15,... | collective-permute-start | bytes 1572872 | tf_op jit(solution)/shard_map/ppermute | solution.py:507
  3.7 15.7 %collective-permute-start.1 = (bf16[128,2048]{1,0:T(8,128)(2,1)}, bf16[128,2048]{1,0:T(8,128)(2,1)}, u32[]{:S(2)}, u32[]{:S(2)}) collective-permute-start(bf16[128,2048]{1,0:T(8,128)(2,1)} %refs_2_.1), channel_id=1, source_target_pairs={{0,2},{1,3},{4,0},{5,1},{8,4},{9,5},{12,8},{13,9},{14,12},{15,13},... | collective-permute-start | bytes 1572872 | tf_op jit(solution)/shard_map/ppermute | solution.py:510
  4.4 18.0 %copy-start = (bf16[1,2048,768]{2,1,0:T(8,128)(2,1)S(1)}, bf16[1,2048,768]{2,1,0:T(8,128)(2,1)}, u32[]{:S(2)}) copy-start(bf16[1,2048,768]{2,1,0:T(8,128)(2,1)} %refs_3_.3) | copy-start | bytes 9437188
  4.4 18.0 %copy-start.2 = (s32[16]{0:T(128)S(1)}, s32[16]{0:T(128)}, u32[]{:S(2)}) copy-start(s32[16]{0:T(128)} %flag_ref.3) | copy-start | bytes 196
  6.7 12.7 %all-to-all-start = ((bf16[16,2,128]{2,1,0:T(2,128)(2,1)}), bf16[16,2,128]{2,1,0:T(2,128)(2,1)S(1)}, u32[]{:S(2)}, u32[]{:S(2)}) async-start(bf16[16,2,128]{2,1,0:T(2,128)(2,1)} %route_table.1), calls=%async_computation | async-start | bytes 16384 | tf_op jit(solution)/shard_map/all_to_all | solution.py:543
  13.1 8.9 %collective-permute-start.2 = (bf16[128,2048]{1,0:T(8,128)(2,1)}, bf16[128,2048]{1,0:T(8,128)(2,1)}, u32[]{:S(2)}, u32[]{:S(2)}) collective-permute-start(bf16[128,2048]{1,0:T(8,128)(2,1)} %refs_2_.1), channel_id=1, source_target_pairs={{0,1},{1,0},{2,3},{3,2},{4,5},{5,4},{6,7},{7,6},{8,9},{9,8},{10,11... | collective-permute-start | bytes 1572872 | tf_op jit(solution)/shard_map/ppermute | solution.py:12
  19.4 2.5 %collective-permute-start.3 = (bf16[128,2048]{1,0:T(8,128)(2,1)}, bf16[128,2048]{1,0:T(8,128)(2,1)S(1)}, u32[]{:S(2)}, u32[]{:S(2)}) collective-permute-start(bf16[128,2048]{1,0:T(8,128)(2,1)} %collective-permute-done.refs_4_), channel_id=1, source_target_pairs={{0,1},{1,0},{2,3},{3,2},{4,5},{5,4},{6,7},{7,6},{8,9},{9,8},{10,11... | collective-permute-start | bytes 1572872 | tf_op jit(solution)/shard_map/ppermute | solution.py:12
  19.5 2.9 %collective-permute-start.4 = (bf16[128,2048]{1,0:T(8,128)(2,1)}, bf16[128,2048]{1,0:T(8,128)(2,1)S(1)}, u32[]{:S(2)}, u32[]{:S(2)}) collective-permute-start(bf16[128,2048]{1,0:T(8,128)(2,1)} %collective-permute-done.1.refs_6_), channel_id=1, source_target_pairs={{0,1},{1,0},{2,3},{3,2},{4,5},{5,4},{6,7},{7,6},{8,9},{9,8},{10,11... | collective-permute-start | bytes 1572872 | tf_op jit(solution)/shard_map/ppermute | solution.py:12
  20.0 14.1 %collective-permute-start.5 = (bf16[128,2048]{1,0:T(8,128)(2,1)}, bf16[128,2048]{1,0:T(8,128)(2,1)S(1)}, u32[]{:S(2)}, u32[]{:S(2)}) collective-permute-start(bf16[128,2048]{1,0:T(8,128)(2,1)} %collective-permute-done.refs_4_), channel_id=1, source_target_pairs={{0,4},{1,5},{4,8},{5,9},{8,12},{9,13},{12,14},{13,15},{14,10},{15,... | collective-permute-start | bytes 1572872 | tf_op jit(solution)/shard_map/ppermute | solution.py:507
  20.5 13.8 %collective-permute-start.6 = (bf16[128,2048]{1,0:T(8,128)(2,1)}, bf16[128,2048]{1,0:T(8,128)(2,1)S(1)}, u32[]{:S(2)}, u32[]{:S(2)}) collective-permute-start(bf16[128,2048]{1,0:T(8,128)(2,1)} %collective-permute-done.1.refs_6_), channel_id=1, source_target_pairs={{0,2},{1,3},{4,0},{5,1},{8,4},{9,5},{12,8},{13,9},{14,12},{15,13},... | collective-permute-start | bytes 1572872 | tf_op jit(solution)/shard_map/ppermute | solution.py:510
  22.3 1.9 %copy-start.1 = (bf16[1,2048,768]{2,1,0:T(8,128)(2,1)S(1)}, bf16[1,2048,768]{2,1,0:T(8,128)(2,1)}, u32[]{:S(2)}) copy-start(bf16[1,2048,768]{2,1,0:T(8,128)(2,1)} %refs_4_.3) | copy-start | bytes 9437188
  24.2 1.0 %copy-start.3 = (bf16[128,2048]{1,0:T(8,128)(2,1)S(1)}, bf16[128,2048]{1,0:T(8,128)(2,1)}, u32[]{:S(2)}) copy-start(bf16[128,2048]{1,0:T(8,128)(2,1)} %refs_2_.1) | copy-start | bytes 1572868
  34.3 4.4 %collective-permute-start.9 = (bf16[768,768]{1,0:T(8,128)(2,1)S(1)}, bf16[768,768]{1,0:T(8,128)(2,1)S(1)}, u32[]{:S(2)}, u32[]{:S(2)}) collective-permute-start(bf16[768,768]{1,0:T(8,128)(2,1)S(1)} %get-tuple-element.71), channel_id=1, source_target_pairs={{0,1},{1,0},{2,3},{3,2},{4,5},{5,4},{6,7},{7,6},{8,9},{9,8},{10,11... | collective-permute-start | bytes 3538952 | tf_op jit(solution)/shard_map/ppermute | solution.py:12
  34.3 3.6 %collective-permute-start.7 = (bf16[128,2048]{1,0:T(8,128)(2,1)S(1)}, bf16[128,2048]{1,0:T(8,128)(2,1)S(1)}, u32[]{:S(2)}, u32[]{:S(2)}) collective-permute-start(bf16[128,2048]{1,0:T(8,128)(2,1)S(1)} %collective-permute-done.5.refs_2_), channel_id=1, source_target_pairs={{0,1},{1,0},{2,3},{3,2},{4,5},{5,4},{6,7},{7,6},{8,9},{9,8},{10,11... | collective-permute-start | bytes 1572872 | tf_op jit(solution)/shard_map/ppermute | solution.py:12
  34.8 3.8 %collective-permute-start.8 = (bf16[128,2048]{1,0:T(8,128)(2,1)S(1)}, bf16[128,2048]{1,0:T(8,128)(2,1)S(1)}, u32[]{:S(2)}, u32[]{:S(2)}) collective-permute-start(bf16[128,2048]{1,0:T(8,128)(2,1)S(1)} %collective-permute-done.6.refs_4_), channel_id=1, source_target_pairs={{0,1},{1,0},{2,3},{3,2},{4,5},{5,4},{6,7},{7,6},{8,9},{9,8},{10,11... | collective-permute-start | bytes 1572872 | tf_op jit(solution)/shard_map/ppermute | solution.py:12
  34.8 14.3 %collective-permute-start.10 = (bf16[128,2048]{1,0:T(8,128)(2,1)S(1)}, bf16[128,2048]{1,0:T(8,128)(2,1)S(1)}, u32[]{:S(2)}, u32[]{:S(2)}) collective-permute-start(bf16[128,2048]{1,0:T(8,128)(2,1)S(1)} %collective-permute-done.5.refs_2_), channel_id=1, source_target_pairs={{0,4},{1,5},{4,8},{5,9},{8,12},{9,13},{12,14},{13,15},{14,10},{15,... | collective-permute-start | bytes 1572872 | tf_op jit(solution)/shard_map/ppermute | solution.py:507
  35.5 14.1 %collective-permute-start.11 = (bf16[128,2048]{1,0:T(8,128)(2,1)S(1)}, bf16[128,2048]{1,0:T(8,128)(2,1)S(1)}, u32[]{:S(2)}, u32[]{:S(2)}) collective-permute-start(bf16[128,2048]{1,0:T(8,128)(2,1)S(1)} %collective-permute-done.6.refs_4_), channel_id=1, source_target_pairs={{0,2},{1,3},{4,0},{5,1},{8,4},{9,5},{12,8},{13,9},{14,12},{15,13},... | collective-permute-start | bytes 1572872 | tf_op jit(solution)/shard_map/ppermute | solution.py:510
  49.6 3.8 %collective-permute-start.14 = (bf16[512,768]{1,0:T(8,128)(2,1)S(1)}, bf16[512,768]{1,0:T(8,128)(2,1)S(1)}, u32[]{:S(2)}, u32[]{:S(2)}) collective-permute-start(bf16[512,768]{1,0:T(8,128)(2,1)S(1)} %get-tuple-element.84), channel_id=1, source_target_pairs={{0,1},{1,0},{2,3},{3,2},{4,5},{5,4},{6,7},{7,6},{8,9},{9,8},{10,11... | collective-permute-start | bytes 2359304 | tf_op jit(solution)/shard_map/ppermute | solution.py:12
  49.6 3.0 %collective-permute-start.12 = (bf16[128,2048]{1,0:T(8,128)(2,1)S(1)}, bf16[128,2048]{1,0:T(8,128)(2,1)S(1)}, u32[]{:S(2)}, u32[]{:S(2)}) collective-permute-start(bf16[128,2048]{1,0:T(8,128)(2,1)S(1)} %collective-permute-done.10.refs_2_.even_ref), channel_id=1, source_target_pairs={{0,1},{1,0},{2,3},{3,2},{4,5},{5,4},{6,7},{7,6},{8,9},{9,8},{10,11... | collective-permute-start | bytes 1572872 | tf_op jit(solution)/shard_map/ppermute | solution.py:12
  50.1 3.3 %collective-permute-start.13 = (bf16[128,2048]{1,0:T(8,128)(2,1)S(1)}, bf16[128,2048]{1,0:T(8,128)(2,1)S(1)}, u32[]{:S(2)}, u32[]{:S(2)}) collective-permute-start(bf16[128,2048]{1,0:T(8,128)(2,1)S(1)} %collective-permute-done.11.refs_4_.odd_ref), channel_id=1, source_target_pairs={{0,1},{1,0},{2,3},{3,2},{4,5},{5,4},{6,7},{7,6},{8,9},{9,8},{10,11... | collective-permute-start | bytes 1572872 | tf_op jit(solution)/shard_map/ppermute | solution.py:12
  50.2 9.6 %collective-permute-start.15 = (bf16[128,2048]{1,0:T(8,128)(2,1)S(1)}, bf16[128,2048]{1,0:T(8,128)(2,1)S(1)}, u32[]{:S(2)}, u32[]{:S(2)}) collective-permute-start(bf16[128,2048]{1,0:T(8,128)(2,1)S(1)} %pick_by_core.1), channel_id=1, source_target_pairs={{0,4},{1,3},{4,8},{5,1},{8,12},{9,5},{12,14},{13,9},{14,10},{15,13... | collective-permute-start | bytes 1572872 | tf_op jit(solution)/shard_map/ppermute | solution.py:556
  59.8 2.3 %collective-permute-start.17 = (bf16[128,2048]{1,0:T(8,128)(2,1)S(1)}, bf16[128,2048]{1,0:T(8,128)(2,1)S(1)}, u32[]{:S(2)}, u32[]{:S(2)}) collective-permute-start(bf16[128,2048]{1,0:T(8,128)(2,1)S(1)} %collective-permute-done.15.refs_2_), channel_id=1, source_target_pairs={{0,1},{1,0},{2,3},{3,2},{4,5},{5,4},{6,7},{7,6},{8,9},{9,8},{10,11... | collective-permute-start | bytes 1572872 | tf_op jit(solution)/shard_map/ppermute | solution.py:12
  60.0 3.9 %collective-permute-start.16 = (bf16[512,768]{1,0:T(8,128)(2,1)S(1)}, bf16[512,768]{1,0:T(8,128)(2,1)S(1)}, u32[]{:S(2)}, u32[]{:S(2)}) collective-permute-start(bf16[512,768]{1,0:T(8,128)(2,1)S(1)} %get-tuple-element.94), channel_id=1, source_target_pairs={{0,1},{1,0},{2,3},{3,2},{4,5},{5,4},{6,7},{7,6},{8,9},{9,8},{10,11... | collective-permute-start | bytes 2359304 | tf_op jit(solution)/shard_map/ppermute | solution.py:12
  63.7 3.3 %collective-permute-start.18 = (bf16[256,768]{1,0:T(8,128)(2,1)S(1)}, bf16[256,768]{1,0:T(8,128)(2,1)S(1)}, u32[]{:S(2)}, u32[]{:S(2)}) collective-permute-start(bf16[256,768]{1,0:T(8,128)(2,1)S(1)} %get-tuple-element.113), channel_id=1, source_target_pairs={{0,1},{1,0},{2,3},{3,2},{4,5},{5,4},{6,7},{7,6},{8,9},{9,8},{10,11... | collective-permute-start | bytes 1179656 | tf_op jit(solution)/shard_map/ppermute | solution.py:12
  (1 other events, 0.7 us)

commit v8 on v7

--- a/solution.py
+++ b/solution.py
@@ -142,12 +142,15 @@
 
 
 def route_table_kernel(
-    quota_ref, pick_in, entry_in, coef_in, out_ref, pick_ref, entry_ref, coef_ref, arrive
+    quota_in, flag_in, pick_in, entry_in, coef_in, out_ref, mark_ref, *scratch
 ):
+    quota_ref, flag_ref, pick_ref, entry_ref, coef_ref, arrive = scratch
     copies = [
         pltpu.make_async_copy(pick_in, pick_ref, arrive.at[0]),
         pltpu.make_async_copy(entry_in, entry_ref, arrive.at[1]),
         pltpu.make_async_copy(coef_in, coef_ref, arrive.at[2]),
+        pltpu.make_async_copy(quota_in, quota_ref, arrive.at[3]),
+        pltpu.make_async_copy(flag_in, flag_ref, arrive.at[4]),
     ]
     for copy in copies:
         copy.start()
@@ -177,31 +180,41 @@
     for expert in range(experts):
         bound = jnp.where(expert_row == expert, quota_ref[expert].astype(jnp.float32), bound)
     used = jnp.where(rank < bound, weight, 0.0).astype(jnp.bfloat16)
+    me = lax.axis_index("expert")
+    keep = flag_ref[me].astype(jnp.float32)
+    merge = keep * (1.0 - flag_ref[jnp.bitwise_xor(me, 1)].astype(jnp.float32))
+    mark_row = lax.broadcasted_iota(jnp.int32, mark_ref.shape, 0)
+    mark_ref[...] = jnp.where(mark_row == 0, keep, merge)
     for receiver in range(experts):
         out_ref[receiver, 0:1, :] = used[receiver : receiver + 1]
         out_ref[receiver, 1:2, :] = used[receiver ^ 1 : (receiver ^ 1) + 1]
 
 
-def route_table(picks, entries, coefficients, quotas):
+def route_table(picks, entries, coefficients, quotas, flags):
     experts = quotas.shape[0]
     tokens = picks.shape[0]
     vmem = pl.BlockSpec(memory_space=pltpu.VMEM)
     outside = pl.BlockSpec(memory_space=pl.ANY)
     return pl.pallas_call(
         route_table_kernel,
-        out_shape=jax.ShapeDtypeStruct((experts, 2, tokens), jnp.bfloat16),
-        in_specs=[pl.BlockSpec(memory_space=pltpu.SMEM), outside, outside, outside],
-        out_specs=vmem,
+        out_shape=(
+            jax.ShapeDtypeStruct((experts, 2, tokens), jnp.bfloat16),
+            pltpu.VMEM((8, 128), jnp.float32),
+        ),
+        in_specs=[outside] * 5,
+        out_specs=(vmem, vmem),
         scratch_shapes=[
+            pltpu.SMEM(quotas.shape, quotas.dtype),
+            pltpu.SMEM(flags.shape, flags.dtype),
             pltpu.VMEM(picks.shape[::-1], jnp.int32),
             pltpu.VMEM(entries.shape[::-1], jnp.int32),
             pltpu.VMEM(coefficients.shape, coefficients.dtype),
-            pltpu.SemaphoreType.DMA((3,)),
+            pltpu.SemaphoreType.DMA((5,)),
         ],
         compiler_params=pltpu.CompilerParams(vmem_limit_bytes=4 << 20),
         cost_estimate=kernel_cost(1 << 34),
         name="route_table",
-    )(quotas, in_hbm(picks.T), in_hbm(entries.T), in_hbm(coefficients))
+    )(*map(in_hbm, (quotas, flags, picks.T, entries.T, coefficients)))
 
 
 def ring_neighbour(me, experts, steps, turn):
@@ -230,7 +243,7 @@
     def take(count):
         return [next(taken) for _ in range(count)]
 
-    table_ref, flag_ref = take(2)
+    table_ref, mark_ref = take(2)
     blocks = take(len(places))
     weights = take(2)
     part = take(4) if before else None
@@ -242,7 +255,7 @@
     scratch = take(2)
     for which in before:
         add_product(sums[which], bases[which], [(part[0], part[1 + which])])
-    hidden_body(places, rows_at, table_ref, flag_ref, blocks, *weights, *hidden_outs, *scratch)
+    hidden_body(places, rows_at, table_ref, mark_ref, blocks, *weights, *hidden_outs, *scratch)
     for which in after:
         base = sums[which] if which in before else bases[which]
         add_product(sums[which], base, [(hidden_outs[0], hidden_outs[1 + which])])
@@ -264,7 +277,7 @@
     places,
     rows_at,
     table_ref,
-    flag_ref,
+    mark_ref,
     block_refs,
     gate_ref,
     up_ref,
@@ -284,8 +297,7 @@
         spans.append(slice(first, first + block_refs[block].shape[0]))
         rows_ref[spans[block], :] = block_refs[block][...]
     me = lax.axis_index("expert")
-    keep = flag_ref[me].astype(jnp.float32)
-    merge = keep * (1.0 - flag_ref[jnp.bitwise_xor(me, 1)].astype(jnp.float32))
+    keep, merge = mark_ref[0:1, 0:1], mark_ref[1:2, 0:1]
     row = lax.broadcasted_iota(jnp.int32, (tokens, tokens), 0)
     col = lax.broadcasted_iota(jnp.int32, (tokens, tokens), 1)
     for block, (steps, turn, offset) in enumerate(places):
@@ -339,13 +351,13 @@
 
 
 def run_stage(
-    places, table, flags, blocks, w_gate, w_up, part, bases, before, after, name, room=1, filled=None
+    places, table, marks, blocks, w_gate, w_up, part, bases, before, after, name, room=1, filled=None
 ):
     width = blocks[0].shape[1]
     rows = sum(block.shape[0] for block in blocks)
     hidden_width = w_gate.shape[2]
     vmem = pl.BlockSpec(memory_space=pltpu.VMEM)
-    operands = [in_vmem(table), flags, *map(in_vmem, blocks), in_vmem(w_gate), in_vmem(w_up)]
+    operands = [in_vmem(table), in_vmem(marks), *map(in_vmem, blocks), in_vmem(w_gate), in_vmem(w_up)]
     out_shape = [
         pltpu.VMEM((hidden_width, room * rows), jnp.bfloat16),
         pltpu.VMEM((room * rows, hidden_width), jnp.bfloat16),
@@ -364,7 +376,6 @@
         aliases |= {len(operands) + index: index for index in range(4)}
         operands += map(in_vmem, filled)
     in_specs = [vmem] * len(operands)
-    in_specs[1] = pl.BlockSpec(memory_space=pltpu.SMEM)
     outs = pl.pallas_call(
         functools.partial(
             stage_kernel, places, before, after, bases is not None, 0 if filled is None else rows
@@ -408,7 +419,7 @@
     )(in_vmem(even), in_vmem(odd))
 
 
-def final_kernel(kinds, part_total, late_total, divisor, flag_ref, *refs):
+def final_kernel(kinds, part_total, late_total, divisor, mark_ref, *refs):
     set_total = len(kinds)
     if late_total:
         late, refs = refs[: 2 * late_total + 1], refs[2 * late_total + 1 :]
@@ -420,17 +431,13 @@
     bases, outs = rest[:set_total], rest[set_total : 2 * set_total]
     done_ref, leave = rest[2 * set_total :]
     hidden_width = lhs[0].shape[0]
-    me = lax.axis_index("expert")
-    keep = flag_ref[me].astype(jnp.float32)
-    keep_partner = flag_ref[jnp.bitwise_xor(me, 1)].astype(jnp.float32)
     tile = 256
     copies = []
     for index in range(set_total):
         factor = 1.0 / divisor
         if kinds[index] != "gram":
-            factor = factor * keep
-        if kinds[index] == "merge":
-            factor = factor * (1.0 - keep_partner)
+            mark = 0 if kinds[index] == "self" else 1
+            factor = factor * mark_ref[mark : mark + 1, 0:1]
         for start in range(0, hidden_width, tile):
             span = slice(start, start + tile)
             total = bases[index][span, :]
@@ -454,7 +461,7 @@
         copy.wait()
 
 
-def final_sums(flags, lhs, rhs, bases, kinds, divisor, name, late=None):
+def final_sums(marks, lhs, rhs, bases, kinds, divisor, name, late=None):
     hidden_width = lhs[0].shape[0]
     total = len(rhs)
     vmem = pl.BlockSpec(memory_space=pltpu.VMEM)
@@ -475,7 +482,7 @@
     return pl.pallas_call(
         functools.partial(final_kernel, kinds, len(lhs), late_total, float(divisor)),
         out_shape=out_shape,
-        in_specs=[pl.BlockSpec(memory_space=pltpu.SMEM)] + [vmem] * len(operands),
+        in_specs=[vmem] * (1 + len(operands)),
         out_specs=out_specs,
         input_output_aliases=aliases,
         scratch_shapes=[
@@ -485,7 +492,7 @@
         compiler_params=pltpu.CompilerParams(vmem_limit_bytes=8 << 20),
         cost_estimate=kernel_cost(1 << 20),
         name=name,
-    )(flags, *map(in_vmem, operands))
+    )(in_vmem(marks), *map(in_vmem, operands))
 
 
 def gathered_shards(
@@ -523,7 +530,7 @@
         return run_stage(
             places,
             table,
-            retained_specialist_flags,
+            marks,
             blocks,
             gating_projection,
             raising_projection,
@@ -537,8 +544,12 @@
 
     tied = lax.optimization_barrier
     left_1, right_1 = onward(layer_inputs), backward(layer_inputs)
-    table = route_table(
-        specialist_picks, coefficient_lookup_entry, dispatch_coefficients, specialist_quotas
+    table, marks = route_table(
+        specialist_picks,
+        coefficient_lookup_entry,
+        dispatch_coefficients,
+        specialist_quotas,
+        retained_specialist_flags,
     )
     table = lax.all_to_all(table, "expert", split_axis=0, concat_axis=0, tiled=True)
 
@@ -564,7 +575,7 @@
     theirs = [(near_far, 4, 1, 0)]
     last, _ = stage(theirs, None, None, (), (), "stage_theirs", room=2, filled=mine)
     gram, self_cross, merge_base = final_sums(
-        retained_specialist_flags,
+        marks,
         [last[0]],
         [[last[1]], [last[2]]],
         bases[:2],
@@ -574,7 +585,7 @@
         ([third[0]], [other(third[3])], bases[2]),
     )
     (merge_cross,) = final_sums(
-        retained_specialist_flags,
+        marks,
         [last[0]],
         [[other(last[3])]],
         [merge_base],

time: 69.8 us -> 67.7 us (0.970)
  Pallas kernels: 32.4 us -> 29.1 us
  waiting for transfers between devices: 14.6 us -> 16.6 us
    pallas_call x5, Pallas kernels: 24.7 us -> 23 us  [run_stage(): pl.pallas_call(functools.partial(stage_kernel, places, before, after, bas...]
    all_to_all x1, waiting for transfers between devices: 5.92 us -> 7.13 us  [gathered_shards(): lax.all_to_all(table, 'expert', split_axis=0, concat_axis=0, tiled=True)]
    pallas_call x2, Pallas kernels: 5.35 us -> 4.27 us  [final_sums(): pl.pallas_call(functools.partial(final_kernel, kinds, len(lhs), late_tota...]
    unnamed x10 -> x6, local copies, waits for them, and re-layouts: 3.59 us -> 2.93 us
  transfers between devices with their start and end apart: 20 -> 20, of which waited for: 10 -> 11; matrix products, arithmetic and copies ran while one was open for 0% -> 0% of each run, Pallas kernels for 43% -> 41%
where the time goes in v8:
time: 67.7 us; the launch traced here: 67.5 us
  Pallas kernels  29.1 us (43%)
  starting transfers between devices  17.9 us (26%)
  waiting for transfers between devices  16.6 us (25%)
  local copies, waits for them, and re-layouts  2.93 us (4%)
  between operations  0.91 us (1%)
    pallas_call x5, Pallas kernels, run_stage(): pl.pallas_call(functools.partial(stage_kernel, places, before, after, bas...  23 us
    all_to_all x1, waiting for transfers between devices, gathered_shards(): lax.all_to_all(table, 'expert', split_axis=0, concat_axis=0, tiled=True)  7.13 us
    all_to_all x1, starting transfers between devices, gathered_shards(): lax.all_to_all(table, 'expert', split_axis=0, concat_axis=0, tiled=True)  6.37 us
    ppermute x3, waiting for transfers between devices, onward(): return lax.ppermute(x, 'expert', ring_pairs(experts, (1, 1)))  4.87 us
    ppermute x3, starting transfers between devices, onward(): return lax.ppermute(x, 'expert', ring_pairs(experts, (1, 1)))  4.38 us
    pallas_call x2, Pallas kernels, final_sums(): pl.pallas_call(functools.partial(final_kernel, kinds, len(lhs), late_tota...  4.27 us
    ppermute x12, waiting for transfers between devices, swapped(): lax.ppermute(x, axis, [(i, i ^ 1 << stride) for i in range(lax.axis_size(...  3.89 us
    unnamed x6, local copies, waits for them, and re-layouts  2.93 us
  transfers between devices with their start and end apart: 20, of which 11 were waited for; matrix products, arithmetic and copies ran while one was open for 0% of the time, Pallas kernels for 41%

profile of v8, /device:TPU:0, one launch (start us, length us, event | category | flops | bytes accessed | tf_op | source)
XLA Modules:
  0.0 67.5 jit_solution(10777770033187823955)
XLA Ops:
  0.6 3.1 %collective-permute-start = (bf16[128,2048]{1,0:T(8,128)(2,1)}, bf16[128,2048]{1,0:T(8,128)(2,1)}, u32[]{:S(2)}, u32[]{:S(2)}) collective-permute-start(bf16[128,2048]{1,0:T(8,128)(2,1)} %refs_2_.1), channel_id=1, source_target_pairs={{0,4},{1,5},{4,8},{5,9},{8,12},{9,13},{12,14},{13,15},{14,10},{15,... | collective-permute-start | bytes 1572872 | tf_op jit(solution)/shard_map/ppermute | solution.py:514
  3.7 1.7 %route_table.1 = (bf16[16,2,128]{2,1,0:T(2,128)(2,1)}, f32[8,128]{1,0:T(8,128)S(1)}) custom-call(s32[16]{0:T(128)} %quota_in.1, s32[16]{0:T(128)} %flag_in.1, s32[8,128]{1,0:T(8,128)} %bitcast.2, s32[8,128]{1,0:T(8,128)} %bitcast.3, bf16[256]{0:T(256)(128)(2,1)} %coef_in.1), custom_call_target="tpu_custom_call" | custom-call | flops 17179869184 | bytes 65536 | tf_op jit(solution)/shard_map/route_table/pallas_call | solution.py:198
  5.5 6.4 %all-to-all-start = ((bf16[16,2,128]{2,1,0:T(2,128)(2,1)}), bf16[16,2,128]{2,1,0:T(2,128)(2,1)S(1)}, u32[]{:S(2)}, u32[]{:S(2)}) async-start(bf16[16,2,128]{2,1,0:T(2,128)(2,1)} %get-tuple-element.62), calls=%async_computation | async-start | bytes 16384 | tf_op jit(solution)/shard_map/all_to_all | solution.py:554
  12.2 7.1 %all-to-all-done.refs_0_ = bf16[16,2,128]{2,1,0:T(2,128)(2,1)S(1)} async-done(((bf16[16,2,128]{2,1,0:T(2,128)(2,1)}), bf16[16,2,128]{2,1,0:T(2,128)(2,1)S(1)}, u32[]{:S(2)}, u32[]{:S(2)}) %all-to-all-start) | async-done | bytes 8224 | tf_op jit(solution)/shard_map/all_to_all | solution.py:554
  19.9 0.6 collective-permute-start.5
  20.5 1.5 %collective-permute-start.6 = (bf16[128,2048]{1,0:T(8,128)(2,1)}, bf16[128,2048]{1,0:T(8,128)(2,1)S(1)}, u32[]{:S(2)}, u32[]{:S(2)}) collective-permute-start(bf16[128,2048]{1,0:T(8,128)(2,1)} %collective-permute-done.1.refs_6_), channel_id=1, source_target_pairs={{0,2},{1,3},{4,0},{5,1},{8,4},{9,5},{12,8},{13,9},{14,12},{15,13},... | collective-permute-start | bytes 1572872 | tf_op jit(solution)/shard_map/ppermute | solution.py:517
  22.3 1.9 %copy-done.1 = bf16[1,2048,768]{2,1,0:T(8,128)(2,1)S(1)} copy-done((bf16[1,2048,768]{2,1,0:T(8,128)(2,1)S(1)}, bf16[1,2048,768]{2,1,0:T(8,128)(2,1)}, u32[]{:S(2)}) %copy-start.1) | copy-done | bytes 3145752
  24.1 1.0 %copy-done.2 = bf16[128,2048]{1,0:T(8,128)(2,1)S(1)} copy-done((bf16[128,2048]{1,0:T(8,128)(2,1)S(1)}, bf16[128,2048]{1,0:T(8,128)(2,1)}, u32[]{:S(2)}) %copy-start.2) | copy-done | bytes 524312
  25.2 6.9 %stage_first.1 = (bf16[768,768]{1,0:T(8,128)(2,1)S(1)}, bf16[768,768]{1,0:T(8,128)(2,1)S(1)}, bf16[768,768]{1,0:T(8,128)(2,1)S(1)}, bf16[768,768]{1,0:T(8,128)(2,1)S(1)}) custom-call(bf16[16,2,128]{2,1,0:T(2,128)(2,1)S(1)} %all-to-all-done.refs_0_, f32[8,128]{1,0:T(8,128)S(1)} %get-tuple-element.61.refs_1_.mark_ref, bf16[128,2048]{1,0:T(8,128)(2,1)S(1)} %copy-done.2, ...), custom_call_target="tpu_custom_call" | custom-call | flops 4831838208 | bytes 65536 | tf_op jit(solution)/shard_map/stage_first/pallas_call | solution.py:379
  32.1 1.9 %collective-permute-done.5.refs_2_ = bf16[128,2048]{1,0:T(8,128)(2,1)S(1)} collective-permute-done((bf16[128,2048]{1,0:T(8,128)(2,1)}, bf16[128,2048]{1,0:T(8,128)(2,1)S(1)}, u32[]{:S(2)}, u32[]{:S(2)}) %collective-permute-start.5) | collective-permute-done | bytes 524320 | tf_op jit(solution)/shard_map/ppermute | solution.py:514
  34.8 0.7 %collective-permute-start.10 = (bf16[128,2048]{1,0:T(8,128)(2,1)S(1)}, bf16[128,2048]{1,0:T(8,128)(2,1)S(1)}, u32[]{:S(2)}, u32[]{:S(2)}) collective-permute-start(bf16[128,2048]{1,0:T(8,128)(2,1)S(1)} %collective-permute-done.5.refs_2_), channel_id=1, source_target_pairs={{0,4},{1,5},{4,8},{5,9},{8,12},{9,13},{12,14},{13,15},{14,10},{15,... | collective-permute-start | bytes 1572872 | tf_op jit(solution)/shard_map/ppermute | solution.py:514
  35.5 1.3 %collective-permute-start.11 = (bf16[128,2048]{1,0:T(8,128)(2,1)S(1)}, bf16[128,2048]{1,0:T(8,128)(2,1)S(1)}, u32[]{:S(2)}, u32[]{:S(2)}) collective-permute-start(bf16[128,2048]{1,0:T(8,128)(2,1)S(1)} %collective-permute-done.6.refs_4_), channel_id=1, source_target_pairs={{0,2},{1,3},{4,0},{5,1},{8,4},{9,5},{12,8},{13,9},{14,12},{15,13},... | collective-permute-start | bytes 1572872 | tf_op jit(solution)/shard_map/ppermute | solution.py:517
  36.8 1.1 %collective-permute-done.7.refs_3_ = bf16[128,2048]{1,0:T(8,128)(2,1)S(1)} collective-permute-done((bf16[128,2048]{1,0:T(8,128)(2,1)S(1)}, bf16[128,2048]{1,0:T(8,128)(2,1)S(1)}, u32[]{:S(2)}, u32[]{:S(2)}) %collective-permute-start.7) | collective-permute-done | bytes 524320 | tf_op jit(solution)/shard_map/ppermute | solution.py:12
  37.9 0.7 %collective-permute-done.8.refs_5_ = bf16[128,2048]{1,0:T(8,128)(2,1)S(1)} collective-permute-done((bf16[128,2048]{1,0:T(8,128)(2,1)S(1)}, bf16[128,2048]{1,0:T(8,128)(2,1)S(1)}, u32[]{:S(2)}, u32[]{:S(2)}) %collective-permute-start.8) | collective-permute-done | bytes 524320 | tf_op jit(solution)/shard_map/ppermute | solution.py:12
  38.6 7.5 %stage_second.1 = (bf16[768,512]{1,0:T(8,128)(2,1)S(1)}, bf16[512,768]{1,0:T(8,128)(2,1)S(1)}, bf16[512,768]{1,0:T(8,128)(2,1)S(1)}, bf16[512,768]{1,0:T(8,128)(...) custom-call(bf16[16,2,128]{2,1,0:T(2,128)(2,1)S(1)} %all-to-all-done.refs_0_, ...), custom_call_target="tpu_custom_call" | custom-call | flops 3221225472 | bytes 65536 | tf_op jit(solution)/shard_map/stage_second/pallas_call | solution.py:379
  46.2 3.0 %collective-permute-done.10.refs_2_.even_ref = bf16[128,2048]{1,0:T(8,128)(2,1)S(1)} collective-permute-done((bf16[128,2048]{1,0:T(8,128)(2,1)S(1)}, bf16[128,2048]{1,0:T(8,128)(2,1)S(1)}, u32[]{:S(2)}, u32[]{:S(2)}) %collective-permute-start.10) | collective-permute-done | bytes 524320 | tf_op jit(solution)/shard_map/ppermute | solution.py:514
  50.2 1.8 %collective-permute-start.15 = (bf16[128,2048]{1,0:T(8,128)(2,1)S(1)}, bf16[128,2048]{1,0:T(8,128)(2,1)S(1)}, u32[]{:S(2)}, u32[]{:S(2)}) collective-permute-start(bf16[128,2048]{1,0:T(8,128)(2,1)S(1)} %pick_by_core.1), channel_id=1, source_target_pairs={{0,4},{1,3},{4,8},{5,1},{8,12},{9,5},{12,14},{13,9},{14,10},{15,13... | collective-permute-start | bytes 1572872 | tf_op jit(solution)/shard_map/ppermute | solution.py:567
  51.9 0.7 %collective-permute-done.12.refs_3_ = bf16[128,2048]{1,0:T(8,128)(2,1)S(1)} collective-permute-done((bf16[128,2048]{1,0:T(8,128)(2,1)S(1)}, bf16[128,2048]{1,0:T(8,128)(2,1)S(1)}, u32[]{:S(2)}, u32[]{:S(2)}) %collective-permute-start.12) | collective-permute-done | bytes 524320 | tf_op jit(solution)/shard_map/ppermute | solution.py:12
  52.6 0.7 %collective-permute-done.13.refs_5_ = bf16[128,2048]{1,0:T(8,128)(2,1)S(1)} collective-permute-done((bf16[128,2048]{1,0:T(8,128)(2,1)S(1)}, bf16[128,2048]{1,0:T(8,128)(2,1)S(1)}, u32[]{:S(2)}, u32[]{:S(2)}) %collective-permute-start.13) | collective-permute-done | bytes 524320 | tf_op jit(solution)/shard_map/ppermute | solution.py:12
  53.4 6.3 %stage_third.1 = (bf16[768,512]{1,0:T(8,128)(2,1)S(1)}, bf16[512,768]{1,0:T(8,128)(2,1)}, bf16[512,768]{1,0:T(8,128)(2,1)}, bf16[512,768]{1,0:T(8,128)(2,1)S(1)}...) custom-call(bf16[16,2,128]{2,1,0:T(2,128)(2,1)S(1)} %all-to-all-done, ...), custom_call_target="tpu_custom_call", output_to_operand_aliasing={{4}: (12, {}), {5}: (13, {}), {6}: (14, {})} | custom-call | flops 3221225472 | bytes 65536 | tf_op jit(solution)/shard_map/stage_third/pallas_call | solution.py:379
  60.2 1.1 %stage_mine.1 = (bf16[768,256]{1,0:T(8,128)(2,1)S(1)}, bf16[256,768]{1,0:T(8,128)(2,1)S(1)}, bf16[256,768]{1,0:T(8,128)(2,1)S(1)}, bf16[256,768]{1,0:T(8,128)(2,1)S(1)}) custom-call(bf16[16,2,128]{2,1,0:T(2,128)(2,1)S(1)} %all-to-all-done.refs_0_, f32[8,128]{1,0:T(8,128)S(1)} %get-tuple-element.61.refs_1_.mark_ref, ...), custom_call_target="tpu_custom_call" | custom-call | flops 805306368 | bytes 65536 | tf_op jit(solution)/shard_map/stage_mine/pallas_call | solution.py:379
  61.6 1.1 %stage_theirs.1 = (bf16[768,256]{1,0:T(8,128)(2,1)S(1)}, bf16[256,768]{1,0:T(8,128)(2,1)S(1)}, bf16[256,768]{1,0:T(8,128)(2,1)S(1)}, bf16[256,768]{1,0:T(8,128)(2,1)S(1)}) custom-call(bf16[16,2,128]{2,1,0:T(2,128)(2,1)S(1)} %all-to-all-done.refs_0_, ...), custom_call_target="tpu_custom_call", output_to_operand_aliasing={{0}: (5, {}), {1}: (6, {}), {2}: (7, {}), {3}: (8, {})} | custom-call | flops 805306368 | bytes 65536 | tf_op jit(solution)/shard_map/stage_theirs/pallas_call | solution.py:379
  63.0 2.6 %own_sums.1 = (f32[1,768,768]{2,1,0:T(8,128)}, f32[1,768,768]{2,1,0:T(8,128)}, f32[768,768]{1,0:T(8,128)S(1)}) custom-call(f32[8,128]{1,0:T(8,128)S(1)} %get-tuple-element.61.refs_1_.mark_ref, bf16[768,512]{1,0:T(8,128)(2,1)S(1)} %get-tuple-element.97.refs_0_, bf16[512,768]{1,0:T(8,128)(2,1)S(1)} %collective-permute-done.16.refs_1_, ...), custom_call_target="tpu_custom_call", output_to_operand_aliasing={{2}: (3, {})} | custom-call | flops 1048576 | bytes 65536 | tf_op jit(solution)/shard_map/own_sums/pallas_call | solution.py:482
  65.6 1.7 %merge_sums.1 = f32[1,768,768]{2,1,0:T(8,128)} custom-call(f32[8,128]{1,0:T(8,128)S(1)} %get-tuple-element.61.refs_1_.mark_ref, bf16[768,256]{1,0:T(8,128)(2,1)S(1)} %get-tuple-element.110.refs_3_.refs_0_, bf16[256,768]{1,0:T(8,128)(2,1)S(1)} %collective-permute-done.18.refs_1_, f32[768,768]{1,0:T(8,128)S(1)} %get-tuple-element.118.refs_2_), custom_call_target="tpu_custom_call" | custom-call | flops 1048576 | bytes 65536 | tf_op jit(solution)/shard_map/merge_sums/pallas_call | solution.py:482
  (31 shorter events, 4.1 us)
Async XLA Ops:
  0.6 18.7 %collective-permute-start = (bf16[128,2048]{1,0:T(8,128)(2,1)}, bf16[128,2048]{1,0:T(8,128)(2,1)}, u32[]{:S(2)}, u32[]{:S(2)}) collective-permute-start(bf16[128,2048]{1,0:T(8,128)(2,1)} %refs_2_.1), channel_id=1, source_target_pairs={{0,4},{1,5},{4,8},{5,9},{8,12},{9,13},{12,14},{13,15},{14,10},{15,... | collective-permute-start | bytes 1572872 | tf_op jit(solution)/shard_map/ppermute | solution.py:514
  3.7 15.7 %collective-permute-start.1 = (bf16[128,2048]{1,0:T(8,128)(2,1)}, bf16[128,2048]{1,0:T(8,128)(2,1)}, u32[]{:S(2)}, u32[]{:S(2)}) collective-permute-start(bf16[128,2048]{1,0:T(8,128)(2,1)} %refs_2_.1), channel_id=1, source_target_pairs={{0,2},{1,3},{4,0},{5,1},{8,4},{9,5},{12,8},{13,9},{14,12},{15,13},... | collective-permute-start | bytes 1572872 | tf_op jit(solution)/shard_map/ppermute | solution.py:517
  3.7 18.5 %copy-start = (bf16[1,2048,768]{2,1,0:T(8,128)(2,1)S(1)}, bf16[1,2048,768]{2,1,0:T(8,128)(2,1)}, u32[]{:S(2)}) copy-start(bf16[1,2048,768]{2,1,0:T(8,128)(2,1)} %refs_3_.3) | copy-start | bytes 9437188
  5.5 13.9 %all-to-all-start = ((bf16[16,2,128]{2,1,0:T(2,128)(2,1)}), bf16[16,2,128]{2,1,0:T(2,128)(2,1)S(1)}, u32[]{:S(2)}, u32[]{:S(2)}) async-start(bf16[16,2,128]{2,1,0:T(2,128)(2,1)} %get-tuple-element.62), calls=%async_computation | async-start | bytes 16384 | tf_op jit(solution)/shard_map/all_to_all | solution.py:554
  11.8 10.1 %collective-permute-start.2 = (bf16[128,2048]{1,0:T(8,128)(2,1)}, bf16[128,2048]{1,0:T(8,128)(2,1)}, u32[]{:S(2)}, u32[]{:S(2)}) collective-permute-start(bf16[128,2048]{1,0:T(8,128)(2,1)} %refs_2_.1), channel_id=1, source_target_pairs={{0,1},{1,0},{2,3},{3,2},{4,5},{5,4},{6,7},{7,6},{8,9},{9,8},{10,11... | collective-permute-start | bytes 1572872 | tf_op jit(solution)/shard_map/ppermute | solution.py:12
  19.4 2.5 %collective-permute-start.3 = (bf16[128,2048]{1,0:T(8,128)(2,1)}, bf16[128,2048]{1,0:T(8,128)(2,1)S(1)}, u32[]{:S(2)}, u32[]{:S(2)}) collective-permute-start(bf16[128,2048]{1,0:T(8,128)(2,1)} %collective-permute-done.refs_4_), channel_id=1, source_target_pairs={{0,1},{1,0},{2,3},{3,2},{4,5},{5,4},{6,7},{7,6},{8,9},{9,8},{10,11... | collective-permute-start | bytes 1572872 | tf_op jit(solution)/shard_map/ppermute | solution.py:12
  19.4 2.9 %collective-permute-start.4 = (bf16[128,2048]{1,0:T(8,128)(2,1)}, bf16[128,2048]{1,0:T(8,128)(2,1)S(1)}, u32[]{:S(2)}, u32[]{:S(2)}) collective-permute-start(bf16[128,2048]{1,0:T(8,128)(2,1)} %collective-permute-done.1.refs_6_), channel_id=1, source_target_pairs={{0,1},{1,0},{2,3},{3,2},{4,5},{5,4},{6,7},{7,6},{8,9},{9,8},{10,11... | collective-permute-start | bytes 1572872 | tf_op jit(solution)/shard_map/ppermute | solution.py:12
  19.9 14.1 %collective-permute-start.5 = (bf16[128,2048]{1,0:T(8,128)(2,1)}, bf16[128,2048]{1,0:T(8,128)(2,1)S(1)}, u32[]{:S(2)}, u32[]{:S(2)}) collective-permute-start(bf16[128,2048]{1,0:T(8,128)(2,1)} %collective-permute-done.refs_4_), channel_id=1, source_target_pairs={{0,4},{1,5},{4,8},{5,9},{8,12},{9,13},{12,14},{13,15},{14,10},{15,... | collective-permute-start | bytes 1572872 | tf_op jit(solution)/shard_map/ppermute | solution.py:514
  20.5 13.8 %collective-permute-start.6 = (bf16[128,2048]{1,0:T(8,128)(2,1)}, bf16[128,2048]{1,0:T(8,128)(2,1)S(1)}, u32[]{:S(2)}, u32[]{:S(2)}) collective-permute-start(bf16[128,2048]{1,0:T(8,128)(2,1)} %collective-permute-done.1.refs_6_), channel_id=1, source_target_pairs={{0,2},{1,3},{4,0},{5,1},{8,4},{9,5},{12,8},{13,9},{14,12},{15,13},... | collective-permute-start | bytes 1572872 | tf_op jit(solution)/shard_map/ppermute | solution.py:517
  22.3 1.9 %copy-start.1 = (bf16[1,2048,768]{2,1,0:T(8,128)(2,1)S(1)}, bf16[1,2048,768]{2,1,0:T(8,128)(2,1)}, u32[]{:S(2)}) copy-start(bf16[1,2048,768]{2,1,0:T(8,128)(2,1)} %refs_4_.3) | copy-start | bytes 9437188
  24.1 1.0 %copy-start.2 = (bf16[128,2048]{1,0:T(8,128)(2,1)S(1)}, bf16[128,2048]{1,0:T(8,128)(2,1)}, u32[]{:S(2)}) copy-start(bf16[128,2048]{1,0:T(8,128)(2,1)} %refs_2_.1) | copy-start | bytes 1572868
  34.3 4.4 %collective-permute-start.9 = (bf16[768,768]{1,0:T(8,128)(2,1)S(1)}, bf16[768,768]{1,0:T(8,128)(2,1)S(1)}, u32[]{:S(2)}, u32[]{:S(2)}) collective-permute-start(bf16[768,768]{1,0:T(8,128)(2,1)S(1)} %get-tuple-element.75), channel_id=1, source_target_pairs={{0,1},{1,0},{2,3},{3,2},{4,5},{5,4},{6,7},{7,6},{8,9},{9,8},{10,11... | collective-permute-start | bytes 3538952 | tf_op jit(solution)/shard_map/ppermute | solution.py:12
  34.3 3.6 %collective-permute-start.7 = (bf16[128,2048]{1,0:T(8,128)(2,1)S(1)}, bf16[128,2048]{1,0:T(8,128)(2,1)S(1)}, u32[]{:S(2)}, u32[]{:S(2)}) collective-permute-start(bf16[128,2048]{1,0:T(8,128)(2,1)S(1)} %collective-permute-done.5.refs_2_), channel_id=1, source_target_pairs={{0,1},{1,0},{2,3},{3,2},{4,5},{5,4},{6,7},{7,6},{8,9},{9,8},{10,11... | collective-permute-start | bytes 1572872 | tf_op jit(solution)/shard_map/ppermute | solution.py:12
  34.8 3.8 %collective-permute-start.8 = (bf16[128,2048]{1,0:T(8,128)(2,1)S(1)}, bf16[128,2048]{1,0:T(8,128)(2,1)S(1)}, u32[]{:S(2)}, u32[]{:S(2)}) collective-permute-start(bf16[128,2048]{1,0:T(8,128)(2,1)S(1)} %collective-permute-done.6.refs_4_), channel_id=1, source_target_pairs={{0,1},{1,0},{2,3},{3,2},{4,5},{5,4},{6,7},{7,6},{8,9},{9,8},{10,11... | collective-permute-start | bytes 1572872 | tf_op jit(solution)/shard_map/ppermute | solution.py:12
  34.8 14.3 %collective-permute-start.10 = (bf16[128,2048]{1,0:T(8,128)(2,1)S(1)}, bf16[128,2048]{1,0:T(8,128)(2,1)S(1)}, u32[]{:S(2)}, u32[]{:S(2)}) collective-permute-start(bf16[128,2048]{1,0:T(8,128)(2,1)S(1)} %collective-permute-done.5.refs_2_), channel_id=1, source_target_pairs={{0,4},{1,5},{4,8},{5,9},{8,12},{9,13},{12,14},{13,15},{14,10},{15,... | collective-permute-start | bytes 1572872 | tf_op jit(solution)/shard_map/ppermute | solution.py:514
  35.5 14.1 %collective-permute-start.11 = (bf16[128,2048]{1,0:T(8,128)(2,1)S(1)}, bf16[128,2048]{1,0:T(8,128)(2,1)S(1)}, u32[]{:S(2)}, u32[]{:S(2)}) collective-permute-start(bf16[128,2048]{1,0:T(8,128)(2,1)S(1)} %collective-permute-done.6.refs_4_), channel_id=1, source_target_pairs={{0,2},{1,3},{4,0},{5,1},{8,4},{9,5},{12,8},{13,9},{14,12},{15,13},... | collective-permute-start | bytes 1572872 | tf_op jit(solution)/shard_map/ppermute | solution.py:517
  49.6 3.8 %collective-permute-start.14 = (bf16[512,768]{1,0:T(8,128)(2,1)S(1)}, bf16[512,768]{1,0:T(8,128)(2,1)S(1)}, u32[]{:S(2)}, u32[]{:S(2)}) collective-permute-start(bf16[512,768]{1,0:T(8,128)(2,1)S(1)} %get-tuple-element.88), channel_id=1, source_target_pairs={{0,1},{1,0},{2,3},{3,2},{4,5},{5,4},{6,7},{7,6},{8,9},{9,8},{10,11... | collective-permute-start | bytes 2359304 | tf_op jit(solution)/shard_map/ppermute | solution.py:12
  49.6 3.0 %collective-permute-start.12 = (bf16[128,2048]{1,0:T(8,128)(2,1)S(1)}, bf16[128,2048]{1,0:T(8,128)(2,1)S(1)}, u32[]{:S(2)}, u32[]{:S(2)}) collective-permute-start(bf16[128,2048]{1,0:T(8,128)(2,1)S(1)} %collective-permute-done.10.refs_2_.even_ref), channel_id=1, source_target_pairs={{0,1},{1,0},{2,3},{3,2},{4,5},{5,4},{6,7},{7,6},{8,9},{9,8},{10,11... | collective-permute-start | bytes 1572872 | tf_op jit(solution)/shard_map/ppermute | solution.py:12
  50.1 3.3 %collective-permute-start.13 = (bf16[128,2048]{1,0:T(8,128)(2,1)S(1)}, bf16[128,2048]{1,0:T(8,128)(2,1)S(1)}, u32[]{:S(2)}, u32[]{:S(2)}) collective-permute-start(bf16[128,2048]{1,0:T(8,128)(2,1)S(1)} %collective-permute-done.11.refs_4_.odd_ref), channel_id=1, source_target_pairs={{0,1},{1,0},{2,3},{3,2},{4,5},{5,4},{6,7},{7,6},{8,9},{9,8},{10,11... | collective-permute-start | bytes 1572872 | tf_op jit(solution)/shard_map/ppermute | solution.py:12
  50.2 9.6 %collective-permute-start.15 = (bf16[128,2048]{1,0:T(8,128)(2,1)S(1)}, bf16[128,2048]{1,0:T(8,128)(2,1)S(1)}, u32[]{:S(2)}, u32[]{:S(2)}) collective-permute-start(bf16[128,2048]{1,0:T(8,128)(2,1)S(1)} %pick_by_core.1), channel_id=1, source_target_pairs={{0,4},{1,3},{4,8},{5,1},{8,12},{9,5},{12,14},{13,9},{14,10},{15,13... | collective-permute-start | bytes 1572872 | tf_op jit(solution)/shard_map/ppermute | solution.py:567
  59.7 1.9 %collective-permute-start.17 = (bf16[128,2048]{1,0:T(8,128)(2,1)S(1)}, bf16[128,2048]{1,0:T(8,128)(2,1)S(1)}, u32[]{:S(2)}, u32[]{:S(2)}) collective-permute-start(bf16[128,2048]{1,0:T(8,128)(2,1)S(1)} %collective-permute-done.15.refs_2_), channel_id=1, source_target_pairs={{0,1},{1,0},{2,3},{3,2},{4,5},{5,4},{6,7},{7,6},{8,9},{9,8},{10,11... | collective-permute-start | bytes 1572872 | tf_op jit(solution)/shard_map/ppermute | solution.py:12
  59.9 3.1 %collective-permute-start.16 = (bf16[512,768]{1,0:T(8,128)(2,1)S(1)}, bf16[512,768]{1,0:T(8,128)(2,1)S(1)}, u32[]{:S(2)}, u32[]{:S(2)}) collective-permute-start(bf16[512,768]{1,0:T(8,128)(2,1)S(1)} %get-tuple-element.98), channel_id=1, source_target_pairs={{0,1},{1,0},{2,3},{3,2},{4,5},{5,4},{6,7},{7,6},{8,9},{9,8},{10,11... | collective-permute-start | bytes 2359304 | tf_op jit(solution)/shard_map/ppermute | solution.py:12
  62.8 2.8 %collective-permute-start.18 = (bf16[256,768]{1,0:T(8,128)(2,1)S(1)}, bf16[256,768]{1,0:T(8,128)(2,1)S(1)}, u32[]{:S(2)}, u32[]{:S(2)}) collective-permute-start(bf16[256,768]{1,0:T(8,128)(2,1)S(1)} %get-tuple-element.117), channel_id=1, source_target_pairs={{0,1},{1,0},{2,3},{3,2},{4,5},{5,4},{6,7},{7,6},{8,9},{9,8},{10,11... | collective-permute-start | bytes 1179656 | tf_op jit(solution)/shard_map/ppermute | solution.py:12
